TPU v7x, 32 devices: a whole 2x2x4 slice. The times are simulated.
32 devices in a mesh: head: 4 (over x, core), blk: 8 (over z, y).
Axes of the slice: x: 2, y: 2, z: 4, core: 2. Of those that a mesh axis runs over, the one named last changes fastest.
Arguments:
- inputs: bfloat16 [2, 8, 256, 2048], P(None, 'blk', 'head'), may hold values from -6 to 6
- norm_gain: bfloat16 [2048], P(('head', 'blk')), may hold values from 0.099609375 to 1.8984375
- norm_bias: bfloat16 [2048], P(('head', 'blk')), may hold values from -4 to 4
- triple_weight: bfloat16 [2048, 6144], P(('head', 'blk')), may hold values from -0.125 to 0.125
- triple_bias: bfloat16 [6144], P(('head', 'blk')), may hold values from -6 to 6
- dense_weight: bfloat16 [2048, 2048], P(('head', 'blk')), may hold values from -1 to 1
- dense_bias: bfloat16 [2048], P(('head', 'blk')), may hold values from -4 to 4
- expand_weight: bfloat16 [2048, 8192], P(('head', 'blk')), may hold values from -0.125 to 0.125
- expand_bias: bfloat16 [8192], P(('head', 'blk')), may hold values from -6 to 6
- shrink_weight: bfloat16 [2048, 8192], P(('head', 'blk')), may hold values from -0.09375 to 0.09375
- shrink_bias: bfloat16 [2048], P(('head', 'blk')), may hold values from -4 to 4
- lengths: int32 [2], replicated, may hold values from 256 to 2048, as said below
- block_order: int32 [8], replicated, may hold values from 0 to 7, each once
- cotangent: bfloat16 [2, 8, 256, 2048], P(None, 'blk', 'head'), may hold values from -6 to 6
Outputs:
- output: bfloat16 [2, 8, 256, 2048], P(None, 'blk', 'head')
- grad_inputs: bfloat16 [2, 8, 256, 2048], P(None, 'blk', 'head')
- grad_norm_gain: float32 [2048], P(('head', 'blk'))
- grad_norm_bias: float32 [2048], P(('head', 'blk'))
- grad_triple_weight: float32 [2048, 6144], P(('head', 'blk'))
- grad_triple_bias: float32 [6144], P(('head', 'blk'))
- grad_dense_weight: float32 [2048, 2048], P(('head', 'blk'))
- grad_dense_bias: float32 [2048], P(('head', 'blk'))
- grad_expand_weight: float32 [2048, 8192], P(('head', 'blk'))
- grad_expand_bias: float32 [8192], P(('head', 'blk'))
- grad_shrink_weight: float32 [2048, 8192], P(('head', 'blk'))
- grad_shrink_bias: float32 [2048], P(('head', 'blk'))
Inputs may be any that keep to these rules, and one draw needn't show every extreme that they name: `lengths`: some micro-batch has all 2048 slots valid. `block_order`: each block index appears once.
All inputs are finite; a program needn't handle non-finite values.
Results may differ from a plain program's by a relative error of at most 0.013.
Values may be sent and summed in bfloat16 or wider, within the bound.
No kernel may reach another device: no remote copies, remote signals or barrier semaphores. Data moves between devices by JAX's collectives and lax.ppermute only.
A program may use at most 704 MiB of HBM per device.

v0:
```python
import jax
import jax.numpy as jnp
from jax import lax
from jax.sharding import PartitionSpec as P

FF = 8192
HEADS = 32
HEAD_DIM = 64
ROT = 32


neg_large = -1e30


def layer_norm(values, gain, shift):
    centred = values - jnp.mean(values, -1, keepdims=True)
    variance = jnp.mean(centred * centred, -1, keepdims=True)
    return centred * lax.rsqrt(variance + 1e-05) * gain + shift


def gelu_tanh(values):
    return jax.nn.gelu(values, approximate=True)


def rotary_tables(positions, rot_dims):
    half = rot_dims // 2
    inverse = 10000.0 ** (-(jnp.arange(half, dtype=jnp.float32) * 2.0) / rot_dims)
    angles = positions.astype(jnp.float32)[:, None] * inverse[None, :]
    return (jnp.cos(angles), jnp.sin(angles))


def rotate(pair, cosine, sine, rot_dims):
    half = rot_dims // 2
    first = pair[..., :half]
    second = pair[..., half:rot_dims]
    return jnp.concatenate(
        [first * cosine - second * sine, second * cosine + first * sine, pair[..., rot_dims:]], -1
    )


def rotate_back(pair, cosine, sine, rot_dims):
    half = rot_dims // 2
    first = pair[..., :half]
    second = pair[..., half:rot_dims]
    return jnp.concatenate(
        [first * cosine + second * sine, second * cosine - first * sine, pair[..., rot_dims:]], -1
    )


def dot_rows(left, right):
    return lax.dot_general(
        left, right, (((1,), (1,)), ((), ())), preferred_element_type=jnp.float32
    )


def dot_cols(left, right):
    return lax.dot_general(
        left, right, (((0,), (0,)), ((), ())), preferred_element_type=jnp.float32
    )


def key_positions(begin_at, row_count, block_order, local_rows):
    indices = begin_at + jnp.arange(row_count, dtype=jnp.int32)
    owners = indices // local_rows
    hits = owners[:, None] == jnp.arange(block_order.shape[0], dtype=jnp.int32)[None, :]
    placed = jnp.sum(jnp.where(hits, block_order[None, :], 0), 1)
    return placed * local_rows + indices % local_rows


def allowed_mask(key_pos, query_pos, lengths):
    causal = key_pos[None, None, :] <= query_pos[None, :, None]
    inside = key_pos[None, None, :] < lengths[:, None, None]
    return (causal & inside)[:, :, None, :]


def block_steps():
    return 512


def score_grads(
    query_rows,
    grad_out_rows,
    lse_rows,
    delta_rows,
    query_at,
    key_rows,
    value_rows,
    key_at,
    lengths,
    scale,
):
    scores = (
        jnp.einsum("bqhd,bkhd->bqhk", query_rows, key_rows, preferred_element_type=jnp.float32)
        * scale
    )
    allowed = allowed_mask(key_at, query_at, lengths)
    masked = jnp.where(allowed, scores, neg_large)
    probs = jnp.where(allowed, jnp.exp(masked - lse_rows[..., None]), 0.0)
    grad_probs = jnp.einsum(
        "bqhd,bkhd->bqhk", grad_out_rows, value_rows, preferred_element_type=jnp.float32
    )
    grad_scores = (probs * (grad_probs - delta_rows[..., None])).astype(jnp.bfloat16)
    return (probs, grad_scores)


def body(
    inputs,
    norm_gain,
    norm_bias,
    triple_weight,
    triple_bias,
    dense_weight,
    dense_bias,
    expand_weight,
    expand_bias,
    shrink_weight,
    shrink_bias,
    lengths,
    block_order,
    cotangent,
):
    batches = inputs.shape[0]
    share = inputs.shape[2]
    width = inputs.shape[3]
    groups = lax.axis_size("head")
    local_rows = groups * share
    blocks = block_order.shape[0]
    whole = local_rows * blocks
    heads_here = HEADS // groups
    head_dim = HEAD_DIM
    lane_width = heads_here * head_dim
    scale = head_dim ** (-0.5)
    rows = batches * share
    own_block = jnp.sum(
        jnp.where(jnp.arange(blocks, dtype=jnp.int32) == lax.axis_index("blk"), block_order, 0)
    )
    query_pos = own_block * local_rows + jnp.arange(local_rows, dtype=jnp.int32)
    token_pos = (
        own_block * local_rows + lax.axis_index("head") * share + jnp.arange(share, dtype=jnp.int32)
    )
    valid = (token_pos[None, :] < lengths[:, None]).astype(jnp.float32).reshape(rows, 1)
    gain_all, shift_all, triple_b, expand_b, dense_b, shrink_b = (
        lax.all_gather(norm_gain, ("head", "blk"), axis=0, tiled=True),
        lax.all_gather(norm_bias, ("head", "blk"), axis=0, tiled=True),
        lax.all_gather(triple_bias, ("head", "blk"), axis=0, tiled=True),
        lax.all_gather(expand_bias, ("head", "blk"), axis=0, tiled=True),
        lax.all_gather(dense_bias, ("head", "blk"), axis=0, tiled=True),
        lax.all_gather(shrink_bias, ("head", "blk"), axis=0, tiled=True),
    )
    source = inputs.reshape(rows, width).astype(jnp.float32)
    gain_f = gain_all.astype(jnp.float32)
    shift_f = shift_all.astype(jnp.float32)
    normed, norm_back = jax.vjp(layer_norm, source, gain_f, shift_f)
    normed_b = normed.astype(jnp.bfloat16)
    triple_rows = lax.all_gather(triple_weight, ("head", "blk"), axis=0, tiled=True)
    expand_rows = lax.all_gather(expand_weight, ("head", "blk"), axis=0, tiled=True)
    columns = normed_b
    lin_acc = jnp.dot(columns, triple_rows, preferred_element_type=jnp.float32)
    exp_acc = jnp.dot(columns, expand_rows, preferred_element_type=jnp.float32)
    linear = (lin_acc + triple_b.astype(jnp.float32)).reshape(rows, 3, HEADS, head_dim)
    expand_pre = exp_acc + expand_b.astype(jnp.float32)
    cosine, sine = rotary_tables(token_pos, ROT)
    cos_rows = jnp.tile(cosine, (batches, 1))[:, None, None, :]
    sin_rows = jnp.tile(sine, (batches, 1))[:, None, None, :]
    turned = jnp.concatenate(
        [rotate(linear[:, :2], cos_rows, sin_rows, ROT), linear[:, 2:]], 1
    ).astype(jnp.bfloat16)
    heads_in = lax.all_to_all(
        turned.reshape(batches, share, 3, groups, lane_width),
        "head",
        split_axis=3,
        concat_axis=1,
        tiled=True,
    )
    queries = heads_in[:, :, 0, 0].reshape(batches, local_rows, heads_here, head_dim)
    keys_local = heads_in[:, :, 1, 0]
    values_local = heads_in[:, :, 2, 0]

    def attend(carried, key_rows, value_rows, key_pos):
        running_max, running_sum, weighted = carried
        row_count = key_rows.shape[1]
        key_four = key_rows.reshape(batches, row_count, heads_here, head_dim)
        value_four = value_rows.reshape(batches, row_count, heads_here, head_dim)
        scores = (
            jnp.einsum("bqhd,bkhd->bqhk", queries, key_four, preferred_element_type=jnp.float32)
            * scale
        )
        allowed = allowed_mask(key_pos, query_pos, lengths)
        masked = jnp.where(allowed, scores, neg_large)
        fresh_max = jnp.maximum(running_max, jnp.max(masked, -1))
        factor = jnp.exp(running_max - fresh_max)
        probs = jnp.where(allowed, jnp.exp(masked - fresh_max[..., None]), 0.0)
        running_sum = running_sum * factor + jnp.sum(probs, -1)
        weighted = weighted * factor[..., None] + jnp.einsum(
            "bqhk,bkhd->bqhd",
            probs.astype(jnp.bfloat16),
            value_four,
            preferred_element_type=jnp.float32,
        )
        return (fresh_max, running_sum, weighted)

    start_state = (
        jnp.full((batches, local_rows, heads_here), neg_large, jnp.float32),
        jnp.zeros((batches, local_rows, heads_here), jnp.float32),
        jnp.zeros((batches, local_rows, heads_here, head_dim), jnp.float32),
    )
    carried = start_state
    key_rows = lax.all_gather(keys_local, "blk", axis=1, tiled=True)
    value_rows = lax.all_gather(values_local, "blk", axis=1, tiled=True)
    row_count = key_rows.shape[1]
    fold_step_rows = block_steps()

    def one_step(inner, offset):
        part_keys = lax.dynamic_slice_in_dim(key_rows, offset, fold_step_rows, 1)
        part_values = lax.dynamic_slice_in_dim(value_rows, offset, fold_step_rows, 1)
        return (
            attend(
                inner,
                part_keys,
                part_values,
                key_positions(offset, fold_step_rows, block_order, local_rows),
            ),
            None,
        )

    carried, unused = lax.scan(
        one_step, carried, jnp.arange(row_count // fold_step_rows, dtype=jnp.int32) * fold_step_rows
    )
    final_max, final_sum, weighted = carried
    log_sum = final_max + jnp.log(final_sum)
    attn_full = weighted / final_sum[..., None]
    attn_heads = attn_full.astype(jnp.bfloat16).reshape(batches, local_rows, 1, lane_width)
    attn_tok = lax.all_to_all(attn_heads, "head", split_axis=1, concat_axis=2, tiled=True).reshape(
        rows, width
    )
    expand_out, gelu_back = jax.vjp(gelu_tanh, expand_pre)
    expand_low = expand_out.astype(jnp.bfloat16)
    carried = jnp.zeros((rows, width), jnp.float32)
    dense_rows = lax.all_gather(dense_weight, ("head", "blk"), axis=0, tiled=True)
    shrink_rows = lax.all_gather(shrink_weight, ("head", "blk"), axis=0, tiled=True)
    columns = attn_tok
    carried = jnp.dot(columns, dense_rows, preferred_element_type=jnp.float32)
    mixed = carried + dot_rows(expand_low, shrink_rows)
    result = valid * (source + mixed + dense_b.astype(jnp.float32) + shrink_b.astype(jnp.float32))
    output = result.astype(jnp.bfloat16).reshape(inputs.shape)
    grad_y = (cotangent.reshape(rows, width).astype(jnp.float32) * valid).astype(jnp.bfloat16)
    dense_rows = lax.all_gather(dense_weight, ("head", "blk"), axis=0, tiled=True)
    shrink_rows = lax.all_gather(shrink_weight, ("head", "blk"), axis=0, tiled=True)
    grad_att = dot_rows(grad_y, dense_rows)
    columns = grad_y
    grad_att, grad_exp = (
        grad_att,
        jnp.dot(columns, shrink_rows, preferred_element_type=jnp.float32),
    )
    grad_pre = gelu_back(grad_exp)[0].astype(jnp.bfloat16)
    grad_heads = lax.all_to_all(
        grad_att.astype(jnp.bfloat16).reshape(batches, share, groups, lane_width),
        "head",
        split_axis=2,
        concat_axis=1,
        tiled=True,
    )
    grad_heads = grad_heads.reshape(batches, local_rows, heads_here, head_dim)
    delta = jnp.sum(grad_heads.astype(jnp.float32) * attn_full, -1)
    keys_all, values_all = (
        lax.all_gather(keys_local, "blk", axis=1, tiled=True),
        lax.all_gather(values_local, "blk", axis=1, tiled=True),
    )
    step_rows = block_steps()
    query_zero = jnp.zeros((batches, local_rows, heads_here, head_dim), jnp.float32)

    def back_step(block_index, state):
        grad_query, grad_key_all, grad_value_all = state
        offset = block_index * step_rows
        part_keys = lax.dynamic_slice_in_dim(keys_all, offset, step_rows, 1).reshape(
            batches, step_rows, heads_here, head_dim
        )
        part_values = lax.dynamic_slice_in_dim(values_all, offset, step_rows, 1).reshape(
            batches, step_rows, heads_here, head_dim
        )
        key_pos = key_positions(offset, step_rows, block_order, local_rows)
        probs, grad_scores = score_grads(
            queries,
            grad_heads,
            log_sum,
            delta,
            query_pos,
            part_keys,
            part_values,
            key_pos,
            lengths,
            scale,
        )
        grad_query = (
            grad_query
            + jnp.einsum(
                "bqhk,bkhd->bqhd", grad_scores, part_keys, preferred_element_type=jnp.float32
            )
            * scale
        )
        key_part = (
            jnp.einsum("bqhk,bqhd->bkhd", grad_scores, queries, preferred_element_type=jnp.float32)
            * scale
        )
        value_part = jnp.einsum(
            "bqhk,bqhd->bkhd",
            probs.astype(jnp.bfloat16),
            grad_heads,
            preferred_element_type=jnp.float32,
        )
        grad_key_all = lax.dynamic_update_slice_in_dim(grad_key_all, key_part, offset, 1)
        grad_value_all = lax.dynamic_update_slice_in_dim(grad_value_all, value_part, offset, 1)
        return (grad_query, grad_key_all, grad_value_all)

    back_state = (
        query_zero,
        jnp.zeros((batches, whole, heads_here, head_dim), jnp.float32),
        jnp.zeros((batches, whole, heads_here, head_dim), jnp.float32),
    )
    grad_query, grad_key_all, grad_value_all = lax.fori_loop(
        0, whole // step_rows, back_step, back_state
    )
    grad_keys, grad_values = (
        lax.psum_scatter(
            grad_key_all.reshape(batches, whole, lane_width).astype(jnp.bfloat16),
            "blk",
            scatter_dimension=1,
            tiled=True,
        ).astype(jnp.float32),
        lax.psum_scatter(
            grad_value_all.reshape(batches, whole, lane_width).astype(jnp.bfloat16),
            "blk",
            scatter_dimension=1,
            tiled=True,
        ).astype(jnp.float32),
    )
    stacked = jnp.stack(
        [grad_query.reshape(batches, local_rows, lane_width), grad_keys, grad_values], 2
    ).astype(jnp.bfloat16)[:, :, :, None, :]
    back_tok = (
        lax.all_to_all(stacked, "head", split_axis=1, concat_axis=3, tiled=True)
        .reshape(rows, 3, HEADS, head_dim)
        .astype(jnp.float32)
    )
    unturned = jnp.concatenate(
        [rotate_back(back_tok[:, :2], cos_rows, sin_rows, ROT), back_tok[:, 2:]], 1
    )
    grad_lin = unturned.reshape(rows, 3 * width).astype(jnp.bfloat16)
    triple_rows = lax.all_gather(triple_weight, ("head", "blk"), axis=0, tiled=True)
    expand_rows = lax.all_gather(expand_weight, ("head", "blk"), axis=0, tiled=True)
    new_cols = dot_rows(grad_lin, triple_rows) + dot_rows(grad_pre, expand_rows)
    grad_source, grad_gain, grad_shift = norm_back(new_cols)
    grad_inputs = (
        (grad_source + grad_y.astype(jnp.float32)).astype(jnp.bfloat16).reshape(inputs.shape)
    )
    summed = lax.psum_scatter(
        jnp.concatenate(
            [
                dot_cols(normed_b, grad_lin),
                dot_cols(normed_b, grad_pre),
                dot_cols(attn_tok, grad_y),
                dot_cols(grad_y, expand_low),
            ],
            1,
        ),
        ("head", "blk"),
        scatter_dimension=0,
        tiled=True,
    )
    edge_one = 3 * width
    edge_two = edge_one + FF
    edge_three = edge_two + width
    grad_triple_weight = summed[:, :edge_one]
    grad_expand_weight = summed[:, edge_one:edge_two]
    grad_dense_weight = summed[:, edge_two:edge_three]
    grad_shrink_weight = summed[:, edge_three:]
    out_sum = jnp.sum(grad_y.astype(jnp.float32), 0)
    small_gain, small_shift, small_triple, small_expand, small_out = (
        lax.psum_scatter(grad_gain, ("head", "blk"), scatter_dimension=0, tiled=True),
        lax.psum_scatter(grad_shift, ("head", "blk"), scatter_dimension=0, tiled=True),
        lax.psum_scatter(
            jnp.sum(grad_lin.astype(jnp.float32), 0),
            ("head", "blk"),
            scatter_dimension=0,
            tiled=True,
        ),
        lax.psum_scatter(
            jnp.sum(grad_pre.astype(jnp.float32), 0),
            ("head", "blk"),
            scatter_dimension=0,
            tiled=True,
        ),
        lax.psum_scatter(out_sum, ("head", "blk"), scatter_dimension=0, tiled=True),
    )
    return (
        output,
        grad_inputs,
        small_gain,
        small_shift,
        grad_triple_weight,
        small_triple,
        grad_dense_weight,
        small_out,
        grad_expand_weight,
        small_expand,
        grad_shrink_weight,
        small_out,
    )


def solution(mesh):
    placed = (
        P(None, "blk", "head", None),
        P(("head", "blk")),
        P(("head", "blk")),
        P(("head", "blk"), None),
        P(("head", "blk")),
        P(("head", "blk"), None),
        P(("head", "blk")),
        P(("head", "blk"), None),
        P(("head", "blk")),
        P(("head", "blk"), None),
        P(("head", "blk")),
        P(),
        P(),
        P(None, "blk", "head", None),
    )
    return jax.shard_map(
        body,
        mesh=mesh,
        in_specs=placed,
        out_specs=(
            P(None, "blk", "head", None),
            P(None, "blk", "head", None),
            P(("head", "blk")),
            P(("head", "blk")),
            P(("head", "blk"), None),
            P(("head", "blk")),
            P(("head", "blk"), None),
            P(("head", "blk")),
            P(("head", "blk"), None),
            P(("head", "blk")),
            P(("head", "blk"), None),
            P(("head", "blk")),
        ),
        check_vma=False,
    )
```

profile of v0, /device:TPU:0, one launch (start us, length us, event | category | flops | bytes accessed | tf_op | source)
XLA Modules:
  0.0 2866.4 jit_solution(13788845547572712688)
XLA Ops:
  16.3 43.8 %all-reduce.11 = (bf16[2048]{0:T(1024)(128)(2,1)S(1)}, bf16[2048]{0:T(1024)(128)(2,1)S(1)}, bf16[6144]{0:T(1024)(128)(2,1)S(1)}, bf16[2048]{0:T(1024)(128)(2,1)}, bf16[2048]{0:T(1024)(128)(2,1)}) all-reduce(bf16[2048]{0:T(1024)(128)(2,1)S(1)} %dynamic-update-slice.1, ...), channel_id=1, replica_groups=mesh['head'=4,'blk'=8] {'head','blk'}, use_global_device_ids=true, to_apply=%add.1 | all-reduce | flops 14336 | bytes 57344
  63.8 105.8 %all-gather.10.cloned.1.call-done = bf16[2048,6144]{1,0:T(8,128)(2,1)} async-done(((bf16[64,6144]{1,0:T(8,128)(2,1)}), bf16[2048,6144]{1,0:T(8,128)(2,1)}) %all-gather.10.cloned.1.call-update) | async-done | bytes 25165840 | tf_op jit(solution)/shard_map/all_gather | solution.py:155
  169.7 13.2 convolution_add_fusion.1
  187.2 3.2 reshape.594
  190.4 3.7 copy.171
  200.4 24.1 all_to_all.57
  228.5 23.3 all-gather.12.cloned.1.call-done
  251.7 6.3 convolution_convert_fusion
  259.3 3.5 all-to-all-start.2
  262.8 8.7 all-to-all-done.2
  274.2 52.2 %all-gather.20.cloned.1.call-done = bf16[2,2048,1,1,512]{4,1,2,0,3:T(8,128)(2,1)} async-done(((bf16[2,256,1,1,512]{4,1,2,0,3:T(8,128)(2,1)}), bf16[2,2048,1,1,512]{4,1,2,0,3:T(8,128)(2,1)}) %all-gather.20.cloned.1.call-update) | async-done | bytes 4194320 | tf_op jit(solution)/shard_map/all_gather | solution.py:209
  326.4 6.3 copy.176
  332.7 68.0 %all-gather.18.cloned.1.call-done = bf16[2,2048,1,1,512]{4,1,2,0,3:T(8,128)(2,1)} async-done(((bf16[2,256,1,1,512]{4,1,2,0,3:T(8,128)(2,1)}), bf16[2,2048,1,1,512]{4,1,2,0,3:T(8,128)(2,1)}) %all-gather.18.cloned.1.call-update) | async-done | bytes 4194320 | tf_op jit(solution)/shard_map/all_gather | solution.py:208
  400.7 6.3 copy.175
  407.0 56.7 %while.37 = (s32[]{:T(128)}, f32[2,256,8]{1,2,0:T(8,128)S(1)}, f32[2,256,8]{1,2,0:T(8,128)S(1)}, f32[2,256,8,64]{1,3,2,0:T(8,128)}, s32[4]{0:T(128)S(1)}, /*inde...) while((s32[]{:T(128)}, f32[2,256,8]{1,2,0:T(8,128)S(1)}, ...), condition=%wide.region_7.8_spmd.clone, body=%wide.region_3.7_spmd.clone.sunk | while | flops 565362432 | bytes 44058932 | solution.py:226
  411.4 3.0 constant_dynamic-slice_fusion.6
  425.8 2.7 constant_dynamic-slice_fusion.6
  439.9 2.7 constant_dynamic-slice_fusion.6
  454.1 2.6 constant_dynamic-slice_fusion.6
  465.9 2.5 broadcast.625.clone
  468.4 2.5 broadcast.625
  470.9 65.6 %while.38 = (s32[]{:T(128)}, f32[2,256,8,64]{1,3,2,0:T(8,128)S(1)}, bf16[2,2048,8,64]{1,3,2,0:T(8,128)(2,1)}, bf16[2,2048,8,64]{1,3,2,0:T(8,128)(2,1)}, bf16[2,2...) while((s32[]{:T(128)}, f32[2,256,8,64]{1,3,2,0:T(8,128)S(1)}, ...), condition=%wide.region_11.12_spmd.clone, body=%wide.region_9.11_spmd.clone.sunk | while | flops 1369075456 | bytes 121702792 | solution.py:320
  474.9 3.2 fusion.153
  481.2 2.8 copy-done.4
  490.9 3.2 fusion.153
  497.2 3.7 copy-done.4
  507.8 3.2 fusion.153
  514.1 2.9 copy-done.4
  523.9 3.2 fusion.153
  530.2 2.9 copy-done.4
  537.1 66.8 %all-gather.2 = bf16[32,1,256]{2,1,0:T(2,128)(2,1)S(1)} all-gather(bf16[1,1,256]{2,1,0:T(2,128)(2,1)S(1)} %reshape.586), channel_id=1, replica_groups=mesh['head'=4,'blk'=8] {'head','blk'}, dimensions={0}, use_global_device_ids=true | all-gather | bytes 16896 | tf_op jit(solution)/shard_map/all_gather | solution.py:146
  606.0 3.5 all-to-all-start.1
  611.8 11.1 all-to-all-done.1
  623.4 8.1 fusion.74
  631.6 18.0 fusion.71
  649.6 143.4 %all-gather.14.cloned.1.call-done = bf16[2048,8192]{1,0:T(8,128)(2,1)} async-done(((bf16[64,8192]{1,0:T(8,128)(2,1)}), bf16[2048,8192]{1,0:T(8,128)(2,1)}) %all-gather.14.cloned.1.call-update) | async-done | bytes 33554448 | tf_op jit(solution)/shard_map/all_gather | solution.py:156
  793.0 19.1 convert_reduce_fusion.1
  812.1 27.2 fusion.62
  839.4 44.0 %reduce-scatter.6.cloned.1.call-done = bf16[2,256,512]{1,2,0:T(8,128)(2,1)} async-done(((bf16[2,2048,512]{1,2,0:T(8,128)(2,1)}), bf16[2,256,512]{1,2,0:T(8,128)(2,1)}) %reduce-scatter.6.cloned.1.call-update) | async-done | bytes 524304 | tf_op jit(solution)/shard_map/reduce_scatter | solution.py:330
  883.3 92.3 %reduce-scatter.4.cloned.1.call-done = bf16[2,256,512]{1,2,0:T(8,128)(2,1)} async-done(((bf16[2,2048,512]{1,2,0:T(8,128)(2,1)}), bf16[2,256,512]{1,2,0:T(8,128)(2,1)}) %reduce-scatter.4.cloned.1.call-update) | async-done | bytes 524304 | tf_op jit(solution)/shard_map/reduce_scatter | solution.py:324
  975.6 2.7 pad_maximum_fusion.2
  978.3 4.9 copy.186
  983.2 4.4 all-to-all-start.3
  987.7 23.5 fusion.73
  1013.3 3.7 copy.188
  1017.0 6.0 reshape.572
  1023.1 2.8 slice.80
  1025.9 2.9 slice.79
  1028.8 8.2 fusion.66
  1037.0 3.8 copy.208
  1040.8 4.4 copy.207
  1047.1 4.5 copy.191
  1051.6 3.8 copy.192
  1055.5 5.5 convert_reduce_fusion
  1061.6 4.5 copy.193
  1066.2 14.2 fusion.70
  1080.4 17.5 fusion.63
  1097.9 20.9 fusion.72
  1120.0 130.9 %pad_maximum_fusion = f32[2048,24576]{1,0:T(8,128)} fusion(f32[2048,8192]{1,0:T(8,128)} %fusion.62, f32[2048,2048]{1,0:T(8,128)} %fusion.74, f32[2048,8192]{1,0:T(8,128)} %fusion.73, f32[2048,6144]{1,0:T(8,128)} %fusion.72), kind=kLoop, calls=%fused_computation.75 | loop fusion | flops 150994944 | bytes 402653184 | tf_op jit(solution)/shard_map/concatenate | solution.py:357
  1252.0 4.7 fusion.69
  1256.8 24.4 fusion.55
  1288.5 1561.2 %reduce-scatter.8.cloned.1.call-done = f32[64,24576]{1,0:T(8,128)} async-done(((f32[2048,24576]{1,0:T(8,128)}), f32[64,24576]{1,0:T(8,128)}) %reduce-scatter.8.cloned.1.call-update) | async-done | bytes 6291472 | tf_op jit(solution)/shard_map/reduce_scatter | solution.py:356
  2851.5 2.7 slice.81
  2854.2 4.6 fusion.65
  (349 shorter events, 132.1 us)
Async XLA Ops:
  7.2 162.5 %all-gather.10.cloned.1.call-start = ((), (), s32[]{:S(2)}) async-start(), calls=%async_computation.7 | async-start | bytes 25952256 | tf_op jit(solution)/shard_map/all_gather | solution.py:155
  7.9 243.8 %all-gather.12.cloned.1.call-start = ((), (), s32[]{:S(2)}) async-start(), calls=%async_computation.8 | async-start | bytes 8650752 | tf_op jit(solution)/shard_map/all_gather | solution.py:239
  8.7 317.7 %all-gather.20.cloned.1.call-start = ((), (), s32[]{:S(2)}) async-start(), calls=%async_computation.15 | async-start | bytes 4718592 | tf_op jit(solution)/shard_map/all_gather | solution.py:209
  9.9 4.6 copy-start.32
  10.0 159.6 %copy-start.34 = (f32[128]{0:T(128)}, f32[128]{0:T(128)S(1)}, u32[]{:S(2)}) copy-start(f32[128]{0:T(128)S(1)} %div.56) | copy-start | bytes 1540
  12.0 157.6 %copy-start.37 = (f32[128]{0:T(128)}, f32[128]{0:T(128)S(1)}, u32[]{:S(2)}) copy-start(f32[128]{0:T(128)S(1)} %rsqrt.13) | copy-start | bytes 1540
  60.1 109.6 %copy-start.28 = (f32[2048]{0:T(1024)}, f32[2048]{0:T(1024)S(1)}, u32[]{:S(2)}) copy-start(f32[2048]{0:T(1024)S(1)} %convert_element_type.193) | copy-start | bytes 24580
  60.1 109.6 %copy-start.21 = (f32[2048]{0:T(1024)}, f32[2048]{0:T(1024)S(1)}, u32[]{:S(2)}) copy-start(f32[2048]{0:T(1024)S(1)} %convert_element_type.192) | copy-start | bytes 24580
  62.3 131.8 %copy-start.24 = (f32[128,16]{0,1:T(8,128)}, f32[128,16]{0,1:T(8,128)S(1)}, u32[]{:S(2)}) copy-start(f32[128,16]{0,1:T(8,128)S(1)} %tile.17) | copy-start | bytes 24580
  62.4 131.7 %copy-start.26 = (f32[128,16]{0,1:T(8,128)}, f32[128,16]{0,1:T(8,128)S(1)}, u32[]{:S(2)}) copy-start(f32[128,16]{0,1:T(8,128)S(1)} %tile.19) | copy-start | bytes 24580
  63.8 105.8 %copy-start.13 = (bf16[128,2048]{1,0:T(8,128)(2,1)}, bf16[128,2048]{1,0:T(8,128)(2,1)S(1)}, u32[]{:S(2)}) copy-start(bf16[128,2048]{1,0:T(8,128)(2,1)S(1)} %add_convert_fusion.2) | copy-start | bytes 1572868
  224.5 3.8 copy-start.15
  225.8 174.8 %all-gather.18.cloned.1.call-start = ((), (), s32[]{:S(2)}) async-start(), calls=%async_computation.14 | async-start | bytes 4718592 | tf_op jit(solution)/shard_map/all_gather | solution.py:208
  226.4 405.2 %all-gather.16.cloned.1.call-start = ((), (), s32[]{:S(2)}) async-start(), calls=%async_computation.10 | async-start | bytes 34603008 | tf_op jit(solution)/shard_map/all_gather | solution.py:240
  227.0 566.0 %all-gather.14.cloned.1.call-start = ((), (), s32[]{:S(2)}) async-start(), calls=%async_computation.9 | async-start | bytes 34603008 | tf_op jit(solution)/shard_map/all_gather | solution.py:156
  228.3 23.4 copy-start.45
  228.4 29.5 %copy-start.9 = (bf16[128,2048]{1,0:T(8,128)(2,1)}, bf16[128,2048]{1,0:T(8,128)(2,1)S(1)}, u32[]{:S(2)}) copy-start(bf16[128,2048]{1,0:T(8,128)(2,1)S(1)} %fusion.56) | copy-start | bytes 1572868
  259.3 12.3 all-to-all-start.2
  262.7 620.6 %reduce-scatter.6.cloned.1.call-start = ((), (), s32[]{:S(2)}) async-start(), calls=%async_computation.12 | async-start | bytes 4718592 | tf_op jit(solution)/shard_map/reduce_scatter | solution.py:330
  400.7 6.3 copy-start.31
  474.9 3.2 copy-start.2
  480.3 5.1 copy-start.3
  480.3 3.7 copy-start.4
  496.3 5.9 copy-start.3
  496.3 4.5 copy-start.4
  513.3 5.1 copy-start.3
  513.3 3.8 copy-start.4
  523.9 3.2 copy-start.2
  529.4 5.1 copy-start.3
  529.4 3.8 copy-start.4
  536.5 67.5 %copy-start.16 = (bf16[2,1,64,2048]{3,2,1,0:T(8,128)(2,1)S(1)}, bf16[2,1,64,2048]{3,2,1,0:T(8,128)(2,1)}, u32[]{:S(2)}) copy-start(bf16[2,1,64,2048]{3,2,1,0:T(8,128)(2,1)} %param.31) | copy-start | bytes 1572868
  536.5 67.5 %copy-start.41 = (f32[2,64]{1,0:T(2,128)S(1)}, f32[2,64]{1,0:T(2,128)}, u32[]{:S(2)}) copy-start(f32[2,64]{1,0:T(2,128)} %copy-done.40) | copy-start | bytes 1540
  536.5 68.3 %copy-start.18 = (bf16[2,256,8,64]{1,3,2,0:T(8,128)(2,1)S(1)}, bf16[2,256,8,64]{1,3,2,0:T(8,128)(2,1)}, u32[]{:S(2)}) copy-start(bf16[2,256,8,64]{1,3,2,0:T(8,128)(2,1)} %get-tuple-element.837) | copy-start | bytes 1572868
  536.5 73.2 %copy-start = (bf16[2,1,64,2048]{3,2,1,0:T(8,128)(2,1)S(1)}, bf16[2,1,64,2048]{3,2,1,0:T(8,128)(2,1)}, u32[]{:S(2)}) copy-start(bf16[2,1,64,2048]{3,2,1,0:T(8,128)(2,1)} %param.18) | copy-start | bytes 1572868
  536.5 73.2 %copy-start.22 = (f32[2048]{0:T(1024)S(1)}, f32[2048]{0:T(1024)}, u32[]{:S(2)}) copy-start(f32[2048]{0:T(1024)} %copy-done.21) | copy-start | bytes 24580
  536.5 73.2 %copy-start.29 = (f32[2048]{0:T(1024)S(1)}, f32[2048]{0:T(1024)}, u32[]{:S(2)}) copy-start(f32[2048]{0:T(1024)} %copy-done.28) | copy-start | bytes 24580
  536.5 73.2 %copy-start.33 = (f32[2,64]{1,0:T(2,128)S(1)}, f32[2,64]{1,0:T(2,128)}, u32[]{:S(2)}) copy-start(f32[2,64]{1,0:T(2,128)} %copy-done.32) | copy-start | bytes 1540
  536.5 73.2 %copy-start.44 = (f32[2,64]{1,0:T(2,128)S(1)}, f32[2,64]{1,0:T(2,128)}, u32[]{:S(2)}) copy-start(f32[2,64]{1,0:T(2,128)} %get-tuple-element.838) | copy-start | bytes 1540
  606.0 16.9 all-to-all-start.1
  609.5 366.2 %reduce-scatter.4.cloned.1.call-start = ((), (), s32[]{:S(2)}) async-start(), calls=%async_computation.11 | async-start | bytes 4718592 | tf_op jit(solution)/shard_map/reduce_scatter | solution.py:324
  623.4 8.2 copy-start.11
  623.4 8.2 copy-start.10
  812.1 175.5 %copy-start.6 = (bf16[128,8192]{1,0:T(8,128)(2,1)}, bf16[128,8192]{1,0:T(8,128)(2,1)S(1)}, u32[]{:S(2)}) copy-start(bf16[128,8192]{1,0:T(8,128)(2,1)S(1)} %get-tuple-element.814) | copy-start | bytes 6291460
  975.6 12.1 copy-start.14
  983.2 28.0 all-to-all-start.3
  987.6 294.9 %all-reduce.14.cloned.1.call-start = ((), (), s32[]{:S(2)}) async-start(), calls=%async_computation.16 | async-start | bytes 163840
  1037.0 8.2 copy-start.25
  1037.0 8.2 copy-start.27
  1066.2 14.2 copy-start.35
  1080.4 17.5 copy-start.52
  1097.9 21.0 copy-start.7
  1097.9 21.0 copy-start.47
  1097.9 21.0 copy-start.38
  1120.0 1729.7 %reduce-scatter.8.cloned.1.call-start = ((), (), s32[]{:S(2)}) async-start(), calls=%async_computation.13 | async-start | bytes 207618048 | tf_op jit(solution)/shard_map/reduce_scatter | solution.py:356
  1252.0 4.7 copy-start.1
  1252.0 4.7 copy-start.46
  1256.7 24.5 copy-start.49
  1256.7 24.5 copy-start.8
  1256.7 24.5 copy-start.17
  1256.7 24.5 copy-start.23
  1256.7 24.5 copy-start.36
  1256.7 24.5 copy-start.39
  1256.7 24.5 copy-start.48
  1284.5 1574.2 %copy-start.53 = (f32[64]{0:T(128)}, f32[64]{0:T(128)S(1)}, u32[]{:S(2)}) copy-start(f32[64]{0:T(128)S(1)} %dynamic-slice.3) | copy-start | bytes 772
  (21 other events, 35.8 us)
Sparse Core Ops, SparseCore 0:
  10.9 158.6 all-gather.9
  172.6 79.0 all-gather.11
  254.5 71.8 all-gather.19
  329.0 71.6 all-gather.17
  403.5 193.4 all-gather.15
  599.8 193.1 all-gather.13
  796.6 86.6 reduce-scatter.5
  887.4 88.1 reduce-scatter.3
  1120.1 122.6 all-reduce.13
  1251.1 1598.5 reduce-scatter.7
where the time goes:
time: 2880 us; the launch traced here: 2870 us
  waiting for transfers between devices  2110 us (73%)
  matrix products  249 us (9%)
  other arithmetic  176 us (6%)
  local copies, waits for them, and re-layouts  157 us (5%)
  blocking collectives  135 us (5%)
    reduce_scatter x1, waiting for transfers between devices, body(): lax.psum_scatter(jnp.concatenate([dot_cols(normed_b, grad_lin), dot_cols(...  1560 us
    all_gather x1, waiting for transfers between devices, body(): lax.all_gather(expand_weight, ('head', 'blk'), axis=0, tiled=True)  143 us
    concatenate x1, other arithmetic, body(): jnp.concatenate([dot_cols(normed_b, grad_lin), dot_cols(normed_b, grad_pr...  131 us
    all_gather x1, waiting for transfers between devices, body(): lax.all_gather(triple_weight, ('head', 'blk'), axis=0, tiled=True)  106 us
    reduce_scatter x1, waiting for transfers between devices, body(): lax.psum_scatter(grad_key_all.reshape(batches, whole, lane_width).astype(...  92.3 us
    dot_general x4, matrix products, dot_cols(): lax.dot_general(left, right, (((0,), (0,)), ((), ())), preferred_element_...  79.8 us
    all_gather x1, waiting for transfers between devices, body(): key_rows = lax.all_gather(keys_local, 'blk', axis=1, tiled=True)  68 us
    all_gather x1, blocking collectives, body(): lax.all_gather(expand_bias, ('head', 'blk'), axis=0, tiled=True)  66.8 us
  transfers between devices with their start and end apart: 13, of which 10 were waited for; matrix products, arithmetic and copies ran while one was open for 15% of the time, Pallas kernels for 0%

commit v1 on v0

v1 whole, which is shorter than its diff:
```python
import functools

import jax
import jax.numpy as jnp
from jax import lax
from jax.experimental import pallas as pl
from jax.experimental.pallas import tpu as pltpu
from jax.sharding import Mesh
from jax.sharding import PartitionSpec as P

HEADS = 32
HEAD_DIM = 64
ROT = 32
EPS = 1e-05
NEG = -1e30
BF = jnp.bfloat16
F32 = jnp.float32

RANK = ("hx", "bz", "by")
ALL = ("hx", "core", "bs", "bz", "by")
Z_LEN = 4
SWAP = [(0, 1), (1, 0)]
UP = [(i, (i + 1) % Z_LEN) for i in range(Z_LEN)]
DOWN = [((i + 1) % Z_LEN, i) for i in range(Z_LEN)]
VMEM_LIMIT = 50 * 1024 * 1024


def swap(value, axis):
    return lax.ppermute(value, axis, SWAP)


def dot_rows(left, right):
    return lax.dot_general(left, right, (((1,), (1,)), ((), ())), preferred_element_type=F32)


def dot_cols(left, right):
    return lax.dot_general(left, right, (((0,), (0,)), ((), ())), preferred_element_type=F32)


def dot(left, right):
    return jnp.dot(left, right, preferred_element_type=F32)


def gather_pieces(own, other):
    first, second = [own], [other]
    both = jnp.stack([own, other])
    for _ in range(Z_LEN - 1):
        both = lax.ppermute(both, "bz", UP)
        first.append(both[0])
        second.append(both[1])
    rows = []
    for a, b in zip(first, second):
        a_y = swap(a, "by")
        b_x = swap(b, "hx")
        a_pair = jnp.stack([a, a_y])
        b_pair = jnp.stack([b, b_x])
        a_far = swap(a_pair, "hx")
        b_far = swap(b_pair, "by")
        rows += [a, b, a_far[0], b_x, a_y, b_far[0], a_far[1], b_far[1]]
    return jnp.concatenate(rows, 0)


def add_low(left, right):
    return (left.astype(F32) + right.astype(F32)).astype(BF)


def scatter_sum(parts, share, width):
    parts = parts.reshape(Z_LEN, 2, 2, 2, share, width)
    carried = None
    for kz in range(Z_LEN - 1, -1, -1):
        a = parts[kz, :, :, 0]
        b = parts[kz, :, :, 1]
        a_half = add_low(a[:, 0], swap(a[:, 1], "hx"))
        b_half = add_low(b[0], swap(b[1], "by"))
        a_sum = a_half[0].astype(F32) + swap(a_half[1], "by").astype(F32)
        b_sum = b_half[0].astype(F32) + swap(b_half[1], "hx").astype(F32)
        total = jnp.stack([a_sum, b_sum])
        if carried is not None:
            total = total + lax.ppermute(carried, "bz", DOWN).astype(F32)
        carried = total.astype(BF)
    return total


def turn(value, cosine, sine, lane):
    near = jnp.where(
        (lane % HEAD_DIM) < ROT // 2,
        pltpu.roll(value, 128 - ROT // 2, 1),
        pltpu.roll(value, ROT // 2, 1),
    )
    return value * cosine + near * sine


def front_kernel(x_ref, gain_ref, shift_ref, w_ref, bias_ref, cos_ref, sin_ref, h_ref, q_ref, kv_ref, pre_ref, out_ref):
    x = x_ref[...].astype(F32)
    centred = x - jnp.mean(x, -1, keepdims=True)
    variance = jnp.mean(centred * centred, -1, keepdims=True)
    h = (centred * lax.rsqrt(variance + EPS) * gain_ref[...] + shift_ref[...]).astype(BF)
    h_ref[...] = h
    linear = dot(h, w_ref[...]) + bias_ref[...]
    lane = lax.broadcasted_iota(jnp.int32, (x.shape[0], 128), 1)
    cosine, sine = cos_ref[...], sin_ref[...]
    q_ref[...] = turn(linear[:, :128], cosine, sine, lane).astype(BF) * BF(HEAD_DIM**-0.5)
    kv_ref[:, :128] = turn(linear[:, 128:256], cosine, sine, lane).astype(BF)
    kv_ref[:, 128:] = linear[:, 256:384].astype(BF)
    pre = linear[:, 384:]
    pre_ref[...] = pre
    out_ref[...] = (0.5 * pre * (1.0 + jnp.tanh(0.7978845608 * (pre + 0.044715 * pre * pre * pre)))).astype(BF)


def front(x, gain, shift, weight, bias, cosine, sine, block):
    rows, width = x.shape
    cols = weight.shape[1]
    wide = cols - 384
    by_row = lambda n: pl.BlockSpec((block, n), lambda i: (i, 0))
    whole = lambda r, n: pl.BlockSpec((r, n), lambda i: (0, 0))
    return pl.pallas_call(
        front_kernel,
        grid=(rows // block,),
        in_specs=[by_row(width), whole(1, width), whole(1, width), whole(width, cols), whole(1, cols), by_row(128), by_row(128)],
        out_specs=[by_row(width), by_row(128), by_row(256), by_row(wide), by_row(wide)],
        out_shape=[
            jax.ShapeDtypeStruct((rows, width), BF),
            jax.ShapeDtypeStruct((rows, 128), BF),
            jax.ShapeDtypeStruct((rows, 256), BF),
            jax.ShapeDtypeStruct((rows, wide), F32),
            jax.ShapeDtypeStruct((rows, wide), BF),
        ],
        compiler_params=pltpu.CompilerParams(vmem_limit_bytes=VMEM_LIMIT),
        cost_estimate=pl.CostEstimate(
            flops=2 * rows * width * cols + 12 * rows * width, bytes_accessed=rows * width * 6, transcendentals=rows * wide
        ),
    )(x, gain, shift, weight, bias, cosine, sine)


def two_heads(value):
    lane = lax.broadcasted_iota(jnp.int32, value.shape, 1)
    zero = jnp.zeros_like(value)
    return jnp.concatenate([jnp.where(lane < HEAD_DIM, value, zero), jnp.where(lane < HEAD_DIM, zero, value)], 0)


def one_row(value):
    half = value.shape[0] // 2
    lane = lax.broadcasted_iota(jnp.int32, (half, 128), 1)
    return jnp.where(lane < HEAD_DIM, value[:half], value[half:])


def allowed_pairs(table_ref, block, query_at, key_at):
    turned, length = table_ref[0], table_ref[1]
    shape = (2 * block, block)
    query = query_at * block + ((lax.broadcasted_iota(jnp.int32, shape, 0) & (block - 1)) ^ turned)
    key = key_at * block + (lax.broadcasted_iota(jnp.int32, shape, 1) ^ turned)
    return (key <= query) & (key < length)


def key_ranges(table_ref, block, query_at):
    length = table_ref[1]
    plain = jnp.minimum(query_at, length // block)
    last = jnp.minimum(query_at + 1, (length + block - 1) // block)
    return plain, last


def attend_kernel(blocks, block, table_ref, q_ref, kv_ref, full_ref, low_ref, lse_ref):
    query_at = table_ref[2 + pl.program_id(0)]
    queries = two_heads(q_ref[...])

    def step(masked, at, state):
        top, total, mixed = state
        begin = pl.multiple_of(table_ref[2 + blocks + at] * block, block)
        keys = kv_ref[pl.ds(begin, block), :128]
        values = kv_ref[pl.ds(begin, block), 128:]
        scores = dot_rows(queries, keys)
        if masked:
            allowed = allowed_pairs(table_ref, block, query_at, at)
            scores = jnp.where(allowed, scores, NEG)
        fresh = jnp.maximum(top, jnp.max(scores, -1, keepdims=True))
        factor = jnp.exp(top - fresh)
        weights = jnp.exp(scores - fresh)
        if masked:
            weights = jnp.where(allowed, weights, 0.0)
        total = total * factor + jnp.sum(weights, -1, keepdims=True)
        return fresh, total, mixed * factor + dot(weights.astype(BF), values)

    state = (
        jnp.full((2 * block, 1), NEG, F32),
        jnp.zeros((2 * block, 1), F32),
        jnp.zeros((2 * block, 128), F32),
    )
    plain, last = key_ranges(table_ref, block, query_at)
    state = lax.fori_loop(0, plain, functools.partial(step, False), state)
    top, total, mixed = lax.fori_loop(plain, last, functools.partial(step, True), state)
    full = one_row(mixed / total)
    full_ref[...] = full
    low_ref[...] = full.astype(BF)
    lse_ref[...] = jnp.broadcast_to(top + jnp.log(total), lse_ref.shape)


def attend(table, q, kv, block):
    rows = q.shape[0]
    keys = kv.shape[0]
    blocks = rows // block
    by_row = lambda r, n: pl.BlockSpec((r, n), lambda i, t: (i, 0))
    whole = lambda r, n: pl.BlockSpec((r, n), lambda i, t: (0, 0))
    return pl.pallas_call(
        functools.partial(attend_kernel, blocks, block),
        grid_spec=pltpu.PrefetchScalarGridSpec(
            num_scalar_prefetch=1,
            grid=(blocks,),
            in_specs=[by_row(block, 128), whole(keys, 256)],
            out_specs=[by_row(block, 128), by_row(block, 128), by_row(2 * block, 128)],
        ),
        out_shape=[
            jax.ShapeDtypeStruct((rows, 128), F32),
            jax.ShapeDtypeStruct((rows, 128), BF),
            jax.ShapeDtypeStruct((2 * rows, 128), F32),
        ],
        compiler_params=pltpu.CompilerParams(vmem_limit_bytes=VMEM_LIMIT),
        cost_estimate=pl.CostEstimate(
            flops=16 * rows * keys * 128, bytes_accessed=rows * 128 * 16, transcendentals=rows * keys
        ),
    )(table, q, kv)


def attend_back_kernel(blocks, block, table_ref, q_ref, kv_ref, full_ref, lse_ref, grad_ref, dq_ref, dkv_ref, dk_acc, dv_acc):
    at_block = pl.program_id(0)
    query_at = table_ref[2 + at_block]
    queries = two_heads(q_ref[...])
    grads = two_heads(grad_ref[...])
    full = full_ref[...]
    delta = jnp.sum(grads.astype(F32) * jnp.concatenate([full, full], 0), -1, keepdims=True)
    lse = lse_ref[:, :1]

    @pl.when(at_block == 0)
    def _():
        dk_acc[...] = jnp.zeros_like(dk_acc)
        dv_acc[...] = jnp.zeros_like(dv_acc)

    def step(masked, at, grad_query):
        begin = pl.multiple_of(table_ref[2 + blocks + at] * block, block)
        rows = pl.ds(begin, block)
        keys = kv_ref[rows, :128]
        values = kv_ref[rows, 128:]
        scores = dot_rows(queries, keys)
        if masked:
            allowed = allowed_pairs(table_ref, block, query_at, at)
            scores = jnp.where(allowed, scores, NEG)
        weights = jnp.exp(scores - lse)
        if masked:
            weights = jnp.where(allowed, weights, 0.0)
        grad_scores = (weights * (dot_rows(grads, values) - delta)).astype(BF)
        dk_acc[rows, :] += dot_cols(grad_scores, queries)
        dv_acc[rows, :] += dot_cols(weights.astype(BF), grads)
        return grad_query + dot(grad_scores, keys)

    plain, last = key_ranges(table_ref, block, query_at)
    grad_query = jnp.zeros((2 * block, 128), F32)
    grad_query = lax.fori_loop(0, plain, functools.partial(step, False), grad_query)
    grad_query = lax.fori_loop(plain, last, functools.partial(step, True), grad_query)
    dq_ref[...] = (one_row(grad_query) * HEAD_DIM**-0.5).astype(BF)

    @pl.when(at_block == blocks - 1)
    def _():
        dkv_ref[:, :128] = dk_acc[...].astype(BF)
        dkv_ref[:, 128:] = dv_acc[...].astype(BF)


def attend_back(table, q, kv, full, lse, grad, block):
    rows = q.shape[0]
    keys = kv.shape[0]
    blocks = rows // block
    by_row = lambda r, n: pl.BlockSpec((r, n), lambda i, t: (i, 0))
    whole = lambda r, n: pl.BlockSpec((r, n), lambda i, t: (0, 0))
    return pl.pallas_call(
        functools.partial(attend_back_kernel, blocks, block),
        grid_spec=pltpu.PrefetchScalarGridSpec(
            num_scalar_prefetch=1,
            grid=(blocks,),
            in_specs=[by_row(block, 128), whole(keys, 256), by_row(block, 128), by_row(2 * block, 128), by_row(block, 128)],
            out_specs=[by_row(block, 128), whole(keys, 256)],
            scratch_shapes=[pltpu.VMEM((keys, 128), F32), pltpu.VMEM((keys, 128), F32)],
        ),
        out_shape=[jax.ShapeDtypeStruct((rows, 128), BF), jax.ShapeDtypeStruct((keys, 256), BF)],
        compiler_params=pltpu.CompilerParams(vmem_limit_bytes=VMEM_LIMIT),
        cost_estimate=pl.CostEstimate(
            flops=40 * rows * keys * 128, bytes_accessed=rows * 128 * 24, transcendentals=rows * keys
        ),
    )(table, q, kv, full, lse, grad)


def turn_tables(positions):
    half = ROT // 2
    inverse = 10000.0 ** (-(jnp.arange(half, dtype=F32) * 2.0) / ROT)
    angles = positions.astype(F32)[:, None] * inverse[None, :]
    cosine, sine = jnp.cos(angles), jnp.sin(angles)
    rest = (positions.shape[0], HEAD_DIM - ROT)
    cosine = jnp.concatenate([cosine, cosine, jnp.ones(rest, F32)], 1)
    sine = jnp.concatenate([-sine, sine, jnp.zeros(rest, F32)], 1)
    return jnp.tile(cosine, (1, 2)), jnp.tile(sine, (1, 2))


def near_columns():
    lane = jnp.arange(256, dtype=jnp.int32)
    within = lane % HEAD_DIM
    source = jnp.where(within < ROT // 2, lane + ROT // 2, jnp.where(within < ROT, lane - ROT // 2, lane))
    return (lane[:, None] == source[None, :]).astype(BF)


def core_pair(own, other, core):
    return jnp.where(core == 0, jnp.stack([own, other], 1), jnp.stack([other, own], 1))


def body(
    inputs,
    norm_gain,
    norm_bias,
    triple_weight,
    triple_bias,
    dense_weight,
    dense_bias,
    expand_weight,
    expand_bias,
    shrink_weight,
    shrink_bias,
    lengths,
    block_order,
    cotangent,
):
    share, width = inputs.shape[2], inputs.shape[3]
    hx, core, bs, bz, by = (lax.axis_index(name) for name in ALL)
    spread = lax.axis_size("bs")
    ranks = 2 * Z_LEN * 2
    devices = 2 * ranks * spread
    block = 4 * share
    rows = ranks * 2 * share
    near_blocks = Z_LEN * 2
    blocks = block_order.shape[0]
    held = width // devices
    ff = expand_weight.shape[1]
    ff_here = ff // ranks
    length = lengths[core]

    def block_at(index):
        return jnp.sum(jnp.where(jnp.arange(blocks, dtype=jnp.int32) == index, block_order, 0))

    token_pos = (
        block_at(bs * near_blocks + bz * 2 + by) * block
        + (hx * 2 + core) * share
        + jnp.arange(share, dtype=jnp.int32)
    )
    valid = (token_pos[None, :] < lengths[:, None]).astype(F32)[:, :, None]

    def near_at(group):
        return jnp.stack(
            [
                block_at(group * near_blocks + ((bz + Z_LEN - kz) % Z_LEN) * 2 + (by + ky) % 2)
                for kz in range(Z_LEN)
                for ky in range(2)
            ]
        )

    query_at = near_at(bs)
    turned = hx * 2 * share + core * share
    row_pos = (query_at[:, None] * block + (jnp.arange(block, dtype=jnp.int32) ^ turned)[None, :]).reshape(rows)
    key_at = jnp.concatenate([near_at(group) for group in range(spread)])
    spots = jnp.arange(blocks, dtype=jnp.int32)
    order = jnp.sum(jnp.where(key_at[None, :] == spots[:, None], spots[None, :], 0), 1)
    table = jnp.concatenate([jnp.stack([turned, length]), query_at, order]).astype(jnp.int32)
    cosine, sine = turn_tables(row_pos)

    x_mine = jnp.where(core == 0, inputs[0, 0], inputs[1, 0])
    x_away = jnp.where(core == 0, inputs[1, 0], inputs[0, 0])
    x_all = gather_pieces(x_mine, swap(x_away, "core"))

    small = jnp.concatenate([norm_gain, norm_bias, triple_bias, expand_bias, dense_bias, shrink_bias])
    cuts = [0]
    for leaf in (norm_gain, norm_bias, triple_bias, expand_bias, dense_bias, shrink_bias):
        cuts.append(cuts[-1] + leaf.shape[0])
    small = lax.all_gather(small, ALL, axis=0, tiled=False).reshape(devices, cuts[-1])
    gain, shift, triple_b, expand_b, dense_b, shrink_b = (
        small[:, low:high].reshape(-1).astype(F32) for low, high in zip(cuts[:-1], cuts[1:])
    )
    rank = hx * near_blocks + bz * 2 + by
    bias_triple = lax.dynamic_index_in_dim(
        triple_b.reshape(3, 2, 2, near_blocks, HEAD_DIM).transpose(1, 3, 0, 2, 4).reshape(ranks, 384), rank, 0
    )
    bias_expand = lax.dynamic_index_in_dim(expand_b.reshape(ranks, ff_here), rank, 0)
    bias_in = jnp.concatenate([bias_triple, bias_expand], 1)
    sent = jnp.concatenate(
        [
            triple_weight.reshape(held, 3, 2, 2, near_blocks, HEAD_DIM).transpose(2, 4, 0, 1, 3, 5).reshape(ranks, held, 384),
            expand_weight.reshape(held, ranks, ff_here).transpose(1, 0, 2),
            shrink_weight.reshape(held, ranks, ff_here).transpose(1, 0, 2),
        ],
        2,
    )
    got = lax.all_to_all(sent, RANK, split_axis=0, concat_axis=0, tiled=True)
    cols = got.shape[2]
    got = got.reshape(2, 1, near_blocks, held, cols)
    if spread > 1:
        got = lax.all_gather(got, "bs", axis=1, tiled=True)
    got = core_pair(got, swap(got, "core"), core).reshape(width, cols)
    edge = 384 + ff_here
    weight_in = got[:, :edge]
    if spread == 1:
        dense_pair = core_pair(dense_weight[None], swap(dense_weight, "core")[None], core).reshape(128, width)
    else:
        dense_all = lax.all_gather(dense_weight, ALL, axis=0, tiled=True).reshape(2, 2, near_blocks, HEAD_DIM, width)
        dense_pair = lax.dynamic_index_in_dim(
            lax.dynamic_index_in_dim(dense_all, hx, 0, keepdims=False), bz * 2 + by, 1, keepdims=False
        ).reshape(128, width)
    weight_out = jnp.concatenate([dense_pair.T, got[:, edge:]], 1)

    h, q, kv, pre, expand_out = front(x_all, gain[None], shift[None], weight_in, bias_in, cosine, sine, block)
    kv_all = kv if spread == 1 else lax.all_gather(kv, "bs", axis=0, tiled=True)
    attn_full, attn_low, lse = attend(table, q, kv_all, block)
    branches = jnp.concatenate([attn_low, expand_out], 1)
    out_parts = dot_rows(branches, weight_out).astype(BF)
    out_sum = scatter_sum(out_parts, share, width)

    grad_y = (cotangent[:, 0].astype(F32) * valid).astype(BF)
    g_mine = jnp.where(core == 0, grad_y[0], grad_y[1])
    g_away = jnp.where(core == 0, grad_y[1], grad_y[0])
    g_all = gather_pieces(g_mine, swap(g_away, "core"))

    out_away = swap(out_sum[1].astype(BF), "core").astype(F32)
    mixed = jnp.where(core == 0, jnp.stack([out_sum[0], out_away]), jnp.stack([out_away, out_sum[0]]))
    source = inputs[:, 0].astype(F32)
    output = (valid * (source + mixed + dense_b + shrink_b)).astype(BF).reshape(inputs.shape)

    grad_branches = dot(g_all, weight_out)
    grad_attention = grad_branches[:, :128].astype(BF)
    _, gelu_back = jax.vjp(lambda u: jax.nn.gelu(u, approximate=True), pre)
    grad_pre = gelu_back(grad_branches[:, 128:])[0].astype(BF)
    dq, dkv = attend_back(table, q, kv_all, attn_full, lse, grad_attention, block)
    if spread > 1:
        dkv = lax.psum_scatter(dkv, "bs", scatter_dimension=0, tiled=True)
    turned_grads = jnp.concatenate([dq, dkv[:, :128]], 1)
    plain_grads = turned_grads.astype(F32) * jnp.tile(cosine, (1, 2)) - dot(turned_grads, near_columns()) * jnp.tile(
        sine, (1, 2)
    )
    grad_in = jnp.concatenate([plain_grads.astype(BF), dkv[:, 128:], grad_pre], 1)
    h_parts = dot_rows(grad_in, weight_in).astype(BF)
    h_sum = scatter_sum(h_parts, share, width)
    grad_weight_out = dot_cols(g_all, branches)
    grad_weight_in = dot_cols(h, grad_in)

    both = jnp.concatenate([grad_weight_in, grad_weight_out[:, 128:]], 1).reshape(2, 2, spread, near_blocks, held, cols)
    mine = lax.dynamic_index_in_dim(both, core, 1, keepdims=False)
    away = lax.dynamic_index_in_dim(both, 1 - core, 1, keepdims=False).astype(BF)
    mine = mine + swap(away, "core").astype(F32)
    if spread > 1:
        mine = lax.psum_scatter(mine.astype(BF), "bs", scatter_dimension=1, tiled=True)
    mine = mine.astype(BF).reshape(ranks, held, cols)
    back = lax.all_to_all(mine, RANK, split_axis=0, concat_axis=0, tiled=True).astype(F32)
    grad_triple = (
        back[:, :, :384]
        .reshape(2, near_blocks, held, 3, 2, HEAD_DIM)
        .transpose(2, 3, 0, 4, 1, 5)
        .reshape(held, 3 * width)
    )
    grad_expand = back[:, :, 384:edge].transpose(1, 0, 2).reshape(held, ff)
    grad_shrink = back[:, :, edge:].transpose(1, 0, 2).reshape(held, ff)
    dense_grads = grad_weight_out[:, :128].T.reshape(2, HEAD_DIM, width)
    if spread == 1:
        dense_mine = lax.dynamic_index_in_dim(dense_grads, core, 0, keepdims=False)
        dense_away = lax.dynamic_index_in_dim(dense_grads, 1 - core, 0, keepdims=False)
        grad_dense = dense_mine + swap(dense_away.astype(BF), "core").astype(F32)
    else:
        spot = jnp.arange(ranks, dtype=jnp.int32).reshape(2, 1, near_blocks, 1, 1) == rank
        dense_whole = jnp.where(spot, dense_grads[None, :, None], 0.0).reshape(width, width)
        grad_dense = lax.psum_scatter(dense_whole, ALL, scatter_dimension=0, tiled=True)

    x_f = x_all.astype(F32)
    x_c = x_f - jnp.mean(x_f, -1, keepdims=True)
    normed_all = x_c * lax.rsqrt(jnp.mean(x_c * x_c, -1, keepdims=True) + EPS)
    parts_f = h_parts.astype(F32)
    sum_gain = jnp.sum(parts_f * normed_all, 0)
    sum_shift = jnp.sum(parts_f, 0)
    sum_in = jnp.sum(grad_in.astype(F32), 0)
    here = jnp.arange(ranks, dtype=jnp.int32)[:, None] == rank
    sum_triple = (
        jnp.where(here, sum_in[None, :384], 0.0)
        .reshape(2, near_blocks, 3, 2, HEAD_DIM)
        .transpose(2, 0, 3, 1, 4)
        .reshape(3 * width)
    )
    sum_expand = jnp.where(here, sum_in[None, 384:], 0.0).reshape(ff)
    sum_y = jnp.sum(grad_y.astype(F32), (0, 1))
    pieces = [leaf.reshape(devices, -1) for leaf in (sum_gain, sum_shift, sum_triple, sum_expand, sum_y)]
    small_sum = lax.psum_scatter(
        jnp.concatenate(pieces, 1).reshape(-1), ALL, scatter_dimension=0, tiled=True
    )
    small_grads = []
    begin = 0
    for piece in pieces:
        small_grads.append(small_sum[begin : begin + piece.shape[1]])
        begin += piece.shape[1]
    small_gain, small_shift, small_triple, small_expand, small_out = small_grads

    h_away = swap(h_sum[1].astype(BF), "core").astype(F32)
    grad_h = jnp.where(core == 0, jnp.stack([h_sum[0], h_away]), jnp.stack([h_away, h_sum[0]]))
    centred = source - jnp.mean(source, -1, keepdims=True)
    scale = lax.rsqrt(jnp.mean(centred * centred, -1, keepdims=True) + EPS)
    normed = centred * scale
    g = grad_h * gain
    grad_source = scale * (
        g - jnp.mean(g, -1, keepdims=True) - normed * jnp.mean(g * normed, -1, keepdims=True)
    )
    grad_inputs = (grad_y.astype(F32) + grad_source).astype(BF).reshape(inputs.shape)
    return (
        output,
        grad_inputs,
        small_gain,
        small_shift,
        grad_triple,
        small_triple,
        grad_dense,
        small_out,
        grad_expand,
        small_expand,
        grad_shrink,
        small_out,
    )


def solution(mesh):
    head, blk = mesh.devices.shape
    split = Mesh(mesh.devices.reshape(head // 2, 2, blk // (2 * Z_LEN), Z_LEN, 2), ALL)
    tokens = P(None, ("bs", "bz", "by"), ("hx", "core"), None)
    vector = P(ALL)
    matrix = P(ALL, None)
    return jax.shard_map(
        body,
        mesh=split,
        in_specs=(
            tokens,
            vector,
            vector,
            matrix,
            vector,
            matrix,
            vector,
            matrix,
            vector,
            matrix,
            vector,
            P(),
            P(),
            tokens,
        ),
        out_specs=(
            tokens,
            tokens,
            vector,
            vector,
            matrix,
            vector,
            matrix,
            vector,
            matrix,
            vector,
            matrix,
            vector,
        ),
        check_vma=False,
    )
```

time: 2880 us -> 891 us (0.31)
  the two profiles are of different devices: /device:TPU:0 before, /device:TPU:9 now
where the time goes in v1:
time: 891 us; the launch traced here: 882 us
  waiting for transfers between devices  300 us (34%)
  starting transfers between devices  167 us (19%)
  local copies, waits for them, and re-layouts  141 us (16%)
  blocking collectives  77.6 us (9%)
  other arithmetic  71.8 us (8%)
  Pallas kernels  55.3 us (6%)
  matrix products  52.5 us (6%)
  between operations  17 us (2%)
    ppermute x72, starting transfers between devices, swap(): return lax.ppermute(value, axis, SWAP)  135 us
    ppermute x72, waiting for transfers between devices, swap(): return lax.ppermute(value, axis, SWAP)  128 us
    unnamed x1, blocking collectives  77.6 us
    unnamed x2, waiting for transfers between devices  77.1 us
    ppermute x6, waiting for transfers between devices, scatter_sum(): total = total + lax.ppermute(carried, 'bz', DOWN).astype(F32)  73.3 us
    unnamed x193, local copies, waits for them, and re-layouts  52.7 us
    ppermute x6, waiting for transfers between devices, gather_pieces(): both = lax.ppermute(both, 'bz', UP)  21.6 us
    dot_general x2, matrix products, dot_rows(): lax.dot_general(left, right, (((1,), (1,)), ((), ())), preferred_element_...  21.6 us
  transfers between devices with their start and end apart: 87, of which 34 were waited for; matrix products, arithmetic and copies ran while one was open for 19% of the time, Pallas kernels for 0%

profile of v1, /device:TPU:9, one launch (start us, length us, event | category | flops | bytes accessed | tf_op | source)
XLA Modules:
  0.0 882.0 jit_solution(13800125172456920306)
XLA Ops:
  12.9 2.5 copy.251
  15.4 2.5 copy.250
  26.9 5.7 all-to-all-start
  38.7 77.6 %all-reduce = bf16[22528]{0:T(1024)(128)(2,1)S(1)} all-reduce(bf16[22528]{0:T(1024)(128)(2,1)S(1)} %dynamic-update-slice), channel_id=2, replica_groups=mesh['hx'=2,'core'=2,'bs'=1,'bz'=4,'by'=2] {'hx','core','bs','bz','by'}, use_global_device_ids=true, to_apply=%add | all-reduce | flops 22528 | bytes 90112
  117.0 5.0 stack.294
  131.0 5.7 concatenate.83.table_ref
  149.9 2.8 collective-permute-done.5
  152.8 3.8 collective-permute-done.2
  160.1 4.6 collective-permute-done.47
  186.0 10.3 %collective-permute-done.52 = bf16[2,64,2048]{2,1,0:T(8,128)(2,1)S(1)} collective-permute-done((bf16[2,64,2048]{2,1,0:T(8,128)(2,1)S(1)}, bf16[2,64,2048]{2,1,0:T(8,128)(2,1)S(1)}, u32[]{:S(2)}, u32[]{:S(2)}) %collective-permute-start.52) | collective-permute-done | bytes 524320 | tf_op jit(solution)/shard_map/ppermute | solution.py:48
  198.1 6.7 collective-permute-done.13
  206.5 6.7 collective-permute-done.55
  213.2 4.3 collective-permute-start.15
  227.0 3.2 collective-permute-done.57
  230.7 2.9 collective-permute-start.18
  235.3 9.4 %collective-permute-done.16 = bf16[64,2048]{1,0:T(8,128)(2,1)S(1)} collective-permute-done((bf16[64,2048]{1,0:T(8,128)(2,1)S(1)}, bf16[64,2048]{1,0:T(8,128)(2,1)S(1)}, u32[]{:S(2)}, u32[]{:S(2)}) %collective-permute-start.16) | collective-permute-done | bytes 262176 | tf_op jit(solution)/shard_map/ppermute | solution.py:29
  246.6 3.8 collective-permute-done.58
  261.2 3.2 collective-permute-done.19
  265.2 2.5 copy-done.2
  268.9 11.7 %collective-permute-start.20 = (bf16[2,1,8,64,1408]{4,3,2,0,1:T(8,128)(2,1)}, bf16[2,1,8,64,1408]{4,3,2,0,1:T(8,128)(2,1)S(1)}, u32[]{:S(2)}, u32[]{:S(2)}) collective-permute-start(bf16[2,1,8,64,1408]{4,3,2,0,1:T(8,128)(2,1)} %bitcast.48), channel_id=1, source_target_pairs={{0,8},{8,0},{1,9},{9,1},{2,10},{10,2},{3,11},{11,3},{4,12},{12,4},... | collective-permute-start | bytes 8650760 | tf_op jit(solution)/shard_map/ppermute | solution.py:29
  280.6 5.7 fusion.2
  291.8 4.6 maximum_select_fusion
  300.1 9.1 %fusion.15 = f32[2048,640]{1,0:T(8,128)S(1)} fusion(bf16[2048,2048]{1,0:T(8,128)(2,1)} %fusion.85, bf16[2048,512]{1,0:T(8,128)(2,1)S(1)} %slice.674, bf16[2048,128]{1,0:T(8,128)(2,1)S(1)} %bitcast.686), kind=kOutput, calls=%fused_computation.40 | convolution fusion | flops 5373952000 | bytes 16252928 | tf_op jit(solution)/shard_map/dot_general | solution.py:41
  311.7 18.8 %shard_map.229 = (bf16[2048,2048]{1,0:T(8,128)(2,1)}, bf16[2048,128]{1,0:T(8,128)(2,1)S(1)}, bf16[2048,256]{1,0:T(8,128)(2,1)S(1)}, f32[2048,512]{1,0:T(8,128)}, bf16[2048,512]{1,0:T(8,128)(2,1)}) custom-call(bf16[2048,2048]{1,0:T(8,128)(2,1)} %copy-done.2, f32[1,2048]{1,0:T(1,128)S(1)} %reshape.701.gain_ref, f32[1,2048]{1,0:T(1,128)S(1)} %reshape.702.shift_ref, ...), custom_call_target="tpu_custom_call" | custom-call | flops 7566524416 | bytes 25165824 | tf_op jit(solution)/shard_map/pallas_call | solution.py:116
  330.4 6.0 fusion.11
  336.4 16.3 %shard_map.230 = (f32[2048,128]{1,0:T(8,128)S(1)}, bf16[2048,128]{1,0:T(8,128)(2,1)S(1)}, f32[4096,128]{1,0:T(8,128)}) custom-call(s32[18]{0:T(128)S(1)} %concatenate.83.table_ref, bf16[2048,128]{1,0:T(8,128)(2,1)S(1)} %get-tuple-element.22.q_ref, bf16[2048,256]{1,0:T(8,128)(2,1)S(1)} %get-tuple-element.23.kv_ref), custom_call_target="tpu_custom_call" | custom-call | flops 8589934592 | bytes 4194304 | tf_op jit(solution)/shard_map/pallas_call | solution.py:203
  353.7 20.3 %shard_map.231 = (bf16[2048,128]{1,0:T(8,128)(2,1)S(1)}, bf16[2048,256]{1,0:T(8,128)(2,1)S(1)}) custom-call(s32[18]{0:T(128)S(1)} %concatenate.83.table_ref, bf16[2048,128]{1,0:T(8,128)(2,1)S(1)} %get-tuple-element.22.q_ref, bf16[2048,256]{1,0:T(8,128)(2,1)S(1)} %get-tuple-element.23.kv_ref, f32[2048,128]{1,0:T(8,128)} %copy-done, ...), custom_call_target="tpu_custom_call" | custom-call | flops 21474836480 | bytes 6291456 | tf_op jit(solution)/shard_map/pallas_call | solution.py:272
  376.2 14.3 %convert_reduce_fusion.1 = (f32[2048]{0:T(1024)S(1)}, f32[2048]{0:T(1024)S(1)}, bf16[2048,2048]{1,0:T(8,128)(2,1)}) fusion(f32[2048]{0:T(1024)S(1)} %add_rsqrt_fusion, f32[2048]{0:T(1024)S(1)} %broadcast_multiply_fusion, bf16[2048,2048]{1,0:T(8,128)(2,1)} %copy-done.2, bf16[2048,1408]{1,0:T(8,128)(2,1)S(1)} %bitcast.633, bf16[2048,512]{1,0:T(8,128)(2,1)} %fusion.11, ...), kind=kOutput, calls=%fused_computation.2 | convolution fusion | flops 7560753152 | bytes 24150016 | tf_op jit(solution)/shard_map/dot_general | solution.py:33
  390.6 3.0 slice_bitcast_fusion.2
  393.6 2.7 fusion.137
  396.6 7.2 convolution_convert_fusion.1
  407.6 8.7 fusion.148
  433.6 12.5 %fusion.134 = f32[2048,896]{0,1:T(8,128)} fusion(bf16[2048,2048]{1,0:T(8,128)(2,1)} %get-tuple-element.31, bf16[2048,512]{1,0:T(8,128)(2,1)S(1)} %copy-done.5, bf16[2048,128]{1,0:T(8,128)(2,1)} %copy-done.29, bf16[2048,256]{1,0:T(8,128)(2,1)} %copy-done.22), kind=kOutput, calls=%fused_computation.437 | convolution fusion | flops 7527202816 | bytes 19398656 | tf_op jit(solution)/shard_map/dot_general | solution.py:37
  446.1 10.4 %pad_maximum_fusion = f32[2048,1408]{0,1:T(8,128)} fusion(f32[2048,512]{0,1:T(8,128)} %slice.779, f32[2048,896]{0,1:T(8,128)} %fusion.134), kind=kLoop, calls=%fused_computation.8 | loop fusion | flops 2883584 | bytes 23068672 | tf_op jit(solution)/shard_map/concatenate | solution.py:446
  456.5 12.2 %copy.218 = f32[2048,1408]{1,0:T(8,128)} copy(f32[2048,1408]{0,1:T(8,128)} %pad_maximum_fusion) | data formatting | bytes 23068672 | tf_op jit(solution)/shard_map/concatenate | solution.py:446
  470.5 20.7 %collective-permute-start.83 = (bf16[64,2048]{1,0:T(8,128)(2,1)}, bf16[64,2048]{1,0:T(8,128)(2,1)S(1)}, u32[]{:S(2)}, u32[]{:S(2)}) collective-permute-start(bf16[64,2048]{1,0:T(8,128)(2,1)} %fusion.78), channel_id=1, source_target_pairs={{0,8},{8,0},{1,9},{9,1},{2,10},{10,2},{3,11},{11,3},{4,12},{12,4},... | collective-permute-start | bytes 786440 | tf_op jit(solution)/shard_map/ppermute | solution.py:29
  491.2 4.7 fusion.12
  495.9 77.0 %all-reduce.4.cloned.1.call-done = f32[20480]{0:T(1024)} async-done(((f32[20480]{0:T(1024)}), f32[20480]{0:T(1024)}) %all-reduce.4.cloned.1.call-update) | async-done | bytes 81936
  581.8 3.0 fusion.45
  586.7 9.8 %collective-permute-done.66 = bf16[2,64,2048]{2,1,0:T(8,128)(2,1)S(1)} collective-permute-done((bf16[2,64,2048]{2,1,0:T(8,128)(2,1)}, bf16[2,64,2048]{2,1,0:T(8,128)(2,1)S(1)}, u32[]{:S(2)}, u32[]{:S(2)}) %collective-permute-start.66) | collective-permute-done | bytes 524320 | tf_op jit(solution)/shard_map/ppermute | solution.py:29
  597.9 9.8 %collective-permute-done.70 = bf16[2,64,2048]{2,1,0:T(8,128)(2,1)S(1)} collective-permute-done((bf16[2,64,2048]{2,1,0:T(8,128)(2,1)}, bf16[2,64,2048]{2,1,0:T(8,128)(2,1)S(1)}, u32[]{:S(2)}, u32[]{:S(2)}) %collective-permute-start.70) | collective-permute-done | bytes 524320 | tf_op jit(solution)/shard_map/ppermute | solution.py:29
  609.2 9.8 %collective-permute-done.74 = bf16[2,64,2048]{2,1,0:T(8,128)(2,1)S(1)} collective-permute-done((bf16[2,64,2048]{2,1,0:T(8,128)(2,1)}, bf16[2,64,2048]{2,1,0:T(8,128)(2,1)S(1)}, u32[]{:S(2)}, u32[]{:S(2)}) %collective-permute-start.74) | collective-permute-done | bytes 524320 | tf_op jit(solution)/shard_map/ppermute | solution.py:29
  622.8 7.3 collective-permute-start.82
  634.0 6.6 collective-permute-done.26
  642.0 9.8 %collective-permute-done.30 = bf16[2,64,2048]{2,1,0:T(8,128)(2,1)S(1)} collective-permute-done((bf16[2,64,2048]{2,1,0:T(8,128)(2,1)S(1)}, bf16[2,64,2048]{2,1,0:T(8,128)(2,1)S(1)}, u32[]{:S(2)}, u32[]{:S(2)}) %collective-permute-start.30) | collective-permute-done | bytes 524320 | tf_op jit(solution)/shard_map/ppermute | solution.py:29
  653.2 9.8 %collective-permute-done.34 = bf16[2,64,2048]{2,1,0:T(8,128)(2,1)S(1)} collective-permute-done((bf16[2,64,2048]{2,1,0:T(8,128)(2,1)S(1)}, bf16[2,64,2048]{2,1,0:T(8,128)(2,1)S(1)}, u32[]{:S(2)}, u32[]{:S(2)}) %collective-permute-start.34) | collective-permute-done | bytes 524320 | tf_op jit(solution)/shard_map/ppermute | solution.py:29
  664.5 4.2 collective-permute-done.65
  676.0 3.9 collective-permute-done.73
  681.6 9.6 %collective-permute-done.25 = bf16[64,2048]{1,0:T(8,128)(2,1)S(1)} collective-permute-done((bf16[64,2048]{1,0:T(8,128)(2,1)S(1)}, bf16[64,2048]{1,0:T(8,128)(2,1)S(1)}, u32[]{:S(2)}, u32[]{:S(2)}) %collective-permute-start.25) | collective-permute-done | bytes 262176 | tf_op jit(solution)/shard_map/ppermute | solution.py:29
  694.3 4.7 collective-permute-done.29
  702.9 7.1 collective-permute-done.37
  711.3 5.0 collective-permute-done.35
  716.3 5.4 collective-permute-start.78
  722.8 5.5 collective-permute-done.78
  730.8 8.8 collective-permute-done.38
  742.7 8.1 collective-permute-done.79
  756.2 4.6 all-to-all-start.1
  765.9 9.4 %collective-permute-done.80 = bf16[2,64,2048]{2,1,0:T(8,128)(2,1)} collective-permute-done((bf16[2,64,2048]{2,1,0:T(8,128)(2,1)}, bf16[2,64,2048]{2,1,0:T(8,128)(2,1)}, u32[]{:S(2)}, u32[]{:S(2)}) %collective-permute-start.80) | collective-permute-done | bytes 524320 | tf_op jit(solution)/shard_map/ppermute | solution.py:79
  776.8 25.0 %collective-permute-start.81 = (bf16[64,2048]{1,0:T(8,128)(2,1)S(1)}, bf16[64,2048]{1,0:T(8,128)(2,1)S(1)}, u32[]{:S(2)}, u32[]{:S(2)}) collective-permute-start(bf16[64,2048]{1,0:T(8,128)(2,1)S(1)} %fusion.84), channel_id=1, source_target_pairs={{0,8},{8,0},{1,9},{9,1},{2,10},{10,2},{3,11},{11,3},{4,12},{12,4},... | collective-permute-start | bytes 786440 | tf_op jit(solution)/shard_map/ppermute | solution.py:29
  801.8 40.1 %collective-permute-done.40 = bf16[2,64,2048]{2,1,0:T(8,128)(2,1)S(1)} collective-permute-done((bf16[2,64,2048]{2,1,0:T(8,128)(2,1)S(1)}, bf16[2,64,2048]{2,1,0:T(8,128)(2,1)S(1)}, u32[]{:S(2)}, u32[]{:S(2)}) %collective-permute-start.40) | collective-permute-done | bytes 524320 | tf_op jit(solution)/shard_map/ppermute | solution.py:79
  843.3 8.9 %collective-permute-start.41 = (bf16[64,2048]{1,0:T(8,128)(2,1)S(1)}, bf16[64,2048]{1,0:T(8,128)(2,1)S(1)}, u32[]{:S(2)}, u32[]{:S(2)}) collective-permute-start(bf16[64,2048]{1,0:T(8,128)(2,1)S(1)} %fusion.83), channel_id=1, source_target_pairs={{0,8},{8,0},{1,9},{9,1},{2,10},{10,2},{3,11},{11,3},{4,12},{12,4},... | collective-permute-start | bytes 786440 | tf_op jit(solution)/shard_map/ppermute | solution.py:29
  856.7 4.5 reshape.696
  861.2 5.4 copy.268
  866.5 3.3 reshape.697
  (515 shorter events, 206.1 us)
Async XLA Ops:
  9.0 115.7 %collective-permute-start = (bf16[64,2048]{1,0:T(8,128)(2,1)}, bf16[64,2048]{1,0:T(8,128)(2,1)}, u32[]{:S(2)}, u32[]{:S(2)}) collective-permute-start(bf16[64,2048]{1,0:T(8,128)(2,1)} %get-tuple-element.108), channel_id=1, source_target_pairs={{0,8},{8,0},{1,9},{9,1},{2,10},{10,2},{3,11},{11,3},{4,12},{12,4},... | collective-permute-start | bytes 786440 | tf_op jit(solution)/shard_map/ppermute | solution.py:29
  11.6 126.7 %collective-permute-start.1 = (bf16[64,2048]{1,0:T(8,128)(2,1)}, bf16[64,2048]{1,0:T(8,128)(2,1)S(1)}, u32[]{:S(2)}, u32[]{:S(2)}) collective-permute-start(bf16[64,2048]{1,0:T(8,128)(2,1)} %get-tuple-element.50), channel_id=1, source_target_pairs={{0,1},{1,0},{2,3},{3,2},{4,5},{5,4},{6,7},{7,6},{8,9},{9,8},{10,11... | collective-permute-start | bytes 786440 | tf_op jit(solution)/shard_map/ppermute | solution.py:29
  26.9 242.0 %all-to-all-start = ((bf16[16,64,1408]{2,1,0:T(8,128)(2,1)}), bf16[16,64,1408]{2,1,0:T(8,128)(2,1)}, u32[]{:S(2)}, u32[]{:S(2)}) async-start(bf16[16,64,1408]{2,1,0:T(8,128)(2,1)} %copy.182), calls=%async_computation | async-start | bytes 5767168 | tf_op jit(solution)/shard_map/all_to_all | solution.py:395
  32.6 540.4 %all-reduce.4.cloned.1.call-start = ((), (), s32[]{:S(2)}) async-start(), calls=%async_computation.2 | async-start | bytes 163840
  35.2 101.5 %collective-permute-start.42 = (bf16[64,2048]{1,0:T(8,128)(2,1)}, bf16[64,2048]{1,0:T(8,128)(2,1)}, u32[]{:S(2)}, u32[]{:S(2)}) collective-permute-start(bf16[64,2048]{1,0:T(8,128)(2,1)} %select_bitcast_fusion), channel_id=1, source_target_pairs={{0,8},{8,0},{1,9},{9,1},{2,10},{10,2},{3,11},{11,3},{4,12},{12,4},... | collective-permute-start | bytes 786440 | tf_op jit(solution)/shard_map/ppermute | solution.py:29
  36.9 110.9 %collective-permute-start.43 = (bf16[64,2048]{1,0:T(8,128)(2,1)}, bf16[64,2048]{1,0:T(8,128)(2,1)}, u32[]{:S(2)}, u32[]{:S(2)}) collective-permute-start(bf16[64,2048]{1,0:T(8,128)(2,1)} %bitcast.110), channel_id=1, source_target_pairs={{0,1},{1,0},{2,3},{3,2},{4,5},{5,4},{6,7},{7,6},{8,9},{9,8},{10,11... | collective-permute-start | bytes 786440 | tf_op jit(solution)/shard_map/ppermute | solution.py:29
  38.1 98.9 %collective-permute-start.21 = (bf16[64,2048]{1,0:T(8,128)(2,1)}, bf16[64,2048]{1,0:T(8,128)(2,1)}, u32[]{:S(2)}, u32[]{:S(2)}) collective-permute-start(bf16[64,2048]{1,0:T(8,128)(2,1)} %param.19), channel_id=1, source_target_pairs={{0,8},{8,0},{1,9},{9,1},{2,10},{10,2},{3,11},{11,3},{4,12},{12,4},... | collective-permute-start | bytes 786440 | tf_op jit(solution)/shard_map/ppermute | solution.py:29
  124.8 13.5 %collective-permute-start.3 = (bf16[64,2048]{1,0:T(8,128)(2,1)}, bf16[64,2048]{1,0:T(8,128)(2,1)}, u32[]{:S(2)}, u32[]{:S(2)}) collective-permute-start(bf16[64,2048]{1,0:T(8,128)(2,1)} %collective-permute-done), channel_id=1, source_target_pairs={{0,16},{16,0},{1,17},{17,1},{2,18},{18,2},{3,19},{19,3},{4,20},{20... | collective-permute-start | bytes 786440 | tf_op jit(solution)/shard_map/ppermute | solution.py:29
  146.6 18.6 %collective-permute-start.4 = (bf16[2,64,2048]{2,1,0:T(8,128)(2,1)}, bf16[2,64,2048]{2,1,0:T(8,128)(2,1)S(1)}, u32[]{:S(2)}, u32[]{:S(2)}) collective-permute-start(bf16[2,64,2048]{2,1,0:T(8,128)(2,1)} %get-tuple-element.115), channel_id=1, source_target_pairs={{0,1},{1,0},{2,3},{3,2},{4,5},{5,4},{6,7},{7,6},{8,9},{9,8},{10,11... | collective-permute-start | bytes 1572872 | tf_op jit(solution)/shard_map/ppermute | solution.py:29
  149.2 20.9 %collective-permute-start.44 = (bf16[2,64,2048]{2,1,0:T(8,128)(2,1)S(1)}, bf16[2,64,2048]{2,1,0:T(8,128)(2,1)S(1)}, u32[]{:S(2)}, u32[]{:S(2)}) collective-permute-start(bf16[2,64,2048]{2,1,0:T(8,128)(2,1)S(1)} %get-tuple-element.113), channel_id=1, source_target_pairs={{0,16},{16,0},{1,17},{17,1},{2,18},{18,2},{3,19},{19,3},{4,20},{20... | collective-permute-start | bytes 1572872 | tf_op jit(solution)/shard_map/ppermute | solution.py:29
  149.5 25.3 %collective-permute-start.46 = (bf16[2,64,2048]{2,1,0:T(8,128)(2,1)S(1)}, bf16[2,64,2048]{2,1,0:T(8,128)(2,1)S(1)}, u32[]{:S(2)}, u32[]{:S(2)}) collective-permute-start(bf16[2,64,2048]{2,1,0:T(8,128)(2,1)S(1)} %get-tuple-element.112), channel_id=1, source_target_pairs={{0,1},{1,0},{2,3},{3,2},{4,5},{5,4},{6,7},{7,6},{8,9},{9,8},{10,11... | collective-permute-start | bytes 1572872 | tf_op jit(solution)/shard_map/ppermute | solution.py:29
  156.7 21.9 %collective-permute-start.6 = (bf16[64,2048]{1,0:T(8,128)(2,1)S(1)}, bf16[64,2048]{1,0:T(8,128)(2,1)S(1)}, u32[]{:S(2)}, u32[]{:S(2)}) collective-permute-start(bf16[64,2048]{1,0:T(8,128)(2,1)S(1)} %get-tuple-element.104), channel_id=1, source_target_pairs={{0,1},{1,0},{2,3},{3,2},{4,5},{5,4},{6,7},{7,6},{8,9},{9,8},{10,11... | collective-permute-start | bytes 786440 | tf_op jit(solution)/shard_map/ppermute | solution.py:29
  164.8 16.2 %collective-permute-start.8 = (bf16[64,2048]{1,0:T(8,128)(2,1)S(1)}, bf16[64,2048]{1,0:T(8,128)(2,1)S(1)}, u32[]{:S(2)}, u32[]{:S(2)}) collective-permute-start(bf16[64,2048]{1,0:T(8,128)(2,1)S(1)} %get-tuple-element.105), channel_id=1, source_target_pairs={{0,16},{16,0},{1,17},{17,1},{2,18},{18,2},{3,19},{19,3},{4,20},{20... | collective-permute-start | bytes 786440 | tf_op jit(solution)/shard_map/ppermute | solution.py:29
  165.2 16.6 %collective-permute-start.48 = (bf16[64,2048]{1,0:T(8,128)(2,1)S(1)}, bf16[64,2048]{1,0:T(8,128)(2,1)S(1)}, u32[]{:S(2)}, u32[]{:S(2)}) collective-permute-start(bf16[64,2048]{1,0:T(8,128)(2,1)S(1)} %get-tuple-element.92), channel_id=1, source_target_pairs={{0,1},{1,0},{2,3},{3,2},{4,5},{5,4},{6,7},{7,6},{8,9},{9,8},{10,11... | collective-permute-start | bytes 786440 | tf_op jit(solution)/shard_map/ppermute | solution.py:29
  178.6 17.7 %collective-permute-start.52 = (bf16[2,64,2048]{2,1,0:T(8,128)(2,1)S(1)}, bf16[2,64,2048]{2,1,0:T(8,128)(2,1)S(1)}, u32[]{:S(2)}, u32[]{:S(2)}) collective-permute-start(bf16[2,64,2048]{2,1,0:T(8,128)(2,1)S(1)} %collective-permute-done.47), channel_id=1, source_target_pairs={{0,2},{2,4},{4,6},{6,0},{1,3},{3,5},{5,7},{7,1},{8,10},{10,12},{12... | collective-permute-start | bytes 1572872 | tf_op jit(solution)/shard_map/ppermute | solution.py:48
  181.0 36.5 %collective-permute-start.7 = (bf16[2,64,2048]{2,1,0:T(8,128)(2,1)S(1)}, bf16[2,64,2048]{2,1,0:T(8,128)(2,1)S(1)}, u32[]{:S(2)}, u32[]{:S(2)}) collective-permute-start(bf16[2,64,2048]{2,1,0:T(8,128)(2,1)S(1)} %pad_maximum_fusion.11), channel_id=1, source_target_pairs={{0,16},{16,0},{1,17},{17,1},{2,18},{18,2},{3,19},{19,3},{4,20},{20... | collective-permute-start | bytes 1572872 | tf_op jit(solution)/shard_map/ppermute | solution.py:29
  181.8 36.0 %collective-permute-start.9 = (bf16[2,64,2048]{2,1,0:T(8,128)(2,1)S(1)}, bf16[2,64,2048]{2,1,0:T(8,128)(2,1)S(1)}, u32[]{:S(2)}, u32[]{:S(2)}) collective-permute-start(bf16[2,64,2048]{2,1,0:T(8,128)(2,1)S(1)} %pad_maximum_fusion.12), channel_id=1, source_target_pairs={{0,1},{1,0},{2,3},{3,2},{4,5},{5,4},{6,7},{7,6},{8,9},{9,8},{10,11... | collective-permute-start | bytes 1572872 | tf_op jit(solution)/shard_map/ppermute | solution.py:29
  182.8 36.7 %collective-permute-start.49 = (bf16[2,64,2048]{2,1,0:T(8,128)(2,1)S(1)}, bf16[2,64,2048]{2,1,0:T(8,128)(2,1)S(1)}, u32[]{:S(2)}, u32[]{:S(2)}) collective-permute-start(bf16[2,64,2048]{2,1,0:T(8,128)(2,1)S(1)} %pad_maximum_fusion.19), channel_id=1, source_target_pairs={{0,16},{16,0},{1,17},{17,1},{2,18},{18,2},{3,19},{19,3},{4,20},{20... | collective-permute-start | bytes 1572872 | tf_op jit(solution)/shard_map/ppermute | solution.py:29
  185.2 12.8 %collective-permute-start.11 = (bf16[64,2048]{1,0:T(8,128)(2,1)S(1)}, bf16[64,2048]{1,0:T(8,128)(2,1)S(1)}, u32[]{:S(2)}, u32[]{:S(2)}) collective-permute-start(bf16[64,2048]{1,0:T(8,128)(2,1)S(1)} %get-tuple-element.100), channel_id=1, source_target_pairs={{0,1},{1,0},{2,3},{3,2},{4,5},{5,4},{6,7},{7,6},{8,9},{9,8},{10,11... | collective-permute-start | bytes 786440 | tf_op jit(solution)/shard_map/ppermute | solution.py:29
  206.3 15.5 %collective-permute-start.51 = (bf16[2,64,2048]{2,1,0:T(8,128)(2,1)S(1)}, bf16[2,64,2048]{2,1,0:T(8,128)(2,1)S(1)}, u32[]{:S(2)}, u32[]{:S(2)}) collective-permute-start(bf16[2,64,2048]{2,1,0:T(8,128)(2,1)S(1)} %pad_maximum_fusion.20), channel_id=1, source_target_pairs={{0,1},{1,0},{2,3},{3,2},{4,5},{5,4},{6,7},{7,6},{8,9},{9,8},{10,11... | collective-permute-start | bytes 1572872 | tf_op jit(solution)/shard_map/ppermute | solution.py:29
  213.2 12.9 %collective-permute-start.15 = (bf16[2,64,2048]{2,1,0:T(8,128)(2,1)S(1)}, bf16[2,64,2048]{2,1,0:T(8,128)(2,1)S(1)}, u32[]{:S(2)}, u32[]{:S(2)}) collective-permute-start(bf16[2,64,2048]{2,1,0:T(8,128)(2,1)S(1)} %collective-permute-done.10), channel_id=1, source_target_pairs={{0,2},{2,4},{4,6},{6,0},{1,3},{3,5},{5,7},{7,1},{8,10},{10,12},{12... | collective-permute-start | bytes 1572872 | tf_op jit(solution)/shard_map/ppermute | solution.py:48
  217.9 12.8 %collective-permute-start.12 = (bf16[2,64,2048]{2,1,0:T(8,128)(2,1)S(1)}, bf16[2,64,2048]{2,1,0:T(8,128)(2,1)S(1)}, u32[]{:S(2)}, u32[]{:S(2)}) collective-permute-start(bf16[2,64,2048]{2,1,0:T(8,128)(2,1)S(1)} %pad_maximum_fusion.13), channel_id=1, source_target_pairs={{0,16},{16,0},{1,17},{17,1},{2,18},{18,2},{3,19},{19,3},{4,20},{20... | collective-permute-start | bytes 1572872 | tf_op jit(solution)/shard_map/ppermute | solution.py:29
  219.5 14.2 %collective-permute-start.14 = (bf16[2,64,2048]{2,1,0:T(8,128)(2,1)S(1)}, bf16[2,64,2048]{2,1,0:T(8,128)(2,1)S(1)}, u32[]{:S(2)}, u32[]{:S(2)}) collective-permute-start(bf16[2,64,2048]{2,1,0:T(8,128)(2,1)S(1)} %pad_maximum_fusion.14), channel_id=1, source_target_pairs={{0,1},{1,0},{2,3},{3,2},{4,5},{5,4},{6,7},{7,6},{8,9},{9,8},{10,11... | collective-permute-start | bytes 1572872 | tf_op jit(solution)/shard_map/ppermute | solution.py:29
  221.8 33.4 %collective-permute-start.54 = (bf16[2,64,2048]{2,1,0:T(8,128)(2,1)S(1)}, bf16[2,64,2048]{2,1,0:T(8,128)(2,1)S(1)}, u32[]{:S(2)}, u32[]{:S(2)}) collective-permute-start(bf16[2,64,2048]{2,1,0:T(8,128)(2,1)S(1)} %pad_maximum_fusion.21), channel_id=1, source_target_pairs={{0,16},{16,0},{1,17},{17,1},{2,18},{18,2},{3,19},{19,3},{4,20},{20... | collective-permute-start | bytes 1572872 | tf_op jit(solution)/shard_map/ppermute | solution.py:29
  226.1 31.3 %collective-permute-start.56 = (bf16[2,64,2048]{2,1,0:T(8,128)(2,1)S(1)}, bf16[2,64,2048]{2,1,0:T(8,128)(2,1)S(1)}, u32[]{:S(2)}, u32[]{:S(2)}) collective-permute-start(bf16[2,64,2048]{2,1,0:T(8,128)(2,1)S(1)} %pad_maximum_fusion.22), channel_id=1, source_target_pairs={{0,1},{1,0},{2,3},{3,2},{4,5},{5,4},{6,7},{7,6},{8,9},{9,8},{10,11... | collective-permute-start | bytes 1572872 | tf_op jit(solution)/shard_map/ppermute | solution.py:29
  230.2 14.5 %collective-permute-start.16 = (bf16[64,2048]{1,0:T(8,128)(2,1)S(1)}, bf16[64,2048]{1,0:T(8,128)(2,1)S(1)}, u32[]{:S(2)}, u32[]{:S(2)}) collective-permute-start(bf16[64,2048]{1,0:T(8,128)(2,1)S(1)} %get-tuple-element.96), channel_id=1, source_target_pairs={{0,1},{1,0},{2,3},{3,2},{4,5},{5,4},{6,7},{7,6},{8,9},{9,8},{10,11... | collective-permute-start | bytes 786440 | tf_op jit(solution)/shard_map/ppermute | solution.py:29
  230.7 15.7 %collective-permute-start.18 = (bf16[64,2048]{1,0:T(8,128)(2,1)S(1)}, bf16[64,2048]{1,0:T(8,128)(2,1)S(1)}, u32[]{:S(2)}, u32[]{:S(2)}) collective-permute-start(bf16[64,2048]{1,0:T(8,128)(2,1)S(1)} %get-tuple-element.97), channel_id=1, source_target_pairs={{0,16},{16,0},{1,17},{17,1},{2,18},{18,2},{3,19},{19,3},{4,20},{20... | collective-permute-start | bytes 786440 | tf_op jit(solution)/shard_map/ppermute | solution.py:29
  233.7 16.7 %collective-permute-start.58 = (bf16[64,2048]{1,0:T(8,128)(2,1)S(1)}, bf16[64,2048]{1,0:T(8,128)(2,1)S(1)}, u32[]{:S(2)}, u32[]{:S(2)}) collective-permute-start(bf16[64,2048]{1,0:T(8,128)(2,1)S(1)} %get-tuple-element.84), channel_id=1, source_target_pairs={{0,1},{1,0},{2,3},{3,2},{4,5},{5,4},{6,7},{7,6},{8,9},{9,8},{10,11... | collective-permute-start | bytes 786440 | tf_op jit(solution)/shard_map/ppermute | solution.py:29
  246.4 14.7 %collective-permute-start.17 = (bf16[2,64,2048]{2,1,0:T(8,128)(2,1)S(1)}, bf16[2,64,2048]{2,1,0:T(8,128)(2,1)S(1)}, u32[]{:S(2)}, u32[]{:S(2)}) collective-permute-start(bf16[2,64,2048]{2,1,0:T(8,128)(2,1)S(1)} %pad_maximum_fusion.15), channel_id=1, source_target_pairs={{0,16},{16,0},{1,17},{17,1},{2,18},{18,2},{3,19},{19,3},{4,20},{20... | collective-permute-start | bytes 1572872 | tf_op jit(solution)/shard_map/ppermute | solution.py:29
  250.4 13.9 %collective-permute-start.19 = (bf16[2,64,2048]{2,1,0:T(8,128)(2,1)S(1)}, bf16[2,64,2048]{2,1,0:T(8,128)(2,1)S(1)}, u32[]{:S(2)}, u32[]{:S(2)}) collective-permute-start(bf16[2,64,2048]{2,1,0:T(8,128)(2,1)S(1)} %pad_maximum_fusion.16), channel_id=1, source_target_pairs={{0,1},{1,0},{2,3},{3,2},{4,5},{5,4},{6,7},{7,6},{8,9},{9,8},{10,11... | collective-permute-start | bytes 1572872 | tf_op jit(solution)/shard_map/ppermute | solution.py:29
  255.2 32.6 %collective-permute-start.61 = (bf16[2,64,2048]{2,1,0:T(8,128)(2,1)}, bf16[2,64,2048]{2,1,0:T(8,128)(2,1)}, u32[]{:S(2)}, u32[]{:S(2)}) collective-permute-start(bf16[2,64,2048]{2,1,0:T(8,128)(2,1)} %pad_maximum_fusion.24), channel_id=1, source_target_pairs={{0,1},{1,0},{2,3},{3,2},{4,5},{5,4},{6,7},{7,6},{8,9},{9,8},{10,11... | collective-permute-start | bytes 1572872 | tf_op jit(solution)/shard_map/ppermute | solution.py:29
  268.9 22.9 %collective-permute-start.20 = (bf16[2,1,8,64,1408]{4,3,2,0,1:T(8,128)(2,1)}, bf16[2,1,8,64,1408]{4,3,2,0,1:T(8,128)(2,1)S(1)}, u32[]{:S(2)}, u32[]{:S(2)}) collective-permute-start(bf16[2,1,8,64,1408]{4,3,2,0,1:T(8,128)(2,1)} %bitcast.48), channel_id=1, source_target_pairs={{0,8},{8,0},{1,9},{9,1},{2,10},{10,2},{3,11},{11,3},{4,12},{12,4},... | collective-permute-start | bytes 8650760 | tf_op jit(solution)/shard_map/ppermute | solution.py:29
  419.8 159.0 %collective-permute-start.76 = (bf16[2,64,2048]{2,1,0:T(8,128)(2,1)}, bf16[2,64,2048]{2,1,0:T(8,128)(2,1)}, u32[]{:S(2)}, u32[]{:S(2)}) collective-permute-start(bf16[2,64,2048]{2,1,0:T(8,128)(2,1)} %get-tuple-element.59), channel_id=1, source_target_pairs={{0,1},{1,0},{2,3},{3,2},{4,5},{5,4},{6,7},{7,6},{8,9},{9,8},{10,11... | collective-permute-start | bytes 1572872 | tf_op jit(solution)/shard_map/ppermute | solution.py:29
  420.6 158.5 %collective-permute-start.72 = (bf16[2,64,2048]{2,1,0:T(8,128)(2,1)}, bf16[2,64,2048]{2,1,0:T(8,128)(2,1)}, u32[]{:S(2)}, u32[]{:S(2)}) collective-permute-start(bf16[2,64,2048]{2,1,0:T(8,128)(2,1)} %get-tuple-element.60), channel_id=1, source_target_pairs={{0,1},{1,0},{2,3},{3,2},{4,5},{5,4},{6,7},{7,6},{8,9},{9,8},{10,11... | collective-permute-start | bytes 1572872 | tf_op jit(solution)/shard_map/ppermute | solution.py:29
  421.3 159.0 %collective-permute-start.68 = (bf16[2,64,2048]{2,1,0:T(8,128)(2,1)}, bf16[2,64,2048]{2,1,0:T(8,128)(2,1)}, u32[]{:S(2)}, u32[]{:S(2)}) collective-permute-start(bf16[2,64,2048]{2,1,0:T(8,128)(2,1)} %get-tuple-element.61), channel_id=1, source_target_pairs={{0,1},{1,0},{2,3},{3,2},{4,5},{5,4},{6,7},{7,6},{8,9},{9,8},{10,11... | collective-permute-start | bytes 1572872 | tf_op jit(solution)/shard_map/ppermute | solution.py:29
  422.1 158.5 %collective-permute-start.64 = (bf16[2,64,2048]{2,1,0:T(8,128)(2,1)}, bf16[2,64,2048]{2,1,0:T(8,128)(2,1)}, u32[]{:S(2)}, u32[]{:S(2)}) collective-permute-start(bf16[2,64,2048]{2,1,0:T(8,128)(2,1)} %get-tuple-element.62), channel_id=1, source_target_pairs={{0,1},{1,0},{2,3},{3,2},{4,5},{5,4},{6,7},{7,6},{8,9},{9,8},{10,11... | collective-permute-start | bytes 1572872 | tf_op jit(solution)/shard_map/ppermute | solution.py:29
  470.5 105.2 %collective-permute-start.83 = (bf16[64,2048]{1,0:T(8,128)(2,1)}, bf16[64,2048]{1,0:T(8,128)(2,1)S(1)}, u32[]{:S(2)}, u32[]{:S(2)}) collective-permute-start(bf16[64,2048]{1,0:T(8,128)(2,1)} %fusion.78), channel_id=1, source_target_pairs={{0,8},{8,0},{1,9},{9,1},{2,10},{10,2},{3,11},{11,3},{4,12},{12,4},... | collective-permute-start | bytes 786440 | tf_op jit(solution)/shard_map/ppermute | solution.py:29
  578.8 17.7 %collective-permute-start.66 = (bf16[2,64,2048]{2,1,0:T(8,128)(2,1)}, bf16[2,64,2048]{2,1,0:T(8,128)(2,1)S(1)}, u32[]{:S(2)}, u32[]{:S(2)}) collective-permute-start(bf16[2,64,2048]{2,1,0:T(8,128)(2,1)} %slice_bitcast_fusion.12), channel_id=1, source_target_pairs={{0,16},{16,0},{1,17},{17,1},{2,18},{18,2},{3,19},{19,3},{4,20},{20... | collective-permute-start | bytes 1572872 | tf_op jit(solution)/shard_map/ppermute | solution.py:29
  579.1 28.6 %collective-permute-start.70 = (bf16[2,64,2048]{2,1,0:T(8,128)(2,1)}, bf16[2,64,2048]{2,1,0:T(8,128)(2,1)S(1)}, u32[]{:S(2)}, u32[]{:S(2)}) collective-permute-start(bf16[2,64,2048]{2,1,0:T(8,128)(2,1)} %slice_bitcast_fusion.8), channel_id=1, source_target_pairs={{0,16},{16,0},{1,17},{17,1},{2,18},{18,2},{3,19},{19,3},{4,20},{20... | collective-permute-start | bytes 1572872 | tf_op jit(solution)/shard_map/ppermute | solution.py:29
  580.3 38.6 %collective-permute-start.74 = (bf16[2,64,2048]{2,1,0:T(8,128)(2,1)}, bf16[2,64,2048]{2,1,0:T(8,128)(2,1)S(1)}, u32[]{:S(2)}, u32[]{:S(2)}) collective-permute-start(bf16[2,64,2048]{2,1,0:T(8,128)(2,1)} %slice_bitcast_fusion.4), channel_id=1, source_target_pairs={{0,16},{16,0},{1,17},{17,1},{2,18},{18,2},{3,19},{19,3},{4,20},{20... | collective-permute-start | bytes 1572872 | tf_op jit(solution)/shard_map/ppermute | solution.py:29
  580.6 39.7 %collective-permute-start.36 = (bf16[2,64,2048]{2,1,0:T(8,128)(2,1)}, bf16[2,64,2048]{2,1,0:T(8,128)(2,1)S(1)}, u32[]{:S(2)}, u32[]{:S(2)}) collective-permute-start(bf16[2,64,2048]{2,1,0:T(8,128)(2,1)} %get-tuple-element.71), channel_id=1, source_target_pairs={{0,1},{1,0},{2,3},{3,2},{4,5},{5,4},{6,7},{7,6},{8,9},{9,8},{10,11... | collective-permute-start | bytes 1572872 | tf_op jit(solution)/shard_map/ppermute | solution.py:29
  585.3 35.4 %collective-permute-start.32 = (bf16[2,64,2048]{2,1,0:T(8,128)(2,1)}, bf16[2,64,2048]{2,1,0:T(8,128)(2,1)S(1)}, u32[]{:S(2)}, u32[]{:S(2)}) collective-permute-start(bf16[2,64,2048]{2,1,0:T(8,128)(2,1)} %get-tuple-element.72), channel_id=1, source_target_pairs={{0,1},{1,0},{2,3},{3,2},{4,5},{5,4},{6,7},{7,6},{8,9},{9,8},{10,11... | collective-permute-start | bytes 1572872 | tf_op jit(solution)/shard_map/ppermute | solution.py:29
  596.5 25.4 %collective-permute-start.28 = (bf16[2,64,2048]{2,1,0:T(8,128)(2,1)S(1)}, bf16[2,64,2048]{2,1,0:T(8,128)(2,1)S(1)}, u32[]{:S(2)}, u32[]{:S(2)}) collective-permute-start(bf16[2,64,2048]{2,1,0:T(8,128)(2,1)S(1)} %copy-done.36), channel_id=1, source_target_pairs={{0,1},{1,0},{2,3},{3,2},{4,5},{5,4},{6,7},{7,6},{8,9},{9,8},{10,11... | collective-permute-start | bytes 1572872 | tf_op jit(solution)/shard_map/ppermute | solution.py:29
  607.7 15.0 %collective-permute-start.24 = (bf16[2,64,2048]{2,1,0:T(8,128)(2,1)S(1)}, bf16[2,64,2048]{2,1,0:T(8,128)(2,1)S(1)}, u32[]{:S(2)}, u32[]{:S(2)}) collective-permute-start(bf16[2,64,2048]{2,1,0:T(8,128)(2,1)S(1)} %copy-done.35), channel_id=1, source_target_pairs={{0,1},{1,0},{2,3},{3,2},{4,5},{5,4},{6,7},{7,6},{8,9},{9,8},{10,11... | collective-permute-start | bytes 1572872 | tf_op jit(solution)/shard_map/ppermute | solution.py:29
  619.0 13.5 %collective-permute-start.22 = (bf16[2,64,2048]{2,1,0:T(8,128)(2,1)S(1)}, bf16[2,64,2048]{2,1,0:T(8,128)(2,1)S(1)}, u32[]{:S(2)}, u32[]{:S(2)}) collective-permute-start(bf16[2,64,2048]{2,1,0:T(8,128)(2,1)S(1)} %copy-done.34), channel_id=1, source_target_pairs={{0,16},{16,0},{1,17},{17,1},{2,18},{18,2},{3,19},{19,3},{4,20},{20... | collective-permute-start | bytes 1572872 | tf_op jit(solution)/shard_map/ppermute | solution.py:29
  620.4 20.2 %collective-permute-start.26 = (bf16[2,64,2048]{2,1,0:T(8,128)(2,1)S(1)}, bf16[2,64,2048]{2,1,0:T(8,128)(2,1)S(1)}, u32[]{:S(2)}, u32[]{:S(2)}) collective-permute-start(bf16[2,64,2048]{2,1,0:T(8,128)(2,1)S(1)} %copy-done.33), channel_id=1, source_target_pairs={{0,16},{16,0},{1,17},{17,1},{2,18},{18,2},{3,19},{19,3},{4,20},{20... | collective-permute-start | bytes 1572872 | tf_op jit(solution)/shard_map/ppermute | solution.py:29
  620.7 31.2 %collective-permute-start.30 = (bf16[2,64,2048]{2,1,0:T(8,128)(2,1)S(1)}, bf16[2,64,2048]{2,1,0:T(8,128)(2,1)S(1)}, u32[]{:S(2)}, u32[]{:S(2)}) collective-permute-start(bf16[2,64,2048]{2,1,0:T(8,128)(2,1)S(1)} %copy-done.32), channel_id=1, source_target_pairs={{0,16},{16,0},{1,17},{17,1},{2,18},{18,2},{3,19},{19,3},{4,20},{20... | collective-permute-start | bytes 1572872 | tf_op jit(solution)/shard_map/ppermute | solution.py:29
  621.9 41.2 %collective-permute-start.34 = (bf16[2,64,2048]{2,1,0:T(8,128)(2,1)S(1)}, bf16[2,64,2048]{2,1,0:T(8,128)(2,1)S(1)}, u32[]{:S(2)}, u32[]{:S(2)}) collective-permute-start(bf16[2,64,2048]{2,1,0:T(8,128)(2,1)S(1)} %copy-done.31), channel_id=1, source_target_pairs={{0,16},{16,0},{1,17},{17,1},{2,18},{18,2},{3,19},{19,3},{4,20},{20... | collective-permute-start | bytes 1572872 | tf_op jit(solution)/shard_map/ppermute | solution.py:29
  622.8 131.1 %collective-permute-start.82 = (bf16[2,1,8,64,1408]{4,3,2,0,1:T(8,128)(2,1)S(1)}, bf16[2,1,8,64,1408]{4,3,2,0,1:T(8,128)(2,1)S(1)}, u32[]{:S(2)}, u32[]{:S(2)}) collective-permute-start(bf16[2,1,8,64,1408]{4,3,2,0,1:T(8,128)(2,1)S(1)} %copy-done.23), channel_id=1, source_target_pairs={{0,8},{8,0},{1,9},{9,1},{2,10},{10,2},{3,11},{11,3},{4,12},{12,4},... | collective-permute-start | bytes 8650760 | tf_op jit(solution)/shard_map/ppermute | solution.py:29
  632.5 36.2 %collective-permute-start.65 = (bf16[64,2048]{1,0:T(8,128)(2,1)S(1)}, bf16[64,2048]{1,0:T(8,128)(2,1)S(1)}, u32[]{:S(2)}, u32[]{:S(2)}) collective-permute-start(bf16[64,2048]{1,0:T(8,128)(2,1)S(1)} %slice_bitcast_fusion.47), channel_id=1, source_target_pairs={{0,16},{16,0},{1,17},{17,1},{2,18},{18,2},{3,19},{19,3},{4,20},{20... | collective-permute-start | bytes 786440 | tf_op jit(solution)/shard_map/ppermute | solution.py:29
  640.6 30.2 %collective-permute-start.63 = (bf16[64,2048]{1,0:T(8,128)(2,1)S(1)}, bf16[64,2048]{1,0:T(8,128)(2,1)S(1)}, u32[]{:S(2)}, u32[]{:S(2)}) collective-permute-start(bf16[64,2048]{1,0:T(8,128)(2,1)S(1)} %slice_bitcast_fusion.49), channel_id=1, source_target_pairs={{0,1},{1,0},{2,3},{3,2},{4,5},{5,4},{6,7},{7,6},{8,9},{9,8},{10,11... | collective-permute-start | bytes 786440 | tf_op jit(solution)/shard_map/ppermute | solution.py:29
  651.8 22.5 %collective-permute-start.69 = (bf16[64,2048]{1,0:T(8,128)(2,1)S(1)}, bf16[64,2048]{1,0:T(8,128)(2,1)S(1)}, u32[]{:S(2)}, u32[]{:S(2)}) collective-permute-start(bf16[64,2048]{1,0:T(8,128)(2,1)S(1)} %slice_bitcast_fusion.43), channel_id=1, source_target_pairs={{0,16},{16,0},{1,17},{17,1},{2,18},{18,2},{3,19},{19,3},{4,20},{20... | collective-permute-start | bytes 786440 | tf_op jit(solution)/shard_map/ppermute | solution.py:29
  674.3 26.9 %collective-permute-start.77 = (bf16[64,2048]{1,0:T(8,128)(2,1)S(1)}, bf16[64,2048]{1,0:T(8,128)(2,1)S(1)}, u32[]{:S(2)}, u32[]{:S(2)}) collective-permute-start(bf16[64,2048]{1,0:T(8,128)(2,1)S(1)} %slice_bitcast_fusion.35), channel_id=1, source_target_pairs={{0,16},{16,0},{1,17},{17,1},{2,18},{18,2},{3,19},{19,3},{4,20},{20... | collective-permute-start | bytes 786440 | tf_op jit(solution)/shard_map/ppermute | solution.py:29
  675.6 25.9 %collective-permute-start.75 = (bf16[64,2048]{1,0:T(8,128)(2,1)S(1)}, bf16[64,2048]{1,0:T(8,128)(2,1)S(1)}, u32[]{:S(2)}, u32[]{:S(2)}) collective-permute-start(bf16[64,2048]{1,0:T(8,128)(2,1)S(1)} %slice_bitcast_fusion.37), channel_id=1, source_target_pairs={{0,1},{1,0},{2,3},{3,2},{4,5},{5,4},{6,7},{7,6},{8,9},{9,8},{10,11... | collective-permute-start | bytes 786440 | tf_op jit(solution)/shard_map/ppermute | solution.py:29
  693.2 28.6 %collective-permute-start.27 = (bf16[64,2048]{1,0:T(8,128)(2,1)S(1)}, bf16[64,2048]{1,0:T(8,128)(2,1)S(1)}, u32[]{:S(2)}, u32[]{:S(2)}) collective-permute-start(bf16[64,2048]{1,0:T(8,128)(2,1)S(1)} %slice_bitcast_fusion.77), channel_id=1, source_target_pairs={{0,1},{1,0},{2,3},{3,2},{4,5},{5,4},{6,7},{7,6},{8,9},{9,8},{10,11... | collective-permute-start | bytes 786440 | tf_op jit(solution)/shard_map/ppermute | solution.py:29
  699.1 23.7 %collective-permute-start.33 = (bf16[64,2048]{1,0:T(8,128)(2,1)S(1)}, bf16[64,2048]{1,0:T(8,128)(2,1)S(1)}, u32[]{:S(2)}, u32[]{:S(2)}) collective-permute-start(bf16[64,2048]{1,0:T(8,128)(2,1)S(1)} %slice_bitcast_fusion.71), channel_id=1, source_target_pairs={{0,16},{16,0},{1,17},{17,1},{2,18},{18,2},{3,19},{19,3},{4,20},{20... | collective-permute-start | bytes 786440 | tf_op jit(solution)/shard_map/ppermute | solution.py:29
  701.2 29.5 %collective-permute-start.31 = (bf16[64,2048]{1,0:T(8,128)(2,1)S(1)}, bf16[64,2048]{1,0:T(8,128)(2,1)S(1)}, u32[]{:S(2)}, u32[]{:S(2)}) collective-permute-start(bf16[64,2048]{1,0:T(8,128)(2,1)S(1)} %slice_bitcast_fusion.73), channel_id=1, source_target_pairs={{0,1},{1,0},{2,3},{3,2},{4,5},{5,4},{6,7},{7,6},{8,9},{9,8},{10,11... | collective-permute-start | bytes 786440 | tf_op jit(solution)/shard_map/ppermute | solution.py:29
  721.8 17.7 %collective-permute-start.38 = (bf16[2,64,2048]{2,1,0:T(8,128)(2,1)S(1)}, bf16[2,64,2048]{2,1,0:T(8,128)(2,1)S(1)}, u32[]{:S(2)}, u32[]{:S(2)}) collective-permute-start(bf16[2,64,2048]{2,1,0:T(8,128)(2,1)S(1)} %pad_maximum_fusion.17), channel_id=1, source_target_pairs={{2,0},{4,2},{6,4},{0,6},{3,1},{5,3},{7,5},{1,7},{10,8},{12,10},{14... | collective-permute-start | bytes 1572872 | tf_op jit(solution)/shard_map/ppermute | solution.py:79
  728.4 22.4 %collective-permute-start.79 = (bf16[2,64,2048]{2,1,0:T(8,128)(2,1)S(1)}, bf16[2,64,2048]{2,1,0:T(8,128)(2,1)S(1)}, u32[]{:S(2)}, u32[]{:S(2)}) collective-permute-start(bf16[2,64,2048]{2,1,0:T(8,128)(2,1)S(1)} %fusion.41), channel_id=1, source_target_pairs={{2,0},{4,2},{6,4},{0,6},{3,1},{5,3},{7,5},{1,7},{10,8},{12,10},{14... | collective-permute-start | bytes 1572872 | tf_op jit(solution)/shard_map/ppermute | solution.py:79
  740.5 21.7 %collective-permute-start.39 = (bf16[2,64,2048]{2,1,0:T(8,128)(2,1)}, bf16[2,64,2048]{2,1,0:T(8,128)(2,1)}, u32[]{:S(2)}, u32[]{:S(2)}) collective-permute-start(bf16[2,64,2048]{2,1,0:T(8,128)(2,1)} %fusion.36), channel_id=1, source_target_pairs={{2,0},{4,2},{6,4},{0,6},{3,1},{5,3},{7,5},{1,7},{10,8},{12,10},{14... | collective-permute-start | bytes 1572872 | tf_op jit(solution)/shard_map/ppermute | solution.py:79
  751.7 23.6 %collective-permute-start.80 = (bf16[2,64,2048]{2,1,0:T(8,128)(2,1)}, bf16[2,64,2048]{2,1,0:T(8,128)(2,1)}, u32[]{:S(2)}, u32[]{:S(2)}) collective-permute-start(bf16[2,64,2048]{2,1,0:T(8,128)(2,1)} %fusion.40), channel_id=1, source_target_pairs={{2,0},{4,2},{6,4},{0,6},{3,1},{5,3},{7,5},{1,7},{10,8},{12,10},{14... | collective-permute-start | bytes 1572872 | tf_op jit(solution)/shard_map/ppermute | solution.py:79
  756.2 99.1 %all-to-all-start.1 = ((bf16[16,64,1408]{2,1,0:T(8,128)(2,1)}), bf16[16,64,1408]{2,1,0:T(8,128)(2,1)S(1)}, u32[]{:S(2)}, u32[]{:S(2)}) async-start(bf16[16,64,1408]{2,1,0:T(8,128)(2,1)} %bitcast.635), calls=%async_computation.1 | async-start | bytes 5767168 | tf_op jit(solution)/shard_map/all_to_all | solution.py:453
  763.6 78.3 %collective-permute-start.40 = (bf16[2,64,2048]{2,1,0:T(8,128)(2,1)S(1)}, bf16[2,64,2048]{2,1,0:T(8,128)(2,1)S(1)}, u32[]{:S(2)}, u32[]{:S(2)}) collective-permute-start(bf16[2,64,2048]{2,1,0:T(8,128)(2,1)S(1)} %fusion.35), channel_id=1, source_target_pairs={{2,0},{4,2},{6,4},{0,6},{3,1},{5,3},{7,5},{1,7},{10,8},{12,10},{14... | collective-permute-start | bytes 1572872 | tf_op jit(solution)/shard_map/ppermute | solution.py:79
  776.8 75.5 %collective-permute-start.81 = (bf16[64,2048]{1,0:T(8,128)(2,1)S(1)}, bf16[64,2048]{1,0:T(8,128)(2,1)S(1)}, u32[]{:S(2)}, u32[]{:S(2)}) collective-permute-start(bf16[64,2048]{1,0:T(8,128)(2,1)S(1)} %fusion.84), channel_id=1, source_target_pairs={{0,8},{8,0},{1,9},{9,1},{2,10},{10,2},{3,11},{11,3},{4,12},{12,4},... | collective-permute-start | bytes 786440 | tf_op jit(solution)/shard_map/ppermute | solution.py:29
  (82 other events, 2619.2 us)
Sparse Core Ops, SparseCore 0:
  433.7 139.1 all-reduce.3

commit v2 on v1

v2 whole, which is shorter than its diff:
```python
import functools

import jax
import jax.numpy as jnp
from jax import lax
from jax.experimental import pallas as pl
from jax.experimental.pallas import tpu as pltpu
from jax.sharding import Mesh
from jax.sharding import PartitionSpec as P

HEADS = 32
HEAD_DIM = 64
ROT = 32
EPS = 1e-05
NEG = -1e30
BF = jnp.bfloat16
F32 = jnp.float32

RANK = ("hx", "bz", "by")
ALL = ("hx", "core", "bs", "bz", "by")
Z_LEN = 4
SWAP = [(0, 1), (1, 0)]
UP = [(i, (i + 1) % Z_LEN) for i in range(Z_LEN)]
DOWN = [((i + 1) % Z_LEN, i) for i in range(Z_LEN)]
VMEM_LIMIT = 60 * 1024 * 1024


def around(far):
    return [(i, (i + far) % Z_LEN) for i in range(Z_LEN)]


def swap(value, axis):
    return lax.ppermute(value, axis, SWAP)


def dot_rows(left, right):
    return lax.dot_general(left, right, (((1,), (1,)), ((), ())), preferred_element_type=F32)


def dot_cols(left, right):
    return lax.dot_general(left, right, (((0,), (0,)), ((), ())), preferred_element_type=F32)


def dot(left, right):
    return jnp.dot(left, right, preferred_element_type=F32)


def fence(now, *then):
    return lax.optimization_barrier((tuple(now),) + then)[0]


def ring(value):
    return lax.ppermute(value, "bz", UP)


def both_ways(value):
    return swap(value, "hx"), swap(value, "by")


def far_ways(x_rows, y_rows):
    half = x_rows.shape[0] // 2
    return swap(y_rows[:half], "hx"), swap(x_rows[half:], "by")


def pair(low, high):
    return jnp.concatenate([low[0], high[0], low[1], high[1]], 0)


def add_low(left, right):
    return (left.astype(F32) + right.astype(F32)).astype(BF)


def far_terms(rest, got):
    half = got[0].shape[0] // 2
    return add_low(rest[2 * half : 3 * half], got[0][:half]), add_low(rest[3 * half :], got[1][:half])


def far_back(terms):
    return swap(terms[0], "by"), swap(terms[1], "hx")


def square_sums(rest, got, far, share):
    half = 2 * share
    a = rest[:half].astype(F32) + got[0][half:].astype(F32) + far[0].astype(F32)
    b = rest[half : 2 * half].astype(F32) + got[1][half:].astype(F32) + far[1].astype(F32)
    return [jnp.stack([a[row : row + share], b[row : row + share]]) for row in (0, share)]


def ring_back(total):
    return lax.ppermute(total.astype(BF), "bz", DOWN).astype(F32)


def other_first(index, pair):
    return jnp.where(index == 0, pair, pair[::-1])


def gather_small(value, devices):
    hx, core, bs, bz, by = (lax.axis_index(name) for name in ALL)
    value = value[None]
    for name, index in (("by", by), ("core", core), ("hx", hx)):
        value = other_first(index, jnp.stack([value, swap(value, name)]))
        value = value.reshape((-1,) + value.shape[2:])
    whole = jnp.stack([value] + [lax.ppermute(value, "bz", around(kz)) for kz in range(1, Z_LEN)])
    places = (bz + Z_LEN - jnp.arange(Z_LEN)) % Z_LEN
    whole = sum(
        jnp.where((places == z)[:, None, None], whole, jnp.zeros_like(whole)).sum(0)[None] * (jnp.arange(Z_LEN) == z)[:, None, None]
        for z in range(Z_LEN)
    )
    whole = whole.astype(value.dtype).reshape(1, Z_LEN, 2, 2, 2, -1)
    if devices > 8 * Z_LEN:
        whole = lax.all_gather(whole, "bs", axis=0, tiled=True)
    return whole.transpose(2, 3, 0, 1, 4, 5).reshape(devices, -1)


def scatter_small(value, devices):
    hx, core, bs, bz, by = (lax.axis_index(name) for name in ALL)
    value = value.reshape(2, 2, devices // (8 * Z_LEN), Z_LEN, 2, -1)
    for axis, name, index in ((0, "hx", hx), (0, "core", core), (2, "by", by)):
        mine = lax.dynamic_index_in_dim(value, index, axis, keepdims=False)
        away = lax.dynamic_index_in_dim(value, 1 - index, axis, keepdims=False)
        value = mine + swap(away, name)
    terms = [lax.dynamic_index_in_dim(value, (bz + kz) % Z_LEN, 1, keepdims=False) for kz in range(Z_LEN)]
    return terms[:1] + [lax.ppermute(terms[kz], "bz", around(kz)) for kz in range(1, Z_LEN)]


def small_sum(terms, devices):
    total = sum(terms)
    if devices > 8 * Z_LEN:
        total = lax.psum_scatter(total, "bs", scatter_dimension=0, tiled=True)
    return total.reshape(-1)


def turn(value, cosine, sine, lane):
    near = jnp.where(
        (lane % HEAD_DIM) < ROT // 2,
        pltpu.roll(value, 128 - ROT // 2, 1),
        pltpu.roll(value, ROT // 2, 1),
    )
    return value * cosine + near * sine


def by_row(block, lanes):
    return pl.BlockSpec((block, lanes), lambda i: (i, 0))


def whole(rows, lanes):
    return pl.BlockSpec((rows, lanes), lambda i: (0, 0))


def take_rows(rows_ref, pieces, begin):
    half = pieces[-1].shape[0]
    step = pl.program_id(0)
    for at in range(3):

        @pl.when(step == begin + at)
        def _(at=at):
            rows_ref[...] = pieces[at][...]

    @pl.when(step == begin + 3)
    def _():
        rows_ref[:half] = pieces[3][...]
        rows_ref[half:] = pieces[4][...]


def piece_specs(pieces):
    return [whole(*piece.shape) for piece in pieces]


def front_kernel(*refs):
    pieces, refs = refs[:5], refs[5:]
    gain_ref, shift_ref, w_ref, bias_ref, cos_ref, sin_ref = refs[:6]
    h_ref, q_ref, kv_ref, pre_ref, out_ref, mean_ref, scale_ref, x_ref = refs[-8:]
    take_rows(x_ref, pieces, 0)
    x = x_ref[...].astype(F32)
    mean = jnp.mean(x, -1, keepdims=True)
    centred = x - mean
    scale = lax.rsqrt(jnp.mean(centred * centred, -1, keepdims=True) + EPS)
    mean_ref[...] = mean
    scale_ref[...] = scale
    h = (centred * scale * gain_ref[...] + shift_ref[...]).astype(BF)
    h_ref[...] = h
    linear = dot(h, w_ref[...]) + bias_ref[...]
    lane = lax.broadcasted_iota(jnp.int32, (x.shape[0], 128), 1)
    cosine, sine = cos_ref[...], sin_ref[...]
    q_ref[...] = turn(linear[:, :128], cosine, sine, lane).astype(BF) * BF(HEAD_DIM**-0.5)
    kv_ref[:, :128] = turn(linear[:, 128:256], cosine, sine, lane).astype(BF)
    kv_ref[:, 128:] = linear[:, 256:384].astype(BF)
    pre = linear[:, 384:]
    pre_ref[...] = pre
    out_ref[...] = (0.5 * pre * (1.0 + jnp.tanh(0.7978845608 * (pre + 0.044715 * pre * pre * pre)))).astype(BF)


def half_rows(begin, block, lanes):
    return pl.BlockSpec((block, lanes), lambda i: (i + begin, 0))


def front(pieces, held, gain, shift, weight, bias, cosine, sine):
    block, width = pieces[0].shape
    rows = 8 * block
    cols = weight.shape[1]
    wide = cols - 384
    here = functools.partial(half_rows, 4 if held else 0, block)
    lanes = (width, 128, 256, wide, wide, 1, 1)
    types = (BF, BF, BF, F32, BF, F32, F32)
    return pl.pallas_call(
        front_kernel,
        grid=(4,),
        in_specs=piece_specs(pieces)
        + [whole(1, width), whole(1, width), whole(width, cols), whole(1, cols), here(128), here(128)]
        + [pl.BlockSpec(memory_space=pl.ANY)] * len(held),
        out_specs=[here(n) for n in lanes],
        out_shape=[jax.ShapeDtypeStruct((rows, n), kind) for n, kind in zip(lanes, types)],
        input_output_aliases={11 + i: i for i in range(len(held))},
        scratch_shapes=[pltpu.VMEM((block, width), BF)],
        compiler_params=pltpu.CompilerParams(vmem_limit_bytes=VMEM_LIMIT),
        cost_estimate=pl.CostEstimate(
            flops=rows * width * cols + 6 * rows * width, bytes_accessed=rows * width * 3, transcendentals=rows * wide
        ),
    )(*pieces, gain, shift, weight, bias, cosine, sine, *held)


def two_heads(value):
    lane = lax.broadcasted_iota(jnp.int32, value.shape, 1)
    zero = jnp.zeros_like(value)
    return jnp.concatenate([jnp.where(lane < HEAD_DIM, value, zero), jnp.where(lane < HEAD_DIM, zero, value)], 0)


def one_row(value):
    half = value.shape[0] // 2
    lane = lax.broadcasted_iota(jnp.int32, (half, 128), 1)
    return jnp.where(lane < HEAD_DIM, value[:half], value[half:])


def allowed_pairs(meta_ref, block, query_at, key_at):
    turned, length = meta_ref[0], meta_ref[1]
    shape = (2 * block, block)
    query = query_at * block + ((lax.broadcasted_iota(jnp.int32, shape, 0) & (block - 1)) ^ turned)
    key = key_at * block + (lax.broadcasted_iota(jnp.int32, shape, 1) ^ turned)
    return (key <= query) & (key < length)


def key_ranges(meta_ref, block, query_at):
    length = meta_ref[1]
    plain = jnp.minimum(query_at, length // block)
    last = jnp.minimum(query_at + 1, (length + block - 1) // block)
    return plain, last


def spot_of(at):
    near = 2 * Z_LEN
    spot = lax.rem(at, near)
    return lax.div(at, near) * 4 + lax.div(spot, 4) * 2 + lax.rem(spot, 2), slice(None), lax.rem(lax.div(spot, 2), 2)


def rows_of(ref, at):
    value = ref[spot_of(at)]
    return value.reshape(value.shape[0] * value.shape[1], value.shape[2])


def add_rows(ref, at, value):
    ref[spot_of(at)] += value.reshape(4, value.shape[0] // 4, value.shape[1])


def flat(ref):
    value = ref[0, :, 0]
    return value.reshape(value.shape[0] * value.shape[1], value.shape[2])


def attend_kernel(block, meta_ref, query_ref, order_ref, q_ref, kv_ref, full_ref, low_ref, lse_ref):
    query_at = query_ref[pl.program_id(0)]
    queries = two_heads(flat(q_ref))

    def step(masked, at, state):
        top, total, mixed = state
        both = rows_of(kv_ref, order_ref[at])
        scores = dot_rows(queries, both[:, :128])
        if masked:
            allowed = allowed_pairs(meta_ref, block, query_at, at)
            scores = jnp.where(allowed, scores, NEG)
        fresh = jnp.maximum(top, jnp.max(scores, -1, keepdims=True))
        factor = jnp.exp(top - fresh)
        weights = jnp.exp(scores - fresh)
        if masked:
            weights = jnp.where(allowed, weights, 0.0)
        total = total * factor + jnp.sum(weights, -1, keepdims=True)
        return fresh, total, mixed * factor + dot(weights.astype(BF), both[:, 128:])

    state = (
        jnp.full((2 * block, 1), NEG, F32),
        jnp.zeros((2 * block, 1), F32),
        jnp.zeros((2 * block, 128), F32),
    )
    plain, last = key_ranges(meta_ref, block, query_at)
    state = lax.fori_loop(0, plain, functools.partial(step, False), state)
    top, total, mixed = lax.fori_loop(plain, last, functools.partial(step, True), state)
    full = one_row(mixed / total)
    shape = full_ref.shape[1:2] + full_ref.shape[3:]
    full_ref[0, :, 0] = full.reshape(shape)
    low_ref[0, :, 0] = full.astype(BF).reshape(shape)
    lse_ref[...] = jnp.broadcast_to(top + jnp.log(total), lse_ref.shape)


def placed(share, lanes):
    return pl.BlockSpec((1, 4, 1, share, lanes), lambda i, *_: ((i // 4) * 2 + i % 2, 0, (i // 2) % 2, 0, 0))


def attend(table, q, kv, share):
    block = 4 * share
    blocks = 2 * Z_LEN
    rows, keys = q.shape[0], kv.shape[0]
    shape = (4, 4, Z_LEN // 2, share, 128)
    kv_shape = (keys // (2 * Z_LEN * share), 4, Z_LEN // 2, share, 256)
    full, low, lse = pl.pallas_call(
        functools.partial(attend_kernel, block),
        grid_spec=pltpu.PrefetchScalarGridSpec(
            num_scalar_prefetch=3,
            grid=(blocks,),
            in_specs=[placed(share, 128), pl.BlockSpec(kv_shape, lambda i, *_: (0, 0, 0, 0, 0))],
            out_specs=[placed(share, 128), placed(share, 128), pl.BlockSpec((2 * block, 128), lambda i, *_: (i, 0))],
        ),
        out_shape=[
            jax.ShapeDtypeStruct(shape, F32),
            jax.ShapeDtypeStruct(shape, BF),
            jax.ShapeDtypeStruct((2 * rows, 128), F32),
        ],
        compiler_params=pltpu.CompilerParams(vmem_limit_bytes=VMEM_LIMIT),
        cost_estimate=pl.CostEstimate(
            flops=16 * rows * keys * 128, bytes_accessed=rows * 128 * 16, transcendentals=rows * keys
        ),
    )(*table, q.reshape(shape), kv.reshape(kv_shape))
    return full, low.reshape(rows, 128), lse


def attend_back_kernel(blocks, block, meta_ref, query_ref, order_ref, q_ref, kv_ref, full_ref, lse_ref, grad_ref, dq_ref, dkv_ref, dk_acc, dv_acc):
    at_block = pl.program_id(0)
    query_at = query_ref[at_block]
    queries = two_heads(flat(q_ref))
    grads = two_heads(flat(grad_ref))
    full = flat(full_ref)
    delta = jnp.sum(grads.astype(F32) * jnp.concatenate([full, full], 0), -1, keepdims=True)
    lse = lse_ref[:, :1]

    @pl.when(at_block == 0)
    def _():
        dk_acc[...] = jnp.zeros_like(dk_acc)
        dv_acc[...] = jnp.zeros_like(dv_acc)

    def step(masked, at, grad_query):
        spot = order_ref[at]
        both = rows_of(kv_ref, spot)
        keys = both[:, :128]
        scores = dot_rows(queries, keys)
        if masked:
            allowed = allowed_pairs(meta_ref, block, query_at, at)
            scores = jnp.where(allowed, scores, NEG)
        weights = jnp.exp(scores - lse)
        if masked:
            weights = jnp.where(allowed, weights, 0.0)
        grad_scores = (weights * (dot_rows(grads, both[:, 128:]) - delta)).astype(BF)
        add_rows(dk_acc, spot, dot_cols(grad_scores, queries))
        add_rows(dv_acc, spot, dot_cols(weights.astype(BF), grads))
        return grad_query + dot(grad_scores, keys)

    plain, last = key_ranges(meta_ref, block, query_at)
    grad_query = jnp.zeros((2 * block, 128), F32)
    grad_query = lax.fori_loop(0, plain, functools.partial(step, False), grad_query)
    grad_query = lax.fori_loop(plain, last, functools.partial(step, True), grad_query)
    shape = dq_ref.shape[1:2] + dq_ref.shape[3:]
    dq_ref[0, :, 0] = (one_row(grad_query) * HEAD_DIM**-0.5).astype(BF).reshape(shape)

    @pl.when(at_block == blocks - 1)
    def _():
        dkv_ref[..., :128] = dk_acc[...].astype(BF)
        dkv_ref[..., 128:] = dv_acc[...].astype(BF)


def attend_back(table, q, kv, full, lse, grad, share):
    block = 4 * share
    blocks = 2 * Z_LEN
    rows, keys = q.shape[0], kv.shape[0]
    shape = (4, 4, Z_LEN // 2, share, 128)
    kv_shape = (keys // (2 * Z_LEN * share), 4, Z_LEN // 2, share, 256)
    kv_spec = pl.BlockSpec(kv_shape, lambda i, *_: (0, 0, 0, 0, 0))
    dq, dkv = pl.pallas_call(
        functools.partial(attend_back_kernel, blocks, block),
        grid_spec=pltpu.PrefetchScalarGridSpec(
            num_scalar_prefetch=3,
            grid=(blocks,),
            in_specs=[
                placed(share, 128),
                kv_spec,
                placed(share, 128),
                pl.BlockSpec((2 * block, 128), lambda i, *_: (i, 0)),
                placed(share, 128),
            ],
            out_specs=[placed(share, 128), kv_spec],
            scratch_shapes=[pltpu.VMEM(kv_shape[:-1] + (128,), F32), pltpu.VMEM(kv_shape[:-1] + (128,), F32)],
        ),
        out_shape=[jax.ShapeDtypeStruct(shape, BF), jax.ShapeDtypeStruct(kv_shape, BF)],
        compiler_params=pltpu.CompilerParams(vmem_limit_bytes=VMEM_LIMIT),
        cost_estimate=pl.CostEstimate(
            flops=40 * rows * keys * 128, bytes_accessed=rows * 128 * 24, transcendentals=rows * keys
        ),
    )(*table, q.reshape(shape), kv.reshape(kv_shape), full, lse, grad.reshape(shape))
    return dq.reshape(rows, 128), dkv.reshape(keys, 256)


def store_spots(parts, total):
    to_x, to_y, rest = parts
    half = total.shape[0] // 2
    total = total.astype(BF)
    places = (((rest, 0), (rest, 1)), ((to_x, 1), (rest, 3)), ((rest, 2), (to_y, 1)), ((to_x, 0), (to_y, 0)))
    for at, (low, high) in enumerate(places):

        @pl.when(pl.program_id(0) == at)
        def _(low=low, high=high):
            low[0][low[1] * half : (low[1] + 1) * half] = total[:half]
            high[0][high[1] * half : (high[1] + 1) * half] = total[half:]


def spot_specs(block, width):
    return [whole(block, width), whole(block, width), whole(2 * block, width)]


def spot_shapes(block, width):
    return [jax.ShapeDtypeStruct((rows, width), BF) for rows in (block, block, 2 * block)]


def out_kernel(attn_ref, units_ref, w_ref, *parts):
    store_spots(parts, dot_rows(attn_ref[...], w_ref[:, :128]) + dot_rows(units_ref[...], w_ref[:, 128:]))


def out_partial(attn, units, weight, block, begin):
    rows, width = attn.shape[0], weight.shape[0]
    return pl.pallas_call(
        out_kernel,
        grid=(4,),
        in_specs=[half_rows(begin, block, 128), half_rows(begin, block, units.shape[1]), whole(*weight.shape)],
        out_specs=spot_specs(block, width),
        out_shape=spot_shapes(block, width),
        compiler_params=pltpu.CompilerParams(vmem_limit_bytes=VMEM_LIMIT),
        cost_estimate=pl.CostEstimate(
            flops=rows * width * weight.shape[1], bytes_accessed=rows * width, transcendentals=0
        ),
    )(attn, units, weight)


def branch_kernel(*refs):
    one, two, (w_ref, pre_ref, attn_ref, grad_ref, g_ref) = refs[:5], refs[5:10], refs[10:]
    take_rows(g_ref, one, 0)
    take_rows(g_ref, two, 4)
    both = dot(g_ref[...], w_ref[...])
    attn_ref[...] = both[:, :128].astype(BF)
    u = pre_ref[...]
    square = u * u
    bend = jnp.tanh(0.7978845608 * u * (1.0 + 0.044715 * square))
    slope = 0.5 * (1.0 + bend) + 0.5 * u * (1.0 - bend * bend) * (0.7978845608 * (1.0 + 3 * 0.044715 * square))
    grad_ref[...] = (both[:, 128:] * slope).astype(BF)


def branch_grads(pieces, weight, pre, block):
    width = weight.shape[0]
    rows, wide = pre.shape
    return pl.pallas_call(
        branch_kernel,
        grid=(rows // block,),
        in_specs=piece_specs(pieces) + [whole(*weight.shape), by_row(block, wide)],
        out_specs=[by_row(block, 128), by_row(block, wide), by_row(block, width)],
        out_shape=[
            jax.ShapeDtypeStruct((rows, 128), BF),
            jax.ShapeDtypeStruct((rows, wide), BF),
            jax.ShapeDtypeStruct((rows, width), BF),
        ],
        compiler_params=pltpu.CompilerParams(vmem_limit_bytes=VMEM_LIMIT),
        cost_estimate=pl.CostEstimate(
            flops=2 * rows * width * weight.shape[1], bytes_accessed=rows * width * 4, transcendentals=rows * wide
        ),
    )(*pieces, weight, pre)


def turn_back(value, cosine, sine, lane):
    return turn(value.astype(F32), cosine, -sine, lane).astype(BF)


def back_kernel(*refs):
    pieces, refs = refs[:5], refs[5:]
    dq_ref, dkv_ref, units_ref, w_ref, cos_ref, sin_ref, mean_ref, scale_ref = refs[:8]
    parts, (linear_ref, gain_ref, shift_ref, small_ref, x_ref) = refs[-8:-5], refs[-5:]
    take_rows(x_ref, pieces, 0)
    lane = lax.broadcasted_iota(jnp.int32, dq_ref.shape, 1)
    cosine, sine = cos_ref[...], sin_ref[...]
    linear_ref[:, :128] = turn_back(dq_ref[...], cosine, sine, lane)
    linear_ref[:, 128:256] = turn_back(dkv_ref[:, :128], cosine, sine, lane)
    linear_ref[:, 256:] = dkv_ref[:, 128:]
    linear = linear_ref[...]
    units = units_ref[...]
    total = dot_rows(linear, w_ref[:, :384]) + dot_rows(units, w_ref[:, 384:])
    store_spots(parts, total)
    normed = (x_ref[...].astype(F32) - mean_ref[...]) * scale_ref[...]

    @pl.when(pl.program_id(0) == 0)
    def _():
        gain_ref[...] = jnp.zeros_like(gain_ref)
        shift_ref[...] = jnp.zeros_like(shift_ref)
        small_ref[...] = jnp.zeros_like(small_ref)

    gain_ref[...] += jnp.sum(total * normed, 0, keepdims=True)
    shift_ref[...] += jnp.sum(total, 0, keepdims=True)
    small_ref[:, :384] += jnp.sum(linear.astype(F32), 0, keepdims=True)
    small_ref[:, 384:] += jnp.sum(units.astype(F32), 0, keepdims=True)


def back_partial(pieces, dq, dkv, units, weight, cosine, sine, mean, scale, block, begin, held):
    rows = dq.shape[0]
    width, cols = weight.shape
    here = lambda lanes: half_rows(begin, block, lanes)
    *parts, linear, gain, shift, small = pl.pallas_call(
        back_kernel,
        grid=(4,),
        in_specs=piece_specs(pieces)
        + [here(128), here(256), here(units.shape[1]), whole(*weight.shape), here(128), here(128), here(1), here(1)]
        + [pl.BlockSpec(memory_space=pl.ANY)] * len(held),
        out_specs=spot_specs(block, width) + [here(384), whole(1, width), whole(1, width), whole(1, cols)],
        out_shape=spot_shapes(block, width)
        + [
            jax.ShapeDtypeStruct((rows, 384), BF),
            jax.ShapeDtypeStruct((1, width), F32),
            jax.ShapeDtypeStruct((1, width), F32),
            jax.ShapeDtypeStruct((1, cols), F32),
        ],
        input_output_aliases={13 + i: 3 + i for i in range(len(held))},
        scratch_shapes=[pltpu.VMEM((block, width), BF)],
        compiler_params=pltpu.CompilerParams(vmem_limit_bytes=VMEM_LIMIT),
        cost_estimate=pl.CostEstimate(
            flops=rows * width * cols, bytes_accessed=rows * width * 2, transcendentals=0
        ),
    )(*pieces, dq, dkv, units, weight, cosine, sine, mean, scale, *held)
    return parts, linear, jnp.concatenate([gain, shift, small], 1)


def weight_kernel(core_ref, rows_ref, *refs):
    *others, out_ref = refs
    rows = rows_ref[...]
    begin = 0
    for other in others:
        end = begin + other.shape[1]
        out_ref[0, 0, :, begin:end] = dot_cols(rows, other[...]).astype(BF)
        begin = end


def weight_grads(core, left, *rights):
    rows, width = left.shape
    cols = sum(right.shape[1] for right in rights)
    quarter = width // 4
    return pl.pallas_call(
        weight_kernel,
        grid_spec=pltpu.PrefetchScalarGridSpec(
            num_scalar_prefetch=1,
            grid=(4,),
            in_specs=[pl.BlockSpec((rows, quarter), lambda i, c: (0, i))]
            + [pl.BlockSpec(right.shape, lambda i, c: (0, 0)) for right in rights],
            out_specs=pl.BlockSpec((1, 1, quarter, cols), lambda i, c: ((i + c[0]) % 2, i // 2, 0, 0)),
        ),
        out_shape=jax.ShapeDtypeStruct((2, 2, quarter, cols), BF),
        compiler_params=pltpu.CompilerParams(vmem_limit_bytes=VMEM_LIMIT),
        cost_estimate=pl.CostEstimate(
            flops=2 * rows * width * cols, bytes_accessed=2 * rows * width, transcendentals=0
        ),
    )(core[None], left, *rights)


def pack_kernel(triple_ref, expand_ref, shrink_ref, in_ref, out_ref):
    ranks = in_ref.shape[0]
    near = ranks // 2
    wide = out_ref.shape[2]
    for rank in range(ranks):
        hx, b8 = rank // near, rank % near
        for s in range(3):
            pair = [
                triple_ref[:, pl.ds((s * HEADS + hx * 2 * near + c * near + b8) * HEAD_DIM, HEAD_DIM)] for c in range(2)
            ]
            in_ref[rank, :, s * 128 : (s + 1) * 128] = jnp.concatenate(pair, 1)
        in_ref[rank, :, 384:] = expand_ref[:, rank * wide : (rank + 1) * wide]
        out_ref[rank] = shrink_ref[:, rank * wide : (rank + 1) * wide]


def pack(triple, expand, shrink, ranks):
    held = triple.shape[0]
    wide = expand.shape[1] // ranks
    return pl.pallas_call(
        pack_kernel,
        out_shape=[
            jax.ShapeDtypeStruct((ranks, held, 384 + wide), BF),
            jax.ShapeDtypeStruct((ranks, held, wide), BF),
        ],
        compiler_params=pltpu.CompilerParams(vmem_limit_bytes=VMEM_LIMIT),
    )(triple, expand, shrink)


def unpack_in_kernel(back_ref, triple_ref, expand_ref):
    ranks = back_ref.shape[0]
    near = ranks // 2
    wide = back_ref.shape[2] - 384
    for rank in range(ranks):
        expand_ref[:, rank * wide : (rank + 1) * wide] = back_ref[rank, :, 384:].astype(F32)
    for rank in range(0, ranks, 2):
        hx, b8 = rank // near, rank % near
        for s in range(3):
            for c in range(2):
                lanes = slice(s * 128 + c * HEAD_DIM, s * 128 + (c + 1) * HEAD_DIM)
                pair = jnp.concatenate([back_ref[rank, :, lanes], back_ref[rank + 1, :, lanes]], 1)
                at = (s * HEADS + hx * 2 * near + c * near + b8) * HEAD_DIM
                triple_ref[:, at : at + 128] = pair.astype(F32)


def unpack_in(back):
    ranks, held, cols = back.shape
    return pl.pallas_call(
        unpack_in_kernel,
        out_shape=[
            jax.ShapeDtypeStruct((held, 3 * HEADS * HEAD_DIM), F32),
            jax.ShapeDtypeStruct((held, ranks * (cols - 384)), F32),
        ],
        compiler_params=pltpu.CompilerParams(vmem_limit_bytes=VMEM_LIMIT),
    )(back)


def unpack_out_kernel(back_ref, shrink_ref):
    wide = back_ref.shape[2]
    for rank in range(back_ref.shape[0]):
        shrink_ref[:, rank * wide : (rank + 1) * wide] = back_ref[rank].astype(F32)


def unpack_out(back):
    ranks, held, cols = back.shape
    return pl.pallas_call(
        unpack_out_kernel,
        out_shape=jax.ShapeDtypeStruct((held, ranks * cols), F32),
        compiler_params=pltpu.CompilerParams(vmem_limit_bytes=VMEM_LIMIT),
    )(back)


def turn_tables(positions):
    half = ROT // 2
    inverse = 10000.0 ** (-(jnp.arange(half, dtype=F32) * 2.0) / ROT)
    angles = positions.astype(F32)[:, None] * inverse[None, :]
    cosine, sine = jnp.cos(angles), jnp.sin(angles)
    rest = (positions.shape[0], HEAD_DIM - ROT)
    cosine = jnp.concatenate([cosine, cosine, jnp.ones(rest, F32)], 1)
    sine = jnp.concatenate([-sine, sine, jnp.zeros(rest, F32)], 1)
    return jnp.tile(cosine, (1, 2)), jnp.tile(sine, (1, 2))


def core_pair(own, other, core):
    return jnp.where(core == 0, jnp.stack([own, other], 1), jnp.stack([other, own], 1))


def body(
    inputs,
    norm_gain,
    norm_bias,
    triple_weight,
    triple_bias,
    dense_weight,
    dense_bias,
    expand_weight,
    expand_bias,
    shrink_weight,
    shrink_bias,
    lengths,
    block_order,
    cotangent,
):
    share, width = inputs.shape[2], inputs.shape[3]
    hx, core, bs, bz, by = (lax.axis_index(name) for name in ALL)
    spread = lax.axis_size("bs")
    ranks = 2 * Z_LEN * 2
    devices = 2 * ranks * spread
    block = 4 * share
    rows = ranks * 2 * share
    near_blocks = Z_LEN * 2
    blocks = block_order.shape[0]
    held = width // devices
    ff = expand_weight.shape[1]
    ff_here = ff // ranks
    length = lengths[core]

    def block_at(index):
        return jnp.sum(jnp.where(jnp.arange(blocks, dtype=jnp.int32) == index, block_order, 0))

    token_pos = (
        block_at(bs * near_blocks + bz * 2 + by) * block
        + (hx * 2 + core) * share
        + jnp.arange(share, dtype=jnp.int32)
    )
    valid = (token_pos[None, :] < lengths[:, None]).astype(F32)[:, :, None]

    spots = jnp.arange(blocks, dtype=jnp.int32)
    within = spots % near_blocks
    index = spots - within + ((bz + Z_LEN - within // 2) % Z_LEN) * 2 + (by + within) % 2
    key_at = jnp.sum(jnp.where(index[:, None] == spots[None, :], block_order[None, :], 0), 1)
    query_at = lax.dynamic_slice_in_dim(key_at, bs * near_blocks, near_blocks)
    turned = hx * 2 * share + core * share
    inside = (jnp.arange(block, dtype=jnp.int32) ^ turned).reshape(1, 1, 4, 1, share)
    block_pos = query_at.reshape(2, Z_LEN // 2, 2).transpose(0, 2, 1)[:, :, None, :, None]
    row_pos = (block_pos * block + inside).reshape(rows)
    order = jnp.sum(jnp.where(key_at[None, :] == spots[:, None], spots[None, :], 0), 1)
    table = jnp.where(jnp.arange(2) == 0, turned, length).astype(jnp.int32), query_at, order
    cosine, sine = turn_tables(row_pos)

    def to_cols(sent):
        got = lax.all_to_all(sent, RANK, split_axis=0, concat_axis=0, tiled=True)
        got = got.reshape(2, 1, near_blocks, held, sent.shape[2])
        return lax.all_gather(got, "bs", axis=1, tiled=True) if spread > 1 else got

    def to_rows(mine):
        cols = mine.shape[-1]
        if spread > 1:
            mine = mine.reshape(2, spread, near_blocks, held, cols)
            mine = lax.psum_scatter(mine, "bs", scatter_dimension=1, tiled=True)
        return lax.all_to_all(mine.reshape(ranks, held, cols), RANK, split_axis=0, concat_axis=0, tiled=True)

    x_a = lax.dynamic_index_in_dim(inputs[:, 0], core, 0, keepdims=False)
    x_b = swap(lax.dynamic_index_in_dim(inputs[:, 0], 1 - core, 0, keepdims=False), "core")
    x_a1, x_b1 = ring(x_a), ring(x_b)
    grad_y = (cotangent[:, 0].astype(F32) * valid).astype(BF)
    g_a = lax.dynamic_index_in_dim(grad_y, core, 0, keepdims=False)
    g_b = swap(lax.dynamic_index_in_dim(grad_y, 1 - core, 0, keepdims=False), "core")
    sent_in, sent_out = pack(triple_weight, expand_weight, shrink_weight, ranks)
    small = jnp.concatenate([norm_gain, norm_bias, triple_bias, expand_bias, dense_bias, shrink_bias])
    g_0 = jnp.stack([g_a, g_b])

    x_1 = jnp.stack([x_a1, x_b1])
    x_1, own_one = fence((x_1, pair((x_a, x_b), x_1)), g_0, sent_in)
    got_one = both_ways(own_one)
    x_2 = ring(x_1)
    x_3 = ring(x_2)

    got_one, own_two, sent_in, small = fence((got_one, pair(x_2, x_3), sent_in, small))
    got_in = to_cols(sent_in)
    far_one = far_ways(*got_one)
    got_two = both_ways(own_two)
    small = gather_small(small, devices)
    x_one = (own_one, *got_one, *far_one)

    got_two, g_0, small = fence((got_two, g_0, small), far_one)
    far_two = far_ways(*got_two)
    g_1 = ring(g_0)
    x_two = (own_two, *got_two, *far_two)
    got_in = fence((got_in,), g_1)[0]
    weight_in = core_pair(got_in, swap(got_in, "core"), core).reshape(width, -1)

    cuts = [0]
    for leaf in (norm_gain, norm_bias, triple_bias, expand_bias, dense_bias, shrink_bias):
        cuts.append(cuts[-1] + leaf.shape[0])
    gain, shift, triple_b, expand_b, dense_b, shrink_b = (
        small[:, low:high].reshape(-1).astype(F32) for low, high in zip(cuts[:-1], cuts[1:])
    )
    rank = hx * near_blocks + bz * 2 + by
    bias_triple = lax.dynamic_index_in_dim(
        triple_b.reshape(3, 2, 2, near_blocks, HEAD_DIM).transpose(1, 3, 0, 2, 4).reshape(ranks, 384), rank, 0
    )
    bias_expand = lax.dynamic_index_in_dim(expand_b.reshape(ranks, ff_here), rank, 0)
    bias_in = jnp.concatenate([bias_triple, bias_expand], 1)

    weight_in, g_1, own_one = fence((weight_in, g_1, pair(g_0, g_1)), far_two)
    got_one = both_ways(own_one)
    g_2 = ring(g_1)
    g_3 = ring(g_2)
    into = (gain[None], shift[None], weight_in, bias_in, cosine, sine)
    h, q, kv, pre, expand_out, mean, scale = front(x_two, front(x_one, (), *into), *into)

    q, got_one, own_two, sent_out = fence((q, got_one, pair(g_2, g_3), sent_out))
    got_out = to_cols(sent_out)
    far_one = far_ways(*got_one)
    got_two = both_ways(own_two)
    g_one = (own_one, *got_one, *far_one)
    kv_all = kv if spread == 1 else lax.all_gather(kv, "bs", axis=0, tiled=True)
    attn_full, attn_low, lse = attend(table, q, kv_all, share)

    attn_low, got_out, got_two = fence((attn_low, got_out, got_two), far_one)
    far_two = far_ways(*got_two)
    g_two = (own_two, *got_two, *far_two)
    shrink_here = core_pair(got_out, swap(got_out, "core"), core).reshape(width, -1)
    if spread == 1:
        dense_pair = core_pair(dense_weight[None], swap(dense_weight, "core")[None], core).reshape(128, width)
    else:
        dense_all = lax.all_gather(dense_weight, ALL, axis=0, tiled=True).reshape(2, 2, near_blocks, HEAD_DIM, width)
        dense_pair = lax.dynamic_index_in_dim(
            lax.dynamic_index_in_dim(dense_all, hx, 0, keepdims=False), bz * 2 + by, 1, keepdims=False
        ).reshape(128, width)
    weight_out = jnp.concatenate([dense_pair.T, shrink_here], 1)
    o_two = out_partial(attn_low, expand_out, weight_out, block, 4)
    o_one = out_partial(attn_low, expand_out, weight_out, block, 0)

    o_one, o_two, g_one, g_two = fence((o_one, o_two, g_one, g_two))
    got_two = swap(o_two[0], "hx"), swap(o_two[1], "by")
    grad_attention, grad_pre, g_all = branch_grads(g_one + g_two, weight_out, pre, block)
    shrink_grads = weight_grads(core, g_all, expand_out)

    grad_attention, shrink_grads, o_one, terms = fence((grad_attention, shrink_grads, o_one, far_terms(o_two[2], got_two)))
    far_two = far_back(terms)
    got_one_out = swap(o_one[0], "hx"), swap(o_one[1], "by")
    dq, dkv = attend_back(table, q, kv_all, attn_full, lse, grad_attention, share)
    if spread > 1:
        dkv = lax.psum_scatter(dkv, "bs", scatter_dimension=0, tiled=True)
    mine = add_low(shrink_grads[0], swap(shrink_grads[1], "core"))

    dq, mine, terms, out_two = fence((dq, mine, far_terms(o_one[2], got_one_out), square_sums(o_two[2], got_two, far_two, share)))
    shrink_rows = to_rows(mine)
    far_one = far_back(terms)
    out_sum = ring_back(out_two[1])
    from_back = (dq, dkv, grad_pre, weight_in, cosine, sine, mean, scale, block)
    h_two, grad_linear, sums_two = back_partial(x_two, *from_back, 4, ())

    h_two, grad_linear, out_sum = fence((h_two, grad_linear, out_sum), far_one)
    got_two = swap(h_two[0], "hx"), swap(h_two[1], "by")
    out_sum = ring_back(out_sum + out_two[0])
    h_one, grad_linear, sums_one = back_partial(x_one, *from_back, 0, (grad_linear,))

    grad_linear, h, h_one, terms, out_sum = fence((grad_linear, h, h_one, far_terms(h_two[2], got_two), out_sum))
    far_two = far_back(terms)
    got_one = swap(h_one[0], "hx"), swap(h_one[1], "by")
    in_grads = weight_grads(core, h, grad_linear, grad_pre)
    mine = add_low(in_grads[0], swap(in_grads[1], "core"))
    in_rows = to_rows(mine)
    out_one = square_sums(o_one[2], got_one_out, far_one, share)
    out_sum = ring_back(out_sum + out_one[1]) + out_one[0]
    sum_gain, sum_shift, sum_in = jnp.split(sums_one + sums_two, [width, 2 * width], 1)

    terms, h_sums, sum_in, g_all = fence(
        (far_terms(h_one[2], got_one), square_sums(h_two[2], got_two, far_two, share), sum_in, g_all), shrink_rows
    )
    far_one = far_back(terms)
    h_sum = ring_back(h_sums[1])
    grad_dense_here = dot_cols(g_all, attn_low)
    grad_shrink = unpack_out(shrink_rows)

    h_sums, h_sum, h_more, out_sum = fence((h_sums, h_sum, square_sums(h_one[2], got_one, far_one, share), out_sum))
    h_sum = ring_back(ring_back(h_sum + h_sums[0]) + h_more[1]) + h_more[0]
    grad_triple, grad_expand = unpack_in(in_rows)

    dense_grads = grad_dense_here.T.reshape(2, HEAD_DIM, width)
    if spread == 1:
        dense_mine = lax.dynamic_index_in_dim(dense_grads, core, 0, keepdims=False)
        dense_away = lax.dynamic_index_in_dim(dense_grads, 1 - core, 0, keepdims=False)
        grad_dense = dense_mine + swap(dense_away.astype(BF), "core").astype(F32)
    else:
        spot = jnp.arange(ranks, dtype=jnp.int32).reshape(2, 1, near_blocks, 1, 1) == rank
        dense_whole = jnp.where(spot, dense_grads[None, :, None], 0.0).reshape(width, width)
        grad_dense = lax.psum_scatter(dense_whole, ALL, scatter_dimension=0, tiled=True)

    here = jnp.arange(ranks, dtype=jnp.int32)[:, None] == rank
    sum_triple = (
        jnp.where(here, sum_in[:, :384], 0.0)
        .reshape(2, near_blocks, 3, 2, HEAD_DIM)
        .transpose(2, 0, 3, 1, 4)
        .reshape(3 * width)
    )
    sum_expand = jnp.where(here, sum_in[:, 384:], 0.0).reshape(ff)
    sum_y = jnp.sum(grad_y.astype(F32), (0, 1))
    pieces = [leaf.reshape(devices, -1) for leaf in (sum_gain, sum_shift, sum_triple, sum_expand, sum_y)]
    terms = scatter_small(jnp.concatenate(pieces, 1), devices)
    terms = fence(terms, h_sum)
    small_all = small_sum(terms, devices)
    small_grads = []
    begin = 0
    for piece in pieces:
        small_grads.append(small_all[begin : begin + piece.shape[1]])
        begin += piece.shape[1]
    small_gain, small_shift, small_triple, small_expand, small_out = small_grads

    source = inputs[:, 0].astype(F32)
    out_away = swap(out_sum[1].astype(BF), "core").astype(F32)
    mixed = jnp.where(core == 0, jnp.stack([out_sum[0], out_away]), jnp.stack([out_away, out_sum[0]]))
    output = (valid * (source + mixed + dense_b + shrink_b)).astype(BF).reshape(inputs.shape)

    h_away = swap(h_sum[1].astype(BF), "core").astype(F32)
    grad_h = jnp.where(core == 0, jnp.stack([h_sum[0], h_away]), jnp.stack([h_away, h_sum[0]]))
    centred = source - jnp.mean(source, -1, keepdims=True)
    scale = lax.rsqrt(jnp.mean(centred * centred, -1, keepdims=True) + EPS)
    normed = centred * scale
    g = grad_h * gain
    grad_source = scale * (
        g - jnp.mean(g, -1, keepdims=True) - normed * jnp.mean(g * normed, -1, keepdims=True)
    )
    grad_inputs = (grad_y.astype(F32) + grad_source).astype(BF).reshape(inputs.shape)
    return (
        output,
        grad_inputs,
        small_gain,
        small_shift,
        grad_triple,
        small_triple,
        grad_dense,
        small_out,
        grad_expand,
        small_expand,
        grad_shrink,
        small_out,
    )


def solution(mesh):
    head, blk = mesh.devices.shape
    split = Mesh(mesh.devices.reshape(head // 2, 2, blk // (2 * Z_LEN), Z_LEN, 2), ALL)
    tokens = P(None, ("bs", "bz", "by"), ("hx", "core"), None)
    vector = P(ALL)
    matrix = P(ALL, None)
    return jax.shard_map(
        body,
        mesh=split,
        in_specs=(
            tokens,
            vector,
            vector,
            matrix,
            vector,
            matrix,
            vector,
            matrix,
            vector,
            matrix,
            vector,
            P(),
            P(),
            tokens,
        ),
        out_specs=(
            tokens,
            tokens,
            vector,
            vector,
            matrix,
            vector,
            matrix,
            vector,
            matrix,
            vector,
            matrix,
            vector,
        ),
        check_vma=False,
    )
```

time: 891 us -> 571 us (0.64)
  the two profiles are of different devices: /device:TPU:9 before, /device:TPU:17 now
where the time goes in v2:
time: 571 us; the launch traced here: 561 us
  Pallas kernels  180 us (32%)
  waiting for transfers between devices  173 us (30%)
  starting transfers between devices  103 us (18%)
  other arithmetic  59.4 us (10%)
  local copies, waits for them, and re-layouts  37 us (6%)
    ppermute x48, waiting for transfers between devices, swap(): return lax.ppermute(value, axis, SWAP)  91.1 us
    ppermute x48, starting transfers between devices, swap(): return lax.ppermute(value, axis, SWAP)  52.9 us
    pallas_call x1, Pallas kernels, attend_back(): pl.pallas_call(functools.partial(attend_back_kernel, blocks, block), grid...  34.6 us
    all_to_all x2, waiting for transfers between devices, to_rows(): lax.all_to_all(mine.reshape(ranks, held, cols), RANK, split_axis=0, conca...  34.3 us
    ppermute x7, waiting for transfers between devices, ring(): return lax.ppermute(value, 'bz', UP)  31.7 us
    pallas_call x2, Pallas kernels, back_partial(): pl.pallas_call(back_kernel, grid=(4,), in_specs=piece_specs(pieces) + [he...  29.7 us
    pallas_call x1, Pallas kernels, attend(): pl.pallas_call(functools.partial(attend_kernel, block), grid_spec=pltpu.P...  26.6 us
    pallas_call x2, Pallas kernels, front(): pl.pallas_call(front_kernel, grid=(4,), in_specs=piece_specs(pieces) + [w...  24.4 us
  transfers between devices with their start and end apart: 71, of which 25 were waited for; matrix products, arithmetic and copies ran while one was open for 16% of the time, Pallas kernels for 31%

profile of v2, /device:TPU:17, one launch (start us, length us, event | category | flops | bytes accessed | tf_op | source)
XLA Modules:
  0.0 561.0 jit_solution(14945403866133877415)
XLA Ops:
  8.0 3.7 shard_map.229
  14.0 5.6 %collective-permute-done.2 = bf16[64,2048]{1,0:T(8,128)(2,1)S(1)} collective-permute-done((bf16[64,2048]{1,0:T(8,128)(2,1)S(1)}, bf16[64,2048]{1,0:T(8,128)(2,1)S(1)}, u32[]{:S(2)}, u32[]{:S(2)}) %collective-permute-start.2) | collective-permute-done | bytes 262176 | tf_op jit(solution)/shard_map/ppermute | solution.py:53
  21.3 10.7 %collective-permute-done.6 = bf16[2,64,2048]{2,1,0:T(8,128)(2,1)S(1)} collective-permute-done((bf16[2,64,2048]{2,1,0:T(8,128)(2,1)S(1)}, bf16[2,64,2048]{2,1,0:T(8,128)(2,1)S(1)}, u32[]{:S(2)}, u32[]{:S(2)}) %collective-permute-start.6) | collective-permute-done | bytes 524320 | tf_op jit(solution)/shard_map/ppermute | solution.py:53
  35.8 7.9 %collective-permute-done.7 = bf16[2,64,2048]{2,1,0:T(8,128)(2,1)S(1)} collective-permute-done((bf16[2,64,2048]{2,1,0:T(8,128)(2,1)S(1)}, bf16[2,64,2048]{2,1,0:T(8,128)(2,1)S(1)}, u32[]{:S(2)}, u32[]{:S(2)}) %collective-permute-start.7) | collective-permute-done | bytes 524320 | tf_op jit(solution)/shard_map/ppermute | solution.py:53
  43.9 12.2 %collective-permute-done.5.refs_2_ = bf16[256,2048]{1,0:T(8,128)(2,1)S(1)} collective-permute-done((bf16[256,2048]{1,0:T(8,128)(2,1)S(1)}, bf16[256,2048]{1,0:T(8,128)(2,1)S(1)}, u32[]{:S(2)}, u32[]{:S(2)}) %collective-permute-start.5) | collective-permute-done | bytes 1048608 | tf_op jit(solution)/shard_map/ppermute | solution.py:33
  57.1 8.6 %all-to-all-start = ((bf16[16,64,896]{2,1,0:T(8,128)(2,1)}), bf16[16,64,896]{2,1,0:T(8,128)(2,1)S(1)}, u32[]{:S(2)}, u32[]{:S(2)}) async-start(bf16[16,64,896]{2,1,0:T(8,128)(2,1)} %get-tuple-element.149), calls=%async_computation | async-start | bytes 3670016 | tf_op jit(solution)/shard_map/all_to_all | solution.py:712
  69.5 4.9 collective-permute-start.13
  76.7 34.2 %collective-permute-done.14 = bf16[4,704]{1,0:T(4,128)(2,1)S(1)} collective-permute-done((bf16[4,704]{1,0:T(4,128)(2,1)S(1)}, bf16[4,704]{1,0:T(4,128)(2,1)S(1)}, u32[]{:S(2)}, u32[]{:S(2)}) %collective-permute-start.14) | collective-permute-done | bytes 5664 | tf_op jit(solution)/shard_map/ppermute | solution.py:33
  111.6 1.9 slice.291
  113.5 1.9 slice.290
  116.7 4.3 collective-permute-start.16
  123.0 2.0 collective-permute-done.15
  126.1 2.5 collective-permute-done.8.refs_3_
  128.6 2.1 collective-permute-start.20
  135.1 6.0 %collective-permute-done.20 = bf16[2,64,2048]{2,1,0:T(8,128)(2,1)} collective-permute-done((bf16[2,64,2048]{2,1,0:T(8,128)(2,1)}, bf16[2,64,2048]{2,1,0:T(8,128)(2,1)}, u32[]{:S(2)}, u32[]{:S(2)}) %collective-permute-start.20) | collective-permute-done | bytes 524320 | tf_op jit(solution)/shard_map/ppermute | solution.py:53
  141.0 2.3 collective-permute-start.21
  153.0 4.2 maximum_select_fusion
  157.2 3.6 collective-permute-done.18.refs_3_
  161.7 2.7 collective-permute-start.24
  166.5 12.2 %shard_map.230 = (bf16[2048,2048]{1,0:T(8,128)(2,1)}, bf16[2048,128]{1,0:T(8,128)(2,1)}, bf16[2048,256]{1,0:T(8,128)(2,1)}, f32[2048,512]{1,0:T(8,128)}, bf16[20...) custom-call(bf16[256,2048]{1,0:T(8,128)(2,1)} %copy-done.3, ...), custom_call_target="tpu_custom_call" | custom-call | flops 3783262208 | bytes 12582912 | tf_op jit(solution)/shard_map/pallas_call | solution.py:205
  178.7 4.1 collective-permute-start.25
  182.8 12.2 %shard_map.231 = (bf16[2048,2048]{1,0:T(8,128)(2,1)}, bf16[2048,128]{1,0:T(8,128)(2,1)}, bf16[2048,256]{1,0:T(8,128)(2,1)}, f32[2048,512]{1,0:T(8,128)}, bf16[20...) custom-call(bf16[256,2048]{1,0:T(8,128)(2,1)} %copy-done.1, ...), custom_call_target="tpu_custom_call", output_to_operand_aliasing={{0}: (11, {}), {1}: (12, {}), {2}: (13, {}), {3}: (14, {}),... | custom-call | flops 3783262208 | bytes 12582912 | tf_op jit(solution)/shard_map/pallas_call | solution.py:205
  195.2 4.8 all-to-all-start.1
  207.6 26.6 %shard_map.232 = (f32[4,4,2,64,128]{4,3,2,1,0:T(8,128)}, bf16[4,4,2,64,128]{4,3,2,1,0:T(8,128)(2,1)}, f32[4096,128]{1,0:T(8,128)}) custom-call(s32[2]{0:T(128)} %compare_select_fusion.6.meta_ref, s32[8]{0:T(128)} %copy-done.44, s32[8]{0:T(128)} %select_reduce_fusion.4.order_ref, bf16[4,4,2,64,128]{4,3,2,1,0:T(8,128)(2,1)} %bitcast.242, ...), custom_call_target="tpu_custom_call" | custom-call | flops 8589934592 | bytes 4194304 | tf_op jit(solution)/shard_map/pallas_call | solution.py:313
  234.3 11.1 %collective-permute-done.29.refs_4_ = bf16[128,2048]{1,0:T(8,128)(2,1)} collective-permute-done((bf16[128,2048]{1,0:T(8,128)(2,1)S(1)}, bf16[128,2048]{1,0:T(8,128)(2,1)}, u32[]{:S(2)}, u32[]{:S(2)}) %collective-permute-start.29) | collective-permute-done | bytes 524320 | tf_op jit(solution)/shard_map/ppermute | solution.py:33
  245.9 2.2 collective-permute-start.31
  248.6 2.1 collective-permute-done.30
  254.7 1.9 maximum_select_fusion.1
  258.3 8.4 %shard_map.234 = (bf16[256,2048]{1,0:T(8,128)(2,1)}, bf16[256,2048]{1,0:T(8,128)(2,1)}, bf16[512,2048]{1,0:T(8,128)(2,1)}) custom-call(bf16[2048,128]{1,0:T(8,128)(2,1)} %bitcast.235, bf16[2048,512]{1,0:T(8,128)(2,1)} %get-tuple-element.174.units_ref.refs_0_, bf16[2048,640]{1,0:T(8,128)(2,1)} %pad_maximum_fusion.w_ref.refs_10_), custom_call_target="tpu_custom_call" | custom-call | flops 2684354560 | bytes 4194304 | tf_op jit(solution)/shard_map/pallas_call | solution.py:435
  266.7 8.4 %shard_map.233 = (bf16[256,2048]{1,0:T(8,128)(2,1)}, bf16[256,2048]{1,0:T(8,128)(2,1)}, bf16[512,2048]{1,0:T(8,128)(2,1)}) custom-call(bf16[2048,128]{1,0:T(8,128)(2,1)} %bitcast.236, bf16[2048,512]{1,0:T(8,128)(2,1)} %get-tuple-element.174.units_ref.refs_0_, bf16[2048,640]{1,0:T(8,128)(2,1)} %pad_maximum_fusion.w_ref.refs_10_), custom_call_target="tpu_custom_call" | custom-call | flops 2684354560 | bytes 4194304 | tf_op jit(solution)/shard_map/pallas_call | solution.py:435
  277.8 15.5 %shard_map.235 = (bf16[2048,128]{1,0:T(8,128)(2,1)}, bf16[2048,512]{1,0:T(8,128)(2,1)}, bf16[2048,2048]{1,0:T(8,128)(2,1)}) custom-call(bf16[256,2048]{1,0:T(8,128)(2,1)} %pad_maximum_fusion.3.refs_0_, bf16[256,2048]{1,0:T(8,128)(2,1)} %collective-permute-done.22.refs_1_, bf16[256,2048]{1,0:T(8,128)(2,1)} %collective-permute-done.23.refs_2_, ...), custom_call_target="tpu_custom_call" | custom-call | flops 5368709120 | bytes 16777216 | tf_op jit(solution)/shard_map/pallas_call | solution.py:464
  293.3 9.0 %shard_map.236 = bf16[2,2,512,512]{3,2,1,0:T(8,128)(2,1)} custom-call(s32[1]{0:T(128)} %bitcast.50.core_ref, bf16[2048,2048]{1,0:T(8,128)(2,1)} %get-tuple-element.264.rows_ref, bf16[2048,512]{1,0:T(8,128)(2,1)} %get-tuple-element.174.units_ref.refs_0_), custom_call_target="tpu_custom_call" | custom-call | flops 4294967296 | bytes 8388608 | tf_op jit(solution)/shard_map/pallas_call | solution.py:555
  302.3 2.5 add_convert_fusion.9
  307.3 1.9 collective-permute-start.36
  310.8 34.6 %shard_map.237 = (bf16[4,4,2,64,128]{4,3,2,1,0:T(8,128)(2,1)}, bf16[4,4,2,64,256]{4,3,2,1,0:T(8,128)(2,1)}) custom-call(s32[2]{0:T(128)} %compare_select_fusion.6.meta_ref, s32[8]{0:T(128)} %copy-done.44, s32[8]{0:T(128)} %select_reduce_fusion.4.order_ref, bf16[4,4,2,64,128]{4,3,2,1,0:T(8,128)(2,1)} %bitcast.243, bf16[4,4,2,64,256]{4,3,2,1,0:T(8,128)(2,1)} %bitcast.239, ...), custom_call_target="tpu_custom_call" | custom-call | flops 21474836480 | bytes 6291456 | tf_op jit(solution)/shard_map/pallas_call | solution.py:384
  345.4 1.9 convert_add_fusion.11
  349.2 2.5 fusion.1
  351.7 2.6 add_convert_fusion.7
  356.2 6.8 %all-to-all-start.2 = ((bf16[16,64,512]{2,1,0:T(8,128)(2,1)}), bf16[16,64,512]{2,1,0:T(8,128)(2,1)S(1)}, u32[]{:S(2)}, u32[]{:S(2)}) async-start(bf16[16,64,512]{2,1,0:T(8,128)(2,1)} %bitcast.64), calls=%async_computation.2 | async-start | bytes 2097152 | tf_op jit(solution)/shard_map/all_to_all | solution.py:721
  363.0 14.9 %shard_map.238 = (bf16[256,2048]{1,0:T(8,128)(2,1)}, bf16[256,2048]{1,0:T(8,128)(2,1)}, bf16[512,2048]{1,0:T(8,128)(2,1)}, bf16[2048,384]{1,0:T(8,128)(2,1)}, f3...) custom-call(bf16[256,2048]{1,0:T(8,128)(2,1)} %copy-done.1, ...), custom_call_target="tpu_custom_call" | custom-call | flops 3758096384 | bytes 8388608 | tf_op jit(solution)/shard_map/pallas_call | solution.py:517
  382.9 2.9 convert_add_fusion.5
  385.7 14.8 %shard_map.239 = (bf16[256,2048]{1,0:T(8,128)(2,1)}, bf16[256,2048]{1,0:T(8,128)(2,1)}, bf16[512,2048]{1,0:T(8,128)(2,1)}, bf16[2048,384]{1,0:T(8,128)(2,1)}, f3...) custom-call(bf16[256,2048]{1,0:T(8,128)(2,1)} %copy-done.3, ...), custom_call_target="tpu_custom_call", output_to_operand_aliasing={{3}: (13, {})} | custom-call | flops 3758096384 | bytes 8388608 | tf_op jit(solution)/shard_map/pallas_call | solution.py:517
  400.5 2.1 slice_bitcast_fusion.6
  405.0 1.9 collective-permute-done.44
  406.9 3.5 collective-permute-done.45
  410.4 2.6 add_convert_fusion.5
  416.9 13.4 %shard_map.240 = bf16[2,2,512,896]{3,2,1,0:T(8,128)(2,1)} custom-call(s32[1]{0:T(128)} %bitcast.50.core_ref, bf16[2048,2048]{1,0:T(8,128)(2,1)} %get-tuple-element.261.rows_ref, bf16[2048,384]{1,0:T(8,128)(2,1)} %get-tuple-element.262.refs_0_, bf16[2048,512]{1,0:T(8,128)(2,1)} %get-tuple-element.213.refs_7_.refs_1_), custom_call_target="tpu_custom_call" | custom-call | flops 7516192768 | bytes 8388608 | tf_op jit(solution)/shard_map/pallas_call | solution.py:555
  430.3 2.9 slice_bitcast_fusion
  434.2 2.7 shard_map.242
  436.9 2.3 collective-permute-start.65
  439.2 2.2 convert_add_fusion.9
  442.6 5.5 collective-permute-done.47
  448.1 2.6 add_convert_fusion.2
  454.3 3.8 collective-permute-start.60
  458.1 4.8 fusion.48
  468.0 9.8 %collective-permute-done.52 = bf16[128,2048]{1,0:T(8,128)(2,1)S(1)} collective-permute-done((bf16[128,2048]{1,0:T(8,128)(2,1)S(1)}, bf16[128,2048]{1,0:T(8,128)(2,1)S(1)}, u32[]{:S(2)}, u32[]{:S(2)}) %collective-permute-start.52) | collective-permute-done | bytes 524320 | tf_op jit(solution)/shard_map/ppermute | solution.py:33
  483.5 10.8 %collective-permute-done.56 = bf16[2,64,2048]{2,1,0:T(8,128)(2,1)S(1)} collective-permute-done((bf16[2,64,2048]{2,1,0:T(8,128)(2,1)S(1)}, bf16[2,64,2048]{2,1,0:T(8,128)(2,1)S(1)}, u32[]{:S(2)}, u32[]{:S(2)}) %collective-permute-start.56) | collective-permute-done | bytes 524320 | tf_op jit(solution)/shard_map/ppermute | solution.py:90
  494.3 2.2 collective-permute-start.55
  497.4 3.2 fusion
  500.6 8.9 %all-to-all-start.3 = ((bf16[16,64,896]{2,1,0:T(8,128)(2,1)}), bf16[16,64,896]{2,1,0:T(8,128)(2,1)S(1)}, u32[]{:S(2)}, u32[]{:S(2)}) async-start(bf16[16,64,896]{2,1,0:T(8,128)(2,1)} %bitcast.222), calls=%async_computation.3 | async-start | bytes 3670016 | tf_op jit(solution)/shard_map/all_to_all | solution.py:721
  510.5 2.8 collective-permute-done.57
  518.8 1.9 fusion.27
  520.7 34.3 %all-to-all-done.3.back_ref = bf16[16,64,896]{2,1,0:T(8,128)(2,1)S(1)} async-done(((bf16[16,64,896]{2,1,0:T(8,128)(2,1)}), bf16[16,64,896]{2,1,0:T(8,128)(2,1)S(1)}, u32[]{:S(2)}, u32[]{:S(2)}) %all-to-all-start.3) | async-done | bytes 1835040 | tf_op jit(solution)/shard_map/all_to_all | solution.py:721
  556.3 3.7 shard_map.241
  (360 shorter events, 104.9 us)
Async XLA Ops:
  1.7 6.2 %collective-permute-start.1 = (bf16[64,2048]{1,0:T(8,128)(2,1)S(1)}, bf16[64,2048]{1,0:T(8,128)(2,1)S(1)}, u32[]{:S(2)}, u32[]{:S(2)}) collective-permute-start(bf16[64,2048]{1,0:T(8,128)(2,1)S(1)} %get-tuple-element.354), channel_id=1, source_target_pairs={{0,8},{8,0},{1,9},{9,1},{2,10},{10,2},{3,11},{11,3},{4,12},{12,4},... | collective-permute-start | bytes 786440 | tf_op jit(solution)/shard_map/ppermute | solution.py:33
  6.4 5.2 collective-permute-start.3
  6.5 7.5 %collective-permute-start = (bf16[64,2048]{1,0:T(8,128)(2,1)S(1)}, bf16[64,2048]{1,0:T(8,128)(2,1)S(1)}, u32[]{:S(2)}, u32[]{:S(2)}) collective-permute-start(bf16[64,2048]{1,0:T(8,128)(2,1)S(1)} %get-tuple-element.353), channel_id=1, source_target_pairs={{0,2},{2,4},{4,6},{6,0},{1,3},{3,5},{5,7},{7,1},{8,10},{10,12},{12... | collective-permute-start | bytes 786440 | tf_op jit(solution)/shard_map/ppermute | solution.py:53
  7.9 11.8 %collective-permute-start.2 = (bf16[64,2048]{1,0:T(8,128)(2,1)S(1)}, bf16[64,2048]{1,0:T(8,128)(2,1)S(1)}, u32[]{:S(2)}, u32[]{:S(2)}) collective-permute-start(bf16[64,2048]{1,0:T(8,128)(2,1)S(1)} %collective-permute-done.1), channel_id=1, source_target_pairs={{0,2},{2,4},{4,6},{6,0},{1,3},{3,5},{5,7},{7,1},{8,10},{10,12},{12... | collective-permute-start | bytes 786440 | tf_op jit(solution)/shard_map/ppermute | solution.py:53
  19.8 12.2 %collective-permute-start.6 = (bf16[2,64,2048]{2,1,0:T(8,128)(2,1)S(1)}, bf16[2,64,2048]{2,1,0:T(8,128)(2,1)S(1)}, u32[]{:S(2)}, u32[]{:S(2)}) collective-permute-start(bf16[2,64,2048]{2,1,0:T(8,128)(2,1)S(1)} %pad_maximum_fusion.11), channel_id=1, source_target_pairs={{0,2},{2,4},{4,6},{6,0},{1,3},{3,5},{5,7},{7,1},{8,10},{10,12},{12... | collective-permute-start | bytes 1572872 | tf_op jit(solution)/shard_map/ppermute | solution.py:53
  32.0 11.8 %collective-permute-start.7 = (bf16[2,64,2048]{2,1,0:T(8,128)(2,1)S(1)}, bf16[2,64,2048]{2,1,0:T(8,128)(2,1)S(1)}, u32[]{:S(2)}, u32[]{:S(2)}) collective-permute-start(bf16[2,64,2048]{2,1,0:T(8,128)(2,1)S(1)} %collective-permute-done.6), channel_id=1, source_target_pairs={{0,2},{2,4},{4,6},{6,0},{1,3},{3,5},{5,7},{7,1},{8,10},{10,12},{12... | collective-permute-start | bytes 1572872 | tf_op jit(solution)/shard_map/ppermute | solution.py:53
  33.5 22.6 %collective-permute-start.5 = (bf16[256,2048]{1,0:T(8,128)(2,1)S(1)}, bf16[256,2048]{1,0:T(8,128)(2,1)S(1)}, u32[]{:S(2)}, u32[]{:S(2)}) collective-permute-start(bf16[256,2048]{1,0:T(8,128)(2,1)S(1)} %pad_maximum_fusion.1.refs_0_), channel_id=1, source_target_pairs={{0,1},{1,0},{2,3},{3,2},{4,5},{5,4},{6,7},{7,6},{8,9},{9,8},{10,11... | collective-permute-start | bytes 3145736 | tf_op jit(solution)/shard_map/ppermute | solution.py:33
  34.6 22.5 %collective-permute-start.4 = (bf16[256,2048]{1,0:T(8,128)(2,1)S(1)}, bf16[256,2048]{1,0:T(8,128)(2,1)}, u32[]{:S(2)}, u32[]{:S(2)}) collective-permute-start(bf16[256,2048]{1,0:T(8,128)(2,1)S(1)} %pad_maximum_fusion.1.refs_0_), channel_id=1, source_target_pairs={{0,16},{16,0},{1,17},{17,1},{2,18},{18,2},{3,19},{19,3},{4,20},{20... | collective-permute-start | bytes 3145736 | tf_op jit(solution)/shard_map/ppermute | solution.py:33
  57.1 83.9 %all-to-all-start = ((bf16[16,64,896]{2,1,0:T(8,128)(2,1)}), bf16[16,64,896]{2,1,0:T(8,128)(2,1)S(1)}, u32[]{:S(2)}, u32[]{:S(2)}) async-start(bf16[16,64,896]{2,1,0:T(8,128)(2,1)} %get-tuple-element.149), calls=%async_computation | async-start | bytes 3670016 | tf_op jit(solution)/shard_map/all_to_all | solution.py:712
  69.5 6.8 %collective-permute-start.13 = (bf16[2,704]{1,0:T(2,128)(2,1)S(1)}, bf16[2,704]{1,0:T(2,128)(2,1)S(1)}, u32[]{:S(2)}, u32[]{:S(2)}) collective-permute-start(bf16[2,704]{1,0:T(2,128)(2,1)S(1)} %get-tuple-element.370), channel_id=1, source_target_pairs={{0,8},{8,0},{1,9},{9,1},{2,10},{10,2},{3,11},{11,3},{4,12},{12,4},... | collective-permute-start | bytes 8456 | tf_op jit(solution)/shard_map/ppermute | solution.py:33
  74.4 54.2 %collective-permute-start.11 = (bf16[256,2048]{1,0:T(8,128)(2,1)S(1)}, bf16[256,2048]{1,0:T(8,128)(2,1)}, u32[]{:S(2)}, u32[]{:S(2)}) collective-permute-start(bf16[256,2048]{1,0:T(8,128)(2,1)S(1)} %pad_maximum_fusion.2.refs_0_), channel_id=1, source_target_pairs={{0,1},{1,0},{2,3},{3,2},{4,5},{5,4},{6,7},{7,6},{8,9},{9,8},{10,11... | collective-permute-start | bytes 3145736 | tf_op jit(solution)/shard_map/ppermute | solution.py:33
  75.1 53.5 %collective-permute-start.10 = (bf16[256,2048]{1,0:T(8,128)(2,1)S(1)}, bf16[256,2048]{1,0:T(8,128)(2,1)}, u32[]{:S(2)}, u32[]{:S(2)}) collective-permute-start(bf16[256,2048]{1,0:T(8,128)(2,1)S(1)} %pad_maximum_fusion.2.refs_0_), channel_id=1, source_target_pairs={{0,16},{16,0},{1,17},{17,1},{2,18},{18,2},{3,19},{19,3},{4,20},{20... | collective-permute-start | bytes 3145736 | tf_op jit(solution)/shard_map/ppermute | solution.py:33
  76.3 34.6 %collective-permute-start.14 = (bf16[4,704]{1,0:T(4,128)(2,1)S(1)}, bf16[4,704]{1,0:T(4,128)(2,1)S(1)}, u32[]{:S(2)}, u32[]{:S(2)}) collective-permute-start(bf16[4,704]{1,0:T(4,128)(2,1)S(1)} %reshape.721), channel_id=1, source_target_pairs={{0,16},{16,0},{1,17},{17,1},{2,18},{18,2},{3,19},{19,3},{4,20},{20... | collective-permute-start | bytes 16904 | tf_op jit(solution)/shard_map/ppermute | solution.py:33
  111.0 5.7 %collective-permute-start.17 = (bf16[8,704]{1,0:T(8,128)(2,1)S(1)}, bf16[8,704]{1,0:T(8,128)(2,1)S(1)}, u32[]{:S(2)}, u32[]{:S(2)}) collective-permute-start(bf16[8,704]{1,0:T(8,128)(2,1)S(1)} %reshape.722), channel_id=1, source_target_pairs={{0,6},{2,0},{4,2},{6,4},{1,7},{3,1},{5,3},{7,5},{8,14},{10,8},{12,... | collective-permute-start | bytes 33800 | tf_op jit(solution)/shard_map/ppermute | solution.py:103
  115.4 13.2 %collective-permute-start.8 = (bf16[128,2048]{1,0:T(8,128)(2,1)}, bf16[128,2048]{1,0:T(8,128)(2,1)S(1)}, u32[]{:S(2)}, u32[]{:S(2)}) collective-permute-start(bf16[128,2048]{1,0:T(8,128)(2,1)} %slice.290), channel_id=1, source_target_pairs={{0,16},{16,0},{1,17},{17,1},{2,18},{18,2},{3,19},{19,3},{4,20},{20... | collective-permute-start | bytes 1572872 | tf_op jit(solution)/shard_map/ppermute | solution.py:33
  115.4 13.2 %collective-permute-start.9 = (bf16[128,2048]{1,0:T(8,128)(2,1)}, bf16[128,2048]{1,0:T(8,128)(2,1)}, u32[]{:S(2)}, u32[]{:S(2)}) collective-permute-start(bf16[128,2048]{1,0:T(8,128)(2,1)} %slice.291), channel_id=1, source_target_pairs={{0,1},{1,0},{2,3},{3,2},{4,5},{5,4},{6,7},{7,6},{8,9},{9,8},{10,11... | collective-permute-start | bytes 1572872 | tf_op jit(solution)/shard_map/ppermute | solution.py:33
  116.7 5.3 collective-permute-start.16
  128.6 12.4 %collective-permute-start.20 = (bf16[2,64,2048]{2,1,0:T(8,128)(2,1)}, bf16[2,64,2048]{2,1,0:T(8,128)(2,1)}, u32[]{:S(2)}, u32[]{:S(2)}) collective-permute-start(bf16[2,64,2048]{2,1,0:T(8,128)(2,1)} %pad_maximum_fusion.12), channel_id=1, source_target_pairs={{0,2},{2,4},{4,6},{6,0},{1,3},{3,5},{5,7},{7,1},{8,10},{10,12},{12... | collective-permute-start | bytes 1572872 | tf_op jit(solution)/shard_map/ppermute | solution.py:53
  141.0 12.0 %collective-permute-start.21 = (bf16[2,1,8,64,896]{4,3,2,0,1:T(8,128)(2,1)S(1)}, bf16[2,1,8,64,896]{4,3,2,0,1:T(8,128)(2,1)}, u32[]{:S(2)}, u32[]{:S(2)}) collective-permute-start(bf16[2,1,8,64,896]{4,3,2,0,1:T(8,128)(2,1)S(1)} %bitcast.220), channel_id=1, source_target_pairs={{0,8},{8,0},{1,9},{9,1},{2,10},{10,2},{3,11},{11,3},{4,12},{12,4},... | collective-permute-start | bytes 5505032 | tf_op jit(solution)/shard_map/ppermute | solution.py:33
  147.2 13.6 %collective-permute-start.18 = (bf16[128,2048]{1,0:T(8,128)(2,1)S(1)}, bf16[128,2048]{1,0:T(8,128)(2,1)S(1)}, u32[]{:S(2)}, u32[]{:S(2)}) collective-permute-start(bf16[128,2048]{1,0:T(8,128)(2,1)S(1)} %slice.292), channel_id=1, source_target_pairs={{0,16},{16,0},{1,17},{17,1},{2,18},{18,2},{3,19},{19,3},{4,20},{20... | collective-permute-start | bytes 1572872 | tf_op jit(solution)/shard_map/ppermute | solution.py:33
  148.4 13.3 %collective-permute-start.19 = (bf16[128,2048]{1,0:T(8,128)(2,1)S(1)}, bf16[128,2048]{1,0:T(8,128)(2,1)S(1)}, u32[]{:S(2)}, u32[]{:S(2)}) collective-permute-start(bf16[128,2048]{1,0:T(8,128)(2,1)S(1)} %slice.293), channel_id=1, source_target_pairs={{0,1},{1,0},{2,3},{3,2},{4,5},{5,4},{6,7},{7,6},{8,9},{9,8},{10,11... | collective-permute-start | bytes 1572872 | tf_op jit(solution)/shard_map/ppermute | solution.py:33
  161.7 17.1 %collective-permute-start.24 = (bf16[2,64,2048]{2,1,0:T(8,128)(2,1)}, bf16[2,64,2048]{2,1,0:T(8,128)(2,1)S(1)}, u32[]{:S(2)}, u32[]{:S(2)}) collective-permute-start(bf16[2,64,2048]{2,1,0:T(8,128)(2,1)} %collective-permute-done.20), channel_id=1, source_target_pairs={{0,2},{2,4},{4,6},{6,0},{1,3},{3,5},{5,7},{7,1},{8,10},{10,12},{12... | collective-permute-start | bytes 1572872 | tf_op jit(solution)/shard_map/ppermute | solution.py:53
  165.0 30.2 %collective-permute-start.23 = (bf16[256,2048]{1,0:T(8,128)(2,1)}, bf16[256,2048]{1,0:T(8,128)(2,1)}, u32[]{:S(2)}, u32[]{:S(2)}) collective-permute-start(bf16[256,2048]{1,0:T(8,128)(2,1)} %pad_maximum_fusion.3.refs_0_), channel_id=1, source_target_pairs={{0,1},{1,0},{2,3},{3,2},{4,5},{5,4},{6,7},{7,6},{8,9},{9,8},{10,11... | collective-permute-start | bytes 3145736 | tf_op jit(solution)/shard_map/ppermute | solution.py:33
  166.1 29.1 %collective-permute-start.22 = (bf16[256,2048]{1,0:T(8,128)(2,1)}, bf16[256,2048]{1,0:T(8,128)(2,1)}, u32[]{:S(2)}, u32[]{:S(2)}) collective-permute-start(bf16[256,2048]{1,0:T(8,128)(2,1)} %pad_maximum_fusion.3.refs_0_), channel_id=1, source_target_pairs={{0,16},{16,0},{1,17},{17,1},{2,18},{18,2},{3,19},{19,3},{4,20},{20... | collective-permute-start | bytes 3145736 | tf_op jit(solution)/shard_map/ppermute | solution.py:33
  178.7 16.3 %collective-permute-start.25 = (bf16[2,64,2048]{2,1,0:T(8,128)(2,1)S(1)}, bf16[2,64,2048]{2,1,0:T(8,128)(2,1)S(1)}, u32[]{:S(2)}, u32[]{:S(2)}) collective-permute-start(bf16[2,64,2048]{2,1,0:T(8,128)(2,1)S(1)} %collective-permute-done.24), channel_id=1, source_target_pairs={{0,2},{2,4},{4,6},{6,0},{1,3},{3,5},{5,7},{7,1},{8,10},{10,12},{12... | collective-permute-start | bytes 1572872 | tf_op jit(solution)/shard_map/ppermute | solution.py:53
  195.2 50.7 %all-to-all-start.1 = ((bf16[16,64,512]{2,1,0:T(8,128)(2,1)}), bf16[16,64,512]{2,1,0:T(8,128)(2,1)S(1)}, u32[]{:S(2)}, u32[]{:S(2)}) async-start(bf16[16,64,512]{2,1,0:T(8,128)(2,1)} %get-tuple-element.169), calls=%async_computation.1 | async-start | bytes 2097152 | tf_op jit(solution)/shard_map/all_to_all | solution.py:712
  200.0 45.9 %collective-permute-start.27 = (bf16[256,2048]{1,0:T(8,128)(2,1)S(1)}, bf16[256,2048]{1,0:T(8,128)(2,1)}, u32[]{:S(2)}, u32[]{:S(2)}) collective-permute-start(bf16[256,2048]{1,0:T(8,128)(2,1)S(1)} %pad_maximum_fusion.4.refs_5_), channel_id=1, source_target_pairs={{0,1},{1,0},{2,3},{3,2},{4,5},{5,4},{6,7},{7,6},{8,9},{9,8},{10,11... | collective-permute-start | bytes 3145736 | tf_op jit(solution)/shard_map/ppermute | solution.py:33
  201.3 44.7 %collective-permute-start.26 = (bf16[256,2048]{1,0:T(8,128)(2,1)S(1)}, bf16[256,2048]{1,0:T(8,128)(2,1)}, u32[]{:S(2)}, u32[]{:S(2)}) collective-permute-start(bf16[256,2048]{1,0:T(8,128)(2,1)S(1)} %pad_maximum_fusion.4.refs_5_), channel_id=1, source_target_pairs={{0,16},{16,0},{1,17},{17,1},{2,18},{18,2},{3,19},{19,3},{4,20},{20... | collective-permute-start | bytes 3145736 | tf_op jit(solution)/shard_map/ppermute | solution.py:33
  207.0 38.4 %collective-permute-start.29 = (bf16[128,2048]{1,0:T(8,128)(2,1)S(1)}, bf16[128,2048]{1,0:T(8,128)(2,1)}, u32[]{:S(2)}, u32[]{:S(2)}) collective-permute-start(bf16[128,2048]{1,0:T(8,128)(2,1)S(1)} %slice.307), channel_id=1, source_target_pairs={{0,1},{1,0},{2,3},{3,2},{4,5},{5,4},{6,7},{7,6},{8,9},{9,8},{10,11... | collective-permute-start | bytes 1572872 | tf_op jit(solution)/shard_map/ppermute | solution.py:33
  207.3 38.6 %collective-permute-start.28 = (bf16[128,2048]{1,0:T(8,128)(2,1)S(1)}, bf16[128,2048]{1,0:T(8,128)(2,1)}, u32[]{:S(2)}, u32[]{:S(2)}) collective-permute-start(bf16[128,2048]{1,0:T(8,128)(2,1)S(1)} %slice.306), channel_id=1, source_target_pairs={{0,16},{16,0},{1,17},{17,1},{2,18},{18,2},{3,19},{19,3},{4,20},{20... | collective-permute-start | bytes 1572872 | tf_op jit(solution)/shard_map/ppermute | solution.py:33
  245.9 8.8 %collective-permute-start.31 = (bf16[2,1,8,64,512]{4,3,2,0,1:T(8,128)(2,1)S(1)}, bf16[2,1,8,64,512]{4,3,2,0,1:T(8,128)(2,1)}, u32[]{:S(2)}, u32[]{:S(2)}) collective-permute-start(bf16[2,1,8,64,512]{4,3,2,0,1:T(8,128)(2,1)S(1)} %bitcast.223), channel_id=1, source_target_pairs={{0,8},{8,0},{1,9},{9,1},{2,10},{10,2},{3,11},{11,3},{4,12},{12,4},... | collective-permute-start | bytes 3145736 | tf_op jit(solution)/shard_map/ppermute | solution.py:33
  253.2 21.9 %collective-permute-start.32 = (bf16[128,2048]{1,0:T(8,128)(2,1)S(1)}, bf16[128,2048]{1,0:T(8,128)(2,1)S(1)}, u32[]{:S(2)}, u32[]{:S(2)}) collective-permute-start(bf16[128,2048]{1,0:T(8,128)(2,1)S(1)} %slice.308), channel_id=1, source_target_pairs={{0,16},{16,0},{1,17},{17,1},{2,18},{18,2},{3,19},{19,3},{4,20},{20... | collective-permute-start | bytes 1572872 | tf_op jit(solution)/shard_map/ppermute | solution.py:33
  254.5 20.7 %collective-permute-start.33 = (bf16[128,2048]{1,0:T(8,128)(2,1)S(1)}, bf16[128,2048]{1,0:T(8,128)(2,1)}, u32[]{:S(2)}, u32[]{:S(2)}) collective-permute-start(bf16[128,2048]{1,0:T(8,128)(2,1)S(1)} %slice.309), channel_id=1, source_target_pairs={{0,1},{1,0},{2,3},{3,2},{4,5},{5,4},{6,7},{7,6},{8,9},{9,8},{10,11... | collective-permute-start | bytes 1572872 | tf_op jit(solution)/shard_map/ppermute | solution.py:33
  276.0 26.3 %collective-permute-start.34 = (bf16[256,2048]{1,0:T(8,128)(2,1)}, bf16[256,2048]{1,0:T(8,128)(2,1)S(1)}, u32[]{:S(2)}, u32[]{:S(2)}) collective-permute-start(bf16[256,2048]{1,0:T(8,128)(2,1)} %get-tuple-element.201), channel_id=1, source_target_pairs={{0,16},{16,0},{1,17},{17,1},{2,18},{18,2},{3,19},{19,3},{4,20},{20... | collective-permute-start | bytes 3145736 | tf_op jit(solution)/shard_map/ppermute | solution.py:33
  277.1 25.2 %collective-permute-start.35 = (bf16[256,2048]{1,0:T(8,128)(2,1)}, bf16[256,2048]{1,0:T(8,128)(2,1)}, u32[]{:S(2)}, u32[]{:S(2)}) collective-permute-start(bf16[256,2048]{1,0:T(8,128)(2,1)} %get-tuple-element.202), channel_id=1, source_target_pairs={{0,1},{1,0},{2,3},{3,2},{4,5},{5,4},{6,7},{7,6},{8,9},{9,8},{10,11... | collective-permute-start | bytes 3145736 | tf_op jit(solution)/shard_map/ppermute | solution.py:33
  304.9 40.5 %collective-permute-start.39 = (bf16[128,2048]{1,0:T(8,128)(2,1)}, bf16[128,2048]{1,0:T(8,128)(2,1)}, u32[]{:S(2)}, u32[]{:S(2)}) collective-permute-start(bf16[128,2048]{1,0:T(8,128)(2,1)} %get-tuple-element.209), channel_id=1, source_target_pairs={{0,1},{1,0},{2,3},{3,2},{4,5},{5,4},{6,7},{7,6},{8,9},{9,8},{10,11... | collective-permute-start | bytes 1572872 | tf_op jit(solution)/shard_map/ppermute | solution.py:33
  306.0 39.4 %collective-permute-start.40 = (bf16[128,2048]{1,0:T(8,128)(2,1)}, bf16[128,2048]{1,0:T(8,128)(2,1)}, u32[]{:S(2)}, u32[]{:S(2)}) collective-permute-start(bf16[128,2048]{1,0:T(8,128)(2,1)} %get-tuple-element.210), channel_id=1, source_target_pairs={{0,16},{16,0},{1,17},{17,1},{2,18},{18,2},{3,19},{19,3},{4,20},{20... | collective-permute-start | bytes 1572872 | tf_op jit(solution)/shard_map/ppermute | solution.py:33
  307.3 41.1 %collective-permute-start.36 = (bf16[2,512,512]{2,1,0:T(8,128)(2,1)}, bf16[2,512,512]{2,1,0:T(8,128)(2,1)}, u32[]{:S(2)}, u32[]{:S(2)}) collective-permute-start(bf16[2,512,512]{2,1,0:T(8,128)(2,1)} %slice_bitcast_fusion.2), channel_id=1, source_target_pairs={{0,8},{8,0},{1,9},{9,1},{2,10},{10,2},{3,11},{11,3},{4,12},{12,4},... | collective-permute-start | bytes 3145736 | tf_op jit(solution)/shard_map/ppermute | solution.py:33
  309.3 42.4 %collective-permute-start.37 = (bf16[256,2048]{1,0:T(8,128)(2,1)}, bf16[256,2048]{1,0:T(8,128)(2,1)}, u32[]{:S(2)}, u32[]{:S(2)}) collective-permute-start(bf16[256,2048]{1,0:T(8,128)(2,1)} %get-tuple-element.207), channel_id=1, source_target_pairs={{0,16},{16,0},{1,17},{17,1},{2,18},{18,2},{3,19},{19,3},{4,20},{20... | collective-permute-start | bytes 3145736 | tf_op jit(solution)/shard_map/ppermute | solution.py:33
  310.4 41.3 %collective-permute-start.38 = (bf16[256,2048]{1,0:T(8,128)(2,1)}, bf16[256,2048]{1,0:T(8,128)(2,1)}, u32[]{:S(2)}, u32[]{:S(2)}) collective-permute-start(bf16[256,2048]{1,0:T(8,128)(2,1)} %get-tuple-element.208), channel_id=1, source_target_pairs={{0,1},{1,0},{2,3},{3,2},{4,5},{5,4},{6,7},{7,6},{8,9},{9,8},{10,11... | collective-permute-start | bytes 3145736 | tf_op jit(solution)/shard_map/ppermute | solution.py:33
  354.3 23.7 %collective-permute-start.41 = (bf16[2,64,2048]{2,1,0:T(8,128)(2,1)}, bf16[2,64,2048]{2,1,0:T(8,128)(2,1)}, u32[]{:S(2)}, u32[]{:S(2)}) collective-permute-start(bf16[2,64,2048]{2,1,0:T(8,128)(2,1)} %pad_maximum_fusion.6), channel_id=1, source_target_pairs={{2,0},{4,2},{6,4},{0,6},{3,1},{5,3},{7,5},{1,7},{10,8},{12,10},{14... | collective-permute-start | bytes 1572872 | tf_op jit(solution)/shard_map/ppermute | solution.py:90
  354.6 24.7 %collective-permute-start.42 = (bf16[128,2048]{1,0:T(8,128)(2,1)}, bf16[128,2048]{1,0:T(8,128)(2,1)S(1)}, u32[]{:S(2)}, u32[]{:S(2)}) collective-permute-start(bf16[128,2048]{1,0:T(8,128)(2,1)} %get-tuple-element.221), channel_id=1, source_target_pairs={{0,1},{1,0},{2,3},{3,2},{4,5},{5,4},{6,7},{7,6},{8,9},{9,8},{10,11... | collective-permute-start | bytes 1572872 | tf_op jit(solution)/shard_map/ppermute | solution.py:33
  355.6 23.6 %collective-permute-start.43 = (bf16[128,2048]{1,0:T(8,128)(2,1)}, bf16[128,2048]{1,0:T(8,128)(2,1)}, u32[]{:S(2)}, u32[]{:S(2)}) collective-permute-start(bf16[128,2048]{1,0:T(8,128)(2,1)} %get-tuple-element.222), channel_id=1, source_target_pairs={{0,16},{16,0},{1,17},{17,1},{2,18},{18,2},{3,19},{19,3},{4,20},{20... | collective-permute-start | bytes 1572872 | tf_op jit(solution)/shard_map/ppermute | solution.py:33
  356.2 77.1 %all-to-all-start.2 = ((bf16[16,64,512]{2,1,0:T(8,128)(2,1)}), bf16[16,64,512]{2,1,0:T(8,128)(2,1)S(1)}, u32[]{:S(2)}, u32[]{:S(2)}) async-start(bf16[16,64,512]{2,1,0:T(8,128)(2,1)} %bitcast.64), calls=%async_computation.2 | async-start | bytes 2097152 | tf_op jit(solution)/shard_map/all_to_all | solution.py:721
  380.2 23.6 %collective-permute-start.46 = (bf16[2,64,2048]{2,1,0:T(8,128)(2,1)}, bf16[2,64,2048]{2,1,0:T(8,128)(2,1)}, u32[]{:S(2)}, u32[]{:S(2)}) collective-permute-start(bf16[2,64,2048]{2,1,0:T(8,128)(2,1)} %add_convert_fusion.4), channel_id=1, source_target_pairs={{2,0},{4,2},{6,4},{0,6},{3,1},{5,3},{7,5},{1,7},{10,8},{12,10},{14... | collective-permute-start | bytes 1572872 | tf_op jit(solution)/shard_map/ppermute | solution.py:90
  380.4 26.4 %collective-permute-start.44 = (bf16[256,2048]{1,0:T(8,128)(2,1)}, bf16[256,2048]{1,0:T(8,128)(2,1)}, u32[]{:S(2)}, u32[]{:S(2)}) collective-permute-start(bf16[256,2048]{1,0:T(8,128)(2,1)} %get-tuple-element.230), channel_id=1, source_target_pairs={{0,16},{16,0},{1,17},{17,1},{2,18},{18,2},{3,19},{19,3},{4,20},{20... | collective-permute-start | bytes 3145736 | tf_op jit(solution)/shard_map/ppermute | solution.py:33
  381.7 28.7 %collective-permute-start.45 = (bf16[256,2048]{1,0:T(8,128)(2,1)}, bf16[256,2048]{1,0:T(8,128)(2,1)}, u32[]{:S(2)}, u32[]{:S(2)}) collective-permute-start(bf16[256,2048]{1,0:T(8,128)(2,1)} %get-tuple-element.231), channel_id=1, source_target_pairs={{0,1},{1,0},{2,3},{3,2},{4,5},{5,4},{6,7},{7,6},{8,9},{9,8},{10,11... | collective-permute-start | bytes 3145736 | tf_op jit(solution)/shard_map/ppermute | solution.py:33
  413.0 23.9 %collective-permute-start.49 = (bf16[128,2048]{1,0:T(8,128)(2,1)}, bf16[128,2048]{1,0:T(8,128)(2,1)S(1)}, u32[]{:S(2)}, u32[]{:S(2)}) collective-permute-start(bf16[128,2048]{1,0:T(8,128)(2,1)} %get-tuple-element.237), channel_id=1, source_target_pairs={{0,1},{1,0},{2,3},{3,2},{4,5},{5,4},{6,7},{7,6},{8,9},{9,8},{10,11... | collective-permute-start | bytes 1572872 | tf_op jit(solution)/shard_map/ppermute | solution.py:33
  413.5 25.7 %collective-permute-start.50 = (bf16[128,2048]{1,0:T(8,128)(2,1)}, bf16[128,2048]{1,0:T(8,128)(2,1)}, u32[]{:S(2)}, u32[]{:S(2)}) collective-permute-start(bf16[128,2048]{1,0:T(8,128)(2,1)} %get-tuple-element.238), channel_id=1, source_target_pairs={{0,16},{16,0},{1,17},{17,1},{2,18},{18,2},{3,19},{19,3},{4,20},{20... | collective-permute-start | bytes 1572872 | tf_op jit(solution)/shard_map/ppermute | solution.py:33
  415.6 37.2 %collective-permute-start.54 = (bf16[2,64,2048]{2,1,0:T(8,128)(2,1)}, bf16[2,64,2048]{2,1,0:T(8,128)(2,1)}, u32[]{:S(2)}, u32[]{:S(2)}) collective-permute-start(bf16[2,64,2048]{2,1,0:T(8,128)(2,1)} %fusion.21), channel_id=1, source_target_pairs={{2,0},{4,2},{6,4},{0,6},{3,1},{5,3},{7,5},{1,7},{10,8},{12,10},{14... | collective-permute-start | bytes 1572872 | tf_op jit(solution)/shard_map/ppermute | solution.py:90
  415.6 32.5 %collective-permute-start.47 = (bf16[256,2048]{1,0:T(8,128)(2,1)}, bf16[256,2048]{1,0:T(8,128)(2,1)}, u32[]{:S(2)}, u32[]{:S(2)}) collective-permute-start(bf16[256,2048]{1,0:T(8,128)(2,1)} %get-tuple-element.235), channel_id=1, source_target_pairs={{0,16},{16,0},{1,17},{17,1},{2,18},{18,2},{3,19},{19,3},{4,20},{20... | collective-permute-start | bytes 3145736 | tf_op jit(solution)/shard_map/ppermute | solution.py:33
  415.9 32.1 %collective-permute-start.48 = (bf16[256,2048]{1,0:T(8,128)(2,1)}, bf16[256,2048]{1,0:T(8,128)(2,1)}, u32[]{:S(2)}, u32[]{:S(2)}) collective-permute-start(bf16[256,2048]{1,0:T(8,128)(2,1)} %get-tuple-element.236), channel_id=1, source_target_pairs={{0,1},{1,0},{2,3},{3,2},{4,5},{5,4},{6,7},{7,6},{8,9},{9,8},{10,11... | collective-permute-start | bytes 3145736 | tf_op jit(solution)/shard_map/ppermute | solution.py:33
  436.9 60.5 %collective-permute-start.65 = (bf16[2,512,896]{2,1,0:T(8,128)(2,1)}, bf16[2,512,896]{2,1,0:T(8,128)(2,1)}, u32[]{:S(2)}, u32[]{:S(2)}) collective-permute-start(bf16[2,512,896]{2,1,0:T(8,128)(2,1)} %slice_bitcast_fusion), channel_id=1, source_target_pairs={{0,8},{8,0},{1,9},{9,1},{2,10},{10,2},{3,11},{11,3},{4,12},{12,4},... | collective-permute-start | bytes 5505032 | tf_op jit(solution)/shard_map/ppermute | solution.py:33
  454.3 8.6 %collective-permute-start.60 = (f32[1,4,2,640]{3,2,1,0:T(2,128)S(1)}, f32[1,4,2,640]{3,2,1,0:T(2,128)S(1)}, u32[]{:S(2)}, u32[]{:S(2)}) collective-permute-start(f32[1,4,2,640]{3,2,1,0:T(2,128)S(1)} %dynamic-slice_bitcast_fusion.4), channel_id=1, source_target_pairs={{0,8},{8,0},{1,9},{9,1},{2,10},{10,2},{3,11},{11,3},{4,12},{12,4},... | collective-permute-start | bytes 61448 | tf_op jit(solution)/shard_map/ppermute | solution.py:33
  464.4 13.3 %collective-permute-start.52 = (bf16[128,2048]{1,0:T(8,128)(2,1)S(1)}, bf16[128,2048]{1,0:T(8,128)(2,1)S(1)}, u32[]{:S(2)}, u32[]{:S(2)}) collective-permute-start(bf16[128,2048]{1,0:T(8,128)(2,1)S(1)} %copy-done.26), channel_id=1, source_target_pairs={{0,1},{1,0},{2,3},{3,2},{4,5},{5,4},{6,7},{7,6},{8,9},{9,8},{10,11... | collective-permute-start | bytes 1572872 | tf_op jit(solution)/shard_map/ppermute | solution.py:33
  464.9 13.2 %collective-permute-start.53 = (bf16[128,2048]{1,0:T(8,128)(2,1)S(1)}, bf16[128,2048]{1,0:T(8,128)(2,1)S(1)}, u32[]{:S(2)}, u32[]{:S(2)}) collective-permute-start(bf16[128,2048]{1,0:T(8,128)(2,1)S(1)} %copy-done.25), channel_id=1, source_target_pairs={{0,16},{16,0},{1,17},{17,1},{2,18},{18,2},{3,19},{19,3},{4,20},{20... | collective-permute-start | bytes 1572872 | tf_op jit(solution)/shard_map/ppermute | solution.py:33
  466.0 15.0 %collective-permute-start.51 = (bf16[2,64,2048]{2,1,0:T(8,128)(2,1)S(1)}, bf16[2,64,2048]{2,1,0:T(8,128)(2,1)S(1)}, u32[]{:S(2)}, u32[]{:S(2)}) collective-permute-start(bf16[2,64,2048]{2,1,0:T(8,128)(2,1)S(1)} %copy-done.24), channel_id=1, source_target_pairs={{2,0},{4,2},{6,4},{0,6},{3,1},{5,3},{7,5},{1,7},{10,8},{12,10},{14... | collective-permute-start | bytes 1572872 | tf_op jit(solution)/shard_map/ppermute | solution.py:90
  466.1 48.4 %collective-permute-start.64 = (f32[1,640]{1,0:T(1,128)S(1)}, f32[1,640]{1,0:T(1,128)S(1)}, u32[]{:S(2)}, u32[]{:S(2)}) collective-permute-start(f32[1,640]{1,0:T(1,128)S(1)} %get-tuple-element.362), channel_id=1, source_target_pairs={{0,6},{2,0},{4,2},{6,4},{1,7},{3,1},{5,3},{7,5},{8,14},{10,8},{12,... | collective-permute-start | bytes 7688 | tf_op jit(solution)/shard_map/ppermute | solution.py:123
  477.7 36.8 %collective-permute-start.63 = (f32[1,640]{1,0:T(1,128)S(1)}, f32[1,640]{1,0:T(1,128)S(1)}, u32[]{:S(2)}, u32[]{:S(2)}) collective-permute-start(f32[1,640]{1,0:T(1,128)S(1)} %get-tuple-element.363), channel_id=1, source_target_pairs={{0,4},{2,6},{4,0},{6,2},{1,5},{3,7},{5,1},{7,3},{8,12},{10,14},{12... | collective-permute-start | bytes 7688 | tf_op jit(solution)/shard_map/ppermute | solution.py:123
  478.1 36.3 %collective-permute-start.62 = (f32[1,640]{1,0:T(1,128)S(1)}, f32[1,640]{1,0:T(1,128)S(1)}, u32[]{:S(2)}, u32[]{:S(2)}) collective-permute-start(f32[1,640]{1,0:T(1,128)S(1)} %get-tuple-element.364), channel_id=1, source_target_pairs={{0,2},{2,4},{4,6},{6,0},{1,3},{3,5},{5,7},{7,1},{8,10},{10,12},{12... | collective-permute-start | bytes 7688 | tf_op jit(solution)/shard_map/ppermute | solution.py:123
  481.2 13.1 %collective-permute-start.56 = (bf16[2,64,2048]{2,1,0:T(8,128)(2,1)S(1)}, bf16[2,64,2048]{2,1,0:T(8,128)(2,1)S(1)}, u32[]{:S(2)}, u32[]{:S(2)}) collective-permute-start(bf16[2,64,2048]{2,1,0:T(8,128)(2,1)S(1)} %add_convert_fusion.1), channel_id=1, source_target_pairs={{2,0},{4,2},{6,4},{0,6},{3,1},{5,3},{7,5},{1,7},{10,8},{12,10},{14... | collective-permute-start | bytes 1572872 | tf_op jit(solution)/shard_map/ppermute | solution.py:90
  494.3 15.2 %collective-permute-start.55 = (bf16[64,2048]{1,0:T(8,128)(2,1)}, bf16[64,2048]{1,0:T(8,128)(2,1)}, u32[]{:S(2)}, u32[]{:S(2)}) collective-permute-start(bf16[64,2048]{1,0:T(8,128)(2,1)} %fusion.29), channel_id=1, source_target_pairs={{0,8},{8,0},{1,9},{9,1},{2,10},{10,2},{3,11},{11,3},{4,12},{12,4},... | collective-permute-start | bytes 786440 | tf_op jit(solution)/shard_map/ppermute | solution.py:33
  497.4 15.9 %collective-permute-start.57 = (bf16[2,64,2048]{2,1,0:T(8,128)(2,1)}, bf16[2,64,2048]{2,1,0:T(8,128)(2,1)}, u32[]{:S(2)}, u32[]{:S(2)}) collective-permute-start(bf16[2,64,2048]{2,1,0:T(8,128)(2,1)} %add_convert_fusion), channel_id=1, source_target_pairs={{2,0},{4,2},{6,4},{0,6},{3,1},{5,3},{7,5},{1,7},{10,8},{12,10},{14... | collective-permute-start | bytes 1572872 | tf_op jit(solution)/shard_map/ppermute | solution.py:90
  500.6 54.4 %all-to-all-start.3 = ((bf16[16,64,896]{2,1,0:T(8,128)(2,1)}), bf16[16,64,896]{2,1,0:T(8,128)(2,1)S(1)}, u32[]{:S(2)}, u32[]{:S(2)}) async-start(bf16[16,64,896]{2,1,0:T(8,128)(2,1)} %bitcast.222), calls=%async_computation.3 | async-start | bytes 3670016 | tf_op jit(solution)/shard_map/all_to_all | solution.py:721
  (53 other events, 550.0 us)

commit v3 on v2

v3 whole, which is shorter than its diff:
```python
import functools

import jax
import jax.numpy as jnp
from jax import lax
from jax.experimental import pallas as pl
from jax.experimental.pallas import tpu as pltpu
from jax.sharding import Mesh
from jax.sharding import PartitionSpec as P

HEADS = 32
HEAD_DIM = 64
ROT = 32
EPS = 1e-05
NEG = -1e30
BF = jnp.bfloat16
F32 = jnp.float32

RANK = ("core", "bz", "by")
ALL = ("hx", "core", "bs", "bz", "by")
Z_LEN = 4
SWAP = [(0, 1), (1, 0)]
UP = [(i, (i + 1) % Z_LEN) for i in range(Z_LEN)]
DOWN = [((i + 1) % Z_LEN, i) for i in range(Z_LEN)]
VMEM_LIMIT = 60 * 1024 * 1024


def around(far):
    return [(i, (i + far) % Z_LEN) for i in range(Z_LEN)]


def swap(value, axis):
    return lax.ppermute(value, axis, SWAP)


def dot_rows(left, right):
    return lax.dot_general(left, right, (((1,), (1,)), ((), ())), preferred_element_type=F32)


def dot_cols(left, right):
    return lax.dot_general(left, right, (((0,), (0,)), ((), ())), preferred_element_type=F32)


def dot(left, right):
    return jnp.dot(left, right, preferred_element_type=F32)


def fence(now, *then):
    return lax.optimization_barrier((tuple(now),) + then)[0]


def ring(value):
    return lax.ppermute(value, "bz", UP)


def flatten(steps):
    return [piece for step in steps for piece in step]


def like(steps, refs):
    refs = list(refs)
    return [[refs.pop(0) for _ in step] for step in steps]


def add_low(left, right):
    return (left.astype(F32) + right.astype(F32)).astype(BF)


def ring_back(total):
    return lax.ppermute(total.astype(BF), "bz", DOWN)


def joined(index, own, other):
    return jnp.where(index == 0, jnp.concatenate([own, other], 0), jnp.concatenate([other, own], 0))


def across(value, far):
    return lax.ppermute(value, "bz", [(i, i ^ far) for i in range(Z_LEN)])


def in_all(value, spread):
    value = value.reshape(1, Z_LEN, 2, 2, 2, -1)
    if spread > 1:
        value = lax.all_gather(value, "bs", axis=0, tiled=True)
    return value.transpose(2, 3, 0, 1, 4, 5).reshape(8 * Z_LEN * spread, -1)


def halved(value, name, axis):
    index = lax.axis_index(name)
    return (
        lax.dynamic_index_in_dim(value, index, axis, keepdims=False),
        lax.dynamic_index_in_dim(value, 1 - index, axis, keepdims=False),
    )


def turn(value, cosine, sine, lane):
    near = jnp.where(
        (lane % HEAD_DIM) < ROT // 2,
        pltpu.roll(value, 128 - ROT // 2, 1),
        pltpu.roll(value, ROT // 2, 1),
    )
    return value * cosine + near * sine


def take_rows(rows_ref, steps, begin):
    for at, pieces in enumerate(steps):

        @pl.when(pl.program_id(0) == begin + at)
        def _(pieces=pieces):
            row = 0
            for piece in pieces:
                rows_ref[row : row + piece.shape[0]] = piece[...]
                row += piece.shape[0]


def by_row(block, lanes, begin=0):
    return pl.BlockSpec((block, lanes), lambda i, *_: (i + begin, 0))


def fixed(*values):
    def spec(value):
        rank = len(value.shape)
        return pl.BlockSpec(value.shape, lambda i, *_: (0,) * rank)

    return [spec(value) for value in values]


def halves(hx, width):
    half = width // 2
    return [pl.ds(pl.multiple_of(at * half, half), half) for at in (hx, 1 - hx)]


def dot_halves(left_ref, hx, own_ref, other_ref):
    own, other = halves(hx, left_ref.shape[1])
    return dot(left_ref[:, own], own_ref[...]) + dot(left_ref[:, other], other_ref[...])


def front_kernel(steps, plane_ref, *refs):
    count = len(flatten(steps))
    pieces, refs = like(steps, refs[:count]), refs[count:]
    gain_ref, shift_ref, own_ref, other_ref, bias_ref, cos_ref, sin_ref = refs[:7]
    h_ref, q_ref, kv_ref, pre_ref, out_ref, mean_ref, scale_ref, x_ref = refs[-8:]
    take_rows(x_ref, pieces, 0)
    x = x_ref[...].astype(F32)
    mean = jnp.mean(x, -1, keepdims=True)
    centred = x - mean
    scale = lax.rsqrt(jnp.mean(centred * centred, -1, keepdims=True) + EPS)
    mean_ref[...] = mean
    scale_ref[...] = scale
    h_ref[...] = (centred * scale * gain_ref[...] + shift_ref[...]).astype(BF)
    linear = dot_halves(h_ref, plane_ref[0], own_ref, other_ref) + bias_ref[...]
    lane = lax.broadcasted_iota(jnp.int32, (x.shape[0], 128), 1)
    cosine, sine = cos_ref[...], sin_ref[...]
    q_ref[...] = turn(linear[:, :128], cosine, sine, lane).astype(BF) * BF(HEAD_DIM**-0.5)
    kv_ref[:, :128] = turn(linear[:, 128:256], cosine, sine, lane).astype(BF)
    kv_ref[:, 128:] = linear[:, 256:384].astype(BF)
    pre = linear[:, 384:]
    pre_ref[...] = pre
    out_ref[...] = (0.5 * pre * (1.0 + jnp.tanh(0.7978845608 * (pre + 0.044715 * pre * pre * pre)))).astype(BF)


def front(plane, pieces, held, gain, shift, own, other, bias, cosine, sine):
    block, width = sum(piece.shape[0] for piece in pieces[0]), gain.shape[1]
    rows = 8 * block
    cols = own.shape[1]
    wide = cols - 384
    flat_pieces = flatten(pieces)
    here = functools.partial(by_row, block, begin=4 if held else 0)
    lanes = (width, 128, 256, wide, wide, 1, 1)
    types = (BF, BF, BF, F32, BF, F32, F32)
    return pl.pallas_call(
        functools.partial(front_kernel, pieces),
        grid_spec=pltpu.PrefetchScalarGridSpec(
            num_scalar_prefetch=1,
            grid=(4,),
            in_specs=fixed(*flat_pieces, gain, shift, own, other, bias)
            + [here(128), here(128)]
            + [pl.BlockSpec(memory_space=pl.ANY)] * len(held),
            out_specs=[here(n) for n in lanes],
            scratch_shapes=[pltpu.VMEM((block, width), BF)],
        ),
        out_shape=[jax.ShapeDtypeStruct((rows, n), kind) for n, kind in zip(lanes, types)],
        input_output_aliases={len(flat_pieces) + 8 + i: i for i in range(len(held))},
        compiler_params=pltpu.CompilerParams(vmem_limit_bytes=VMEM_LIMIT),
        cost_estimate=pl.CostEstimate(
            flops=rows * width * cols + 6 * rows * width, bytes_accessed=rows * width * 3, transcendentals=rows * wide
        ),
    )(plane[None], *flat_pieces, gain, shift, own, other, bias, cosine, sine, *held)


def two_heads(value):
    lane = lax.broadcasted_iota(jnp.int32, value.shape, 1)
    zero = jnp.zeros_like(value)
    return jnp.concatenate([jnp.where(lane < HEAD_DIM, value, zero), jnp.where(lane < HEAD_DIM, zero, value)], 0)


def one_row(value):
    half = value.shape[0] // 2
    lane = lax.broadcasted_iota(jnp.int32, (half, 128), 1)
    return jnp.where(lane < HEAD_DIM, value[:half], value[half:])


def place_in(row, share):
    return ((row & share) << 1) | ((row & (2 * share)) >> 1) | (row & (share - 1))


def allowed_pairs(meta_ref, block, query_at, key_at):
    turned, length = meta_ref[0], meta_ref[1]
    shape = (block, 2 * block)
    row = lax.broadcasted_iota(jnp.int32, shape, 1) & (block - 1)
    query = query_at * block + (place_in(row, block // 4) ^ turned)
    key = key_at * block + (place_in(lax.broadcasted_iota(jnp.int32, shape, 0), block // 4) ^ turned)
    return (key <= query) & (key < length)


def key_ranges(meta_ref, block, query_at):
    length = meta_ref[1]
    plain = jnp.minimum(query_at, length // block)
    last = jnp.minimum(query_at + 1, (length + block - 1) // block)
    return plain, last


def spot_of(at):
    near = 2 * Z_LEN
    spot = lax.rem(at, near)
    return lax.div(at, near) * 2 + lax.div(spot, 4), slice(None), lax.rem(spot, 2), lax.rem(lax.div(spot, 2), 2)


def rows_of(ref, at):
    value = ref[spot_of(at)]
    return value.reshape(value.shape[0] * value.shape[1], value.shape[2])


def add_rows(ref, at, value):
    ref[spot_of(at)] += value.reshape(2, value.shape[0] // 2, value.shape[1])


def flat(ref):
    value = ref[0, :, 0, 0]
    return value.reshape(value.shape[0] * value.shape[1], value.shape[2])


def key_rows(kv_ref, order_ref, at, count):
    return jnp.concatenate([rows_of(kv_ref, order_ref[at + i]) for i in range(count)], 0)


def over_keys(meta_ref, block, query_at, step, state):
    plain, last = key_ranges(meta_ref, block, query_at)
    pairs = plain // 2
    state = lax.fori_loop(0, pairs, lambda i, carried: step(False, 2, 2 * i, carried), state)
    state = lax.fori_loop(2 * pairs, plain, functools.partial(step, False, 1), state)
    return lax.fori_loop(plain, last, functools.partial(step, True, 1), state)


def attend_kernel(block, meta_ref, query_ref, order_ref, q_ref, kv_ref, full_ref, low_ref, lse_ref):
    query_at = query_ref[pl.program_id(0)]
    queries = two_heads(flat(q_ref))

    def step(masked, count, at, state):
        top, total, mixed = state
        both = key_rows(kv_ref, order_ref, at, count)
        scores = dot_rows(both[:, :128], queries)
        if masked:
            allowed = allowed_pairs(meta_ref, block, query_at, at)
            scores = jnp.where(allowed, scores, NEG)
        fresh = jnp.maximum(top, jnp.max(scores, 0, keepdims=True))
        factor = jnp.exp(top - fresh)
        weights = jnp.exp(scores - fresh)
        if masked:
            weights = jnp.where(allowed, weights, 0.0)
        total = total * factor + jnp.sum(weights, 0, keepdims=True)
        return fresh, total, mixed * factor + dot_cols(both[:, 128:], weights.astype(BF))

    state = (
        jnp.full((1, 2 * block), NEG, F32),
        jnp.zeros((1, 2 * block), F32),
        jnp.zeros((128, 2 * block), F32),
    )
    top, total, mixed = over_keys(meta_ref, block, query_at, step, state)
    mixed = mixed / total
    full = jnp.concatenate([mixed[:HEAD_DIM, :block], mixed[HEAD_DIM:, block:]], 0).T
    shape = full_ref.shape[1:2] + full_ref.shape[4:]
    full_ref[0, :, 0, 0] = full.reshape(shape)
    low_ref[0, :, 0, 0] = full.astype(BF).reshape(shape)
    lse_ref[...] = jnp.broadcast_to((top + jnp.log(total))[None], lse_ref.shape)


def placed(share, lanes):
    return pl.BlockSpec((1, 2, 1, 1, 2 * share, lanes), lambda i, *_: (i // 4, 0, i % 2, (i // 2) % 2, 0, 0))


def attend(table, q, kv, share):
    block = 4 * share
    blocks = 2 * Z_LEN
    rows, keys = q.shape[0], kv.shape[0]
    shape = (2, 2, 2, Z_LEN // 2, 2 * share, 128)
    kv_shape = (keys // (4 * Z_LEN * share), 2, 2, Z_LEN // 2, 2 * share, 256)
    full, low, lse = pl.pallas_call(
        functools.partial(attend_kernel, block),
        grid_spec=pltpu.PrefetchScalarGridSpec(
            num_scalar_prefetch=3,
            grid=(blocks,),
            in_specs=[placed(share, 128), pl.BlockSpec(kv_shape, lambda i, *_: (0, 0, 0, 0, 0, 0))],
            out_specs=[placed(share, 128), placed(share, 128), pl.BlockSpec((1, 8, 2 * block), lambda i, *_: (i, 0, 0))],
        ),
        out_shape=[
            jax.ShapeDtypeStruct(shape, F32),
            jax.ShapeDtypeStruct(shape, BF),
            jax.ShapeDtypeStruct((blocks, 8, 2 * block), F32),
        ],
        compiler_params=pltpu.CompilerParams(vmem_limit_bytes=VMEM_LIMIT),
        cost_estimate=pl.CostEstimate(
            flops=16 * rows * keys * 128, bytes_accessed=rows * 128 * 16, transcendentals=rows * keys
        ),
    )(*table, q.reshape(shape), kv.reshape(kv_shape))
    return full, low.reshape(rows, 128), lse


def attend_back_kernel(blocks, block, meta_ref, query_ref, order_ref, q_ref, kv_ref, full_ref, lse_ref, grad_ref, dq_ref, dkv_ref, dk_acc, dv_acc):
    at_block = pl.program_id(0)
    query_at = query_ref[at_block]
    queries = two_heads(flat(q_ref))
    grads = two_heads(flat(grad_ref))
    full = flat(full_ref)
    delta = jnp.sum(grads.astype(F32) * jnp.concatenate([full, full], 0), -1, keepdims=True)
    delta = jnp.broadcast_to(delta, (2 * block, 128)).T[:1]
    lse = lse_ref[0, :1]

    @pl.when(at_block == 0)
    def _():
        dk_acc[...] = jnp.zeros_like(dk_acc)
        dv_acc[...] = jnp.zeros_like(dv_acc)

    def step(masked, count, at, grad_query):
        both = key_rows(kv_ref, order_ref, at, count)
        keys = both[:, :128]
        scores = dot_rows(keys, queries)
        if masked:
            allowed = allowed_pairs(meta_ref, block, query_at, at)
            scores = jnp.where(allowed, scores, NEG)
        weights = jnp.exp(scores - lse)
        if masked:
            weights = jnp.where(allowed, weights, 0.0)
        grad_scores = (weights * (dot_rows(both[:, 128:], grads) - delta)).astype(BF)
        grad_keys = dot(grad_scores, queries)
        grad_values = dot(weights.astype(BF), grads)
        for i in range(count):
            spot = order_ref[at + i]
            add_rows(dk_acc, spot, grad_keys[i * block : (i + 1) * block])
            add_rows(dv_acc, spot, grad_values[i * block : (i + 1) * block])
        return grad_query + dot_cols(grad_scores, keys)

    grad_query = over_keys(meta_ref, block, query_at, step, jnp.zeros((2 * block, 128), F32))
    shape = dq_ref.shape[1:2] + dq_ref.shape[4:]
    dq_ref[0, :, 0, 0] = (one_row(grad_query) * HEAD_DIM**-0.5).astype(BF).reshape(shape)

    @pl.when(at_block == blocks - 1)
    def _():
        dkv_ref[..., :128] = dk_acc[...].astype(BF)
        dkv_ref[..., 128:] = dv_acc[...].astype(BF)


def attend_back(table, q, kv, full, lse, grad, share):
    block = 4 * share
    blocks = 2 * Z_LEN
    rows, keys = q.shape[0], kv.shape[0]
    shape = (2, 2, 2, Z_LEN // 2, 2 * share, 128)
    kv_shape = (keys // (4 * Z_LEN * share), 2, 2, Z_LEN // 2, 2 * share, 256)
    kv_spec = pl.BlockSpec(kv_shape, lambda i, *_: (0, 0, 0, 0, 0, 0))
    dq, dkv = pl.pallas_call(
        functools.partial(attend_back_kernel, blocks, block),
        grid_spec=pltpu.PrefetchScalarGridSpec(
            num_scalar_prefetch=3,
            grid=(blocks,),
            in_specs=[
                placed(share, 128),
                kv_spec,
                placed(share, 128),
                pl.BlockSpec((1, 8, 2 * block), lambda i, *_: (i, 0, 0)),
                placed(share, 128),
            ],
            out_specs=[placed(share, 128), kv_spec],
            scratch_shapes=[pltpu.VMEM(kv_shape[:-1] + (128,), F32), pltpu.VMEM(kv_shape[:-1] + (128,), F32)],
        ),
        out_shape=[jax.ShapeDtypeStruct(shape, BF), jax.ShapeDtypeStruct(kv_shape, BF)],
        compiler_params=pltpu.CompilerParams(vmem_limit_bytes=VMEM_LIMIT),
        cost_estimate=pl.CostEstimate(
            flops=40 * rows * keys * 128, bytes_accessed=rows * 128 * 24, transcendentals=rows * keys
        ),
    )(*table, q.reshape(shape), kv.reshape(kv_shape), full, lse, grad.reshape(shape))
    return dq.reshape(rows, 128), dkv.reshape(keys, 256)


def store_parts(parts, total_ref):
    rows = total_ref.shape[0]
    for at in range(8):
        half, core, ky = at // 4, at // 2 % 2, at % 2

        @pl.when(pl.program_id(0) == at)
        def _(ref=parts[2 - 2 * core + 1 - ky], half=half):
            ref[half * rows : (half + 1) * rows] = total_ref[...]


def part_shapes(rows, width):
    return [jax.ShapeDtypeStruct((2 * rows, width), BF)] * 4


def out_kernel(plane_ref, attn_ref, units_ref, dense_ref, own_ref, other_ref, *refs):
    parts, total_ref = refs[:-1], refs[-1]
    attn, units = attn_ref[...], units_ref[...]
    for part, weight_ref in zip(halves(plane_ref[0], total_ref.shape[1]), (own_ref, other_ref)):
        total_ref[:, part] = (dot(attn, dense_ref[:, part]) + dot_rows(units, weight_ref[...])).astype(BF)
    store_parts(parts, total_ref)


def out_partial(plane, attn, units, dense, own, other, block):
    rows, width = attn.shape[0], dense.shape[1]
    wide = units.shape[1]
    shapes = part_shapes(block, width)
    return pl.pallas_call(
        out_kernel,
        grid_spec=pltpu.PrefetchScalarGridSpec(
            num_scalar_prefetch=1,
            grid=(rows // block,),
            in_specs=[by_row(block, 128), by_row(block, wide)] + fixed(dense, own, other),
            out_specs=fixed(*shapes),
            scratch_shapes=[pltpu.VMEM((block, width), BF)],
        ),
        out_shape=shapes,
        compiler_params=pltpu.CompilerParams(vmem_limit_bytes=VMEM_LIMIT),
        cost_estimate=pl.CostEstimate(
            flops=2 * rows * width * (128 + wide), bytes_accessed=2 * rows * width, transcendentals=0
        ),
    )(plane[None], attn, units, dense, own, other)


def branch_kernel(steps, plane_ref, *refs):
    count = len(flatten(steps))
    pieces, refs = like(steps, refs[:count]), refs[count:]
    dense_ref, own_ref, other_ref, pre_ref, attn_ref, grad_ref, g_ref = refs
    take_rows(g_ref, pieces, 0)
    attn_ref[...] = dot_rows(g_ref[...], dense_ref[...]).astype(BF)
    grad = dot_halves(g_ref, plane_ref[0], own_ref, other_ref)
    u = pre_ref[...]
    square = u * u
    bend = jnp.tanh(0.7978845608 * u * (1.0 + 0.044715 * square))
    slope = 0.5 * (1.0 + bend) + 0.5 * u * (1.0 - bend * bend) * (0.7978845608 * (1.0 + 3 * 0.044715 * square))
    grad_ref[...] = (grad * slope).astype(BF)


def branch_grads(plane, pieces, dense, own, other, pre, block):
    width = dense.shape[1]
    rows, wide = pre.shape
    flat_pieces = flatten(pieces)
    return pl.pallas_call(
        functools.partial(branch_kernel, pieces),
        grid_spec=pltpu.PrefetchScalarGridSpec(
            num_scalar_prefetch=1,
            grid=(rows // block,),
            in_specs=fixed(*flat_pieces, dense, own, other) + [by_row(block, wide)],
            out_specs=[by_row(block, 128), by_row(block, wide), by_row(block, width)],
        ),
        out_shape=[
            jax.ShapeDtypeStruct((rows, 128), BF),
            jax.ShapeDtypeStruct((rows, wide), BF),
            jax.ShapeDtypeStruct((rows, width), BF),
        ],
        compiler_params=pltpu.CompilerParams(vmem_limit_bytes=VMEM_LIMIT),
        cost_estimate=pl.CostEstimate(
            flops=2 * rows * width * (128 + wide), bytes_accessed=rows * width * 4, transcendentals=rows * wide
        ),
    )(plane[None], *flat_pieces, dense, own, other, pre)


def turn_back(value, cosine, sine, lane):
    return turn(value.astype(F32), cosine, -sine, lane).astype(BF)


def back_kernel(steps, plane_ref, *refs):
    count = len(flatten(steps))
    pieces, refs = like(steps, refs[:count]), refs[count:]
    linear_ref, units_ref, own_ref, other_ref, mean_ref, scale_ref = refs[:6]
    parts, (gain_ref, shift_ref, small_ref, x_ref, total_ref) = refs[6:10], refs[10:]
    take_rows(x_ref, pieces, 0)
    linear, units = linear_ref[...], units_ref[...]

    @pl.when(pl.program_id(0) == 0)
    def _():
        gain_ref[...] = jnp.zeros_like(gain_ref)
        shift_ref[...] = jnp.zeros_like(shift_ref)
        small_ref[...] = jnp.zeros_like(small_ref)

    small_ref[:, :384] += jnp.sum(linear.astype(F32), 0, keepdims=True)
    small_ref[:, 384:] += jnp.sum(units.astype(F32), 0, keepdims=True)
    mean, scale = mean_ref[...], scale_ref[...]
    for part, weight_ref in zip(halves(plane_ref[0], total_ref.shape[1]), (own_ref, other_ref)):
        total = dot_rows(linear, weight_ref[:, :384]) + dot_rows(units, weight_ref[:, 384:])
        total_ref[:, part] = total.astype(BF)
        gain_ref[:, part] += jnp.sum(total * ((x_ref[:, part].astype(F32) - mean) * scale), 0, keepdims=True)
        shift_ref[:, part] += jnp.sum(total, 0, keepdims=True)
    store_parts(parts, total_ref)


def back_partial(plane, pieces, linear, units, own, other, mean, scale):
    rows = linear.shape[0]
    block = sum(piece.shape[0] for piece in pieces[0])
    width, cols = 2 * own.shape[0], own.shape[1]
    flat_pieces = flatten(pieces)
    shapes = part_shapes(block, width)
    sums = [jax.ShapeDtypeStruct((1, n), F32) for n in (width, width, cols)]
    *parts, gain, shift, small = pl.pallas_call(
        functools.partial(back_kernel, pieces),
        grid_spec=pltpu.PrefetchScalarGridSpec(
            num_scalar_prefetch=1,
            grid=(rows // block,),
            in_specs=fixed(*flat_pieces)
            + [by_row(block, 384), by_row(block, cols - 384)]
            + fixed(own, other)
            + [by_row(block, 1), by_row(block, 1)],
            out_specs=fixed(*shapes) + fixed(*sums),
            scratch_shapes=[pltpu.VMEM((block, width), BF), pltpu.VMEM((block, width), BF)],
        ),
        out_shape=shapes + sums,
        compiler_params=pltpu.CompilerParams(vmem_limit_bytes=VMEM_LIMIT),
        cost_estimate=pl.CostEstimate(
            flops=2 * rows * width * cols, bytes_accessed=4 * rows * width, transcendentals=0
        ),
    )(plane[None], *flat_pieces, linear, units, own, other, mean, scale)
    return parts, (gain, shift, small)


def weight_kernel(plane_ref, *refs):
    *pairs, away_ref, mine_ref = refs
    for out_ref, this in ((away_ref, pl.program_id(0) < 2), (mine_ref, pl.program_id(0) >= 2)):

        @pl.when(this)
        def _(out_ref=out_ref):
            begin = 0
            for left, right in zip(pairs[::2], pairs[1::2]):
                end = begin + right.shape[1]
                out_ref[:, begin:end] = dot_cols(left[...], right[...]).astype(BF)
                begin = end


def weight_rows(rows, quarter):
    return pl.BlockSpec((rows, quarter), lambda i, p: (0, ((p[0] + 1 - i // 2) % 2) * 2 + i % 2))


def weight_outs(quarter, cols):
    return [
        pl.BlockSpec((quarter, cols), lambda i, p: (jnp.minimum(i, 1), 0)),
        pl.BlockSpec((quarter, cols), lambda i, p: (jnp.maximum(i - 2, 0), 0)),
    ]


def weight_grads(plane, *pairs):
    rows, width = pairs[0][0].shape
    cols = sum(right.shape[1] for _, right in pairs)
    quarter = width // 4
    out = jax.ShapeDtypeStruct((2 * quarter, cols), BF)
    specs = [spec for _, right in pairs for spec in (weight_rows(rows, quarter), *fixed(right))]
    return pl.pallas_call(
        weight_kernel,
        grid_spec=pltpu.PrefetchScalarGridSpec(
            num_scalar_prefetch=1,
            grid=(4,),
            in_specs=specs,
            out_specs=weight_outs(quarter, cols),
        ),
        out_shape=[out, out],
        compiler_params=pltpu.CompilerParams(vmem_limit_bytes=VMEM_LIMIT),
        cost_estimate=pl.CostEstimate(
            flops=2 * rows * width * cols, bytes_accessed=2 * rows * width, transcendentals=0
        ),
    )(plane[None], *[value for pair in pairs for value in pair])


def triple_grads_kernel(plane_ref, h_ref, dq_ref, dkv_ref, cos_ref, sin_ref, away_ref, mine_ref, linear_ref):
    @pl.when(pl.program_id(0) == 0)
    def _():
        rows = 256

        def step(at, carry):
            here = pl.ds(pl.multiple_of(at * rows, rows), rows)
            lane = lax.broadcasted_iota(jnp.int32, (rows, 128), 1)
            cosine, sine = cos_ref[here, :], sin_ref[here, :]
            linear_ref[here, :128] = turn_back(dq_ref[here, :], cosine, sine, lane)
            linear_ref[here, 128:256] = turn_back(dkv_ref[here, :128], cosine, sine, lane)
            linear_ref[here, 256:] = dkv_ref[here, 128:]
            return carry

        lax.fori_loop(0, dq_ref.shape[0] // rows, step, 0)

    weight_kernel(plane_ref, h_ref, linear_ref, away_ref, mine_ref)


def triple_grads(plane, h, dq, dkv, cosine, sine):
    rows, width = h.shape
    quarter = width // 4
    out = jax.ShapeDtypeStruct((2 * quarter, 384), BF)
    linear = jax.ShapeDtypeStruct((rows, 384), BF)
    return pl.pallas_call(
        triple_grads_kernel,
        grid_spec=pltpu.PrefetchScalarGridSpec(
            num_scalar_prefetch=1,
            grid=(4,),
            in_specs=[weight_rows(rows, quarter)] + fixed(dq, dkv, cosine, sine),
            out_specs=weight_outs(quarter, 384) + fixed(linear),
        ),
        out_shape=[out, out, linear],
        compiler_params=pltpu.CompilerParams(vmem_limit_bytes=VMEM_LIMIT),
        cost_estimate=pl.CostEstimate(
            flops=2 * rows * width * 384, bytes_accessed=2 * rows * width, transcendentals=0
        ),
    )(plane[None], h, dq, dkv, cosine, sine)


def pack_kernel(triple_ref, expand_ref, shrink_ref, in_ref, out_ref):
    ranks, wide = in_ref.shape[0], out_ref.shape[2]
    for rank in range(ranks):
        for s in range(3):
            pair = [triple_ref[:, pl.ds((s * HEADS + x * ranks + rank) * HEAD_DIM, HEAD_DIM)] for x in range(2)]
            in_ref[rank, :, s * 128 : (s + 1) * 128] = jnp.concatenate(pair, 1)
        in_ref[rank, :, 384:] = expand_ref[:, rank * wide : (rank + 1) * wide]
        out_ref[rank] = shrink_ref[:, rank * wide : (rank + 1) * wide]


def pack(triple, expand, shrink, ranks):
    held = triple.shape[0]
    wide = expand.shape[1] // ranks
    return pl.pallas_call(
        pack_kernel,
        out_shape=[
            jax.ShapeDtypeStruct((ranks, held, 384 + wide), BF),
            jax.ShapeDtypeStruct((ranks, held, wide), BF),
        ],
        compiler_params=pltpu.CompilerParams(vmem_limit_bytes=VMEM_LIMIT),
    )(triple, expand, shrink)


def unpack_triple_kernel(back_ref, triple_ref):
    ranks = back_ref.shape[0]
    for rank in range(0, ranks, 2):
        for s in range(3):
            for x in range(2):
                lanes = slice(s * 128 + x * HEAD_DIM, s * 128 + (x + 1) * HEAD_DIM)
                pair = jnp.concatenate([back_ref[rank, :, lanes], back_ref[rank + 1, :, lanes]], 1)
                at = (s * HEADS + x * ranks + rank) * HEAD_DIM
                triple_ref[:, at : at + 128] = pair.astype(F32)


def unpack_triple(back):
    held = back.shape[1]
    return pl.pallas_call(
        unpack_triple_kernel,
        out_shape=jax.ShapeDtypeStruct((held, 3 * HEADS * HEAD_DIM), F32),
        compiler_params=pltpu.CompilerParams(vmem_limit_bytes=VMEM_LIMIT),
    )(back)


def unpack_units_kernel(back_ref, shrink_ref, expand_ref):
    wide = back_ref.shape[2] // 2
    for rank in range(back_ref.shape[0]):
        shrink_ref[:, rank * wide : (rank + 1) * wide] = back_ref[rank, :, :wide].astype(F32)
        expand_ref[:, rank * wide : (rank + 1) * wide] = back_ref[rank, :, wide:].astype(F32)


def unpack_units(back):
    ranks, held, cols = back.shape
    out = jax.ShapeDtypeStruct((held, ranks * cols // 2), F32)
    return pl.pallas_call(
        unpack_units_kernel,
        out_shape=[out, out],
        compiler_params=pltpu.CompilerParams(vmem_limit_bytes=VMEM_LIMIT),
    )(back)


def turn_tables(positions):
    half = ROT // 2
    inverse = 10000.0 ** (-(jnp.arange(half, dtype=F32) * 2.0) / ROT)
    angles = positions.astype(F32)[:, None] * inverse[None, :]
    cosine, sine = jnp.cos(angles), jnp.sin(angles)
    rest = (positions.shape[0], HEAD_DIM - ROT)
    cosine = jnp.concatenate([cosine, cosine, jnp.ones(rest, F32)], 1)
    sine = jnp.concatenate([-sine, sine, jnp.zeros(rest, F32)], 1)
    return jnp.tile(cosine, (1, 2)), jnp.tile(sine, (1, 2))


def core_pair(own, other, core):
    return jnp.where(core == 0, jnp.stack([own, other], 1), jnp.stack([other, own], 1))


def body(
    inputs,
    norm_gain,
    norm_bias,
    triple_weight,
    triple_bias,
    dense_weight,
    dense_bias,
    expand_weight,
    expand_bias,
    shrink_weight,
    shrink_bias,
    lengths,
    block_order,
    cotangent,
):
    share, width = inputs.shape[2], inputs.shape[3]
    hx, core, bs, bz, by = (lax.axis_index(name) for name in ALL)
    spread = lax.axis_size("bs")
    ranks = 2 * Z_LEN * 2
    devices = 2 * ranks * spread
    block = 4 * share
    rows = ranks * 2 * share
    near_blocks = Z_LEN * 2
    blocks = block_order.shape[0]
    held = width // devices
    ff = expand_weight.shape[1]
    ff_here = ff // ranks
    length = lengths[hx]

    def block_at(index):
        return jnp.sum(jnp.where(jnp.arange(blocks, dtype=jnp.int32) == index, block_order, 0))

    token_pos = (
        block_at(bs * near_blocks + bz * 2 + by) * block
        + (hx * 2 + core) * share
        + jnp.arange(share, dtype=jnp.int32)
    )
    valid = (token_pos[None, :] < lengths[:, None]).astype(F32)[:, :, None]

    spots = jnp.arange(blocks, dtype=jnp.int32)
    within = spots % near_blocks
    index = spots - within + ((bz + Z_LEN - within // 2) % Z_LEN) * 2 + (by + within) % 2
    key_at = jnp.sum(jnp.where(index[:, None] == spots[None, :], block_order[None, :], 0), 1)
    query_at = lax.dynamic_slice_in_dim(key_at, bs * near_blocks, near_blocks)
    turned = hx * 2 * share + core * share
    inside = place_in(jnp.arange(block, dtype=jnp.int32), share) ^ turned
    block_pos = query_at.reshape(2, Z_LEN // 2, 2).transpose(0, 2, 1)[:, None, :, :, None]
    row_pos = (block_pos * block + inside.reshape(1, 2, 1, 1, 2 * share)).reshape(rows)
    order = jnp.sum(jnp.where(key_at[None, :] == spots[:, None], spots[None, :], 0), 1)
    table = jnp.where(jnp.arange(2) == 0, turned, length).astype(jnp.int32), query_at, order
    cosine, sine = turn_tables(row_pos)

    def to_cols(sent):
        cols = sent.shape[2]
        got = lax.all_to_all(sent, RANK, split_axis=0, concat_axis=0, tiled=True)
        if spread > 1:
            got = lax.all_gather(got.reshape(2, 1, near_blocks, held, cols), "bs", axis=1, tiled=True)
        return got.reshape(width // 2, cols)

    def to_rows(mine):
        cols = mine.shape[-1]
        if spread > 1:
            mine = mine.reshape(2, spread, near_blocks, held, cols)
            mine = lax.psum_scatter(mine, "bs", scatter_dimension=1, tiled=True)
        return lax.all_to_all(mine.reshape(ranks, held, cols), RANK, split_axis=0, concat_axis=0, tiled=True)

    def both(low, high):
        return jnp.concatenate([low, high], 0)

    x_a = lax.dynamic_index_in_dim(inputs[:, 0], hx, 0, keepdims=False)
    x_b = swap(lax.dynamic_index_in_dim(inputs[:, 0], 1 - hx, 0, keepdims=False), "hx")
    vectors = (norm_gain, norm_bias, triple_bias, expand_bias, dense_bias, shrink_bias)
    sent_in, sent_out = pack(triple_weight, expand_weight, shrink_weight, ranks)
    small = jnp.concatenate(vectors)[None]

    x_b, small, cotangent, sent_in, sent_out = fence((x_b, small, cotangent, sent_in, sent_out))
    in_own = to_cols(sent_in)
    x_0 = both(x_a, x_b)
    grad_y = (cotangent[:, 0].astype(F32) * valid).astype(BF)
    g_a = lax.dynamic_index_in_dim(grad_y, hx, 0, keepdims=False)
    g_b = swap(lax.dynamic_index_in_dim(grad_y, 1 - hx, 0, keepdims=False), "hx")
    small = joined(by, small, swap(small, "by"))
    small = joined(core, small, swap(small, "core"))
    more = swap(small, "hx")
    cosine, sine = turn_tables(row_pos)

    x_0, in_own, g_b, small, more, cosine, sine = fence((x_0, in_own, g_b, small, more, cosine, sine), table)
    in_other = swap(in_own, "hx")
    y_0 = swap(x_0, "by")
    x_1 = ring(x_0)
    g_0 = both(g_a, g_b)
    small = joined(hx, small, more)
    more = across(small, 1)

    y_0, x_1, g_0, small, more = fence((y_0, x_1, g_0, small, more))
    y_1 = swap(x_1, "by")
    x_2 = ring(x_1)
    small = joined(bz % 2, small, more)
    more = across(small, 2)

    y_1, x_2, small, more = fence((y_1, x_2, small, more))
    y_2 = swap(x_2, "by")
    x_3 = ring(x_2)
    own_one, y_one = both(x_0, x_1), both(y_0, y_1)
    c_one = swap(own_one, "core"), swap(y_one, "core")
    small = in_all(joined(bz // 2, small, more), spread)

    cuts = [0]
    for leaf in (norm_gain, norm_bias, triple_bias, expand_bias, dense_bias, shrink_bias):
        cuts.append(cuts[-1] + leaf.shape[0])
    gain, shift, triple_b, expand_b, dense_b, shrink_b = (
        small[:, low:high].reshape(-1).astype(F32) for low, high in zip(cuts[:-1], cuts[1:])
    )
    rank = core * near_blocks + bz * 2 + by
    bias_triple = lax.dynamic_index_in_dim(
        triple_b.reshape(3, 2, ranks, HEAD_DIM).transpose(2, 0, 1, 3).reshape(ranks, 384), rank, 0
    )
    bias_expand = lax.dynamic_index_in_dim(expand_b.reshape(ranks, ff_here), rank, 0)
    bias_in = jnp.concatenate([bias_triple, bias_expand], 1)

    y_2, x_3, c_one, in_other, bias_in = fence((y_2, x_3, c_one, in_other, bias_in))
    y_3 = swap(x_3, "by")
    g_1 = ring(g_0)
    own_two = both(x_2, x_3)
    c_two = (swap(own_two, "core"),)
    x_one = ((own_one,), (y_one,), (c_one[0],), (c_one[1],))
    into = (gain[None], shift[None], in_own, in_other, bias_in, cosine, sine)
    held_one = front(hx, x_one, (), *into)

    held_one, y_3, g_1, c_two, sent_out = fence((held_one, y_3, g_1, c_two, sent_out))
    y_two = both(y_2, y_3)
    out_own = to_cols(sent_out)
    c_two = c_two[0], swap(y_two, "core")

    held_one, c_two = fence((held_one, c_two))
    x_two = ((own_two,), (y_two,), (c_two[0],), (c_two[1],))
    h, q, kv, pre, expand_out, mean, scale = front(hx, x_two, held_one, *into)

    q, g_0, g_1, out_own = fence((q, g_0, g_1, out_own))
    out_other = swap(out_own, "hx")
    own_one = both(g_0, g_1)
    y_one = swap(own_one, "by")
    g_2 = ring(g_1)
    g_3 = lax.ppermute(g_0, "bz", around(3))
    kv_all = kv if spread == 1 else lax.all_gather(kv, "bs", axis=0, tiled=True)
    attn_full, attn_low, lse = attend(table, q, kv_all, share)
    if spread == 1:
        dense_away = swap(dense_weight, "hx")
        dense_pair = jnp.where(hx == 0, both(dense_weight, dense_away), both(dense_away, dense_weight))
    else:
        dense_all = lax.all_gather(dense_weight, ALL, axis=0, tiled=True).reshape(2, ranks, HEAD_DIM, width)
        dense_pair = lax.dynamic_index_in_dim(dense_all, rank, 1, keepdims=False).reshape(128, width)

    attn_low, y_one, g_2, g_3, own_one, out_other, dense_pair = fence(
        (attn_low, y_one, g_2, g_3, own_one, out_other, dense_pair)
    )
    own_two = both(g_2, g_3)
    y_two = swap(own_two, "by")
    c_one = swap(own_one, "core"), swap(y_one, "core")
    c_two = (swap(own_two, "core"),)
    onto = (dense_pair, out_own, out_other)
    out_parts = out_partial(hx, attn_low, expand_out, *onto, block)

    y_two, c_one, c_two, out_parts = fence((y_two, c_one, c_two, out_parts))
    g_one = own_one, y_one
    c_two = c_two[0], swap(y_two, "core")
    g_pieces = tuple((piece,) for piece in g_one + c_one + (own_two, y_two) + c_two)

    out_parts, g_pieces = fence((out_parts, g_pieces))
    got_far, got_near = swap(out_parts[0], "core"), swap(out_parts[1], "core")
    grad_attention, grad_pre, g_all = branch_grads(hx, g_pieces, *onto, pre, block)

    grad_attention, grad_pre, g_all, got_far, got_near = fence((grad_attention, grad_pre, g_all, got_far, got_near))
    far = add_low(out_parts[2], got_far)

    grad_attention, grad_pre, g_all, far = fence((grad_attention, grad_pre, g_all, far))
    out_y = swap(far, "by")
    units_away, units_mine = weight_grads(hx, (g_all, expand_out), (h, grad_pre))

    grad_attention, units_away = fence((grad_attention, units_away))
    units_away = swap(units_away, "hx")
    dq, dkv = attend_back(table, q, kv_all, attn_full, lse, grad_attention, share)
    if spread > 1:
        dkv = lax.psum_scatter(dkv, "bs", scatter_dimension=0, tiled=True)

    def three(at, near_part, got, y_part):
        rows = slice(at * 2 * share, (at + 1) * 2 * share)
        return near_part[rows].astype(F32) + got[rows].astype(F32) + y_part[rows].astype(F32)

    dq, out_y, stay_near, got_near = fence((dq, out_y, out_parts[3], got_near))
    out_sum = three(3, stay_near, got_near, out_y)

    dq, out_sum = fence((dq, out_sum))
    ringed = ring_back(out_sum)
    triple_away, triple_mine, grad_linear = triple_grads(hx, h, dq, dkv, cosine, sine)

    units_away, triple_away, grad_linear, ringed = fence((units_away, triple_away, grad_linear, ringed))
    mine = add_low(units_mine, units_away)

    mine, triple_away, grad_linear = fence((mine, triple_away, grad_linear))
    units_rows = to_rows(mine)
    triple_away = swap(triple_away, "hx")
    h_parts, sums = back_partial(hx, x_one + x_two, grad_linear, grad_pre, in_own, in_other, mean, scale)

    sum_gain, sum_shift, sum_in = sums
    here = jnp.arange(ranks, dtype=jnp.int32)[:, None] == rank
    sum_triple = (
        jnp.where(here, sum_in[:, :384], 0.0)
        .reshape(ranks, 3, 2, HEAD_DIM)
        .transpose(1, 2, 0, 3)
        .reshape(3 * width)
    )
    sum_expand = jnp.where(here, sum_in[:, 384:], 0.0).reshape(ff)
    sum_y = jnp.sum(grad_y.astype(F32), (0, 1))
    pieces = [leaf.reshape(devices, -1) for leaf in (sum_gain, sum_shift, sum_triple, sum_expand, sum_y)]
    small = jnp.concatenate(pieces, 1).reshape(2, 2, spread, Z_LEN, 2, -1)

    grad_dense_here = dot_cols(g_all, attn_low)

    h_parts, small, units_rows, triple_away, ringed = fence(
        (h_parts, small, units_rows, triple_away, ringed), grad_dense_here
    )
    h_got_far, h_got_near = swap(h_parts[0], "core"), swap(h_parts[1], "core")
    small, away = halved(small, "core", 1)

    h_got_far, h_got_near, small, away = fence((h_got_far, h_got_near, small, away))
    one, two = slice(0, block), slice(block, 2 * block)
    far_two, far_one = add_low(h_parts[2][two], h_got_far[two]), add_low(h_parts[2][one], h_got_far[one])

    far_one, far_two, small, away = fence((far_one, far_two, small, away))
    h_y_two = swap(far_two, "by")
    away = swap(away, "core")
    mine = add_low(triple_mine, triple_away)
    out_ringed = ring_back(three(2, stay_near, got_near, out_y) + ringed)
    grad_shrink, grad_expand = unpack_units(units_rows)

    h_y_two, far_one, small, away, mine, out_ringed = fence(
        (h_y_two, far_one, small, away, mine, out_ringed), grad_shrink
    )
    h_sum = three(1, h_parts[3][two], h_got_near[two], h_y_two)
    small, away = halved(small + away, "hx", 0)

    h_sum, far_one, small, away, mine = fence((h_sum, far_one, small, away, mine))
    h_y_one = swap(far_one, "by")
    ringed = ring_back(h_sum)
    triple_rows = to_rows(mine)
    away = swap(away, "hx")
    out_sum = three(1, stay_near, got_near, out_y) + out_ringed

    h_y_one, ringed, small, away, out_sum, triple_rows = fence((h_y_one, ringed, small, away, out_sum, triple_rows))
    h_sum = three(0, h_parts[3][two], h_got_near[two], h_y_two) + ringed
    small, away = halved(small + away, "by", 2)

    h_sum, small, away, out_sum = fence((h_sum, small, away, out_sum))
    ringed = ring_back(h_sum)
    away = swap(away, "by")
    h_last = [three(at, h_parts[3][one], h_got_near[one], h_y_one) for at in (0, 1)]
    grad_triple = unpack_triple(triple_rows)

    ringed, small, away, h_last, out_sum = fence((ringed, small, away, h_last, out_sum), grad_triple)
    h_sum = h_last[1] + ringed
    small = small + away

    h_sum, small, out_sum = fence((h_sum, small, out_sum))
    ringed = ring_back(h_sum)
    out_ringed = ring_back(out_sum)
    terms = [lax.dynamic_index_in_dim(small, (bz + kz) % Z_LEN, 1, keepdims=False) for kz in range(Z_LEN)]
    terms = terms[:1] + [lax.ppermute(terms[kz], "bz", around(kz)) for kz in range(1, Z_LEN)]

    ringed, out_ringed, terms = fence((ringed, out_ringed, terms))
    h_sum = (h_last[0] + ringed).reshape(2, share, width)
    out_sum = (three(0, stay_near, got_near, out_y) + out_ringed).reshape(2, share, width)

    dense_grads = grad_dense_here.T.reshape(2, HEAD_DIM, width)
    if spread == 1:
        dense_mine = lax.dynamic_index_in_dim(dense_grads, hx, 0, keepdims=False)
        dense_away = lax.dynamic_index_in_dim(dense_grads, 1 - hx, 0, keepdims=False)
        grad_dense = dense_mine + swap(dense_away.astype(BF), "hx").astype(F32)
    else:
        spot = jnp.arange(ranks, dtype=jnp.int32)[None, :, None, None] == rank
        dense_whole = jnp.where(spot, dense_grads[:, None], 0.0).reshape(width, width)
        grad_dense = lax.psum_scatter(dense_whole, ALL, scatter_dimension=0, tiled=True)

    small = sum(terms)
    if spread > 1:
        small = lax.psum_scatter(small, "bs", scatter_dimension=0, tiled=True)
    small = small.reshape(-1)
    small_grads = []
    begin = 0
    for piece in pieces:
        small_grads.append(small[begin : begin + piece.shape[1]])
        begin += piece.shape[1]
    small_gain, small_shift, small_triple, small_expand, small_out = small_grads

    source = inputs[:, 0].astype(F32)
    out_away = swap(out_sum[1].astype(BF), "hx").astype(F32)
    mixed = jnp.where(hx == 0, jnp.stack([out_sum[0], out_away]), jnp.stack([out_away, out_sum[0]]))
    output = (valid * (source + mixed + dense_b + shrink_b)).astype(BF).reshape(inputs.shape)

    h_away = swap(h_sum[1].astype(BF), "hx").astype(F32)
    grad_h = jnp.where(hx == 0, jnp.stack([h_sum[0], h_away]), jnp.stack([h_away, h_sum[0]]))
    centred = source - jnp.mean(source, -1, keepdims=True)
    scale = lax.rsqrt(jnp.mean(centred * centred, -1, keepdims=True) + EPS)
    normed = centred * scale
    g = grad_h * gain
    grad_source = scale * (
        g - jnp.mean(g, -1, keepdims=True) - normed * jnp.mean(g * normed, -1, keepdims=True)
    )
    grad_inputs = (grad_y.astype(F32) + grad_source).astype(BF).reshape(inputs.shape)
    return (
        output,
        grad_inputs,
        small_gain,
        small_shift,
        grad_triple,
        small_triple,
        grad_dense,
        small_out,
        grad_expand,
        small_expand,
        grad_shrink,
        small_out,
    )


def solution(mesh):
    head, blk = mesh.devices.shape
    split = Mesh(mesh.devices.reshape(head // 2, 2, blk // (2 * Z_LEN), Z_LEN, 2), ALL)
    tokens = P(None, ("bs", "bz", "by"), ("hx", "core"), None)
    vector = P(ALL)
    matrix = P(ALL, None)
    return jax.shard_map(
        body,
        mesh=split,
        in_specs=(
            tokens,
            vector,
            vector,
            matrix,
            vector,
            matrix,
            vector,
            matrix,
            vector,
            matrix,
            vector,
            P(),
            P(),
            tokens,
        ),
        out_specs=(
            tokens,
            tokens,
            vector,
            vector,
            matrix,
            vector,
            matrix,
            vector,
            matrix,
            vector,
            matrix,
            vector,
        ),
        check_vma=False,
    )
```

time: 571 us -> 521 us (0.912)
  the two profiles are of different devices: /device:TPU:17 before, /device:TPU:0 now
where the time goes in v3:
time: 521 us; the launch traced here: 512 us
  waiting for transfers between devices  184 us (35%)
  Pallas kernels  159 us (31%)
  starting transfers between devices  73.7 us (14%)
  other arithmetic  47.7 us (9%)
  local copies, waits for them, and re-layouts  39.6 us (8%)
  matrix products  5.72 us (1%)
    ppermute x37, waiting for transfers between devices, swap(): return lax.ppermute(value, axis, SWAP)  62.4 us
    all_to_all x2, waiting for transfers between devices, to_cols(): got = lax.all_to_all(sent, RANK, split_axis=0, concat_axis=0, tiled=True)  31.3 us
    pallas_call x2, Pallas kernels, front(): pl.pallas_call(functools.partial(front_kernel, pieces), grid_spec=pltpu.P...  28.4 us
    ppermute x6, waiting for transfers between devices, ring_back(): return lax.ppermute(total.astype(BF), 'bz', DOWN)  25.6 us
    ppermute x37, starting transfers between devices, swap(): return lax.ppermute(value, axis, SWAP)  25.4 us
    pallas_call x1, Pallas kernels, attend_back(): pl.pallas_call(functools.partial(attend_back_kernel, blocks, block), grid...  23.5 us
    pallas_call x1, Pallas kernels, back_partial(): pl.pallas_call(functools.partial(back_kernel, pieces), grid_spec=pltpu.Pr...  21.2 us
    ppermute x2, waiting for transfers between devices, across(): return lax.ppermute(value, 'bz', [(i, i ^ far) for i in range(Z_LEN)])  19.8 us
  transfers between devices with their start and end apart: 58, of which 26 were waited for; matrix products, arithmetic and copies ran while one was open for 12% of the time, Pallas kernels for 31%

profile of v3, /device:TPU:0, one launch (start us, length us, event | category | flops | bytes accessed | tf_op | source)
XLA Modules:
  0.0 511.8 jit_solution(18062366779396844026)
XLA Ops:
  0.6 1.8 dynamic-slice_bitcast_fusion.3
  2.4 2.9 collective-permute-start
  6.8 4.1 concatenate.110
  10.8 3.7 shard_map.229
  15.3 5.9 %all-to-all-start = ((bf16[16,64,896]{2,1,0:T(8,128)(2,1)}), bf16[16,64,896]{2,1,0:T(8,128)(2,1)S(1)}, u32[]{:S(2)}, u32[]{:S(2)}) async-start(bf16[16,64,896]{2,1,0:T(8,128)(2,1)} %get-tuple-element.211), calls=%async_computation | async-start | bytes 3670016 | tf_op jit(solution)/shard_map/all_to_all | solution.py:748
  26.4 1.9 collective-permute-start.2
  33.0 1.8 pad_maximum_fusion
  34.7 4.9 collective-permute-done.4
  39.7 23.8 %all-to-all-done = bf16[16,64,896]{2,1,0:T(8,128)(2,1)S(1)} async-done(((bf16[16,64,896]{2,1,0:T(8,128)(2,1)}), bf16[16,64,896]{2,1,0:T(8,128)(2,1)S(1)}, u32[]{:S(2)}, u32[]{:S(2)}) %all-to-all-start) | async-done | bytes 1835040 | tf_op jit(solution)/shard_map/all_to_all | solution.py:748
  66.2 2.5 collective-permute-start.6
  72.3 9.0 %collective-permute-done.7 = bf16[8,704]{1,0:T(8,128)(2,1)S(1)} collective-permute-done((bf16[8,704]{1,0:T(8,128)(2,1)S(1)}, bf16[8,704]{1,0:T(8,128)(2,1)S(1)}, u32[]{:S(2)}, u32[]{:S(2)}) %collective-permute-start.7) | collective-permute-done | bytes 11296 | tf_op jit(solution)/shard_map/ppermute | solution.py:78
  86.4 10.8 %collective-permute-done.10 = bf16[16,704]{1,0:T(8,128)(2,1)S(1)} collective-permute-done((bf16[16,704]{1,0:T(8,128)(2,1)S(1)}, bf16[16,704]{1,0:T(8,128)(2,1)S(1)}, u32[]{:S(2)}, u32[]{:S(2)}) %collective-permute-start.10) | collective-permute-done | bytes 22560 | tf_op jit(solution)/shard_map/ppermute | solution.py:78
  101.1 1.9 constant_dynamic-update-slice_fusion.5
  103.0 10.2 %collective-permute-done.12 = bf16[128,2048]{1,0:T(8,128)(2,1)} collective-permute-done((bf16[128,2048]{1,0:T(8,128)(2,1)}, bf16[128,2048]{1,0:T(8,128)(2,1)}, u32[]{:S(2)}, u32[]{:S(2)}) %collective-permute-start.12) | collective-permute-done | bytes 524320 | tf_op jit(solution)/shard_map/ppermute | solution.py:53
  113.2 1.9 constant_dynamic-update-slice_fusion.4.refs_0_.refs_4_
  116.4 2.5 copy.79.refs_10_.sin_ref
  120.9 14.2 %shard_map.230 = (bf16[2048,2048]{1,0:T(8,128)(2,1)}, bf16[2048,128]{1,0:T(8,128)(2,1)}, bf16[2048,256]{1,0:T(8,128)(2,1)}, f32[2048,512]{1,0:T(8,128)}, bf16[20...) custom-call(s32[1]{0:T(128)} %bitcast.2.plane_ref, ...), custom_call_target="tpu_custom_call" | custom-call | flops 3783262208 | bytes 12582912 | tf_op jit(solution)/shard_map/pallas_call | solution.py:171
  135.2 6.3 %all-to-all-start.1 = ((bf16[16,64,512]{2,1,0:T(8,128)(2,1)}), bf16[16,64,512]{2,1,0:T(8,128)(2,1)}, u32[]{:S(2)}, u32[]{:S(2)}) async-start(bf16[16,64,512]{2,1,0:T(8,128)(2,1)} %get-tuple-element.264), calls=%async_computation.1 | async-start | bytes 2097152 | tf_op jit(solution)/shard_map/all_to_all | solution.py:748
  146.4 14.2 %shard_map.231 = (bf16[2048,2048]{1,0:T(8,128)(2,1)}, bf16[2048,128]{1,0:T(8,128)(2,1)}, bf16[2048,256]{1,0:T(8,128)(2,1)}, f32[2048,512]{1,0:T(8,128)}, bf16[20...) custom-call(s32[1]{0:T(128)} %bitcast.2.plane_ref, ...), custom_call_target="tpu_custom_call", output_to_operand_aliasing={{0}: (12, {}), {1}: (13, {}), {2}: (14, {}), {3}: (15, {}),... | custom-call | flops 3783262208 | bytes 12582912 | tf_op jit(solution)/shard_map/pallas_call | solution.py:171
  160.6 7.4 %all-to-all-done.1 = bf16[16,64,512]{2,1,0:T(8,128)(2,1)} async-done(((bf16[16,64,512]{2,1,0:T(8,128)(2,1)}), bf16[16,64,512]{2,1,0:T(8,128)(2,1)}, u32[]{:S(2)}, u32[]{:S(2)}) %all-to-all-start.1) | async-done | bytes 1048608 | tf_op jit(solution)/shard_map/all_to_all | solution.py:748
  173.7 19.0 %shard_map.232 = (f32[2,2,2,2,128,128]{5,4,3,2,1,0:T(8,128)}, bf16[2,2,2,2,128,128]{5,4,3,2,1,0:T(8,128)(2,1)}, f32[8,8,512]{2,1,0:T(8,128)}) custom-call(s32[2]{0:T(128)} %compare_select_fusion.4.meta_ref, s32[8]{0:T(128)} %copy-done.43, s32[8]{0:T(128)} %select_reduce_fusion.order_ref, bf16[2,2,2,2,128,128]{5,4,3,2,1,0:T(8,128)(2,1)} %bitcast.137, ...), custom_call_target="tpu_custom_call" | custom-call | flops 8589934592 | bytes 4194304 | tf_op jit(solution)/shard_map/pallas_call | solution.py:298
  192.7 4.5 collective-permute-done.21
  199.9 14.2 %shard_map.233 = (bf16[512,2048]{1,0:T(8,128)(2,1)}, bf16[512,2048]{1,0:T(8,128)(2,1)}, bf16[512,2048]{1,0:T(8,128)(2,1)}, bf16[512,2048]{1,0:T(8,128)(2,1)}) custom-call(s32[1]{0:T(128)} %bitcast.2.plane_ref, bf16[2048,128]{1,0:T(8,128)(2,1)} %bitcast.149, bf16[2048,512]{1,0:T(8,128)(2,1)} %get-tuple-element.278.units_ref.refs_1_, ...), custom_call_target="tpu_custom_call" | custom-call | flops 5368709120 | bytes 8388608 | tf_op jit(solution)/shard_map/pallas_call | solution.py:420
  214.1 10.1 %collective-permute-done.25.refs_5_ = bf16[256,2048]{1,0:T(8,128)(2,1)} collective-permute-done((bf16[256,2048]{1,0:T(8,128)(2,1)S(1)}, bf16[256,2048]{1,0:T(8,128)(2,1)}, u32[]{:S(2)}, u32[]{:S(2)}) %collective-permute-start.25) | collective-permute-done | bytes 1048608 | tf_op jit(solution)/shard_map/ppermute | solution.py:33
  224.1 2.9 collective-permute-done.29.refs_7_
  228.0 16.3 %shard_map.234 = (bf16[2048,128]{1,0:T(8,128)(2,1)}, bf16[2048,512]{1,0:T(8,128)(2,1)}, bf16[2048,2048]{1,0:T(8,128)(2,1)}) custom-call(s32[1]{0:T(128)} %bitcast.2.plane_ref, bf16[256,2048]{1,0:T(8,128)(2,1)} %constant_dynamic-update-slice_fusion.8.refs_0_, bf16[256,2048]{1,0:T(8,128)(2,1)} %copy-done.37, ...), custom_call_target="tpu_custom_call" | custom-call | flops 5368709120 | bytes 16777216 | tf_op jit(solution)/shard_map/pallas_call | solution.py:455
  244.3 3.8 add_convert_fusion.1
  248.6 14.6 %shard_map.235 = (bf16[1024,1024]{1,0:T(8,128)(2,1)}, bf16[1024,1024]{1,0:T(8,128)(2,1)}) custom-call(s32[1]{0:T(128)} %bitcast.2.plane_ref, bf16[2048,2048]{1,0:T(8,128)(2,1)} %get-tuple-element.313.refs_0_, bf16[2048,512]{1,0:T(8,128)(2,1)} %get-tuple-element.278.units_ref.refs_1_, bf16[2048,2048]{1,0:T(8,128)(2,1)} %get-tuple-element.314.refs_2_.h_ref, ...), custom_call_target="tpu_custom_call" | custom-call | flops 8589934592 | bytes 8388608 | tf_op jit(solution)/shard_map/pallas_call | solution.py:562
  264.8 23.5 %shard_map.236 = (bf16[2,2,2,2,128,128]{5,4,3,2,1,0:T(8,128)(2,1)}, bf16[2,2,2,2,128,256]{5,4,3,2,1,0:T(8,128)(2,1)}) custom-call(s32[2]{0:T(128)} %compare_select_fusion.4.meta_ref, s32[8]{0:T(128)} %copy-done.43, s32[8]{0:T(128)} %select_reduce_fusion.order_ref, bf16[2,2,2,2,128,128]{5,4,3,2,1,0:T(8,128)(2,1)} %bitcast.138, ...), custom_call_target="tpu_custom_call" | custom-call | flops 21474836480 | bytes 6291456 | tf_op jit(solution)/shard_map/pallas_call | solution.py:370
  288.2 7.7 %collective-permute-done.32 = bf16[512,2048]{1,0:T(8,128)(2,1)S(1)} collective-permute-done((bf16[512,2048]{1,0:T(8,128)(2,1)}, bf16[512,2048]{1,0:T(8,128)(2,1)S(1)}, u32[]{:S(2)}, u32[]{:S(2)}) %collective-permute-start.32) | collective-permute-done | bytes 2097184 | tf_op jit(solution)/shard_map/ppermute | solution.py:33
  296.0 2.2 convert_add_fusion.9
  298.2 2.0 collective-permute-start.34
  300.2 11.3 %shard_map.237 = (bf16[1024,384]{1,0:T(8,128)(2,1)}, bf16[1024,384]{1,0:T(8,128)(2,1)}, bf16[2048,384]{1,0:T(8,128)(2,1)}) custom-call(s32[1]{0:T(128)} %bitcast.2.plane_ref, bf16[2048,2048]{1,0:T(8,128)(2,1)} %get-tuple-element.314.refs_2_.h_ref, bf16[2048,128]{1,0:T(8,128)(2,1)} %bitcast.139, bf16[2048,256]{1,0:T(8,128)(2,1)} %bitcast.134, ...), custom_call_target="tpu_custom_call" | custom-call | flops 3221225472 | bytes 8388608 | tf_op jit(solution)/shard_map/pallas_call | solution.py:602
  311.7 4.1 add_convert_fusion
  315.7 5.2 %all-to-all-start.2 = ((bf16[16,64,1024]{2,1,0:T(8,128)(2,1)}), bf16[16,64,1024]{2,1,0:T(8,128)(2,1)S(1)}, u32[]{:S(2)}, u32[]{:S(2)}) async-start(bf16[16,64,1024]{2,1,0:T(8,128)(2,1)} %bitcast.26), calls=%async_computation.2 | async-start | bytes 4194304 | tf_op jit(solution)/shard_map/all_to_all | solution.py:758
  321.1 5.7 %fusion.38 = f32[2048,128]{0,1:T(8,128)} fusion(bf16[2048,2048]{1,0:T(8,128)(2,1)} %get-tuple-element.313.refs_0_, bf16[2048,128]{1,0:T(8,128)(2,1)S(1)} %bitcast.150), kind=kOutput, calls=%fused_computation.159 | convolution fusion | flops 1073741824 | bytes 9961472 | tf_op jit(solution)/shard_map/dot_general | solution.py:41
  328.3 21.2 %shard_map.238 = (bf16[512,2048]{1,0:T(8,128)(2,1)}, bf16[512,2048]{1,0:T(8,128)(2,1)}, bf16[512,2048]{1,0:T(8,128)(2,1)}, bf16[512,2048]{1,0:T(8,128)(2,1)}, f3...) custom-call(s32[1]{0:T(128)} %bitcast.2.plane_ref, ...), custom_call_target="tpu_custom_call" | custom-call | flops 7516192768 | bytes 16777216 | tf_op jit(solution)/shard_map/pallas_call | solution.py:511
  354.9 13.6 %all-to-all-done.2.back_ref = bf16[16,64,1024]{2,1,0:T(8,128)(2,1)S(1)} async-done(((bf16[16,64,1024]{2,1,0:T(8,128)(2,1)}), bf16[16,64,1024]{2,1,0:T(8,128)(2,1)S(1)}, u32[]{:S(2)}, u32[]{:S(2)}) %all-to-all-start.2) | async-done | bytes 2097184 | tf_op jit(solution)/shard_map/all_to_all | solution.py:758
  369.1 4.0 collective-permute-done.36
  373.1 3.0 collective-permute-done.37
  376.1 4.5 add_convert_fusion.2
  381.2 2.5 add_convert_fusion.5
  386.4 3.9 shard_map.239
  390.3 8.5 %collective-permute-done.40 = bf16[128,2048]{1,0:T(8,128)(2,1)S(1)} collective-permute-done((bf16[128,2048]{1,0:T(8,128)(2,1)}, bf16[128,2048]{1,0:T(8,128)(2,1)S(1)}, u32[]{:S(2)}, u32[]{:S(2)}) %collective-permute-start.40) | collective-permute-done | bytes 524320 | tf_op jit(solution)/shard_map/ppermute | solution.py:70
  398.8 7.2 %collective-permute-done.38 = bf16[256,2048]{1,0:T(8,128)(2,1)S(1)} collective-permute-done((bf16[256,2048]{1,0:T(8,128)(2,1)}, bf16[256,2048]{1,0:T(8,128)(2,1)S(1)}, u32[]{:S(2)}, u32[]{:S(2)}) %collective-permute-start.38) | collective-permute-done | bytes 1048608 | tf_op jit(solution)/shard_map/ppermute | solution.py:33
  406.1 2.2 convert_add_fusion.8
  408.3 5.1 all-to-all-start.3
  413.6 2.0 collective-permute-start.41
  416.1 3.3 collective-permute-start.42
  423.1 2.6 convert_add_fusion.7
  425.8 3.8 collective-permute-done.43
  429.6 10.8 %collective-permute-done.42 = bf16[128,2048]{1,0:T(8,128)(2,1)S(1)} collective-permute-done((bf16[128,2048]{1,0:T(8,128)(2,1)}, bf16[128,2048]{1,0:T(8,128)(2,1)S(1)}, u32[]{:S(2)}, u32[]{:S(2)}) %collective-permute-start.42) | collective-permute-done | bytes 524320 | tf_op jit(solution)/shard_map/ppermute | solution.py:70
  441.2 6.2 %collective-permute-done.41 = bf16[256,2048]{1,0:T(8,128)(2,1)S(1)} collective-permute-done((bf16[256,2048]{1,0:T(8,128)(2,1)}, bf16[256,2048]{1,0:T(8,128)(2,1)S(1)}, u32[]{:S(2)}, u32[]{:S(2)}) %collective-permute-start.41) | collective-permute-done | bytes 1048608 | tf_op jit(solution)/shard_map/ppermute | solution.py:33
  447.4 3.1 convert_add_fusion.6
  451.1 3.7 collective-permute-start.44
  454.8 2.4 convert_add_fusion.4
  457.2 2.6 shard_map.240
  459.8 6.0 %collective-permute-done.44 = bf16[128,2048]{1,0:T(8,128)(2,1)} collective-permute-done((bf16[128,2048]{1,0:T(8,128)(2,1)}, bf16[128,2048]{1,0:T(8,128)(2,1)}, u32[]{:S(2)}, u32[]{:S(2)}) %collective-permute-start.44) | collective-permute-done | bytes 524320 | tf_op jit(solution)/shard_map/ppermute | solution.py:70
  467.0 4.3 collective-permute-start.46
  471.5 3.3 collective-permute-start.49
  474.8 1.8 bitcast_add_fusion
  476.6 15.9 %collective-permute-done.50 = f32[1,640]{1,0:T(1,128)S(1)} collective-permute-done((f32[1,640]{1,0:T(1,128)S(1)}, f32[1,640]{1,0:T(1,128)S(1)}, u32[]{:S(2)}, u32[]{:S(2)}) %collective-permute-start.50) | collective-permute-done | bytes 2592 | tf_op jit(solution)/shard_map/ppermute | solution.py:961
  499.1 9.2 %collective-permute-done.52 = bf16[64,2048]{1,0:T(8,128)(2,1)S(1)} collective-permute-done((bf16[64,2048]{1,0:T(8,128)(2,1)S(1)}, bf16[64,2048]{1,0:T(8,128)(2,1)S(1)}, u32[]{:S(2)}, u32[]{:S(2)}) %collective-permute-start.52) | collective-permute-done | bytes 262176 | tf_op jit(solution)/shard_map/ppermute | solution.py:33
  508.9 1.9 fusion.24
  (277 shorter events, 71.8 us)
Async XLA Ops:
  2.4 12.1 %collective-permute-start = (bf16[64,2048]{1,0:T(8,128)(2,1)S(1)}, bf16[64,2048]{1,0:T(8,128)(2,1)S(1)}, u32[]{:S(2)}, u32[]{:S(2)}) collective-permute-start(bf16[64,2048]{1,0:T(8,128)(2,1)S(1)} %get-tuple-element.467), channel_id=1, source_target_pairs={{0,16},{16,0},{1,17},{17,1},{2,18},{18,2},{3,19},{19,3},{4,20},{20... | collective-permute-start | bytes 786440 | tf_op jit(solution)/shard_map/ppermute | solution.py:33
  15.3 48.3 %all-to-all-start = ((bf16[16,64,896]{2,1,0:T(8,128)(2,1)}), bf16[16,64,896]{2,1,0:T(8,128)(2,1)S(1)}, u32[]{:S(2)}, u32[]{:S(2)}) async-start(bf16[16,64,896]{2,1,0:T(8,128)(2,1)} %get-tuple-element.211), calls=%async_computation | async-start | bytes 3670016 | tf_op jit(solution)/shard_map/all_to_all | solution.py:748
  26.4 3.6 collective-permute-start.2
  30.0 1.4 collective-permute-start.3
  30.8 8.8 %collective-permute-start.1 = (bf16[64,2048]{1,0:T(8,128)(2,1)S(1)}, bf16[64,2048]{1,0:T(8,128)(2,1)S(1)}, u32[]{:S(2)}, u32[]{:S(2)}) collective-permute-start(bf16[64,2048]{1,0:T(8,128)(2,1)S(1)} %get-tuple-element.465), channel_id=1, source_target_pairs={{0,16},{16,0},{1,17},{17,1},{2,18},{18,2},{3,19},{19,3},{4,20},{20... | collective-permute-start | bytes 786440 | tf_op jit(solution)/shard_map/ppermute | solution.py:33
  31.4 8.3 %collective-permute-start.4 = (bf16[4,704]{1,0:T(4,128)(2,1)S(1)}, bf16[4,704]{1,0:T(4,128)(2,1)S(1)}, u32[]{:S(2)}, u32[]{:S(2)}) collective-permute-start(bf16[4,704]{1,0:T(4,128)(2,1)S(1)} %maximum_select_fusion.7), channel_id=1, source_target_pairs={{0,16},{16,0},{1,17},{17,1},{2,18},{18,2},{3,19},{19,3},{4,20},{20... | collective-permute-start | bytes 16904 | tf_op jit(solution)/shard_map/ppermute | solution.py:33
  39.7 23.8 %copy-start.30 = (bf16[64,2048]{1,0:T(8,128)(2,1)}, bf16[64,2048]{1,0:T(8,128)(2,1)S(1)}, u32[]{:S(2)}) copy-start(bf16[64,2048]{1,0:T(8,128)(2,1)S(1)} %collective-permute-done.1) | copy-start | bytes 786436
  66.2 15.1 %collective-permute-start.6 = (bf16[128,2048]{1,0:T(8,128)(2,1)S(1)}, bf16[128,2048]{1,0:T(8,128)(2,1)S(1)}, u32[]{:S(2)}, u32[]{:S(2)}) collective-permute-start(bf16[128,2048]{1,0:T(8,128)(2,1)S(1)} %copy-done.10), channel_id=1, source_target_pairs={{0,2},{2,4},{4,6},{6,0},{1,3},{3,5},{5,7},{7,1},{8,10},{10,12},{12... | collective-permute-start | bytes 1572872 | tf_op jit(solution)/shard_map/ppermute | solution.py:53
  68.8 13.2 %collective-permute-start.5 = (bf16[128,2048]{1,0:T(8,128)(2,1)S(1)}, bf16[128,2048]{1,0:T(8,128)(2,1)S(1)}, u32[]{:S(2)}, u32[]{:S(2)}) collective-permute-start(bf16[128,2048]{1,0:T(8,128)(2,1)S(1)} %copy-done.10), channel_id=1, source_target_pairs={{0,1},{1,0},{2,3},{3,2},{4,5},{5,4},{6,7},{7,6},{8,9},{9,8},{10,11... | collective-permute-start | bytes 1572872 | tf_op jit(solution)/shard_map/ppermute | solution.py:33
  69.4 11.9 %collective-permute-start.7 = (bf16[8,704]{1,0:T(8,128)(2,1)S(1)}, bf16[8,704]{1,0:T(8,128)(2,1)S(1)}, u32[]{:S(2)}, u32[]{:S(2)}) collective-permute-start(bf16[8,704]{1,0:T(8,128)(2,1)S(1)} %maximum_select_fusion.6), channel_id=1, source_target_pairs={{0,2},{2,0},{4,6},{6,4},{1,3},{3,1},{5,7},{7,5},{8,10},{10,8},{12,... | collective-permute-start | bytes 33800 | tf_op jit(solution)/shard_map/ppermute | solution.py:78
  70.8 42.4 %collective-permute-start.15 = (bf16[1024,896]{1,0:T(8,128)(2,1)S(1)}, bf16[1024,896]{1,0:T(8,128)(2,1)}, u32[]{:S(2)}, u32[]{:S(2)}) collective-permute-start(bf16[1024,896]{1,0:T(8,128)(2,1)S(1)} %bitcast.126), channel_id=1, source_target_pairs={{0,16},{16,0},{1,17},{17,1},{2,18},{18,2},{3,19},{19,3},{4,20},{20... | collective-permute-start | bytes 5505032 | tf_op jit(solution)/shard_map/ppermute | solution.py:33
  82.0 15.2 %collective-permute-start.9 = (bf16[128,2048]{1,0:T(8,128)(2,1)S(1)}, bf16[128,2048]{1,0:T(8,128)(2,1)}, u32[]{:S(2)}, u32[]{:S(2)}) collective-permute-start(bf16[128,2048]{1,0:T(8,128)(2,1)S(1)} %collective-permute-done.6), channel_id=1, source_target_pairs={{0,2},{2,4},{4,6},{6,0},{1,3},{3,5},{5,7},{7,1},{8,10},{10,12},{12... | collective-permute-start | bytes 1572872 | tf_op jit(solution)/shard_map/ppermute | solution.py:53
  82.8 14.4 %collective-permute-start.8 = (bf16[128,2048]{1,0:T(8,128)(2,1)S(1)}, bf16[128,2048]{1,0:T(8,128)(2,1)S(1)}, u32[]{:S(2)}, u32[]{:S(2)}) collective-permute-start(bf16[128,2048]{1,0:T(8,128)(2,1)S(1)} %collective-permute-done.6), channel_id=1, source_target_pairs={{0,1},{1,0},{2,3},{3,2},{4,5},{5,4},{6,7},{7,6},{8,9},{9,8},{10,11... | collective-permute-start | bytes 1572872 | tf_op jit(solution)/shard_map/ppermute | solution.py:33
  84.4 12.8 %collective-permute-start.10 = (bf16[16,704]{1,0:T(8,128)(2,1)S(1)}, bf16[16,704]{1,0:T(8,128)(2,1)S(1)}, u32[]{:S(2)}, u32[]{:S(2)}) collective-permute-start(bf16[16,704]{1,0:T(8,128)(2,1)S(1)} %maximum_select_fusion.5), channel_id=1, source_target_pairs={{0,4},{2,6},{4,0},{6,2},{1,5},{3,7},{5,1},{7,3},{8,12},{10,14},{12... | collective-permute-start | bytes 67592 | tf_op jit(solution)/shard_map/ppermute | solution.py:78
  86.4 26.7 %collective-permute-start.13 = (bf16[256,2048]{1,0:T(8,128)(2,1)}, bf16[256,2048]{1,0:T(8,128)(2,1)}, u32[]{:S(2)}, u32[]{:S(2)}) collective-permute-start(bf16[256,2048]{1,0:T(8,128)(2,1)} %constant_dynamic-update-slice_fusion.refs_0_), channel_id=1, source_target_pairs={{0,8},{8,0},{1,9},{9,1},{2,10},{10,2},{3,11},{11,3},{4,12},{12,4},... | collective-permute-start | bytes 3145736 | tf_op jit(solution)/shard_map/ppermute | solution.py:33
  97.2 16.0 %collective-permute-start.12 = (bf16[128,2048]{1,0:T(8,128)(2,1)}, bf16[128,2048]{1,0:T(8,128)(2,1)}, u32[]{:S(2)}, u32[]{:S(2)}) collective-permute-start(bf16[128,2048]{1,0:T(8,128)(2,1)} %collective-permute-done.9), channel_id=1, source_target_pairs={{0,2},{2,4},{4,6},{6,0},{1,3},{3,5},{5,7},{7,1},{8,10},{10,12},{12... | collective-permute-start | bytes 1572872 | tf_op jit(solution)/shard_map/ppermute | solution.py:53
  97.3 15.8 %collective-permute-start.11 = (bf16[128,2048]{1,0:T(8,128)(2,1)}, bf16[128,2048]{1,0:T(8,128)(2,1)}, u32[]{:S(2)}, u32[]{:S(2)}) collective-permute-start(bf16[128,2048]{1,0:T(8,128)(2,1)} %collective-permute-done.9), channel_id=1, source_target_pairs={{0,1},{1,0},{2,3},{3,2},{4,5},{5,4},{6,7},{7,6},{8,9},{9,8},{10,11... | collective-permute-start | bytes 1572872 | tf_op jit(solution)/shard_map/ppermute | solution.py:33
  98.7 14.4 %collective-permute-start.14 = (bf16[256,2048]{1,0:T(8,128)(2,1)}, bf16[256,2048]{1,0:T(8,128)(2,1)}, u32[]{:S(2)}, u32[]{:S(2)}) collective-permute-start(bf16[256,2048]{1,0:T(8,128)(2,1)} %constant_dynamic-update-slice_fusion.2.refs_1_), channel_id=1, source_target_pairs={{0,8},{8,0},{1,9},{9,1},{2,10},{10,2},{3,11},{11,3},{4,12},{12,4},... | collective-permute-start | bytes 3145736 | tf_op jit(solution)/shard_map/ppermute | solution.py:33
  115.1 20.1 %collective-permute-start.18 = (bf16[256,2048]{1,0:T(8,128)(2,1)}, bf16[256,2048]{1,0:T(8,128)(2,1)S(1)}, u32[]{:S(2)}, u32[]{:S(2)}) collective-permute-start(bf16[256,2048]{1,0:T(8,128)(2,1)} %constant_dynamic-update-slice_fusion.4.refs_0_.refs_4_), channel_id=1, source_target_pairs={{0,8},{8,0},{1,9},{9,1},{2,10},{10,2},{3,11},{11,3},{4,12},{12,4},... | collective-permute-start | bytes 3145736 | tf_op jit(solution)/shard_map/ppermute | solution.py:33
  118.9 16.2 %collective-permute-start.17 = (bf16[128,2048]{1,0:T(8,128)(2,1)S(1)}, bf16[128,2048]{1,0:T(8,128)(2,1)S(1)}, u32[]{:S(2)}, u32[]{:S(2)}) collective-permute-start(bf16[128,2048]{1,0:T(8,128)(2,1)S(1)} %pad_maximum_fusion.1), channel_id=1, source_target_pairs={{0,2},{2,4},{4,6},{6,0},{1,3},{3,5},{5,7},{7,1},{8,10},{10,12},{12... | collective-permute-start | bytes 1572872 | tf_op jit(solution)/shard_map/ppermute | solution.py:53
  118.9 16.2 %collective-permute-start.16 = (bf16[128,2048]{1,0:T(8,128)(2,1)}, bf16[128,2048]{1,0:T(8,128)(2,1)S(1)}, u32[]{:S(2)}, u32[]{:S(2)}) collective-permute-start(bf16[128,2048]{1,0:T(8,128)(2,1)} %collective-permute-done.12), channel_id=1, source_target_pairs={{0,1},{1,0},{2,3},{3,2},{4,5},{5,4},{6,7},{7,6},{8,9},{9,8},{10,11... | collective-permute-start | bytes 1572872 | tf_op jit(solution)/shard_map/ppermute | solution.py:33
  135.2 32.8 %all-to-all-start.1 = ((bf16[16,64,512]{2,1,0:T(8,128)(2,1)}), bf16[16,64,512]{2,1,0:T(8,128)(2,1)}, u32[]{:S(2)}, u32[]{:S(2)}) async-start(bf16[16,64,512]{2,1,0:T(8,128)(2,1)} %get-tuple-element.264), calls=%async_computation.1 | async-start | bytes 2097152 | tf_op jit(solution)/shard_map/all_to_all | solution.py:748
  142.7 2.7 collective-permute-start.19
  143.1 25.8 %copy-start.25 = (bf16[128,2048]{1,0:T(8,128)(2,1)S(1)}, bf16[128,2048]{1,0:T(8,128)(2,1)}, u32[]{:S(2)}) copy-start(bf16[128,2048]{1,0:T(8,128)(2,1)} %copy-done.24) | copy-start | bytes 1572868
  143.1 27.7 %collective-permute-start.24 = (bf16[64,2048]{1,0:T(8,128)(2,1)S(1)}, bf16[64,2048]{1,0:T(8,128)(2,1)S(1)}, u32[]{:S(2)}, u32[]{:S(2)}) collective-permute-start(bf16[64,2048]{1,0:T(8,128)(2,1)S(1)} %copy-done.27), channel_id=1, source_target_pairs={{0,16},{16,0},{1,17},{17,1},{2,18},{18,2},{3,19},{19,3},{4,20},{20... | collective-permute-start | bytes 786440 | tf_op jit(solution)/shard_map/ppermute | solution.py:33
  169.7 27.5 %collective-permute-start.20 = (bf16[256,2048]{1,0:T(8,128)(2,1)}, bf16[256,2048]{1,0:T(8,128)(2,1)S(1)}, u32[]{:S(2)}, u32[]{:S(2)}) collective-permute-start(bf16[256,2048]{1,0:T(8,128)(2,1)} %constant_dynamic-update-slice_fusion.8.refs_0_), channel_id=1, source_target_pairs={{0,1},{1,0},{2,3},{3,2},{4,5},{5,4},{6,7},{7,6},{8,9},{9,8},{10,11... | collective-permute-start | bytes 3145736 | tf_op jit(solution)/shard_map/ppermute | solution.py:33
  170.2 27.0 %collective-permute-start.23 = (bf16[1024,512]{1,0:T(8,128)(2,1)}, bf16[1024,512]{1,0:T(8,128)(2,1)}, u32[]{:S(2)}, u32[]{:S(2)}) collective-permute-start(bf16[1024,512]{1,0:T(8,128)(2,1)} %bitcast.16.own_ref.refs_9_), channel_id=1, source_target_pairs={{0,16},{16,0},{1,17},{17,1},{2,18},{18,2},{3,19},{19,3},{4,20},{20... | collective-permute-start | bytes 3145736 | tf_op jit(solution)/shard_map/ppermute | solution.py:33
  171.7 21.0 %collective-permute-start.22 = (bf16[128,2048]{1,0:T(8,128)(2,1)S(1)}, bf16[128,2048]{1,0:T(8,128)(2,1)S(1)}, u32[]{:S(2)}, u32[]{:S(2)}) collective-permute-start(bf16[128,2048]{1,0:T(8,128)(2,1)S(1)} %pad_maximum_fusion.1), channel_id=1, source_target_pairs={{0,6},{2,0},{4,2},{6,4},{1,7},{3,1},{5,3},{7,5},{8,14},{10,8},{12,... | collective-permute-start | bytes 1572872 | tf_op jit(solution)/shard_map/ppermute | solution.py:837
  172.5 24.7 %collective-permute-start.21 = (bf16[128,2048]{1,0:T(8,128)(2,1)S(1)}, bf16[128,2048]{1,0:T(8,128)(2,1)S(1)}, u32[]{:S(2)}, u32[]{:S(2)}) collective-permute-start(bf16[128,2048]{1,0:T(8,128)(2,1)S(1)} %copy-done.25), channel_id=1, source_target_pairs={{0,2},{2,4},{4,6},{6,0},{1,3},{3,5},{5,7},{7,1},{8,10},{10,12},{12... | collective-permute-start | bytes 1572872 | tf_op jit(solution)/shard_map/ppermute | solution.py:53
  198.4 15.7 %collective-permute-start.28 = (bf16[256,2048]{1,0:T(8,128)(2,1)S(1)}, bf16[256,2048]{1,0:T(8,128)(2,1)S(1)}, u32[]{:S(2)}, u32[]{:S(2)}) collective-permute-start(bf16[256,2048]{1,0:T(8,128)(2,1)S(1)} %constant_dynamic-update-slice_fusion.10.refs_4_), channel_id=1, source_target_pairs={{0,8},{8,0},{1,9},{9,1},{2,10},{10,2},{3,11},{11,3},{4,12},{12,4},... | collective-permute-start | bytes 3145736 | tf_op jit(solution)/shard_map/ppermute | solution.py:33
  198.4 25.7 %collective-permute-start.25 = (bf16[256,2048]{1,0:T(8,128)(2,1)S(1)}, bf16[256,2048]{1,0:T(8,128)(2,1)}, u32[]{:S(2)}, u32[]{:S(2)}) collective-permute-start(bf16[256,2048]{1,0:T(8,128)(2,1)S(1)} %constant_dynamic-update-slice_fusion.10.refs_4_), channel_id=1, source_target_pairs={{0,1},{1,0},{2,3},{3,2},{4,5},{5,4},{6,7},{7,6},{8,9},{9,8},{10,11... | collective-permute-start | bytes 3145736 | tf_op jit(solution)/shard_map/ppermute | solution.py:33
  199.0 25.1 %collective-permute-start.26 = (bf16[256,2048]{1,0:T(8,128)(2,1)}, bf16[256,2048]{1,0:T(8,128)(2,1)}, u32[]{:S(2)}, u32[]{:S(2)}) collective-permute-start(bf16[256,2048]{1,0:T(8,128)(2,1)} %constant_dynamic-update-slice_fusion.8.refs_0_), channel_id=1, source_target_pairs={{0,8},{8,0},{1,9},{9,1},{2,10},{10,2},{3,11},{11,3},{4,12},{12,4},... | collective-permute-start | bytes 3145736 | tf_op jit(solution)/shard_map/ppermute | solution.py:33
  199.9 24.3 %collective-permute-start.27 = (bf16[256,2048]{1,0:T(8,128)(2,1)S(1)}, bf16[256,2048]{1,0:T(8,128)(2,1)}, u32[]{:S(2)}, u32[]{:S(2)}) collective-permute-start(bf16[256,2048]{1,0:T(8,128)(2,1)S(1)} %copy-done.38), channel_id=1, source_target_pairs={{0,8},{8,0},{1,9},{9,1},{2,10},{10,2},{3,11},{11,3},{4,12},{12,4},... | collective-permute-start | bytes 3145736 | tf_op jit(solution)/shard_map/ppermute | solution.py:33
  224.1 2.9 collective-permute-start.29
  227.0 17.3 %collective-permute-start.30 = (bf16[512,2048]{1,0:T(8,128)(2,1)}, bf16[512,2048]{1,0:T(8,128)(2,1)}, u32[]{:S(2)}, u32[]{:S(2)}) collective-permute-start(bf16[512,2048]{1,0:T(8,128)(2,1)} %get-tuple-element.305), channel_id=1, source_target_pairs={{0,8},{8,0},{1,9},{9,1},{2,10},{10,2},{3,11},{11,3},{4,12},{12,4},... | collective-permute-start | bytes 6291464 | tf_op jit(solution)/shard_map/ppermute | solution.py:33
  227.1 17.1 %collective-permute-start.31 = (bf16[512,2048]{1,0:T(8,128)(2,1)}, bf16[512,2048]{1,0:T(8,128)(2,1)}, u32[]{:S(2)}, u32[]{:S(2)}) collective-permute-start(bf16[512,2048]{1,0:T(8,128)(2,1)} %get-tuple-element.306), channel_id=1, source_target_pairs={{0,8},{8,0},{1,9},{9,1},{2,10},{10,2},{3,11},{11,3},{4,12},{12,4},... | collective-permute-start | bytes 6291464 | tf_op jit(solution)/shard_map/ppermute | solution.py:33
  228.0 16.3 %copy-start.5 = (bf16[512,2048]{1,0:T(8,128)(2,1)S(1)}, bf16[512,2048]{1,0:T(8,128)(2,1)}, u32[]{:S(2)}) copy-start(bf16[512,2048]{1,0:T(8,128)(2,1)} %get-tuple-element.310) | copy-start | bytes 6291460
  248.1 47.9 %collective-permute-start.32 = (bf16[512,2048]{1,0:T(8,128)(2,1)}, bf16[512,2048]{1,0:T(8,128)(2,1)S(1)}, u32[]{:S(2)}, u32[]{:S(2)}) collective-permute-start(bf16[512,2048]{1,0:T(8,128)(2,1)} %add_convert_fusion.1), channel_id=1, source_target_pairs={{0,1},{1,0},{2,3},{3,2},{4,5},{5,4},{6,7},{7,6},{8,9},{9,8},{10,11... | collective-permute-start | bytes 6291464 | tf_op jit(solution)/shard_map/ppermute | solution.py:33
  263.3 48.2 %collective-permute-start.33 = (bf16[1024,1024]{1,0:T(8,128)(2,1)}, bf16[1024,1024]{1,0:T(8,128)(2,1)}, u32[]{:S(2)}, u32[]{:S(2)}) collective-permute-start(bf16[1024,1024]{1,0:T(8,128)(2,1)} %get-tuple-element.326), channel_id=1, source_target_pairs={{0,16},{16,0},{1,17},{17,1},{2,18},{18,2},{3,19},{19,3},{4,20},{20... | collective-permute-start | bytes 6291464 | tf_op jit(solution)/shard_map/ppermute | solution.py:33
  298.2 13.5 %collective-permute-start.34 = (bf16[128,2048]{1,0:T(8,128)(2,1)S(1)}, bf16[128,2048]{1,0:T(8,128)(2,1)S(1)}, u32[]{:S(2)}, u32[]{:S(2)}) collective-permute-start(bf16[128,2048]{1,0:T(8,128)(2,1)S(1)} %convert_add_fusion.9), channel_id=1, source_target_pairs={{2,0},{4,2},{6,4},{0,6},{3,1},{5,3},{7,5},{1,7},{10,8},{12,10},{14... | collective-permute-start | bytes 1572872 | tf_op jit(solution)/shard_map/ppermute | solution.py:70
  315.7 52.8 %all-to-all-start.2 = ((bf16[16,64,1024]{2,1,0:T(8,128)(2,1)}), bf16[16,64,1024]{2,1,0:T(8,128)(2,1)S(1)}, u32[]{:S(2)}, u32[]{:S(2)}) async-start(bf16[16,64,1024]{2,1,0:T(8,128)(2,1)} %bitcast.26), calls=%async_computation.2 | async-start | bytes 4194304 | tf_op jit(solution)/shard_map/all_to_all | solution.py:758
  326.8 28.1 %collective-permute-start.35 = (bf16[1024,384]{1,0:T(8,128)(2,1)}, bf16[1024,384]{1,0:T(8,128)(2,1)S(1)}, u32[]{:S(2)}, u32[]{:S(2)}) collective-permute-start(bf16[1024,384]{1,0:T(8,128)(2,1)} %get-tuple-element.347), channel_id=1, source_target_pairs={{0,16},{16,0},{1,17},{17,1},{2,18},{18,2},{3,19},{19,3},{4,20},{20... | collective-permute-start | bytes 2359304 | tf_op jit(solution)/shard_map/ppermute | solution.py:33
  354.9 25.6 %copy-start.16 = (bf16[1024,384]{1,0:T(8,128)(2,1)}, bf16[1024,384]{1,0:T(8,128)(2,1)S(1)}, u32[]{:S(2)}) copy-start(bf16[1024,384]{1,0:T(8,128)(2,1)S(1)} %collective-permute-done.35) | copy-start | bytes 2359300
  368.5 4.5 collective-permute-start.36
  368.6 7.5 %collective-permute-start.37 = (bf16[512,2048]{1,0:T(8,128)(2,1)}, bf16[512,2048]{1,0:T(8,128)(2,1)}, u32[]{:S(2)}, u32[]{:S(2)}) collective-permute-start(bf16[512,2048]{1,0:T(8,128)(2,1)} %get-tuple-element.351), channel_id=1, source_target_pairs={{0,8},{8,0},{1,9},{9,1},{2,10},{10,2},{3,11},{11,3},{4,12},{12,4},... | collective-permute-start | bytes 6291464 | tf_op jit(solution)/shard_map/ppermute | solution.py:33
  380.5 25.5 %collective-permute-start.38 = (bf16[256,2048]{1,0:T(8,128)(2,1)}, bf16[256,2048]{1,0:T(8,128)(2,1)S(1)}, u32[]{:S(2)}, u32[]{:S(2)}) collective-permute-start(bf16[256,2048]{1,0:T(8,128)(2,1)} %get-tuple-element.358), channel_id=1, source_target_pairs={{0,1},{1,0},{2,3},{3,2},{4,5},{5,4},{6,7},{7,6},{8,9},{9,8},{10,11... | collective-permute-start | bytes 3145736 | tf_op jit(solution)/shard_map/ppermute | solution.py:33
  383.6 15.2 %collective-permute-start.40 = (bf16[128,2048]{1,0:T(8,128)(2,1)}, bf16[128,2048]{1,0:T(8,128)(2,1)S(1)}, u32[]{:S(2)}, u32[]{:S(2)}) collective-permute-start(bf16[128,2048]{1,0:T(8,128)(2,1)} %add_convert_fusion.5), channel_id=1, source_target_pairs={{2,0},{4,2},{6,4},{0,6},{3,1},{5,3},{7,5},{1,7},{10,8},{12,10},{14... | collective-permute-start | bytes 1572872 | tf_op jit(solution)/shard_map/ppermute | solution.py:70
  385.3 13.5 %collective-permute-start.39 = (f32[2,1,4,2,640]{4,3,2,0,1:T(2,128)S(1)}, f32[2,1,4,2,640]{4,3,2,0,1:T(2,128)S(1)}, u32[]{:S(2)}, u32[]{:S(2)}) collective-permute-start(f32[2,1,4,2,640]{4,3,2,0,1:T(2,128)S(1)} %get-tuple-element.361), channel_id=1, source_target_pairs={{0,8},{8,0},{1,9},{9,1},{2,10},{10,2},{3,11},{11,3},{4,12},{12,4},... | collective-permute-start | bytes 122888 | tf_op jit(solution)/shard_map/ppermute | solution.py:33
  390.3 23.1 %copy-start = (bf16[2,1,64,2048]{3,2,1,0:T(8,128)(2,1)S(1)}, bf16[2,1,64,2048]{3,2,1,0:T(8,128)(2,1)}, u32[]{:S(2)}) copy-start(bf16[2,1,64,2048]{3,2,1,0:T(8,128)(2,1)} %param.14) | copy-start | bytes 1572868
  408.3 39.1 %all-to-all-start.3 = ((bf16[16,64,384]{2,1,0:T(8,128)(2,1)}), bf16[16,64,384]{2,1,0:T(8,128)(2,1)S(1)}, u32[]{:S(2)}, u32[]{:S(2)}) async-start(bf16[16,64,384]{2,1,0:T(8,128)(2,1)} %bitcast.31), calls=%async_computation.3 | async-start | bytes 1572864 | tf_op jit(solution)/shard_map/all_to_all | solution.py:758
  413.6 33.9 %collective-permute-start.41 = (bf16[256,2048]{1,0:T(8,128)(2,1)}, bf16[256,2048]{1,0:T(8,128)(2,1)S(1)}, u32[]{:S(2)}, u32[]{:S(2)}) collective-permute-start(bf16[256,2048]{1,0:T(8,128)(2,1)} %get-tuple-element.372), channel_id=1, source_target_pairs={{0,1},{1,0},{2,3},{3,2},{4,5},{5,4},{6,7},{7,6},{8,9},{9,8},{10,11... | collective-permute-start | bytes 3145736 | tf_op jit(solution)/shard_map/ppermute | solution.py:33
  416.1 24.3 %collective-permute-start.42 = (bf16[128,2048]{1,0:T(8,128)(2,1)}, bf16[128,2048]{1,0:T(8,128)(2,1)S(1)}, u32[]{:S(2)}, u32[]{:S(2)}) collective-permute-start(bf16[128,2048]{1,0:T(8,128)(2,1)} %convert_add_fusion.8), channel_id=1, source_target_pairs={{2,0},{4,2},{6,4},{0,6},{3,1},{5,3},{7,5},{1,7},{10,8},{12,10},{14... | collective-permute-start | bytes 1572872 | tf_op jit(solution)/shard_map/ppermute | solution.py:70
  421.1 53.7 %collective-permute-start.53 = (bf16[64,2048]{1,0:T(8,128)(2,1)}, bf16[64,2048]{1,0:T(8,128)(2,1)}, u32[]{:S(2)}, u32[]{:S(2)}) collective-permute-start(bf16[64,2048]{1,0:T(8,128)(2,1)} %fusion.25), channel_id=1, source_target_pairs={{0,16},{16,0},{1,17},{17,1},{2,18},{18,2},{3,19},{19,3},{4,20},{20... | collective-permute-start | bytes 786440 | tf_op jit(solution)/shard_map/ppermute | solution.py:33
  422.6 7.0 %collective-permute-start.43 = (f32[1,4,2,640]{3,2,1,0:T(2,128)S(1)}, f32[1,4,2,640]{3,2,1,0:T(2,128)S(1)}, u32[]{:S(2)}, u32[]{:S(2)}) collective-permute-start(f32[1,4,2,640]{3,2,1,0:T(2,128)S(1)} %get-tuple-element.375), channel_id=1, source_target_pairs={{0,16},{16,0},{1,17},{17,1},{2,18},{18,2},{3,19},{19,3},{4,20},{20... | collective-permute-start | bytes 61448 | tf_op jit(solution)/shard_map/ppermute | solution.py:33
  450.6 9.2 %collective-permute-start.45 = (f32[1,4,640]{2,0,1:T(1,128)S(1)}, f32[1,4,640]{2,0,1:T(1,128)S(1)}, u32[]{:S(2)}, u32[]{:S(2)}) collective-permute-start(f32[1,4,640]{2,0,1:T(1,128)S(1)} %get-tuple-element.384), channel_id=1, source_target_pairs={{0,1},{1,0},{2,3},{3,2},{4,5},{5,4},{6,7},{7,6},{8,9},{9,8},{10,11... | collective-permute-start | bytes 30728 | tf_op jit(solution)/shard_map/ppermute | solution.py:33
  451.1 14.7 %collective-permute-start.44 = (bf16[128,2048]{1,0:T(8,128)(2,1)}, bf16[128,2048]{1,0:T(8,128)(2,1)}, u32[]{:S(2)}, u32[]{:S(2)}) collective-permute-start(bf16[128,2048]{1,0:T(8,128)(2,1)} %convert_add_fusion.6), channel_id=1, source_target_pairs={{2,0},{4,2},{6,4},{0,6},{3,1},{5,3},{7,5},{1,7},{10,8},{12,10},{14... | collective-permute-start | bytes 1572872 | tf_op jit(solution)/shard_map/ppermute | solution.py:70
  467.0 26.3 %collective-permute-start.46 = (bf16[128,2048]{1,0:T(8,128)(2,1)S(1)}, bf16[128,2048]{1,0:T(8,128)(2,1)S(1)}, u32[]{:S(2)}, u32[]{:S(2)}) collective-permute-start(bf16[128,2048]{1,0:T(8,128)(2,1)S(1)} %convert_add_fusion.3), channel_id=1, source_target_pairs={{2,0},{4,2},{6,4},{0,6},{3,1},{5,3},{7,5},{1,7},{10,8},{12,10},{14... | collective-permute-start | bytes 1572872 | tf_op jit(solution)/shard_map/ppermute | solution.py:70
  471.3 21.9 %collective-permute-start.47 = (bf16[128,2048]{1,0:T(8,128)(2,1)S(1)}, bf16[128,2048]{1,0:T(8,128)(2,1)S(1)}, u32[]{:S(2)}, u32[]{:S(2)}) collective-permute-start(bf16[128,2048]{1,0:T(8,128)(2,1)S(1)} %copy-done.22), channel_id=1, source_target_pairs={{2,0},{4,2},{6,4},{0,6},{3,1},{5,3},{7,5},{1,7},{10,8},{12,10},{14... | collective-permute-start | bytes 1572872 | tf_op jit(solution)/shard_map/ppermute | solution.py:70
  471.4 21.1 %collective-permute-start.50 = (f32[1,640]{1,0:T(1,128)S(1)}, f32[1,640]{1,0:T(1,128)S(1)}, u32[]{:S(2)}, u32[]{:S(2)}) collective-permute-start(f32[1,640]{1,0:T(1,128)S(1)} %get-tuple-element.480), channel_id=1, source_target_pairs={{0,6},{2,0},{4,2},{6,4},{1,7},{3,1},{5,3},{7,5},{8,14},{10,8},{12,... | collective-permute-start | bytes 7688 | tf_op jit(solution)/shard_map/ppermute | solution.py:961
  471.5 21.0 %collective-permute-start.49 = (f32[1,640]{1,0:T(1,128)S(1)}, f32[1,640]{1,0:T(1,128)S(1)}, u32[]{:S(2)}, u32[]{:S(2)}) collective-permute-start(f32[1,640]{1,0:T(1,128)S(1)} %get-tuple-element.481), channel_id=1, source_target_pairs={{0,4},{2,6},{4,0},{6,2},{1,5},{3,7},{5,1},{7,3},{8,12},{10,14},{12... | collective-permute-start | bytes 7688 | tf_op jit(solution)/shard_map/ppermute | solution.py:961
  474.8 18.4 %collective-permute-start.48 = (f32[1,640]{1,0:T(1,128)S(1)}, f32[1,640]{1,0:T(1,128)S(1)}, u32[]{:S(2)}, u32[]{:S(2)}) collective-permute-start(f32[1,640]{1,0:T(1,128)S(1)} %get-tuple-element.482), channel_id=1, source_target_pairs={{0,2},{2,4},{4,6},{6,0},{1,3},{3,5},{5,7},{7,1},{8,10},{10,12},{12... | collective-permute-start | bytes 7688 | tf_op jit(solution)/shard_map/ppermute | solution.py:961
  495.0 15.8 %copy-start.36 = (f32[64]{0:T(128)}, f32[64]{0:T(128)S(1)}, u32[]{:S(2)}) copy-start(f32[64]{0:T(128)S(1)} %get-tuple-element.515) | copy-start | bytes 772
  497.0 11.9 %collective-permute-start.51 = (bf16[64,2048]{1,0:T(8,128)(2,1)S(1)}, bf16[64,2048]{1,0:T(8,128)(2,1)S(1)}, u32[]{:S(2)}, u32[]{:S(2)}) collective-permute-start(bf16[64,2048]{1,0:T(8,128)(2,1)S(1)} %slice.287), channel_id=1, source_target_pairs={{0,16},{16,0},{1,17},{17,1},{2,18},{18,2},{3,19},{19,3},{4,20},{20... | collective-permute-start | bytes 786440 | tf_op jit(solution)/shard_map/ppermute | solution.py:33
  498.5 9.8 %collective-permute-start.52 = (bf16[64,2048]{1,0:T(8,128)(2,1)S(1)}, bf16[64,2048]{1,0:T(8,128)(2,1)S(1)}, u32[]{:S(2)}, u32[]{:S(2)}) collective-permute-start(bf16[64,2048]{1,0:T(8,128)(2,1)S(1)} %slice.286), channel_id=1, source_target_pairs={{0,16},{16,0},{1,17},{17,1},{2,18},{18,2},{3,19},{19,3},{4,20},{20... | collective-permute-start | bytes 786440 | tf_op jit(solution)/shard_map/ppermute | solution.py:33
  (38 other events, 272.4 us)

commit v4 on v3

--- a/solution.py
+++ b/solution.py
@@ -392,17 +392,16 @@
 
 
 def store_parts(parts, total_ref):
-    rows = total_ref.shape[0]
     for at in range(8):
         half, core, ky = at // 4, at // 2 % 2, at % 2
 
         @pl.when(pl.program_id(0) == at)
-        def _(ref=parts[2 - 2 * core + 1 - ky], half=half):
-            ref[half * rows : (half + 1) * rows] = total_ref[...]
+        def _(ref=parts[4 * (1 - core) + 2 * (1 - ky) + half]):
+            ref[...] = total_ref[...]
 
 
 def part_shapes(rows, width):
-    return [jax.ShapeDtypeStruct((2 * rows, width), BF)] * 4
+    return [jax.ShapeDtypeStruct((rows, width), BF)] * 8
 
 
 def out_kernel(plane_ref, attn_ref, units_ref, dense_ref, own_ref, other_ref, *refs):
@@ -480,7 +479,7 @@
     count = len(flatten(steps))
     pieces, refs = like(steps, refs[:count]), refs[count:]
     linear_ref, units_ref, own_ref, other_ref, mean_ref, scale_ref = refs[:6]
-    parts, (gain_ref, shift_ref, small_ref, x_ref, total_ref) = refs[6:10], refs[10:]
+    parts, (gain_ref, shift_ref, small_ref, x_ref, total_ref) = refs[6:14], refs[14:]
     take_rows(x_ref, pieces, 0)
     linear, units = linear_ref[...], units_ref[...]
 
@@ -538,7 +537,8 @@
             begin = 0
             for left, right in zip(pairs[::2], pairs[1::2]):
                 end = begin + right.shape[1]
-                out_ref[:, begin:end] = dot_cols(left[...], right[...]).astype(BF)
+                value = dot_cols(left[...], right[...]).astype(BF)
+                out_ref[:, 0, :, begin:end] = value.reshape(out_ref.shape[0], out_ref.shape[2], end - begin)
                 begin = end
 
 
@@ -546,10 +546,15 @@
     return pl.BlockSpec((rows, quarter), lambda i, p: (0, ((p[0] + 1 - i // 2) % 2) * 2 + i % 2))
 
 
+def weight_shape(quarter, cols):
+    return jax.ShapeDtypeStruct((Z_LEN, 2, quarter // Z_LEN, cols), BF)
+
+
 def weight_outs(quarter, cols):
+    shape = (Z_LEN, 1, quarter // Z_LEN, cols)
     return [
-        pl.BlockSpec((quarter, cols), lambda i, p: (jnp.minimum(i, 1), 0)),
-        pl.BlockSpec((quarter, cols), lambda i, p: (jnp.maximum(i - 2, 0), 0)),
+        pl.BlockSpec(shape, lambda i, p: (0, jnp.minimum(i, 1), 0, 0)),
+        pl.BlockSpec(shape, lambda i, p: (0, jnp.maximum(i - 2, 0), 0, 0)),
     ]
 
 
@@ -557,7 +562,7 @@
     rows, width = pairs[0][0].shape
     cols = sum(right.shape[1] for _, right in pairs)
     quarter = width // 4
-    out = jax.ShapeDtypeStruct((2 * quarter, cols), BF)
+    out = weight_shape(quarter, cols)
     specs = [spec for _, right in pairs for spec in (weight_rows(rows, quarter), *fixed(right))]
     return pl.pallas_call(
         weight_kernel,
@@ -597,7 +602,7 @@
 def triple_grads(plane, h, dq, dkv, cosine, sine):
     rows, width = h.shape
     quarter = width // 4
-    out = jax.ShapeDtypeStruct((2 * quarter, 384), BF)
+    out = weight_shape(quarter, 384)
     linear = jax.ShapeDtypeStruct((rows, 384), BF)
     return pl.pallas_call(
         triple_grads_kernel,
@@ -638,39 +643,35 @@
     )(triple, expand, shrink)
 
 
-def unpack_triple_kernel(back_ref, triple_ref):
-    ranks = back_ref.shape[0]
+def from_rank(rank):
+    return rank // (2 * Z_LEN) * 2 + rank % 2, rank // 2 % Z_LEN
+
+
+def unpack_kernel(back_ref, shrink_ref, expand_ref, triple_ref):
+    ranks = back_ref.shape[0] * back_ref.shape[1]
+    wide = (back_ref.shape[3] - 384) // 2
+    for rank in range(ranks):
+        for out_ref, begin in ((shrink_ref, 0), (expand_ref, wide)):
+            value = back_ref[(*from_rank(rank), slice(None), slice(begin, begin + wide))]
+            out_ref[:, rank * wide : (rank + 1) * wide] = value.astype(F32)
     for rank in range(0, ranks, 2):
         for s in range(3):
             for x in range(2):
-                lanes = slice(s * 128 + x * HEAD_DIM, s * 128 + (x + 1) * HEAD_DIM)
-                pair = jnp.concatenate([back_ref[rank, :, lanes], back_ref[rank + 1, :, lanes]], 1)
+                begin = 2 * wide + s * 128 + x * HEAD_DIM
+                pair = jnp.concatenate(
+                    [back_ref[(*from_rank(one), slice(None), slice(begin, begin + HEAD_DIM))] for one in (rank, rank + 1)],
+                    1,
+                )
                 at = (s * HEADS + x * ranks + rank) * HEAD_DIM
                 triple_ref[:, at : at + 128] = pair.astype(F32)
 
 
-def unpack_triple(back):
-    held = back.shape[1]
+def unpack(back):
+    four, along, held, cols = back.shape
+    wide = jax.ShapeDtypeStruct((held, four * along * (cols - 384) // 2), F32)
     return pl.pallas_call(
-        unpack_triple_kernel,
-        out_shape=jax.ShapeDtypeStruct((held, 3 * HEADS * HEAD_DIM), F32),
-        compiler_params=pltpu.CompilerParams(vmem_limit_bytes=VMEM_LIMIT),
-    )(back)
-
-
-def unpack_units_kernel(back_ref, shrink_ref, expand_ref):
-    wide = back_ref.shape[2] // 2
-    for rank in range(back_ref.shape[0]):
-        shrink_ref[:, rank * wide : (rank + 1) * wide] = back_ref[rank, :, :wide].astype(F32)
-        expand_ref[:, rank * wide : (rank + 1) * wide] = back_ref[rank, :, wide:].astype(F32)
-
-
-def unpack_units(back):
-    ranks, held, cols = back.shape
-    out = jax.ShapeDtypeStruct((held, ranks * cols // 2), F32)
-    return pl.pallas_call(
-        unpack_units_kernel,
-        out_shape=[out, out],
+        unpack_kernel,
+        out_shape=[wide, wide, jax.ShapeDtypeStruct((held, 3 * HEADS * HEAD_DIM), F32)],
         compiler_params=pltpu.CompilerParams(vmem_limit_bytes=VMEM_LIMIT),
     )(back)
 
@@ -750,24 +751,37 @@
             got = lax.all_gather(got.reshape(2, 1, near_blocks, held, cols), "bs", axis=1, tiled=True)
         return got.reshape(width // 2, cols)
 
-    def to_rows(mine):
+    def to_rows_z(mine):
         cols = mine.shape[-1]
-        if spread > 1:
-            mine = mine.reshape(2, spread, near_blocks, held, cols)
-            mine = lax.psum_scatter(mine, "bs", scatter_dimension=1, tiled=True)
-        return lax.all_to_all(mine.reshape(ranks, held, cols), RANK, split_axis=0, concat_axis=0, tiled=True)
+        got = lax.all_to_all(mine, "bz", split_axis=0, concat_axis=0, tiled=True)
+        return got.reshape(Z_LEN, 2, 2, held, cols)
+
+    def over_bs(mine):
+        if spread == 1:
+            return mine
+        cols = mine.shape[-1]
+        mine = mine.transpose(1, 0, 2, 3).reshape(2, spread, Z_LEN, 2 * held, cols)
+        mine = lax.psum_scatter(mine, "bs", scatter_dimension=1, tiled=True)
+        return mine.reshape(2, Z_LEN, 2 * held, cols).transpose(1, 0, 2, 3)
+
+    def to_send(got):
+        return got.transpose(1, 2, 0, 3, 4).reshape(4, Z_LEN, held, got.shape[-1])
+
+    def to_rows_y(got):
+        return lax.all_to_all(got, ("core", "by"), split_axis=0, concat_axis=0, tiled=True)
 
     def both(low, high):
         return jnp.concatenate([low, high], 0)
 
     x_a = lax.dynamic_index_in_dim(inputs[:, 0], hx, 0, keepdims=False)
-    x_b = swap(lax.dynamic_index_in_dim(inputs[:, 0], 1 - hx, 0, keepdims=False), "hx")
+    x_b = lax.dynamic_index_in_dim(inputs[:, 0], 1 - hx, 0, keepdims=False)
     vectors = (norm_gain, norm_bias, triple_bias, expand_bias, dense_bias, shrink_bias)
     sent_in, sent_out = pack(triple_weight, expand_weight, shrink_weight, ranks)
+
+    sent_in, sent_out, vectors, cotangent, x_b = fence((sent_in, sent_out, vectors, cotangent, x_b))
+    in_own = to_cols(sent_in)
+    x_b = swap(x_b, "hx")
     small = jnp.concatenate(vectors)[None]
-
-    x_b, small, cotangent, sent_in, sent_out = fence((x_b, small, cotangent, sent_in, sent_out))
-    in_own = to_cols(sent_in)
     x_0 = both(x_a, x_b)
     grad_y = (cotangent[:, 0].astype(F32) * valid).astype(BF)
     g_a = lax.dynamic_index_in_dim(grad_y, hx, 0, keepdims=False)
@@ -860,11 +874,11 @@
     g_pieces = tuple((piece,) for piece in g_one + c_one + (own_two, y_two) + c_two)
 
     out_parts, g_pieces = fence((out_parts, g_pieces))
-    got_far, got_near = swap(out_parts[0], "core"), swap(out_parts[1], "core")
+    got = [swap(part, "core") for part in out_parts[:4]]
     grad_attention, grad_pre, g_all = branch_grads(hx, g_pieces, *onto, pre, block)
 
-    grad_attention, grad_pre, g_all, got_far, got_near = fence((grad_attention, grad_pre, g_all, got_far, got_near))
-    far = add_low(out_parts[2], got_far)
+    grad_attention, grad_pre, g_all, got = fence((grad_attention, grad_pre, g_all, got))
+    far = add_low(both(*out_parts[4:6]), both(*got[:2]))
 
     grad_attention, grad_pre, g_all, far = fence((grad_attention, grad_pre, g_all, far))
     out_y = swap(far, "by")
@@ -876,12 +890,16 @@
     if spread > 1:
         dkv = lax.psum_scatter(dkv, "bs", scatter_dimension=0, tiled=True)
 
-    def three(at, near_part, got, y_part):
-        rows = slice(at * 2 * share, (at + 1) * 2 * share)
-        return near_part[rows].astype(F32) + got[rows].astype(F32) + y_part[rows].astype(F32)
-
-    dq, out_y, stay_near, got_near = fence((dq, out_y, out_parts[3], got_near))
-    out_sum = three(3, stay_near, got_near, out_y)
+    def three(k, near_part, got_part, y_part):
+        rows = slice(k * 2 * share, (k + 1) * 2 * share)
+        return near_part[rows].astype(F32) + got_part[rows].astype(F32) + y_part[rows].astype(F32)
+
+    def out_three(kz):
+        half = kz // 2
+        return three(kz % 2, out_parts[6 + half], got[2 + half], out_y[half * block : (half + 1) * block])
+
+    dq, out_y, out_parts, got = fence((dq, out_y, out_parts, got))
+    out_sum = out_three(3)
 
     dq, out_sum = fence((dq, out_sum))
     ringed = ring_back(out_sum)
@@ -891,9 +909,15 @@
     mine = add_low(units_mine, units_away)
 
     mine, triple_away, grad_linear = fence((mine, triple_away, grad_linear))
-    units_rows = to_rows(mine)
+    units_rows = to_rows_z(over_bs(mine))
     triple_away = swap(triple_away, "hx")
     h_parts, sums = back_partial(hx, x_one + x_two, grad_linear, grad_pre, in_own, in_other, mean, scale)
+
+    h_parts, sums, triple_away, ringed, g_all = fence((h_parts, sums, triple_away, ringed, g_all))
+    h_got = [swap(part, "core") for part in h_parts[:4]]
+    mine = add_low(triple_mine, triple_away)
+    grad_dense_here = dot_cols(g_all, attn_low)
+    out_sum = out_three(2) + ringed
 
     sum_gain, sum_shift, sum_in = sums
     here = jnp.arange(ranks, dtype=jnp.int32)[:, None] == rank
@@ -908,61 +932,57 @@
     pieces = [leaf.reshape(devices, -1) for leaf in (sum_gain, sum_shift, sum_triple, sum_expand, sum_y)]
     small = jnp.concatenate(pieces, 1).reshape(2, 2, spread, Z_LEN, 2, -1)
 
-    grad_dense_here = dot_cols(g_all, attn_low)
-
-    h_parts, small, units_rows, triple_away, ringed = fence(
-        (h_parts, small, units_rows, triple_away, ringed), grad_dense_here
-    )
-    h_got_far, h_got_near = swap(h_parts[0], "core"), swap(h_parts[1], "core")
+
+    h_got, units_rows, out_sum, small, mine = fence((h_got, units_rows, out_sum, small, mine), grad_dense_here)
+    far_one, far_two = add_low(h_parts[4], h_got[0]), add_low(h_parts[5], h_got[1])
+
+    far_one, far_two, out_sum, small, mine = fence((far_one, far_two, out_sum, small, mine))
+    h_y_two = swap(far_two, "by")
+    triple_rows = to_rows_z(over_bs(mine))
+    ringed = ring_back(out_sum)
     small, away = halved(small, "core", 1)
 
-    h_got_far, h_got_near, small, away = fence((h_got_far, h_got_near, small, away))
-    one, two = slice(0, block), slice(block, 2 * block)
-    far_two, far_one = add_low(h_parts[2][two], h_got_far[two]), add_low(h_parts[2][one], h_got_far[one])
-
-    far_one, far_two, small, away = fence((far_one, far_two, small, away))
-    h_y_two = swap(far_two, "by")
+    h_y_two, far_one, small, away, ringed, triple_rows = fence((h_y_two, far_one, small, away, ringed, triple_rows))
+    h_sum = three(1, h_parts[7], h_got[3], h_y_two)
+    out_sum = out_three(1) + ringed
+
+    h_sum, far_one, small, away, out_sum = fence((h_sum, far_one, small, away, out_sum))
+    h_y_one = swap(far_one, "by")
+    ringed, out_ringed = ring_back(h_sum), ring_back(out_sum)
     away = swap(away, "core")
-    mine = add_low(triple_mine, triple_away)
-    out_ringed = ring_back(three(2, stay_near, got_near, out_y) + ringed)
-    grad_shrink, grad_expand = unpack_units(units_rows)
-
-    h_y_two, far_one, small, away, mine, out_ringed = fence(
-        (h_y_two, far_one, small, away, mine, out_ringed), grad_shrink
-    )
-    h_sum = three(1, h_parts[3][two], h_got_near[two], h_y_two)
+    all_rows = jnp.concatenate([to_send(units_rows), to_send(triple_rows)], 3)
+
+    h_y_one, ringed, out_ringed, small, away, all_rows = fence((h_y_one, ringed, out_ringed, small, away, all_rows))
+    h_sum = three(0, h_parts[7], h_got[3], h_y_two) + ringed
+    out_sum = (out_three(0) + out_ringed).reshape(2, share, width)
+    out_away = out_sum[1].astype(BF)
     small, away = halved(small + away, "hx", 0)
 
-    h_sum, far_one, small, away, mine = fence((h_sum, far_one, small, away, mine))
-    h_y_one = swap(far_one, "by")
+    h_sum, out_sum, out_away, small, away, all_rows = fence((h_sum, out_sum, out_away, small, away, all_rows))
     ringed = ring_back(h_sum)
-    triple_rows = to_rows(mine)
+    all_rows = to_rows_y(all_rows)
+    out_away = swap(out_away, "hx")
     away = swap(away, "hx")
-    out_sum = three(1, stay_near, got_near, out_y) + out_ringed
-
-    h_y_one, ringed, small, away, out_sum, triple_rows = fence((h_y_one, ringed, small, away, out_sum, triple_rows))
-    h_sum = three(0, h_parts[3][two], h_got_near[two], h_y_two) + ringed
+    h_last = [three(at, h_parts[6], h_got[2], h_y_one) for at in (0, 1)]
+
+    ringed, out_away, small, away, h_last = fence((ringed, out_away, small, away, h_last))
+    h_sum = h_last[1] + ringed
     small, away = halved(small + away, "by", 2)
 
-    h_sum, small, away, out_sum = fence((h_sum, small, away, out_sum))
+    h_sum, small, away = fence((h_sum, small, away))
     ringed = ring_back(h_sum)
-    away = swap(away, "by")
-    h_last = [three(at, h_parts[3][one], h_got_near[one], h_y_one) for at in (0, 1)]
-    grad_triple = unpack_triple(triple_rows)
-
-    ringed, small, away, h_last, out_sum = fence((ringed, small, away, h_last, out_sum), grad_triple)
-    h_sum = h_last[1] + ringed
-    small = small + away
-
-    h_sum, small, out_sum = fence((h_sum, small, out_sum))
-    ringed = ring_back(h_sum)
-    out_ringed = ring_back(out_sum)
+    small = small + swap(away, "by")
     terms = [lax.dynamic_index_in_dim(small, (bz + kz) % Z_LEN, 1, keepdims=False) for kz in range(Z_LEN)]
     terms = terms[:1] + [lax.ppermute(terms[kz], "bz", around(kz)) for kz in range(1, Z_LEN)]
 
-    ringed, out_ringed, terms = fence((ringed, out_ringed, terms))
+    source = inputs[:, 0].astype(F32)
+    out_away = out_away.astype(F32)
+    mixed = jnp.where(hx == 0, jnp.stack([out_sum[0], out_away]), jnp.stack([out_away, out_sum[0]]))
+    output = (valid * (source + mixed + dense_b + shrink_b)).astype(BF).reshape(inputs.shape)
+
+    ringed, terms, output, all_rows = fence((ringed, terms, output, all_rows))
+    grad_shrink, grad_expand, grad_triple = unpack(all_rows)
     h_sum = (h_last[0] + ringed).reshape(2, share, width)
-    out_sum = (three(0, stay_near, got_near, out_y) + out_ringed).reshape(2, share, width)
 
     dense_grads = grad_dense_here.T.reshape(2, HEAD_DIM, width)
     if spread == 1:
@@ -984,11 +1004,6 @@
         small_grads.append(small[begin : begin + piece.shape[1]])
         begin += piece.shape[1]
     small_gain, small_shift, small_triple, small_expand, small_out = small_grads
-
-    source = inputs[:, 0].astype(F32)
-    out_away = swap(out_sum[1].astype(BF), "hx").astype(F32)
-    mixed = jnp.where(hx == 0, jnp.stack([out_sum[0], out_away]), jnp.stack([out_away, out_sum[0]]))
-    output = (valid * (source + mixed + dense_b + shrink_b)).astype(BF).reshape(inputs.shape)
 
     h_away = swap(h_sum[1].astype(BF), "hx").astype(F32)
     grad_h = jnp.where(hx == 0, jnp.stack([h_sum[0], h_away]), jnp.stack([h_away, h_sum[0]]))

time: 521 us -> 504 us (0.967)
  waiting for transfers between devices: 184 us -> 168 us
  Pallas kernels: 159 us -> 146 us
  starting transfers between devices: 73.7 us -> 82.7 us
    ppermute x37 -> x41, waiting for transfers between devices: 62.4 us -> 42.1 us  [swap(): return lax.ppermute(value, axis, SWAP)]
    ppermute x6, waiting for transfers between devices: 25.6 us -> 41.4 us  [ring_back(): return lax.ppermute(total.astype(BF), 'bz', DOWN)]
    ppermute x3, waiting for transfers between devices: 16.6 us -> 5.15 us  [body(): lax.ppermute(terms[kz], 'bz', around(kz))]
    all_to_all x2 -> x3, waiting for transfers between devices: 13.6 us -> 7.79 us  [the longest x2 7.79 us: to_rows_z(): got = lax.all_to_all(mine, 'bz', split_axis=0, concat_axis=0, tiled=True)]
    pallas_call x1, Pallas kernels: 23.5 us -> 17.9 us  [attend_back(): pl.pallas_call(functools.partial(attend_back_kernel, blocks, block), grid...]
    ppermute x37 -> x41, starting transfers between devices: 25.4 us -> 27.3 us  [swap(): return lax.ppermute(value, axis, SWAP)]
    convert_element_type x4 -> x5, other arithmetic: 13.4 us -> 15.2 us  [add_low(): return (left.astype(F32) + right.astype(F32)).astype(BF)]
    all_to_all x2 -> x3, starting transfers between devices: 10.3 us -> 11.6 us  [the longest x2 7.93 us: to_rows_z(): got = lax.all_to_all(mine, 'bz', split_axis=0, concat_axis=0, tiled=True)]
  transfers between devices with their start and end apart: 58 -> 63, of which waited for: 26 -> 23; matrix products, arithmetic and copies ran while one was open for 12% -> 12% of each run, Pallas kernels for 31% -> 29%
where the time goes in v4:
time: 504 us; the launch traced here: 494 us
  waiting for transfers between devices  168 us (33%)
  Pallas kernels  146 us (29%)
  starting transfers between devices  82.7 us (16%)
  other arithmetic  52.3 us (10%)
  local copies, waits for them, and re-layouts  36 us (7%)
  matrix products  5.71 us (1%)
    ppermute x41, waiting for transfers between devices, swap(): return lax.ppermute(value, axis, SWAP)  42.1 us
    ppermute x6, waiting for transfers between devices, ring_back(): return lax.ppermute(total.astype(BF), 'bz', DOWN)  41.4 us
    all_to_all x2, waiting for transfers between devices, to_cols(): got = lax.all_to_all(sent, RANK, split_axis=0, concat_axis=0, tiled=True)  34.4 us
    pallas_call x2, Pallas kernels, front(): pl.pallas_call(functools.partial(front_kernel, pieces), grid_spec=pltpu.P...  28.4 us
    ppermute x41, starting transfers between devices, swap(): return lax.ppermute(value, axis, SWAP)  27.3 us
    pallas_call x1, Pallas kernels, back_partial(): pl.pallas_call(functools.partial(back_kernel, pieces), grid_spec=pltpu.Pr...  21.3 us
    ppermute x5, waiting for transfers between devices, ring(): return lax.ppermute(value, 'bz', UP)  19.5 us
    ppermute x6, starting transfers between devices, ring_back(): return lax.ppermute(total.astype(BF), 'bz', DOWN)  19 us
  transfers between devices with their start and end apart: 63, of which 23 were waited for; matrix products, arithmetic and copies ran while one was open for 12% of the time, Pallas kernels for 29%

profile of v4, /device:TPU:0, one launch (start us, length us, event | category | flops | bytes accessed | tf_op | source)
XLA Modules:
  0.0 494.0 jit_solution(16062751745369537405)
XLA Ops:
  0.6 1.8 dynamic-slice_bitcast_fusion.3
  2.4 3.7 shard_map.229
  6.2 7.5 %all-to-all-start = ((bf16[16,64,896]{2,1,0:T(8,128)(2,1)}), bf16[16,64,896]{2,1,0:T(8,128)(2,1)S(1)}, u32[]{:S(2)}, u32[]{:S(2)}) async-start(bf16[16,64,896]{2,1,0:T(8,128)(2,1)} %get-tuple-element.251), calls=%async_computation | async-start | bytes 3670016 | tf_op jit(solution)/shard_map/all_to_all | solution.py:749
  13.9 2.0 collective-permute-start.2
  25.4 1.6 collective-permute-start.4
  27.0 1.8 pad_maximum_fusion.1
  29.9 26.1 %all-to-all-done = bf16[16,64,896]{2,1,0:T(8,128)(2,1)S(1)} async-done(((bf16[16,64,896]{2,1,0:T(8,128)(2,1)}), bf16[16,64,896]{2,1,0:T(8,128)(2,1)S(1)}, u32[]{:S(2)}, u32[]{:S(2)}) %all-to-all-start) | async-done | bytes 1835040 | tf_op jit(solution)/shard_map/all_to_all | solution.py:749
  56.1 1.6 tile.8
  58.8 2.5 collective-permute-start.6
  66.7 7.1 %collective-permute-done.7 = bf16[8,704]{1,0:T(8,128)(2,1)S(1)} collective-permute-done((bf16[8,704]{1,0:T(8,128)(2,1)S(1)}, bf16[8,704]{1,0:T(8,128)(2,1)S(1)}, u32[]{:S(2)}, u32[]{:S(2)}) %collective-permute-start.7) | collective-permute-done | bytes 11296 | tf_op jit(solution)/shard_map/ppermute | solution.py:78
  75.3 1.6 collective-permute-start.8
  78.9 10.8 %collective-permute-done.10 = bf16[16,704]{1,0:T(8,128)(2,1)S(1)} collective-permute-done((bf16[16,704]{1,0:T(8,128)(2,1)S(1)}, bf16[16,704]{1,0:T(8,128)(2,1)S(1)}, u32[]{:S(2)}, u32[]{:S(2)}) %collective-permute-start.10) | collective-permute-done | bytes 22560 | tf_op jit(solution)/shard_map/ppermute | solution.py:78
  93.7 1.9 constant_dynamic-update-slice_fusion.5
  95.6 10.1 %collective-permute-done.12 = bf16[128,2048]{1,0:T(8,128)(2,1)} collective-permute-done((bf16[128,2048]{1,0:T(8,128)(2,1)}, bf16[128,2048]{1,0:T(8,128)(2,1)}, u32[]{:S(2)}, u32[]{:S(2)}) %collective-permute-start.12) | collective-permute-done | bytes 524320 | tf_op jit(solution)/shard_map/ppermute | solution.py:53
  105.7 1.9 constant_dynamic-update-slice_fusion.4.refs_0_.refs_4_
  109.0 2.6 copy.84.refs_10_.sin_ref
  114.2 14.2 %shard_map.230 = (bf16[2048,2048]{1,0:T(8,128)(2,1)}, bf16[2048,128]{1,0:T(8,128)(2,1)}, bf16[2048,256]{1,0:T(8,128)(2,1)}, f32[2048,512]{1,0:T(8,128)}, bf16[20...) custom-call(s32[1]{0:T(128)} %bitcast.plane_ref, ...), custom_call_target="tpu_custom_call" | custom-call | flops 3783262208 | bytes 12582912 | tf_op jit(solution)/shard_map/pallas_call | solution.py:171
  128.4 6.3 %all-to-all-start.1 = ((bf16[16,64,512]{2,1,0:T(8,128)(2,1)}), bf16[16,64,512]{2,1,0:T(8,128)(2,1)}, u32[]{:S(2)}, u32[]{:S(2)}) async-start(bf16[16,64,512]{2,1,0:T(8,128)(2,1)} %get-tuple-element.309), calls=%async_computation.1 | async-start | bytes 2097152 | tf_op jit(solution)/shard_map/all_to_all | solution.py:749
  138.7 14.2 %shard_map.231 = (bf16[2048,2048]{1,0:T(8,128)(2,1)}, bf16[2048,128]{1,0:T(8,128)(2,1)}, bf16[2048,256]{1,0:T(8,128)(2,1)}, f32[2048,512]{1,0:T(8,128)}, bf16[20...) custom-call(s32[1]{0:T(128)} %bitcast.plane_ref, ...), custom_call_target="tpu_custom_call", output_to_operand_aliasing={{0}: (12, {}), {1}: (13, {}), {2}: (14, {}), {3}: (15, {}),... | custom-call | flops 3783262208 | bytes 12582912 | tf_op jit(solution)/shard_map/pallas_call | solution.py:171
  152.9 8.3 %all-to-all-done.1 = bf16[16,64,512]{2,1,0:T(8,128)(2,1)} async-done(((bf16[16,64,512]{2,1,0:T(8,128)(2,1)}), bf16[16,64,512]{2,1,0:T(8,128)(2,1)}, u32[]{:S(2)}, u32[]{:S(2)}) %all-to-all-start.1) | async-done | bytes 1048608 | tf_op jit(solution)/shard_map/all_to_all | solution.py:749
  166.5 14.0 %shard_map.232 = (f32[2,2,2,2,128,128]{5,4,3,2,1,0:T(8,128)}, bf16[2,2,2,2,128,128]{5,4,3,2,1,0:T(8,128)(2,1)}, f32[8,8,512]{2,1,0:T(8,128)}) custom-call(s32[2]{0:T(128)} %compare_select_fusion.4.meta_ref, s32[8]{0:T(128)} %copy-done.51, s32[8]{0:T(128)} %select_reduce_fusion.order_ref, bf16[2,2,2,2,128,128]{5,4,3,2,1,0:T(8,128)(2,1)} %bitcast.146, ...), custom_call_target="tpu_custom_call" | custom-call | flops 8589934592 | bytes 4194304 | tf_op jit(solution)/shard_map/pallas_call | solution.py:298
  180.5 9.4 %collective-permute-done.21 = bf16[128,2048]{1,0:T(8,128)(2,1)S(1)} collective-permute-done((bf16[128,2048]{1,0:T(8,128)(2,1)S(1)}, bf16[128,2048]{1,0:T(8,128)(2,1)S(1)}, u32[]{:S(2)}, u32[]{:S(2)}) %collective-permute-start.21) | collective-permute-done | bytes 524320 | tf_op jit(solution)/shard_map/ppermute | solution.py:53
  191.2 14.3 %shard_map.233 = (bf16[256,2048]{1,0:T(8,128)(2,1)}, bf16[256,2048]{1,0:T(8,128)(2,1)}, bf16[256,2048]{1,0:T(8,128)(2,1)}, bf16[256,2048]{1,0:T(8,128)(2,1)}, bf...) custom-call(s32[1]{0:T(128)} %bitcast.plane_ref, ...), custom_call_target="tpu_custom_call" | custom-call | flops 5368709120 | bytes 8388608 | tf_op jit(solution)/shard_map/pallas_call | solution.py:419
  205.5 10.3 %collective-permute-done.25.refs_5_ = bf16[256,2048]{1,0:T(8,128)(2,1)} collective-permute-done((bf16[256,2048]{1,0:T(8,128)(2,1)S(1)}, bf16[256,2048]{1,0:T(8,128)(2,1)}, u32[]{:S(2)}, u32[]{:S(2)}) %collective-permute-start.25) | collective-permute-done | bytes 1048608 | tf_op jit(solution)/shard_map/ppermute | solution.py:33
  215.8 2.9 collective-permute-done.29.refs_7_
  220.1 16.1 %shard_map.234 = (bf16[2048,128]{1,0:T(8,128)(2,1)}, bf16[2048,512]{1,0:T(8,128)(2,1)}, bf16[2048,2048]{1,0:T(8,128)(2,1)}) custom-call(s32[1]{0:T(128)} %bitcast.plane_ref, bf16[256,2048]{1,0:T(8,128)(2,1)} %copy-done.31, bf16[256,2048]{1,0:T(8,128)(2,1)} %collective-permute-done.20.refs_1_, bf16[256,2048]{1,0:T(8,128)(2,1)} %collective-permute-done.26.refs_2_, ...), custom_call_target="tpu_custom_call" | custom-call | flops 5368709120 | bytes 16777216 | tf_op jit(solution)/shard_map/pallas_call | solution.py:454
  237.6 2.9 add_convert_fusion.1
  241.1 14.6 %shard_map.235 = (bf16[4,2,128,1024]{3,2,1,0:T(8,128)(2,1)}, bf16[4,2,128,1024]{3,2,1,0:T(8,128)(2,1)}) custom-call(s32[1]{0:T(128)} %bitcast.plane_ref, bf16[2048,2048]{1,0:T(8,128)(2,1)} %get-tuple-element.423.refs_0_, bf16[2048,512]{1,0:T(8,128)(2,1)} %get-tuple-element.321.units_ref.refs_1_, bf16[2048,2048]{1,0:T(8,128)(2,1)} %get-tuple-element.368.refs_2_.h_ref, ...), custom_call_target="tpu_custom_call" | custom-call | flops 8589934592 | bytes 8388608 | tf_op jit(solution)/shard_map/pallas_call | solution.py:567
  256.3 17.9 %shard_map.236 = (bf16[2,2,2,2,128,128]{5,4,3,2,1,0:T(8,128)(2,1)}, bf16[2,2,2,2,128,256]{5,4,3,2,1,0:T(8,128)(2,1)}) custom-call(s32[2]{0:T(128)} %compare_select_fusion.4.meta_ref, s32[8]{0:T(128)} %copy-done.51, s32[8]{0:T(128)} %select_reduce_fusion.order_ref, bf16[2,2,2,2,128,128]{5,4,3,2,1,0:T(8,128)(2,1)} %bitcast.147, ...), custom_call_target="tpu_custom_call" | custom-call | flops 21474836480 | bytes 6291456 | tf_op jit(solution)/shard_map/pallas_call | solution.py:370
  274.2 14.2 %collective-permute-done.35 = bf16[512,2048]{1,0:T(8,128)(2,1)} collective-permute-done((bf16[512,2048]{1,0:T(8,128)(2,1)S(1)}, bf16[512,2048]{1,0:T(8,128)(2,1)}, u32[]{:S(2)}, u32[]{:S(2)}) %collective-permute-start.35) | collective-permute-done | bytes 2097184 | tf_op jit(solution)/shard_map/ppermute | solution.py:33
  289.8 1.8 collective-permute-start.36
  291.6 11.2 %shard_map.237 = (bf16[4,2,128,384]{3,2,1,0:T(8,128)(2,1)}, bf16[4,2,128,384]{3,2,1,0:T(8,128)(2,1)}, bf16[2048,384]{1,0:T(8,128)(2,1)}) custom-call(s32[1]{0:T(128)} %bitcast.plane_ref, bf16[2048,2048]{1,0:T(8,128)(2,1)} %get-tuple-element.368.refs_2_.h_ref, bf16[2048,128]{1,0:T(8,128)(2,1)} %bitcast.148, bf16[2048,256]{1,0:T(8,128)(2,1)} %bitcast.143, ...), custom_call_target="tpu_custom_call" | custom-call | flops 3221225472 | bytes 8388608 | tf_op jit(solution)/shard_map/pallas_call | solution.py:607
  303.5 4.1 add_convert_fusion
  307.7 4.4 all-to-all-start.2
  312.8 21.3 %shard_map.238 = (bf16[256,2048]{1,0:T(8,128)(2,1)}, bf16[256,2048]{1,0:T(8,128)(2,1)}, bf16[256,2048]{1,0:T(8,128)(2,1)}, bf16[256,2048]{1,0:T(8,128)(2,1)}, bf...) custom-call(s32[1]{0:T(128)} %bitcast.plane_ref, ...), custom_call_target="tpu_custom_call" | custom-call | flops 7516192768 | bytes 16777216 | tf_op jit(solution)/shard_map/pallas_call | solution.py:510
  340.6 2.6 add_convert_fusion.4
  343.2 2.3 convert_add_fusion.9
  345.5 5.7 %fusion.37 = f32[2048,128]{0,1:T(8,128)} fusion(bf16[2048,2048]{1,0:T(8,128)(2,1)} %get-tuple-element.423.refs_0_, bf16[2048,128]{1,0:T(8,128)(2,1)S(1)} %bitcast.160), kind=kOutput, calls=%fused_computation.159 | convolution fusion | flops 1073741824 | bytes 9961472 | tf_op jit(solution)/shard_map/dot_general | solution.py:41
  351.2 7.8 %all-to-all-done.2 = bf16[4,2,128,1024]{3,2,1,0:T(8,128)(2,1)S(1)} async-done(((bf16[4,2,128,1024]{3,2,1,0:T(8,128)(2,1)}), bf16[4,2,128,1024]{3,2,1,0:T(8,128)(2,1)S(1)}, u32[]{:S(2)}, u32[]{:S(2)}) %all-to-all-start.2) | async-done | bytes 2097184 | tf_op jit(solution)/shard_map/all_to_all | solution.py:756
  359.0 3.0 add_convert_fusion.3
  362.0 2.6 add_convert_fusion.2
  364.6 3.5 all-to-all-start.3
  368.1 1.5 collective-permute-start.42
  369.7 4.0 collective-permute-start.43
  373.6 1.8 fusion.24
  376.5 17.2 %collective-permute-done.43 = bf16[128,2048]{1,0:T(8,128)(2,1)S(1)} collective-permute-done((bf16[128,2048]{1,0:T(8,128)(2,1)}, bf16[128,2048]{1,0:T(8,128)(2,1)S(1)}, u32[]{:S(2)}, u32[]{:S(2)}) %collective-permute-start.43) | collective-permute-done | bytes 524320 | tf_op jit(solution)/shard_map/ppermute | solution.py:70
  394.6 1.9 convert_add_fusion.7
  396.5 2.2 convert_add_fusion.8
  400.4 5.9 %collective-permute-start.45 = (bf16[128,2048]{1,0:T(8,128)(2,1)}, bf16[128,2048]{1,0:T(8,128)(2,1)S(1)}, u32[]{:S(2)}, u32[]{:S(2)}) collective-permute-start(bf16[128,2048]{1,0:T(8,128)(2,1)} %convert_add_fusion.8), channel_id=1, source_target_pairs={{2,0},{4,2},{6,4},{0,6},{3,1},{5,3},{7,5},{1,7},{10,8},{12,10},{14... | collective-permute-start | bytes 1572872 | tf_op jit(solution)/shard_map/ppermute | solution.py:70
  406.6 2.0 bitcast_add_fusion
  409.5 1.8 pad_maximum_fusion
  411.3 7.8 %collective-permute-done.45 = bf16[128,2048]{1,0:T(8,128)(2,1)S(1)} collective-permute-done((bf16[128,2048]{1,0:T(8,128)(2,1)}, bf16[128,2048]{1,0:T(8,128)(2,1)S(1)}, u32[]{:S(2)}, u32[]{:S(2)}) %collective-permute-start.45) | collective-permute-done | bytes 524320 | tf_op jit(solution)/shard_map/ppermute | solution.py:70
  419.1 9.2 %collective-permute-done.46 = bf16[128,2048]{1,0:T(8,128)(2,1)S(1)} collective-permute-done((bf16[128,2048]{1,0:T(8,128)(2,1)S(1)}, bf16[128,2048]{1,0:T(8,128)(2,1)S(1)}, u32[]{:S(2)}, u32[]{:S(2)}) %collective-permute-start.46) | collective-permute-done | bytes 524320 | tf_op jit(solution)/shard_map/ppermute | solution.py:70
  429.8 2.7 convert_add_fusion.6
  433.3 3.7 all-to-all-start.4
  439.1 2.8 collective-permute-start.48
  441.9 3.3 convert_add_fusion.3
  446.3 7.1 %collective-permute-done.48 = bf16[128,2048]{1,0:T(8,128)(2,1)S(1)} collective-permute-done((bf16[128,2048]{1,0:T(8,128)(2,1)}, bf16[128,2048]{1,0:T(8,128)(2,1)S(1)}, u32[]{:S(2)}, u32[]{:S(2)}) %collective-permute-start.48) | collective-permute-done | bytes 524320 | tf_op jit(solution)/shard_map/ppermute | solution.py:70
  453.6 1.7 collective-permute-start.52
  455.3 4.2 collective-permute-start.51
  461.0 10.3 %collective-permute-done.52 = f32[1,4,640]{2,0,1:T(1,128)S(1)} collective-permute-done((f32[1,4,640]{2,0,1:T(1,128)S(1)}, f32[1,4,640]{2,0,1:T(1,128)S(1)}, u32[]{:S(2)}, u32[]{:S(2)}) %collective-permute-start.52) | collective-permute-done | bytes 10272 | tf_op jit(solution)/shard_map/ppermute | solution.py:33
  471.3 2.9 collective-permute-start.55
  475.5 3.2 collective-permute-done.54
  485.2 4.8 shard_map.239
  (306 shorter events, 75.0 us)
Async XLA Ops:
  6.2 49.8 %all-to-all-start = ((bf16[16,64,896]{2,1,0:T(8,128)(2,1)}), bf16[16,64,896]{2,1,0:T(8,128)(2,1)S(1)}, u32[]{:S(2)}, u32[]{:S(2)}) async-start(bf16[16,64,896]{2,1,0:T(8,128)(2,1)} %get-tuple-element.251), calls=%async_computation | async-start | bytes 3670016 | tf_op jit(solution)/shard_map/all_to_all | solution.py:749
  13.9 10.3 %collective-permute-start.2 = (bf16[1,704]{1,0:T(2,128)(2,1)S(1)}, bf16[1,704]{1,0:T(2,128)(2,1)S(1)}, u32[]{:S(2)}, u32[]{:S(2)}) collective-permute-start(bf16[1,704]{1,0:T(2,128)(2,1)S(1)} %broadcast_in_dim.114), channel_id=1, source_target_pairs={{0,1},{1,0},{2,3},{3,2},{4,5},{5,4},{6,7},{7,6},{8,9},{9,8},{10,11... | collective-permute-start | bytes 4232 | tf_op jit(solution)/shard_map/ppermute | solution.py:33
  15.9 11.1 %collective-permute-start = (bf16[64,2048]{1,0:T(8,128)(2,1)}, bf16[64,2048]{1,0:T(8,128)(2,1)}, u32[]{:S(2)}, u32[]{:S(2)}) collective-permute-start(bf16[64,2048]{1,0:T(8,128)(2,1)} %get-tuple-element.250), channel_id=1, source_target_pairs={{0,16},{16,0},{1,17},{17,1},{2,18},{18,2},{3,19},{19,3},{4,20},{20... | collective-permute-start | bytes 786440 | tf_op jit(solution)/shard_map/ppermute | solution.py:33
  20.3 9.7 %collective-permute-start.1 = (bf16[64,2048]{1,0:T(8,128)(2,1)S(1)}, bf16[64,2048]{1,0:T(8,128)(2,1)}, u32[]{:S(2)}, u32[]{:S(2)}) collective-permute-start(bf16[64,2048]{1,0:T(8,128)(2,1)S(1)} %get-tuple-element.543), channel_id=1, source_target_pairs={{0,16},{16,0},{1,17},{17,1},{2,18},{18,2},{3,19},{19,3},{4,20},{20... | collective-permute-start | bytes 786440 | tf_op jit(solution)/shard_map/ppermute | solution.py:33
  24.2 1.2 collective-permute-start.3
  25.4 4.5 collective-permute-start.4
  58.8 15.1 %collective-permute-start.6 = (bf16[128,2048]{1,0:T(8,128)(2,1)S(1)}, bf16[128,2048]{1,0:T(8,128)(2,1)S(1)}, u32[]{:S(2)}, u32[]{:S(2)}) collective-permute-start(bf16[128,2048]{1,0:T(8,128)(2,1)S(1)} %copy-done.12), channel_id=1, source_target_pairs={{0,2},{2,4},{4,6},{6,0},{1,3},{3,5},{5,7},{7,1},{8,10},{10,12},{12... | collective-permute-start | bytes 1572872 | tf_op jit(solution)/shard_map/ppermute | solution.py:53
  61.3 13.2 %collective-permute-start.5 = (bf16[128,2048]{1,0:T(8,128)(2,1)S(1)}, bf16[128,2048]{1,0:T(8,128)(2,1)S(1)}, u32[]{:S(2)}, u32[]{:S(2)}) collective-permute-start(bf16[128,2048]{1,0:T(8,128)(2,1)S(1)} %copy-done.12), channel_id=1, source_target_pairs={{0,1},{1,0},{2,3},{3,2},{4,5},{5,4},{6,7},{7,6},{8,9},{9,8},{10,11... | collective-permute-start | bytes 1572872 | tf_op jit(solution)/shard_map/ppermute | solution.py:33
  61.9 11.9 %collective-permute-start.7 = (bf16[8,704]{1,0:T(8,128)(2,1)S(1)}, bf16[8,704]{1,0:T(8,128)(2,1)S(1)}, u32[]{:S(2)}, u32[]{:S(2)}) collective-permute-start(bf16[8,704]{1,0:T(8,128)(2,1)S(1)} %maximum_select_fusion.6), channel_id=1, source_target_pairs={{0,2},{2,0},{4,6},{6,4},{1,3},{3,1},{5,7},{7,5},{8,10},{10,8},{12,... | collective-permute-start | bytes 33800 | tf_op jit(solution)/shard_map/ppermute | solution.py:78
  63.3 42.4 %collective-permute-start.15 = (bf16[1024,896]{1,0:T(8,128)(2,1)S(1)}, bf16[1024,896]{1,0:T(8,128)(2,1)}, u32[]{:S(2)}, u32[]{:S(2)}) collective-permute-start(bf16[1024,896]{1,0:T(8,128)(2,1)S(1)} %bitcast.132), channel_id=1, source_target_pairs={{0,16},{16,0},{1,17},{17,1},{2,18},{18,2},{3,19},{19,3},{4,20},{20... | collective-permute-start | bytes 5505032 | tf_op jit(solution)/shard_map/ppermute | solution.py:33
  66.7 44.9 %copy-start.10 = (bf16[128,2048]{1,0:T(8,128)(2,1)}, bf16[128,2048]{1,0:T(8,128)(2,1)S(1)}, u32[]{:S(2)}) copy-start(bf16[128,2048]{1,0:T(8,128)(2,1)S(1)} %pad_maximum_fusion.2) | copy-start | bytes 1572868
  74.5 15.2 %collective-permute-start.9 = (bf16[128,2048]{1,0:T(8,128)(2,1)S(1)}, bf16[128,2048]{1,0:T(8,128)(2,1)}, u32[]{:S(2)}, u32[]{:S(2)}) collective-permute-start(bf16[128,2048]{1,0:T(8,128)(2,1)S(1)} %collective-permute-done.6), channel_id=1, source_target_pairs={{0,2},{2,4},{4,6},{6,0},{1,3},{3,5},{5,7},{7,1},{8,10},{10,12},{12... | collective-permute-start | bytes 1572872 | tf_op jit(solution)/shard_map/ppermute | solution.py:53
  75.3 14.4 %collective-permute-start.8 = (bf16[128,2048]{1,0:T(8,128)(2,1)S(1)}, bf16[128,2048]{1,0:T(8,128)(2,1)S(1)}, u32[]{:S(2)}, u32[]{:S(2)}) collective-permute-start(bf16[128,2048]{1,0:T(8,128)(2,1)S(1)} %collective-permute-done.6), channel_id=1, source_target_pairs={{0,1},{1,0},{2,3},{3,2},{4,5},{5,4},{6,7},{7,6},{8,9},{9,8},{10,11... | collective-permute-start | bytes 1572872 | tf_op jit(solution)/shard_map/ppermute | solution.py:33
  76.9 12.8 %collective-permute-start.10 = (bf16[16,704]{1,0:T(8,128)(2,1)S(1)}, bf16[16,704]{1,0:T(8,128)(2,1)S(1)}, u32[]{:S(2)}, u32[]{:S(2)}) collective-permute-start(bf16[16,704]{1,0:T(8,128)(2,1)S(1)} %maximum_select_fusion.5), channel_id=1, source_target_pairs={{0,4},{2,6},{4,0},{6,2},{1,5},{3,7},{5,1},{7,3},{8,12},{10,14},{12... | collective-permute-start | bytes 67592 | tf_op jit(solution)/shard_map/ppermute | solution.py:78
  78.9 26.8 %collective-permute-start.13 = (bf16[256,2048]{1,0:T(8,128)(2,1)}, bf16[256,2048]{1,0:T(8,128)(2,1)}, u32[]{:S(2)}, u32[]{:S(2)}) collective-permute-start(bf16[256,2048]{1,0:T(8,128)(2,1)} %constant_dynamic-update-slice_fusion.refs_0_), channel_id=1, source_target_pairs={{0,8},{8,0},{1,9},{9,1},{2,10},{10,2},{3,11},{11,3},{4,12},{12,4},... | collective-permute-start | bytes 3145736 | tf_op jit(solution)/shard_map/ppermute | solution.py:33
  89.7 16.0 %collective-permute-start.12 = (bf16[128,2048]{1,0:T(8,128)(2,1)}, bf16[128,2048]{1,0:T(8,128)(2,1)}, u32[]{:S(2)}, u32[]{:S(2)}) collective-permute-start(bf16[128,2048]{1,0:T(8,128)(2,1)} %collective-permute-done.9), channel_id=1, source_target_pairs={{0,2},{2,4},{4,6},{6,0},{1,3},{3,5},{5,7},{7,1},{8,10},{10,12},{12... | collective-permute-start | bytes 1572872 | tf_op jit(solution)/shard_map/ppermute | solution.py:53
  89.9 15.8 %collective-permute-start.11 = (bf16[128,2048]{1,0:T(8,128)(2,1)}, bf16[128,2048]{1,0:T(8,128)(2,1)}, u32[]{:S(2)}, u32[]{:S(2)}) collective-permute-start(bf16[128,2048]{1,0:T(8,128)(2,1)} %collective-permute-done.9), channel_id=1, source_target_pairs={{0,1},{1,0},{2,3},{3,2},{4,5},{5,4},{6,7},{7,6},{8,9},{9,8},{10,11... | collective-permute-start | bytes 1572872 | tf_op jit(solution)/shard_map/ppermute | solution.py:33
  91.3 14.4 %collective-permute-start.14 = (bf16[256,2048]{1,0:T(8,128)(2,1)}, bf16[256,2048]{1,0:T(8,128)(2,1)}, u32[]{:S(2)}, u32[]{:S(2)}) collective-permute-start(bf16[256,2048]{1,0:T(8,128)(2,1)} %constant_dynamic-update-slice_fusion.2.refs_1_), channel_id=1, source_target_pairs={{0,8},{8,0},{1,9},{9,1},{2,10},{10,2},{3,11},{11,3},{4,12},{12,4},... | collective-permute-start | bytes 3145736 | tf_op jit(solution)/shard_map/ppermute | solution.py:33
  107.6 20.7 %collective-permute-start.18 = (bf16[256,2048]{1,0:T(8,128)(2,1)}, bf16[256,2048]{1,0:T(8,128)(2,1)S(1)}, u32[]{:S(2)}, u32[]{:S(2)}) collective-permute-start(bf16[256,2048]{1,0:T(8,128)(2,1)} %constant_dynamic-update-slice_fusion.4.refs_0_.refs_4_), channel_id=1, source_target_pairs={{0,8},{8,0},{1,9},{9,1},{2,10},{10,2},{3,11},{11,3},{4,12},{12,4},... | collective-permute-start | bytes 3145736 | tf_op jit(solution)/shard_map/ppermute | solution.py:33
  111.5 16.8 %collective-permute-start.17 = (bf16[128,2048]{1,0:T(8,128)(2,1)S(1)}, bf16[128,2048]{1,0:T(8,128)(2,1)S(1)}, u32[]{:S(2)}, u32[]{:S(2)}) collective-permute-start(bf16[128,2048]{1,0:T(8,128)(2,1)S(1)} %pad_maximum_fusion.2), channel_id=1, source_target_pairs={{0,2},{2,4},{4,6},{6,0},{1,3},{3,5},{5,7},{7,1},{8,10},{10,12},{12... | collective-permute-start | bytes 1572872 | tf_op jit(solution)/shard_map/ppermute | solution.py:53
  111.6 16.8 %collective-permute-start.16 = (bf16[128,2048]{1,0:T(8,128)(2,1)}, bf16[128,2048]{1,0:T(8,128)(2,1)S(1)}, u32[]{:S(2)}, u32[]{:S(2)}) collective-permute-start(bf16[128,2048]{1,0:T(8,128)(2,1)} %collective-permute-done.12), channel_id=1, source_target_pairs={{0,1},{1,0},{2,3},{3,2},{4,5},{5,4},{6,7},{7,6},{8,9},{9,8},{10,11... | collective-permute-start | bytes 1572872 | tf_op jit(solution)/shard_map/ppermute | solution.py:33
  128.4 32.8 %all-to-all-start.1 = ((bf16[16,64,512]{2,1,0:T(8,128)(2,1)}), bf16[16,64,512]{2,1,0:T(8,128)(2,1)}, u32[]{:S(2)}, u32[]{:S(2)}) async-start(bf16[16,64,512]{2,1,0:T(8,128)(2,1)} %get-tuple-element.309), calls=%async_computation.1 | async-start | bytes 2097152 | tf_op jit(solution)/shard_map/all_to_all | solution.py:749
  135.8 2.9 collective-permute-start.19
  136.3 27.2 %collective-permute-start.24 = (bf16[64,2048]{1,0:T(8,128)(2,1)S(1)}, bf16[64,2048]{1,0:T(8,128)(2,1)S(1)}, u32[]{:S(2)}, u32[]{:S(2)}) collective-permute-start(bf16[64,2048]{1,0:T(8,128)(2,1)S(1)} %copy-done.32), channel_id=1, source_target_pairs={{0,16},{16,0},{1,17},{17,1},{2,18},{18,2},{3,19},{19,3},{4,20},{20... | collective-permute-start | bytes 786440 | tf_op jit(solution)/shard_map/ppermute | solution.py:33
  161.3 28.6 %collective-permute-start.20 = (bf16[256,2048]{1,0:T(8,128)(2,1)S(1)}, bf16[256,2048]{1,0:T(8,128)(2,1)}, u32[]{:S(2)}, u32[]{:S(2)}) collective-permute-start(bf16[256,2048]{1,0:T(8,128)(2,1)S(1)} %constant_dynamic-update-slice_fusion.8.refs_0_), channel_id=1, source_target_pairs={{0,1},{1,0},{2,3},{3,2},{4,5},{5,4},{6,7},{7,6},{8,9},{9,8},{10,11... | collective-permute-start | bytes 3145736 | tf_op jit(solution)/shard_map/ppermute | solution.py:33
  162.0 28.0 %collective-permute-start.23 = (bf16[1024,512]{1,0:T(8,128)(2,1)}, bf16[1024,512]{1,0:T(8,128)(2,1)}, u32[]{:S(2)}, u32[]{:S(2)}) collective-permute-start(bf16[1024,512]{1,0:T(8,128)(2,1)} %bitcast.15.own_ref.refs_9_), channel_id=1, source_target_pairs={{0,16},{16,0},{1,17},{17,1},{2,18},{18,2},{3,19},{19,3},{4,20},{20... | collective-permute-start | bytes 3145736 | tf_op jit(solution)/shard_map/ppermute | solution.py:33
  164.4 16.1 %collective-permute-start.22 = (bf16[128,2048]{1,0:T(8,128)(2,1)S(1)}, bf16[128,2048]{1,0:T(8,128)(2,1)S(1)}, u32[]{:S(2)}, u32[]{:S(2)}) collective-permute-start(bf16[128,2048]{1,0:T(8,128)(2,1)S(1)} %copy-done.11), channel_id=1, source_target_pairs={{0,6},{2,0},{4,2},{6,4},{1,7},{3,1},{5,3},{7,5},{8,14},{10,8},{12,... | collective-permute-start | bytes 1572872 | tf_op jit(solution)/shard_map/ppermute | solution.py:851
  165.2 24.7 %collective-permute-start.21 = (bf16[128,2048]{1,0:T(8,128)(2,1)S(1)}, bf16[128,2048]{1,0:T(8,128)(2,1)S(1)}, u32[]{:S(2)}, u32[]{:S(2)}) collective-permute-start(bf16[128,2048]{1,0:T(8,128)(2,1)S(1)} %collective-permute-done.17), channel_id=1, source_target_pairs={{0,2},{2,4},{4,6},{6,0},{1,3},{3,5},{5,7},{7,1},{8,10},{10,12},{12... | collective-permute-start | bytes 1572872 | tf_op jit(solution)/shard_map/ppermute | solution.py:53
  190.0 15.5 %collective-permute-start.28 = (bf16[256,2048]{1,0:T(8,128)(2,1)S(1)}, bf16[256,2048]{1,0:T(8,128)(2,1)S(1)}, u32[]{:S(2)}, u32[]{:S(2)}) collective-permute-start(bf16[256,2048]{1,0:T(8,128)(2,1)S(1)} %constant_dynamic-update-slice_fusion.10.refs_4_), channel_id=1, source_target_pairs={{0,8},{8,0},{1,9},{9,1},{2,10},{10,2},{3,11},{11,3},{4,12},{12,4},... | collective-permute-start | bytes 3145736 | tf_op jit(solution)/shard_map/ppermute | solution.py:33
  190.1 25.7 %collective-permute-start.25 = (bf16[256,2048]{1,0:T(8,128)(2,1)S(1)}, bf16[256,2048]{1,0:T(8,128)(2,1)}, u32[]{:S(2)}, u32[]{:S(2)}) collective-permute-start(bf16[256,2048]{1,0:T(8,128)(2,1)S(1)} %constant_dynamic-update-slice_fusion.10.refs_4_), channel_id=1, source_target_pairs={{0,1},{1,0},{2,3},{3,2},{4,5},{5,4},{6,7},{7,6},{8,9},{9,8},{10,11... | collective-permute-start | bytes 3145736 | tf_op jit(solution)/shard_map/ppermute | solution.py:33
  190.7 25.1 %collective-permute-start.26 = (bf16[256,2048]{1,0:T(8,128)(2,1)S(1)}, bf16[256,2048]{1,0:T(8,128)(2,1)}, u32[]{:S(2)}, u32[]{:S(2)}) collective-permute-start(bf16[256,2048]{1,0:T(8,128)(2,1)S(1)} %constant_dynamic-update-slice_fusion.8.refs_0_), channel_id=1, source_target_pairs={{0,8},{8,0},{1,9},{9,1},{2,10},{10,2},{3,11},{11,3},{4,12},{12,4},... | collective-permute-start | bytes 3145736 | tf_op jit(solution)/shard_map/ppermute | solution.py:33
  190.9 24.9 %collective-permute-start.27 = (bf16[256,2048]{1,0:T(8,128)(2,1)}, bf16[256,2048]{1,0:T(8,128)(2,1)}, u32[]{:S(2)}, u32[]{:S(2)}) collective-permute-start(bf16[256,2048]{1,0:T(8,128)(2,1)} %collective-permute-done.20.refs_1_), channel_id=1, source_target_pairs={{0,8},{8,0},{1,9},{9,1},{2,10},{10,2},{3,11},{11,3},{4,12},{12,4},... | collective-permute-start | bytes 3145736 | tf_op jit(solution)/shard_map/ppermute | solution.py:33
  215.8 2.9 collective-permute-start.29
  218.7 17.6 %collective-permute-start.30 = (bf16[256,2048]{1,0:T(8,128)(2,1)}, bf16[256,2048]{1,0:T(8,128)(2,1)}, u32[]{:S(2)}, u32[]{:S(2)}) collective-permute-start(bf16[256,2048]{1,0:T(8,128)(2,1)} %get-tuple-element.356), channel_id=1, source_target_pairs={{0,8},{8,0},{1,9},{9,1},{2,10},{10,2},{3,11},{11,3},{4,12},{12,4},... | collective-permute-start | bytes 3145736 | tf_op jit(solution)/shard_map/ppermute | solution.py:33
  218.8 17.5 %collective-permute-start.31 = (bf16[256,2048]{1,0:T(8,128)(2,1)}, bf16[256,2048]{1,0:T(8,128)(2,1)}, u32[]{:S(2)}, u32[]{:S(2)}) collective-permute-start(bf16[256,2048]{1,0:T(8,128)(2,1)} %get-tuple-element.357), channel_id=1, source_target_pairs={{0,8},{8,0},{1,9},{9,1},{2,10},{10,2},{3,11},{11,3},{4,12},{12,4},... | collective-permute-start | bytes 3145736 | tf_op jit(solution)/shard_map/ppermute | solution.py:33
  219.6 16.7 %collective-permute-start.32 = (bf16[256,2048]{1,0:T(8,128)(2,1)}, bf16[256,2048]{1,0:T(8,128)(2,1)S(1)}, u32[]{:S(2)}, u32[]{:S(2)}) collective-permute-start(bf16[256,2048]{1,0:T(8,128)(2,1)} %get-tuple-element.358), channel_id=1, source_target_pairs={{0,8},{8,0},{1,9},{9,1},{2,10},{10,2},{3,11},{11,3},{4,12},{12,4},... | collective-permute-start | bytes 3145736 | tf_op jit(solution)/shard_map/ppermute | solution.py:33
  219.8 16.5 %collective-permute-start.33 = (bf16[256,2048]{1,0:T(8,128)(2,1)}, bf16[256,2048]{1,0:T(8,128)(2,1)S(1)}, u32[]{:S(2)}, u32[]{:S(2)}) collective-permute-start(bf16[256,2048]{1,0:T(8,128)(2,1)} %get-tuple-element.359), channel_id=1, source_target_pairs={{0,8},{8,0},{1,9},{9,1},{2,10},{10,2},{3,11},{11,3},{4,12},{12,4},... | collective-permute-start | bytes 3145736 | tf_op jit(solution)/shard_map/ppermute | solution.py:33
  240.5 47.8 %collective-permute-start.35 = (bf16[512,2048]{1,0:T(8,128)(2,1)S(1)}, bf16[512,2048]{1,0:T(8,128)(2,1)}, u32[]{:S(2)}, u32[]{:S(2)}) collective-permute-start(bf16[512,2048]{1,0:T(8,128)(2,1)S(1)} %add_convert_fusion.1), channel_id=1, source_target_pairs={{0,1},{1,0},{2,3},{3,2},{4,5},{5,4},{6,7},{7,6},{8,9},{9,8},{10,11... | collective-permute-start | bytes 6291464 | tf_op jit(solution)/shard_map/ppermute | solution.py:33
  255.8 47.7 %collective-permute-start.34 = (bf16[4,2,128,1024]{3,2,1,0:T(8,128)(2,1)}, bf16[4,2,128,1024]{3,2,1,0:T(8,128)(2,1)}, u32[]{:S(2)}, u32[]{:S(2)}) collective-permute-start(bf16[4,2,128,1024]{3,2,1,0:T(8,128)(2,1)} %get-tuple-element.373), channel_id=1, source_target_pairs={{0,16},{16,0},{1,17},{17,1},{2,18},{18,2},{3,19},{19,3},{4,20},{20... | collective-permute-start | bytes 6291464 | tf_op jit(solution)/shard_map/ppermute | solution.py:33
  289.8 13.7 %collective-permute-start.36 = (bf16[128,2048]{1,0:T(8,128)(2,1)S(1)}, bf16[128,2048]{1,0:T(8,128)(2,1)S(1)}, u32[]{:S(2)}, u32[]{:S(2)}) collective-permute-start(bf16[128,2048]{1,0:T(8,128)(2,1)S(1)} %convert_add_fusion.10), channel_id=1, source_target_pairs={{2,0},{4,2},{6,4},{0,6},{3,1},{5,3},{7,5},{1,7},{10,8},{12,10},{14... | collective-permute-start | bytes 1572872 | tf_op jit(solution)/shard_map/ppermute | solution.py:70
  307.7 51.4 %all-to-all-start.2 = ((bf16[4,2,128,1024]{3,2,1,0:T(8,128)(2,1)}), bf16[4,2,128,1024]{3,2,1,0:T(8,128)(2,1)S(1)}, u32[]{:S(2)}, u32[]{:S(2)}) async-start(bf16[4,2,128,1024]{3,2,1,0:T(8,128)(2,1)} %add_convert_fusion), calls=%async_computation.2 | async-start | bytes 4194304 | tf_op jit(solution)/shard_map/all_to_all | solution.py:756
  312.2 21.9 %collective-permute-start.37 = (bf16[4,2,128,384]{3,2,1,0:T(8,128)(2,1)}, bf16[4,2,128,384]{3,2,1,0:T(8,128)(2,1)S(1)}, u32[]{:S(2)}, u32[]{:S(2)}) collective-permute-start(bf16[4,2,128,384]{3,2,1,0:T(8,128)(2,1)} %get-tuple-element.409), channel_id=1, source_target_pairs={{0,16},{16,0},{1,17},{17,1},{2,18},{18,2},{3,19},{19,3},{4,20},{20... | collective-permute-start | bytes 2359304 | tf_op jit(solution)/shard_map/ppermute | solution.py:33
  339.1 12.1 %collective-permute-start.38 = (bf16[256,2048]{1,0:T(8,128)(2,1)}, bf16[256,2048]{1,0:T(8,128)(2,1)}, u32[]{:S(2)}, u32[]{:S(2)}) collective-permute-start(bf16[256,2048]{1,0:T(8,128)(2,1)} %get-tuple-element.412), channel_id=1, source_target_pairs={{0,8},{8,0},{1,9},{9,1},{2,10},{10,2},{3,11},{11,3},{4,12},{12,4},... | collective-permute-start | bytes 3145736 | tf_op jit(solution)/shard_map/ppermute | solution.py:33
  339.2 12.0 %collective-permute-start.39 = (bf16[256,2048]{1,0:T(8,128)(2,1)}, bf16[256,2048]{1,0:T(8,128)(2,1)}, u32[]{:S(2)}, u32[]{:S(2)}) collective-permute-start(bf16[256,2048]{1,0:T(8,128)(2,1)} %get-tuple-element.413), channel_id=1, source_target_pairs={{0,8},{8,0},{1,9},{9,1},{2,10},{10,2},{3,11},{11,3},{4,12},{12,4},... | collective-permute-start | bytes 3145736 | tf_op jit(solution)/shard_map/ppermute | solution.py:33
  339.7 11.5 %collective-permute-start.40 = (bf16[256,2048]{1,0:T(8,128)(2,1)}, bf16[256,2048]{1,0:T(8,128)(2,1)S(1)}, u32[]{:S(2)}, u32[]{:S(2)}) collective-permute-start(bf16[256,2048]{1,0:T(8,128)(2,1)} %get-tuple-element.414), channel_id=1, source_target_pairs={{0,8},{8,0},{1,9},{9,1},{2,10},{10,2},{3,11},{11,3},{4,12},{12,4},... | collective-permute-start | bytes 3145736 | tf_op jit(solution)/shard_map/ppermute | solution.py:33
  339.8 11.4 %collective-permute-start.41 = (bf16[256,2048]{1,0:T(8,128)(2,1)}, bf16[256,2048]{1,0:T(8,128)(2,1)}, u32[]{:S(2)}, u32[]{:S(2)}) collective-permute-start(bf16[256,2048]{1,0:T(8,128)(2,1)} %get-tuple-element.415), channel_id=1, source_target_pairs={{0,8},{8,0},{1,9},{9,1},{2,10},{10,2},{3,11},{11,3},{4,12},{12,4},... | collective-permute-start | bytes 3145736 | tf_op jit(solution)/shard_map/ppermute | solution.py:33
  364.6 29.2 %all-to-all-start.3 = ((bf16[4,2,128,384]{3,2,1,0:T(8,128)(2,1)}), bf16[4,2,128,384]{3,2,1,0:T(8,128)(2,1)S(1)}, u32[]{:S(2)}, u32[]{:S(2)}) async-start(bf16[4,2,128,384]{3,2,1,0:T(8,128)(2,1)} %add_convert_fusion.4), calls=%async_computation.3 | async-start | bytes 1572864 | tf_op jit(solution)/shard_map/all_to_all | solution.py:756
  368.1 25.7 %collective-permute-start.42 = (bf16[256,2048]{1,0:T(8,128)(2,1)}, bf16[256,2048]{1,0:T(8,128)(2,1)}, u32[]{:S(2)}, u32[]{:S(2)}) collective-permute-start(bf16[256,2048]{1,0:T(8,128)(2,1)} %add_convert_fusion.2), channel_id=1, source_target_pairs={{0,1},{1,0},{2,3},{3,2},{4,5},{5,4},{6,7},{7,6},{8,9},{9,8},{10,11... | collective-permute-start | bytes 3145736 | tf_op jit(solution)/shard_map/ppermute | solution.py:33
  369.7 24.1 %collective-permute-start.43 = (bf16[128,2048]{1,0:T(8,128)(2,1)}, bf16[128,2048]{1,0:T(8,128)(2,1)S(1)}, u32[]{:S(2)}, u32[]{:S(2)}) collective-permute-start(bf16[128,2048]{1,0:T(8,128)(2,1)} %convert_add_fusion.9), channel_id=1, source_target_pairs={{2,0},{4,2},{6,4},{0,6},{3,1},{5,3},{7,5},{1,7},{10,8},{12,10},{14... | collective-permute-start | bytes 1572872 | tf_op jit(solution)/shard_map/ppermute | solution.py:70
  375.4 31.2 %collective-permute-start.57 = (bf16[64,2048]{1,0:T(8,128)(2,1)}, bf16[64,2048]{1,0:T(8,128)(2,1)}, u32[]{:S(2)}, u32[]{:S(2)}) collective-permute-start(bf16[64,2048]{1,0:T(8,128)(2,1)} %fusion.24), channel_id=1, source_target_pairs={{0,16},{16,0},{1,17},{17,1},{2,18},{18,2},{3,19},{19,3},{4,20},{20... | collective-permute-start | bytes 786440 | tf_op jit(solution)/shard_map/ppermute | solution.py:33
  398.7 29.7 %collective-permute-start.44 = (bf16[256,2048]{1,0:T(8,128)(2,1)}, bf16[256,2048]{1,0:T(8,128)(2,1)}, u32[]{:S(2)}, u32[]{:S(2)}) collective-permute-start(bf16[256,2048]{1,0:T(8,128)(2,1)} %add_convert_fusion.3), channel_id=1, source_target_pairs={{0,1},{1,0},{2,3},{3,2},{4,5},{5,4},{6,7},{7,6},{8,9},{9,8},{10,11... | collective-permute-start | bytes 3145736 | tf_op jit(solution)/shard_map/ppermute | solution.py:33
  400.4 18.7 %collective-permute-start.45 = (bf16[128,2048]{1,0:T(8,128)(2,1)}, bf16[128,2048]{1,0:T(8,128)(2,1)S(1)}, u32[]{:S(2)}, u32[]{:S(2)}) collective-permute-start(bf16[128,2048]{1,0:T(8,128)(2,1)} %convert_add_fusion.8), channel_id=1, source_target_pairs={{2,0},{4,2},{6,4},{0,6},{3,1},{5,3},{7,5},{1,7},{10,8},{12,10},{14... | collective-permute-start | bytes 1572872 | tf_op jit(solution)/shard_map/ppermute | solution.py:70
  406.3 22.1 %collective-permute-start.46 = (bf16[128,2048]{1,0:T(8,128)(2,1)S(1)}, bf16[128,2048]{1,0:T(8,128)(2,1)S(1)}, u32[]{:S(2)}, u32[]{:S(2)}) collective-permute-start(bf16[128,2048]{1,0:T(8,128)(2,1)S(1)} %convert_add_fusion.7), channel_id=1, source_target_pairs={{2,0},{4,2},{6,4},{0,6},{3,1},{5,3},{7,5},{1,7},{10,8},{12,10},{14... | collective-permute-start | bytes 1572872 | tf_op jit(solution)/shard_map/ppermute | solution.py:70
  409.4 1.9 collective-permute-start.47
  433.3 46.7 %all-to-all-start.4 = ((bf16[4,4,64,1408]{3,2,1,0:T(8,128)(2,1)}), bf16[4,4,64,1408]{3,2,1,0:T(8,128)(2,1)S(1)}, u32[]{:S(2)}, u32[]{:S(2)}) async-start(bf16[4,4,64,1408]{3,2,1,0:T(8,128)(2,1)} %pad_maximum_fusion), calls=%async_computation.4 | async-start | bytes 5767168 | tf_op jit(solution)/shard_map/all_to_all | solution.py:771
  437.0 8.3 %collective-permute-start.50 = (f32[1,4,2,640]{3,2,1,0:T(2,128)S(1)}, f32[1,4,2,640]{3,2,1,0:T(2,128)S(1)}, u32[]{:S(2)}, u32[]{:S(2)}) collective-permute-start(f32[1,4,2,640]{3,2,1,0:T(2,128)S(1)} %get-tuple-element.459), channel_id=1, source_target_pairs={{0,16},{16,0},{1,17},{17,1},{2,18},{18,2},{3,19},{19,3},{4,20},{20... | collective-permute-start | bytes 61448 | tf_op jit(solution)/shard_map/ppermute | solution.py:33
  437.6 8.8 %collective-permute-start.49 = (bf16[64,2048]{1,0:T(8,128)(2,1)}, bf16[64,2048]{1,0:T(8,128)(2,1)S(1)}, u32[]{:S(2)}, u32[]{:S(2)}) collective-permute-start(bf16[64,2048]{1,0:T(8,128)(2,1)} %slice.257), channel_id=1, source_target_pairs={{0,16},{16,0},{1,17},{17,1},{2,18},{18,2},{3,19},{19,3},{4,20},{20... | collective-permute-start | bytes 786440 | tf_op jit(solution)/shard_map/ppermute | solution.py:33
  439.1 14.3 %collective-permute-start.48 = (bf16[128,2048]{1,0:T(8,128)(2,1)}, bf16[128,2048]{1,0:T(8,128)(2,1)S(1)}, u32[]{:S(2)}, u32[]{:S(2)}) collective-permute-start(bf16[128,2048]{1,0:T(8,128)(2,1)} %convert_add_fusion.6), channel_id=1, source_target_pairs={{2,0},{4,2},{6,4},{0,6},{3,1},{5,3},{7,5},{1,7},{10,8},{12,10},{14... | collective-permute-start | bytes 1572872 | tf_op jit(solution)/shard_map/ppermute | solution.py:70
  453.6 17.7 %collective-permute-start.52 = (f32[1,4,640]{2,0,1:T(1,128)S(1)}, f32[1,4,640]{2,0,1:T(1,128)S(1)}, u32[]{:S(2)}, u32[]{:S(2)}) collective-permute-start(f32[1,4,640]{2,0,1:T(1,128)S(1)} %get-tuple-element.469), channel_id=1, source_target_pairs={{0,1},{1,0},{2,3},{3,2},{4,5},{5,4},{6,7},{7,6},{8,9},{9,8},{10,11... | collective-permute-start | bytes 30728 | tf_op jit(solution)/shard_map/ppermute | solution.py:33
  455.3 24.7 %collective-permute-start.51 = (bf16[128,2048]{1,0:T(8,128)(2,1)S(1)}, bf16[128,2048]{1,0:T(8,128)(2,1)}, u32[]{:S(2)}, u32[]{:S(2)}) collective-permute-start(bf16[128,2048]{1,0:T(8,128)(2,1)S(1)} %convert_add_fusion.2), channel_id=1, source_target_pairs={{2,0},{4,2},{6,4},{0,6},{3,1},{5,3},{7,5},{1,7},{10,8},{12,10},{14... | collective-permute-start | bytes 1572872 | tf_op jit(solution)/shard_map/ppermute | solution.py:70
  471.3 4.2 collective-permute-start.55
  474.2 4.5 collective-permute-start.54
  474.6 5.4 %collective-permute-start.53 = (f32[1,640]{1,0:T(1,128)S(1)}, f32[1,640]{1,0:T(1,128)S(1)}, u32[]{:S(2)}, u32[]{:S(2)}) collective-permute-start(f32[1,640]{1,0:T(1,128)S(1)} %get-tuple-element.560), channel_id=1, source_target_pairs={{0,2},{2,4},{4,6},{6,0},{1,3},{3,5},{5,7},{7,1},{8,10},{10,12},{12... | collective-permute-start | bytes 7688 | tf_op jit(solution)/shard_map/ppermute | solution.py:976
  484.6 6.5 %collective-permute-start.56 = (bf16[64,2048]{1,0:T(8,128)(2,1)S(1)}, bf16[64,2048]{1,0:T(8,128)(2,1)S(1)}, u32[]{:S(2)}, u32[]{:S(2)}) collective-permute-start(bf16[64,2048]{1,0:T(8,128)(2,1)S(1)} %slice.256), channel_id=1, source_target_pairs={{0,16},{16,0},{1,17},{17,1},{2,18},{18,2},{3,19},{19,3},{4,20},{20... | collective-permute-start | bytes 786440 | tf_op jit(solution)/shard_map/ppermute | solution.py:33
  (51 other events, 477.6 us)

commit v5 on v4

--- a/solution.py
+++ b/solution.py
@@ -643,37 +643,48 @@
     )(triple, expand, shrink)
 
 
-def from_rank(rank):
-    return rank // (2 * Z_LEN) * 2 + rank % 2, rank // 2 % Z_LEN
-
-
-def unpack_kernel(back_ref, shrink_ref, expand_ref, triple_ref):
-    ranks = back_ref.shape[0] * back_ref.shape[1]
-    wide = (back_ref.shape[3] - 384) // 2
-    for rank in range(ranks):
-        for out_ref, begin in ((shrink_ref, 0), (expand_ref, wide)):
-            value = back_ref[(*from_rank(rank), slice(None), slice(begin, begin + wide))]
-            out_ref[:, rank * wide : (rank + 1) * wide] = value.astype(F32)
-    for rank in range(0, ranks, 2):
-        for s in range(3):
-            for x in range(2):
-                begin = 2 * wide + s * 128 + x * HEAD_DIM
-                pair = jnp.concatenate(
-                    [back_ref[(*from_rank(one), slice(None), slice(begin, begin + HEAD_DIM))] for one in (rank, rank + 1)],
-                    1,
-                )
-                at = (s * HEADS + x * ranks + rank) * HEAD_DIM
-                triple_ref[:, at : at + 128] = pair.astype(F32)
-
-
-def unpack(back):
-    four, along, held, cols = back.shape
-    wide = jax.ShapeDtypeStruct((held, four * along * (cols - 384) // 2), F32)
+def unpack_units_kernel(place_ref, *refs):
+    units, (shrink_ref, expand_ref) = refs[:4], refs[4:]
+    core, by = place_ref[0], place_ref[1]
+    wide = units[0].shape[2] // 2
+    for away in range(2):
+        for bz in range(Z_LEN):
+            first = jnp.bitwise_xor(core, away) * 2 * Z_LEN + bz * 2
+            for across_y in range(2):
+                value = units[2 * away + across_y][bz].astype(F32)
+                at = pl.ds(pl.multiple_of((first + jnp.bitwise_xor(by, across_y)) * wide, wide), wide)
+                shrink_ref[:, at] = value[:, :wide]
+                expand_ref[:, at] = value[:, wide:]
+
+
+def unpack_triple_kernel(place_ref, *refs):
+    triples, triple_ref = refs[:4], refs[4]
+    core, by = place_ref[0], place_ref[1]
+    for away in range(2):
+        for bz in range(Z_LEN):
+            first = jnp.bitwise_xor(core, away) * 2 * Z_LEN + bz * 2
+            own, other = triples[2 * away][bz].astype(F32), triples[2 * away + 1][bz].astype(F32)
+            low, high = jnp.where(by == 0, own, other), jnp.where(by == 0, other, own)
+            for s in range(3):
+                for x in range(2):
+                    lanes = slice(s * 128 + x * HEAD_DIM, s * 128 + (x + 1) * HEAD_DIM)
+                    at = pl.multiple_of((s * HEADS + x * 4 * Z_LEN + first) * HEAD_DIM, 128)
+                    triple_ref[:, pl.ds(at, 128)] = jnp.concatenate([low[:, lanes], high[:, lanes]], 1)
+
+
+def unpack(kernel, widths, core, by, pieces):
+    shapes = [jax.ShapeDtypeStruct((pieces[0].shape[1], width), F32) for width in widths]
     return pl.pallas_call(
-        unpack_kernel,
-        out_shape=[wide, wide, jax.ShapeDtypeStruct((held, 3 * HEADS * HEAD_DIM), F32)],
+        kernel,
+        grid_spec=pltpu.PrefetchScalarGridSpec(
+            num_scalar_prefetch=1,
+            grid=(1,),
+            in_specs=fixed(*pieces),
+            out_specs=fixed(*shapes),
+        ),
+        out_shape=shapes,
         compiler_params=pltpu.CompilerParams(vmem_limit_bytes=VMEM_LIMIT),
-    )(back)
+    )(jnp.where(jnp.arange(2) == 0, core, by).astype(jnp.int32), *pieces)
 
 
 def turn_tables(positions):
@@ -764,11 +775,11 @@
         mine = lax.psum_scatter(mine, "bs", scatter_dimension=1, tiled=True)
         return mine.reshape(2, Z_LEN, 2 * held, cols).transpose(1, 0, 2, 3)
 
-    def to_send(got):
-        return got.transpose(1, 2, 0, 3, 4).reshape(4, Z_LEN, held, got.shape[-1])
-
-    def to_rows_y(got):
-        return lax.all_to_all(got, ("core", "by"), split_axis=0, concat_axis=0, tiled=True)
+    def split(value, index, axis):
+        return (
+            lax.dynamic_index_in_dim(value, index, axis, keepdims=False),
+            lax.dynamic_index_in_dim(value, 1 - index, axis, keepdims=False),
+        )
 
     def both(low, high):
         return jnp.concatenate([low, high], 0)
@@ -950,27 +961,33 @@
     h_y_one = swap(far_one, "by")
     ringed, out_ringed = ring_back(h_sum), ring_back(out_sum)
     away = swap(away, "core")
-    all_rows = jnp.concatenate([to_send(units_rows), to_send(triple_rows)], 3)
-
-    h_y_one, ringed, out_ringed, small, away, all_rows = fence((h_y_one, ringed, out_ringed, small, away, all_rows))
+    units_parts, triple_parts = split(units_rows, by, 2), split(triple_rows, by, 2)
+
+    h_y_one, ringed, out_ringed, small, away, units_parts, triple_parts = fence(
+        (h_y_one, ringed, out_ringed, small, away, units_parts, triple_parts)
+    )
     h_sum = three(0, h_parts[7], h_got[3], h_y_two) + ringed
     out_sum = (out_three(0) + out_ringed).reshape(2, share, width)
     out_away = out_sum[1].astype(BF)
     small, away = halved(small + away, "hx", 0)
 
-    h_sum, out_sum, out_away, small, away, all_rows = fence((h_sum, out_sum, out_away, small, away, all_rows))
+    h_sum, out_sum, out_away, small, away, units_parts = fence((h_sum, out_sum, out_away, small, away, units_parts))
     ringed = ring_back(h_sum)
-    all_rows = to_rows_y(all_rows)
+    units_got = swap(units_parts[1], "by")
     out_away = swap(out_away, "hx")
     away = swap(away, "hx")
     h_last = [three(at, h_parts[6], h_got[2], h_y_one) for at in (0, 1)]
 
-    ringed, out_away, small, away, h_last = fence((ringed, out_away, small, away, h_last))
+    ringed, out_away, small, away, h_last, units_got = fence((ringed, out_away, small, away, h_last, units_got))
     h_sum = h_last[1] + ringed
     small, away = halved(small + away, "by", 2)
 
-    h_sum, small, away = fence((h_sum, small, away))
+    h_sum, small, away, triple_parts, units_got = fence((h_sum, small, away, triple_parts, units_got))
     ringed = ring_back(h_sum)
+    triple_got = swap(triple_parts[1], "by")
+    units_own, units_away = split(jnp.stack([units_parts[0], units_got]), core, 2)
+    units_away = swap(units_away, "core")
+    grad_shrink, grad_expand = unpack(unpack_units_kernel, (ff, ff), core, by, (*units_own, *units_away))
     small = small + swap(away, "by")
     terms = [lax.dynamic_index_in_dim(small, (bz + kz) % Z_LEN, 1, keepdims=False) for kz in range(Z_LEN)]
     terms = terms[:1] + [lax.ppermute(terms[kz], "bz", around(kz)) for kz in range(1, Z_LEN)]
@@ -980,8 +997,10 @@
     mixed = jnp.where(hx == 0, jnp.stack([out_sum[0], out_away]), jnp.stack([out_away, out_sum[0]]))
     output = (valid * (source + mixed + dense_b + shrink_b)).astype(BF).reshape(inputs.shape)
 
-    ringed, terms, output, all_rows = fence((ringed, terms, output, all_rows))
-    grad_shrink, grad_expand, grad_triple = unpack(all_rows)
+    ringed, terms, output, triple_got = fence((ringed, terms, output, triple_got), grad_shrink, grad_expand)
+    triple_own, triple_away = split(jnp.stack([triple_parts[0], triple_got]), core, 2)
+    triple_away = swap(triple_away, "core")
+    (grad_triple,) = unpack(unpack_triple_kernel, (3 * width,), core, by, (*triple_own, *triple_away))
     h_sum = (h_last[0] + ringed).reshape(2, share, width)
 
     dense_grads = grad_dense_here.T.reshape(2, HEAD_DIM, width)

time: 504 us -> 496 us (0.984)
  Pallas kernels: 146 us -> 162 us
  waiting for transfers between devices: 168 us -> 156 us
  other arithmetic: 52.3 us -> 45.3 us
    pallas_call x1, Pallas kernels: 17.9 us -> 24.9 us  [attend_back(): pl.pallas_call(functools.partial(attend_back_kernel, blocks, block), grid...]
    ppermute x5, waiting for transfers between devices: 19.5 us -> 13.8 us  [ring(): return lax.ppermute(value, 'bz', UP)]
    pallas_call x1, Pallas kernels: 14 us -> 19.7 us  [attend(): pl.pallas_call(functools.partial(attend_kernel, block), grid_spec=pltpu.P...]
    ppermute x3, waiting for transfers between devices: 5.15 us -> 0.01 us  [body(): lax.ppermute(terms[kz], 'bz', around(kz))]
    ppermute x41 -> x45, waiting for transfers between devices: 42.1 us -> 38.3 us  [swap(): return lax.ppermute(value, axis, SWAP)]
    ppermute x41 -> x45, starting transfers between devices: 27.3 us -> 29.5 us  [swap(): return lax.ppermute(value, axis, SWAP)]
  transfers between devices with their start and end apart: 63 -> 66, of which waited for: 23 -> 22; matrix products, arithmetic and copies ran while one was open for 12% -> 12% of each run, Pallas kernels for 29% -> 32%
where the time goes in v5:
time: 496 us; the launch traced here: 487 us
  Pallas kernels  162 us (33%)
  waiting for transfers between devices  156 us (31%)
  starting transfers between devices  78.6 us (16%)
  other arithmetic  45.3 us (9%)
  local copies, waits for them, and re-layouts  36.6 us (7%)
  matrix products  5.7 us (1%)
    ppermute x6, waiting for transfers between devices, ring_back(): return lax.ppermute(total.astype(BF), 'bz', DOWN)  44.5 us
    ppermute x45, waiting for transfers between devices, swap(): return lax.ppermute(value, axis, SWAP)  38.3 us
    all_to_all x2, waiting for transfers between devices, to_cols(): got = lax.all_to_all(sent, RANK, split_axis=0, concat_axis=0, tiled=True)  33.8 us
    ppermute x45, starting transfers between devices, swap(): return lax.ppermute(value, axis, SWAP)  29.5 us
    pallas_call x2, Pallas kernels, front(): pl.pallas_call(functools.partial(front_kernel, pieces), grid_spec=pltpu.P...  28.4 us
    pallas_call x1, Pallas kernels, attend_back(): pl.pallas_call(functools.partial(attend_back_kernel, blocks, block), grid...  24.9 us
    pallas_call x1, Pallas kernels, back_partial(): pl.pallas_call(functools.partial(back_kernel, pieces), grid_spec=pltpu.Pr...  21.3 us
    pallas_call x1, Pallas kernels, attend(): pl.pallas_call(functools.partial(attend_kernel, block), grid_spec=pltpu.P...  19.7 us
  transfers between devices with their start and end apart: 66, of which 22 were waited for; matrix products, arithmetic and copies ran while one was open for 12% of the time, Pallas kernels for 32%

profile of v5, /device:TPU:0, one launch (start us, length us, event | category | flops | bytes accessed | tf_op | source)
XLA Modules:
  0.0 486.9 jit_solution(16727925536802876440)
XLA Ops:
  1.7 3.7 shard_map.229
  5.5 7.5 %all-to-all-start = ((bf16[16,64,896]{2,1,0:T(8,128)(2,1)}), bf16[16,64,896]{2,1,0:T(8,128)(2,1)S(1)}, u32[]{:S(2)}, u32[]{:S(2)}) async-start(bf16[16,64,896]{2,1,0:T(8,128)(2,1)} %get-tuple-element.258), calls=%async_computation | async-start | bytes 3670016 | tf_op jit(solution)/shard_map/all_to_all | solution.py:760
  13.2 2.0 collective-permute-start.2
  15.2 1.5 collective-permute-start
  24.7 1.6 collective-permute-start.4
  27.1 1.9 collective-permute-done.4
  29.0 26.3 %all-to-all-done = bf16[16,64,896]{2,1,0:T(8,128)(2,1)S(1)} async-done(((bf16[16,64,896]{2,1,0:T(8,128)(2,1)}), bf16[16,64,896]{2,1,0:T(8,128)(2,1)S(1)}, u32[]{:S(2)}, u32[]{:S(2)}) %all-to-all-start) | async-done | bytes 1835040 | tf_op jit(solution)/shard_map/all_to_all | solution.py:760
  55.3 1.6 tile.8
  58.0 2.5 collective-permute-start.6
  62.6 1.5 collective-permute-start.15
  65.9 7.2 %collective-permute-done.7 = bf16[8,704]{1,0:T(8,128)(2,1)S(1)} collective-permute-done((bf16[8,704]{1,0:T(8,128)(2,1)S(1)}, bf16[8,704]{1,0:T(8,128)(2,1)S(1)}, u32[]{:S(2)}, u32[]{:S(2)}) %collective-permute-start.7) | collective-permute-done | bytes 11296 | tf_op jit(solution)/shard_map/ppermute | solution.py:78
  74.6 1.6 collective-permute-start.8
  78.2 10.8 %collective-permute-done.10 = bf16[16,704]{1,0:T(8,128)(2,1)S(1)} collective-permute-done((bf16[16,704]{1,0:T(8,128)(2,1)S(1)}, bf16[16,704]{1,0:T(8,128)(2,1)S(1)}, u32[]{:S(2)}, u32[]{:S(2)}) %collective-permute-start.10) | collective-permute-done | bytes 22560 | tf_op jit(solution)/shard_map/ppermute | solution.py:78
  92.9 1.9 constant_dynamic-update-slice_fusion.5
  94.8 10.1 %collective-permute-done.12 = bf16[128,2048]{1,0:T(8,128)(2,1)} collective-permute-done((bf16[128,2048]{1,0:T(8,128)(2,1)}, bf16[128,2048]{1,0:T(8,128)(2,1)}, u32[]{:S(2)}, u32[]{:S(2)}) %collective-permute-start.12) | collective-permute-done | bytes 524320 | tf_op jit(solution)/shard_map/ppermute | solution.py:53
  105.0 1.9 constant_dynamic-update-slice_fusion.4.refs_0_.refs_4_
  108.2 2.6 copy.90.refs_10_.sin_ref
  113.4 14.2 %shard_map.230 = (bf16[2048,2048]{1,0:T(8,128)(2,1)}, bf16[2048,128]{1,0:T(8,128)(2,1)}, bf16[2048,256]{1,0:T(8,128)(2,1)}, f32[2048,512]{1,0:T(8,128)}, bf16[20...) custom-call(s32[1]{0:T(128)} %bitcast.plane_ref, ...), custom_call_target="tpu_custom_call" | custom-call | flops 3783262208 | bytes 12582912 | tf_op jit(solution)/shard_map/pallas_call | solution.py:171
  127.6 6.3 %all-to-all-start.1 = ((bf16[16,64,512]{2,1,0:T(8,128)(2,1)}), bf16[16,64,512]{2,1,0:T(8,128)(2,1)}, u32[]{:S(2)}, u32[]{:S(2)}) async-start(bf16[16,64,512]{2,1,0:T(8,128)(2,1)} %get-tuple-element.316), calls=%async_computation.1 | async-start | bytes 2097152 | tf_op jit(solution)/shard_map/all_to_all | solution.py:760
  135.5 1.5 collective-permute-start.24
  138.8 14.2 %shard_map.231 = (bf16[2048,2048]{1,0:T(8,128)(2,1)}, bf16[2048,128]{1,0:T(8,128)(2,1)}, bf16[2048,256]{1,0:T(8,128)(2,1)}, f32[2048,512]{1,0:T(8,128)}, bf16[20...) custom-call(s32[1]{0:T(128)} %bitcast.plane_ref, ...), custom_call_target="tpu_custom_call", output_to_operand_aliasing={{0}: (12, {}), {1}: (13, {}), {2}: (14, {}), {3}: (15, {}),... | custom-call | flops 3783262208 | bytes 12582912 | tf_op jit(solution)/shard_map/pallas_call | solution.py:171
  153.0 7.5 %all-to-all-done.1 = bf16[16,64,512]{2,1,0:T(8,128)(2,1)} async-done(((bf16[16,64,512]{2,1,0:T(8,128)(2,1)}), bf16[16,64,512]{2,1,0:T(8,128)(2,1)}, u32[]{:S(2)}, u32[]{:S(2)}) %all-to-all-start.1) | async-done | bytes 1048608 | tf_op jit(solution)/shard_map/all_to_all | solution.py:760
  161.2 1.5 collective-permute-start.23
  165.8 19.7 %shard_map.232 = (f32[2,2,2,2,128,128]{5,4,3,2,1,0:T(8,128)}, bf16[2,2,2,2,128,128]{5,4,3,2,1,0:T(8,128)(2,1)}, f32[8,8,512]{2,1,0:T(8,128)}) custom-call(s32[2]{0:T(128)} %compare_select_fusion.9.meta_ref, s32[8]{0:T(128)} %copy-done.51, s32[8]{0:T(128)} %select_reduce_fusion.order_ref, bf16[2,2,2,2,128,128]{5,4,3,2,1,0:T(8,128)(2,1)} %bitcast.173, ...), custom_call_target="tpu_custom_call" | custom-call | flops 8589934592 | bytes 4194304 | tf_op jit(solution)/shard_map/pallas_call | solution.py:298
  185.5 3.7 collective-permute-done.21
  190.4 14.3 %shard_map.233 = (bf16[256,2048]{1,0:T(8,128)(2,1)}, bf16[256,2048]{1,0:T(8,128)(2,1)}, bf16[256,2048]{1,0:T(8,128)(2,1)}, bf16[256,2048]{1,0:T(8,128)(2,1)}, bf...) custom-call(s32[1]{0:T(128)} %bitcast.plane_ref, ...), custom_call_target="tpu_custom_call" | custom-call | flops 5368709120 | bytes 8388608 | tf_op jit(solution)/shard_map/pallas_call | solution.py:419
  204.7 10.3 %collective-permute-done.25.refs_5_ = bf16[256,2048]{1,0:T(8,128)(2,1)} collective-permute-done((bf16[256,2048]{1,0:T(8,128)(2,1)S(1)}, bf16[256,2048]{1,0:T(8,128)(2,1)}, u32[]{:S(2)}, u32[]{:S(2)}) %collective-permute-start.25) | collective-permute-done | bytes 1048608 | tf_op jit(solution)/shard_map/ppermute | solution.py:33
  215.0 2.9 collective-permute-done.29.refs_7_
  218.9 16.1 %shard_map.234 = (bf16[2048,128]{1,0:T(8,128)(2,1)}, bf16[2048,512]{1,0:T(8,128)(2,1)}, bf16[2048,2048]{1,0:T(8,128)(2,1)}) custom-call(s32[1]{0:T(128)} %bitcast.plane_ref, bf16[256,2048]{1,0:T(8,128)(2,1)} %copy-done.31, bf16[256,2048]{1,0:T(8,128)(2,1)} %collective-permute-done.20.refs_1_, bf16[256,2048]{1,0:T(8,128)(2,1)} %collective-permute-done.26.refs_2_, ...), custom_call_target="tpu_custom_call" | custom-call | flops 5368709120 | bytes 16777216 | tf_op jit(solution)/shard_map/pallas_call | solution.py:454
  236.4 2.9 add_convert_fusion.1
  240.0 14.6 %shard_map.235 = (bf16[4,2,128,1024]{3,2,1,0:T(8,128)(2,1)}, bf16[4,2,128,1024]{3,2,1,0:T(8,128)(2,1)}) custom-call(s32[1]{0:T(128)} %bitcast.plane_ref, bf16[2048,2048]{1,0:T(8,128)(2,1)} %get-tuple-element.430.refs_0_, bf16[2048,512]{1,0:T(8,128)(2,1)} %get-tuple-element.328.units_ref.refs_1_, bf16[2048,2048]{1,0:T(8,128)(2,1)} %get-tuple-element.375.refs_2_.h_ref, ...), custom_call_target="tpu_custom_call" | custom-call | flops 8589934592 | bytes 8388608 | tf_op jit(solution)/shard_map/pallas_call | solution.py:567
  255.1 24.9 %shard_map.236 = (bf16[2,2,2,2,128,128]{5,4,3,2,1,0:T(8,128)(2,1)}, bf16[2,2,2,2,128,256]{5,4,3,2,1,0:T(8,128)(2,1)}) custom-call(s32[2]{0:T(128)} %compare_select_fusion.9.meta_ref, s32[8]{0:T(128)} %copy-done.51, s32[8]{0:T(128)} %select_reduce_fusion.order_ref, bf16[2,2,2,2,128,128]{5,4,3,2,1,0:T(8,128)(2,1)} %bitcast.174, ...), custom_call_target="tpu_custom_call" | custom-call | flops 21474836480 | bytes 6291456 | tf_op jit(solution)/shard_map/pallas_call | solution.py:370
  280.0 7.2 %collective-permute-done.35 = bf16[512,2048]{1,0:T(8,128)(2,1)} collective-permute-done((bf16[512,2048]{1,0:T(8,128)(2,1)S(1)}, bf16[512,2048]{1,0:T(8,128)(2,1)}, u32[]{:S(2)}, u32[]{:S(2)}) %collective-permute-start.35) | collective-permute-done | bytes 2097184 | tf_op jit(solution)/shard_map/ppermute | solution.py:33
  288.6 1.8 collective-permute-start.36
  290.4 11.2 %shard_map.237 = (bf16[4,2,128,384]{3,2,1,0:T(8,128)(2,1)}, bf16[4,2,128,384]{3,2,1,0:T(8,128)(2,1)}, bf16[2048,384]{1,0:T(8,128)(2,1)}) custom-call(s32[1]{0:T(128)} %bitcast.plane_ref, bf16[2048,2048]{1,0:T(8,128)(2,1)} %get-tuple-element.375.refs_2_.h_ref, bf16[2048,128]{1,0:T(8,128)(2,1)} %bitcast.175, bf16[2048,256]{1,0:T(8,128)(2,1)} %bitcast.170, ...), custom_call_target="tpu_custom_call" | custom-call | flops 3221225472 | bytes 8388608 | tf_op jit(solution)/shard_map/pallas_call | solution.py:607
  302.3 4.1 add_convert_fusion
  306.4 4.5 all-to-all-start.2
  311.6 21.3 %shard_map.238 = (bf16[256,2048]{1,0:T(8,128)(2,1)}, bf16[256,2048]{1,0:T(8,128)(2,1)}, bf16[256,2048]{1,0:T(8,128)(2,1)}, bf16[256,2048]{1,0:T(8,128)(2,1)}, bf...) custom-call(s32[1]{0:T(128)} %bitcast.plane_ref, ...), custom_call_target="tpu_custom_call" | custom-call | flops 7516192768 | bytes 16777216 | tf_op jit(solution)/shard_map/pallas_call | solution.py:510
  339.4 2.6 add_convert_fusion.4
  342.0 2.3 convert_add_fusion.9
  344.3 5.7 %fusion.43 = f32[2048,128]{0,1:T(8,128)} fusion(bf16[2048,2048]{1,0:T(8,128)(2,1)} %get-tuple-element.430.refs_0_, bf16[2048,128]{1,0:T(8,128)(2,1)S(1)} %bitcast.188), kind=kOutput, calls=%fused_computation.185 | convolution fusion | flops 1073741824 | bytes 9961472 | tf_op jit(solution)/shard_map/dot_general | solution.py:41
  350.1 7.7 %all-to-all-done.2 = bf16[4,2,128,1024]{3,2,1,0:T(8,128)(2,1)S(1)} async-done(((bf16[4,2,128,1024]{3,2,1,0:T(8,128)(2,1)}), bf16[4,2,128,1024]{3,2,1,0:T(8,128)(2,1)S(1)}, u32[]{:S(2)}, u32[]{:S(2)}) %all-to-all-start.2) | async-done | bytes 2097184 | tf_op jit(solution)/shard_map/all_to_all | solution.py:767
  357.8 3.0 add_convert_fusion.3
  360.8 2.6 add_convert_fusion.2
  363.4 3.5 all-to-all-start.3
  366.9 1.5 collective-permute-start.42
  368.4 4.0 collective-permute-start.43
  373.0 19.5 %collective-permute-done.43 = bf16[128,2048]{1,0:T(8,128)(2,1)S(1)} collective-permute-done((bf16[128,2048]{1,0:T(8,128)(2,1)}, bf16[128,2048]{1,0:T(8,128)(2,1)S(1)}, u32[]{:S(2)}, u32[]{:S(2)}) %collective-permute-start.43) | collective-permute-done | bytes 524320 | tf_op jit(solution)/shard_map/ppermute | solution.py:70
  393.3 1.9 convert_add_fusion.7
  395.2 2.2 convert_add_fusion.8
  401.4 5.9 %collective-permute-start.45 = (bf16[128,2048]{1,0:T(8,128)(2,1)}, bf16[128,2048]{1,0:T(8,128)(2,1)S(1)}, u32[]{:S(2)}, u32[]{:S(2)}) collective-permute-start(bf16[128,2048]{1,0:T(8,128)(2,1)} %convert_add_fusion.8), channel_id=1, source_target_pairs={{2,0},{4,2},{6,4},{0,6},{3,1},{5,3},{7,5},{1,7},{10,8},{12,10},{14... | collective-permute-start | bytes 1572872 | tf_op jit(solution)/shard_map/ppermute | solution.py:70
  409.1 11.0 %collective-permute-done.45 = bf16[128,2048]{1,0:T(8,128)(2,1)S(1)} collective-permute-done((bf16[128,2048]{1,0:T(8,128)(2,1)}, bf16[128,2048]{1,0:T(8,128)(2,1)S(1)}, u32[]{:S(2)}, u32[]{:S(2)}) %collective-permute-start.45) | collective-permute-done | bytes 524320 | tf_op jit(solution)/shard_map/ppermute | solution.py:70
  420.1 9.0 %collective-permute-done.46 = bf16[128,2048]{1,0:T(8,128)(2,1)S(1)} collective-permute-done((bf16[128,2048]{1,0:T(8,128)(2,1)S(1)}, bf16[128,2048]{1,0:T(8,128)(2,1)S(1)}, u32[]{:S(2)}, u32[]{:S(2)}) %collective-permute-start.46) | collective-permute-done | bytes 524320 | tf_op jit(solution)/shard_map/ppermute | solution.py:70
  430.5 1.7 convert_add_fusion.6
  435.8 2.8 collective-permute-start.48
  438.6 1.7 convert_add_fusion.3
  441.6 5.0 %collective-permute-done.48 = bf16[128,2048]{1,0:T(8,128)(2,1)S(1)} collective-permute-done((bf16[128,2048]{1,0:T(8,128)(2,1)S(1)}, bf16[128,2048]{1,0:T(8,128)(2,1)S(1)}, u32[]{:S(2)}, u32[]{:S(2)}) %collective-permute-start.48) | collective-permute-done | bytes 524320 | tf_op jit(solution)/shard_map/ppermute | solution.py:70
  446.6 8.8 %collective-permute-done.51 = bf16[4,2,64,1024]{3,2,0,1:T(8,128)(2,1)S(1)} collective-permute-done((bf16[4,2,64,1024]{3,2,0,1:T(8,128)(2,1)S(1)}, bf16[4,2,64,1024]{3,2,0,1:T(8,128)(2,1)S(1)}, u32[]{:S(2)}, u32[]{:S(2)}) %collective-permute-start.51) | collective-permute-done | bytes 1048608 | tf_op jit(solution)/shard_map/ppermute | solution.py:33
  456.2 1.5 collective-permute-start.57
  457.7 2.7 collective-permute-start.52
  467.5 4.5 shard_map.239
  472.8 1.5 collective-permute-start.59
  476.5 3.4 collective-permute-done.59
  482.6 3.4 shard_map.240
  (319 shorter events, 74.2 us)
Async XLA Ops:
  5.5 49.8 %all-to-all-start = ((bf16[16,64,896]{2,1,0:T(8,128)(2,1)}), bf16[16,64,896]{2,1,0:T(8,128)(2,1)S(1)}, u32[]{:S(2)}, u32[]{:S(2)}) async-start(bf16[16,64,896]{2,1,0:T(8,128)(2,1)} %get-tuple-element.258), calls=%async_computation | async-start | bytes 3670016 | tf_op jit(solution)/shard_map/all_to_all | solution.py:760
  13.2 10.3 %collective-permute-start.2 = (bf16[1,704]{1,0:T(2,128)(2,1)S(1)}, bf16[1,704]{1,0:T(2,128)(2,1)S(1)}, u32[]{:S(2)}, u32[]{:S(2)}) collective-permute-start(bf16[1,704]{1,0:T(2,128)(2,1)S(1)} %broadcast_in_dim.122), channel_id=1, source_target_pairs={{0,1},{1,0},{2,3},{3,2},{4,5},{5,4},{6,7},{7,6},{8,9},{9,8},{10,11... | collective-permute-start | bytes 4232 | tf_op jit(solution)/shard_map/ppermute | solution.py:33
  15.2 11.1 %collective-permute-start = (bf16[64,2048]{1,0:T(8,128)(2,1)S(1)}, bf16[64,2048]{1,0:T(8,128)(2,1)S(1)}, u32[]{:S(2)}, u32[]{:S(2)}) collective-permute-start(bf16[64,2048]{1,0:T(8,128)(2,1)S(1)} %get-tuple-element.257), channel_id=1, source_target_pairs={{0,16},{16,0},{1,17},{17,1},{2,18},{18,2},{3,19},{19,3},{4,20},{20... | collective-permute-start | bytes 786440 | tf_op jit(solution)/shard_map/ppermute | solution.py:33
  19.6 9.5 %collective-permute-start.1 = (bf16[64,2048]{1,0:T(8,128)(2,1)S(1)}, bf16[64,2048]{1,0:T(8,128)(2,1)}, u32[]{:S(2)}, u32[]{:S(2)}) collective-permute-start(bf16[64,2048]{1,0:T(8,128)(2,1)S(1)} %get-tuple-element.569), channel_id=1, source_target_pairs={{0,16},{16,0},{1,17},{17,1},{2,18},{18,2},{3,19},{19,3},{4,20},{20... | collective-permute-start | bytes 786440 | tf_op jit(solution)/shard_map/ppermute | solution.py:33
  24.7 4.3 collective-permute-start.4
  58.0 15.1 %collective-permute-start.6 = (bf16[128,2048]{1,0:T(8,128)(2,1)S(1)}, bf16[128,2048]{1,0:T(8,128)(2,1)S(1)}, u32[]{:S(2)}, u32[]{:S(2)}) collective-permute-start(bf16[128,2048]{1,0:T(8,128)(2,1)S(1)} %copy-done.6), channel_id=1, source_target_pairs={{0,2},{2,4},{4,6},{6,0},{1,3},{3,5},{5,7},{7,1},{8,10},{10,12},{12... | collective-permute-start | bytes 1572872 | tf_op jit(solution)/shard_map/ppermute | solution.py:53
  60.6 13.2 %collective-permute-start.5 = (bf16[128,2048]{1,0:T(8,128)(2,1)S(1)}, bf16[128,2048]{1,0:T(8,128)(2,1)S(1)}, u32[]{:S(2)}, u32[]{:S(2)}) collective-permute-start(bf16[128,2048]{1,0:T(8,128)(2,1)S(1)} %copy-done.6), channel_id=1, source_target_pairs={{0,1},{1,0},{2,3},{3,2},{4,5},{5,4},{6,7},{7,6},{8,9},{9,8},{10,11... | collective-permute-start | bytes 1572872 | tf_op jit(solution)/shard_map/ppermute | solution.py:33
  61.2 11.9 %collective-permute-start.7 = (bf16[8,704]{1,0:T(8,128)(2,1)S(1)}, bf16[8,704]{1,0:T(8,128)(2,1)S(1)}, u32[]{:S(2)}, u32[]{:S(2)}) collective-permute-start(bf16[8,704]{1,0:T(8,128)(2,1)S(1)} %maximum_select_fusion.6), channel_id=1, source_target_pairs={{0,2},{2,0},{4,6},{6,4},{1,3},{3,1},{5,7},{7,5},{8,10},{10,8},{12,... | collective-permute-start | bytes 33800 | tf_op jit(solution)/shard_map/ppermute | solution.py:78
  62.6 42.4 %collective-permute-start.15 = (bf16[1024,896]{1,0:T(8,128)(2,1)S(1)}, bf16[1024,896]{1,0:T(8,128)(2,1)}, u32[]{:S(2)}, u32[]{:S(2)}) collective-permute-start(bf16[1024,896]{1,0:T(8,128)(2,1)S(1)} %bitcast.157), channel_id=1, source_target_pairs={{0,16},{16,0},{1,17},{17,1},{2,18},{18,2},{3,19},{19,3},{4,20},{20... | collective-permute-start | bytes 5505032 | tf_op jit(solution)/shard_map/ppermute | solution.py:33
  73.8 15.2 %collective-permute-start.9 = (bf16[128,2048]{1,0:T(8,128)(2,1)S(1)}, bf16[128,2048]{1,0:T(8,128)(2,1)}, u32[]{:S(2)}, u32[]{:S(2)}) collective-permute-start(bf16[128,2048]{1,0:T(8,128)(2,1)S(1)} %collective-permute-done.6), channel_id=1, source_target_pairs={{0,2},{2,4},{4,6},{6,0},{1,3},{3,5},{5,7},{7,1},{8,10},{10,12},{12... | collective-permute-start | bytes 1572872 | tf_op jit(solution)/shard_map/ppermute | solution.py:53
  74.6 14.4 %collective-permute-start.8 = (bf16[128,2048]{1,0:T(8,128)(2,1)S(1)}, bf16[128,2048]{1,0:T(8,128)(2,1)S(1)}, u32[]{:S(2)}, u32[]{:S(2)}) collective-permute-start(bf16[128,2048]{1,0:T(8,128)(2,1)S(1)} %collective-permute-done.6), channel_id=1, source_target_pairs={{0,1},{1,0},{2,3},{3,2},{4,5},{5,4},{6,7},{7,6},{8,9},{9,8},{10,11... | collective-permute-start | bytes 1572872 | tf_op jit(solution)/shard_map/ppermute | solution.py:33
  76.2 12.8 %collective-permute-start.10 = (bf16[16,704]{1,0:T(8,128)(2,1)S(1)}, bf16[16,704]{1,0:T(8,128)(2,1)S(1)}, u32[]{:S(2)}, u32[]{:S(2)}) collective-permute-start(bf16[16,704]{1,0:T(8,128)(2,1)S(1)} %maximum_select_fusion.5), channel_id=1, source_target_pairs={{0,4},{2,6},{4,0},{6,2},{1,5},{3,7},{5,1},{7,3},{8,12},{10,14},{12... | collective-permute-start | bytes 67592 | tf_op jit(solution)/shard_map/ppermute | solution.py:78
  78.2 26.8 %collective-permute-start.13 = (bf16[256,2048]{1,0:T(8,128)(2,1)}, bf16[256,2048]{1,0:T(8,128)(2,1)}, u32[]{:S(2)}, u32[]{:S(2)}) collective-permute-start(bf16[256,2048]{1,0:T(8,128)(2,1)} %constant_dynamic-update-slice_fusion.refs_0_), channel_id=1, source_target_pairs={{0,8},{8,0},{1,9},{9,1},{2,10},{10,2},{3,11},{11,3},{4,12},{12,4},... | collective-permute-start | bytes 3145736 | tf_op jit(solution)/shard_map/ppermute | solution.py:33
  89.0 16.0 %collective-permute-start.12 = (bf16[128,2048]{1,0:T(8,128)(2,1)}, bf16[128,2048]{1,0:T(8,128)(2,1)}, u32[]{:S(2)}, u32[]{:S(2)}) collective-permute-start(bf16[128,2048]{1,0:T(8,128)(2,1)} %collective-permute-done.9), channel_id=1, source_target_pairs={{0,2},{2,4},{4,6},{6,0},{1,3},{3,5},{5,7},{7,1},{8,10},{10,12},{12... | collective-permute-start | bytes 1572872 | tf_op jit(solution)/shard_map/ppermute | solution.py:53
  89.1 15.8 %collective-permute-start.11 = (bf16[128,2048]{1,0:T(8,128)(2,1)}, bf16[128,2048]{1,0:T(8,128)(2,1)}, u32[]{:S(2)}, u32[]{:S(2)}) collective-permute-start(bf16[128,2048]{1,0:T(8,128)(2,1)} %collective-permute-done.9), channel_id=1, source_target_pairs={{0,1},{1,0},{2,3},{3,2},{4,5},{5,4},{6,7},{7,6},{8,9},{9,8},{10,11... | collective-permute-start | bytes 1572872 | tf_op jit(solution)/shard_map/ppermute | solution.py:33
  90.6 14.4 %collective-permute-start.14 = (bf16[256,2048]{1,0:T(8,128)(2,1)}, bf16[256,2048]{1,0:T(8,128)(2,1)}, u32[]{:S(2)}, u32[]{:S(2)}) collective-permute-start(bf16[256,2048]{1,0:T(8,128)(2,1)} %constant_dynamic-update-slice_fusion.2.refs_1_), channel_id=1, source_target_pairs={{0,8},{8,0},{1,9},{9,1},{2,10},{10,2},{3,11},{11,3},{4,12},{12,4},... | collective-permute-start | bytes 3145736 | tf_op jit(solution)/shard_map/ppermute | solution.py:33
  106.9 20.7 %collective-permute-start.18 = (bf16[256,2048]{1,0:T(8,128)(2,1)}, bf16[256,2048]{1,0:T(8,128)(2,1)S(1)}, u32[]{:S(2)}, u32[]{:S(2)}) collective-permute-start(bf16[256,2048]{1,0:T(8,128)(2,1)} %constant_dynamic-update-slice_fusion.4.refs_0_.refs_4_), channel_id=1, source_target_pairs={{0,8},{8,0},{1,9},{9,1},{2,10},{10,2},{3,11},{11,3},{4,12},{12,4},... | collective-permute-start | bytes 3145736 | tf_op jit(solution)/shard_map/ppermute | solution.py:33
  110.8 16.8 %collective-permute-start.17 = (bf16[128,2048]{1,0:T(8,128)(2,1)S(1)}, bf16[128,2048]{1,0:T(8,128)(2,1)S(1)}, u32[]{:S(2)}, u32[]{:S(2)}) collective-permute-start(bf16[128,2048]{1,0:T(8,128)(2,1)S(1)} %pad_maximum_fusion.1), channel_id=1, source_target_pairs={{0,2},{2,4},{4,6},{6,0},{1,3},{3,5},{5,7},{7,1},{8,10},{10,12},{12... | collective-permute-start | bytes 1572872 | tf_op jit(solution)/shard_map/ppermute | solution.py:53
  110.8 16.8 %collective-permute-start.16 = (bf16[128,2048]{1,0:T(8,128)(2,1)}, bf16[128,2048]{1,0:T(8,128)(2,1)S(1)}, u32[]{:S(2)}, u32[]{:S(2)}) collective-permute-start(bf16[128,2048]{1,0:T(8,128)(2,1)} %collective-permute-done.12), channel_id=1, source_target_pairs={{0,1},{1,0},{2,3},{3,2},{4,5},{5,4},{6,7},{7,6},{8,9},{9,8},{10,11... | collective-permute-start | bytes 1572872 | tf_op jit(solution)/shard_map/ppermute | solution.py:33
  127.6 32.8 %all-to-all-start.1 = ((bf16[16,64,512]{2,1,0:T(8,128)(2,1)}), bf16[16,64,512]{2,1,0:T(8,128)(2,1)}, u32[]{:S(2)}, u32[]{:S(2)}) async-start(bf16[16,64,512]{2,1,0:T(8,128)(2,1)} %get-tuple-element.316), calls=%async_computation.1 | async-start | bytes 2097152 | tf_op jit(solution)/shard_map/all_to_all | solution.py:760
  135.1 2.7 collective-permute-start.19
  135.5 27.2 %collective-permute-start.24 = (bf16[64,2048]{1,0:T(8,128)(2,1)S(1)}, bf16[64,2048]{1,0:T(8,128)(2,1)S(1)}, u32[]{:S(2)}, u32[]{:S(2)}) collective-permute-start(bf16[64,2048]{1,0:T(8,128)(2,1)S(1)} %copy-done.32), channel_id=1, source_target_pairs={{0,16},{16,0},{1,17},{17,1},{2,18},{18,2},{3,19},{19,3},{4,20},{20... | collective-permute-start | bytes 786440 | tf_op jit(solution)/shard_map/ppermute | solution.py:33
  160.6 28.6 %collective-permute-start.20 = (bf16[256,2048]{1,0:T(8,128)(2,1)S(1)}, bf16[256,2048]{1,0:T(8,128)(2,1)}, u32[]{:S(2)}, u32[]{:S(2)}) collective-permute-start(bf16[256,2048]{1,0:T(8,128)(2,1)S(1)} %constant_dynamic-update-slice_fusion.8.refs_0_), channel_id=1, source_target_pairs={{0,1},{1,0},{2,3},{3,2},{4,5},{5,4},{6,7},{7,6},{8,9},{9,8},{10,11... | collective-permute-start | bytes 3145736 | tf_op jit(solution)/shard_map/ppermute | solution.py:33
  161.2 27.9 %collective-permute-start.23 = (bf16[1024,512]{1,0:T(8,128)(2,1)}, bf16[1024,512]{1,0:T(8,128)(2,1)}, u32[]{:S(2)}, u32[]{:S(2)}) collective-permute-start(bf16[1024,512]{1,0:T(8,128)(2,1)} %bitcast.15.own_ref.refs_9_), channel_id=1, source_target_pairs={{0,16},{16,0},{1,17},{17,1},{2,18},{18,2},{3,19},{19,3},{4,20},{20... | collective-permute-start | bytes 3145736 | tf_op jit(solution)/shard_map/ppermute | solution.py:33
  163.6 21.9 %collective-permute-start.22 = (bf16[128,2048]{1,0:T(8,128)(2,1)S(1)}, bf16[128,2048]{1,0:T(8,128)(2,1)S(1)}, u32[]{:S(2)}, u32[]{:S(2)}) collective-permute-start(bf16[128,2048]{1,0:T(8,128)(2,1)S(1)} %pad_maximum_fusion.1), channel_id=1, source_target_pairs={{0,6},{2,0},{4,2},{6,4},{1,7},{3,1},{5,3},{7,5},{8,14},{10,8},{12,... | collective-permute-start | bytes 1572872 | tf_op jit(solution)/shard_map/ppermute | solution.py:862
  164.4 24.7 %collective-permute-start.21 = (bf16[128,2048]{1,0:T(8,128)(2,1)S(1)}, bf16[128,2048]{1,0:T(8,128)(2,1)S(1)}, u32[]{:S(2)}, u32[]{:S(2)}) collective-permute-start(bf16[128,2048]{1,0:T(8,128)(2,1)S(1)} %copy-done.29), channel_id=1, source_target_pairs={{0,2},{2,4},{4,6},{6,0},{1,3},{3,5},{5,7},{7,1},{8,10},{10,12},{12... | collective-permute-start | bytes 1572872 | tf_op jit(solution)/shard_map/ppermute | solution.py:53
  189.3 15.5 %collective-permute-start.28 = (bf16[256,2048]{1,0:T(8,128)(2,1)S(1)}, bf16[256,2048]{1,0:T(8,128)(2,1)S(1)}, u32[]{:S(2)}, u32[]{:S(2)}) collective-permute-start(bf16[256,2048]{1,0:T(8,128)(2,1)S(1)} %constant_dynamic-update-slice_fusion.10.refs_4_), channel_id=1, source_target_pairs={{0,8},{8,0},{1,9},{9,1},{2,10},{10,2},{3,11},{11,3},{4,12},{12,4},... | collective-permute-start | bytes 3145736 | tf_op jit(solution)/shard_map/ppermute | solution.py:33
  189.3 25.7 %collective-permute-start.25 = (bf16[256,2048]{1,0:T(8,128)(2,1)S(1)}, bf16[256,2048]{1,0:T(8,128)(2,1)}, u32[]{:S(2)}, u32[]{:S(2)}) collective-permute-start(bf16[256,2048]{1,0:T(8,128)(2,1)S(1)} %constant_dynamic-update-slice_fusion.10.refs_4_), channel_id=1, source_target_pairs={{0,1},{1,0},{2,3},{3,2},{4,5},{5,4},{6,7},{7,6},{8,9},{9,8},{10,11... | collective-permute-start | bytes 3145736 | tf_op jit(solution)/shard_map/ppermute | solution.py:33
  189.9 25.1 %collective-permute-start.26 = (bf16[256,2048]{1,0:T(8,128)(2,1)S(1)}, bf16[256,2048]{1,0:T(8,128)(2,1)}, u32[]{:S(2)}, u32[]{:S(2)}) collective-permute-start(bf16[256,2048]{1,0:T(8,128)(2,1)S(1)} %constant_dynamic-update-slice_fusion.8.refs_0_), channel_id=1, source_target_pairs={{0,8},{8,0},{1,9},{9,1},{2,10},{10,2},{3,11},{11,3},{4,12},{12,4},... | collective-permute-start | bytes 3145736 | tf_op jit(solution)/shard_map/ppermute | solution.py:33
  190.1 24.9 %collective-permute-start.27 = (bf16[256,2048]{1,0:T(8,128)(2,1)}, bf16[256,2048]{1,0:T(8,128)(2,1)}, u32[]{:S(2)}, u32[]{:S(2)}) collective-permute-start(bf16[256,2048]{1,0:T(8,128)(2,1)} %collective-permute-done.20.refs_1_), channel_id=1, source_target_pairs={{0,8},{8,0},{1,9},{9,1},{2,10},{10,2},{3,11},{11,3},{4,12},{12,4},... | collective-permute-start | bytes 3145736 | tf_op jit(solution)/shard_map/ppermute | solution.py:33
  215.0 2.9 collective-permute-start.29
  217.9 17.1 %collective-permute-start.30 = (bf16[256,2048]{1,0:T(8,128)(2,1)}, bf16[256,2048]{1,0:T(8,128)(2,1)}, u32[]{:S(2)}, u32[]{:S(2)}) collective-permute-start(bf16[256,2048]{1,0:T(8,128)(2,1)} %get-tuple-element.363), channel_id=1, source_target_pairs={{0,8},{8,0},{1,9},{9,1},{2,10},{10,2},{3,11},{11,3},{4,12},{12,4},... | collective-permute-start | bytes 3145736 | tf_op jit(solution)/shard_map/ppermute | solution.py:33
  218.0 17.0 %collective-permute-start.31 = (bf16[256,2048]{1,0:T(8,128)(2,1)}, bf16[256,2048]{1,0:T(8,128)(2,1)}, u32[]{:S(2)}, u32[]{:S(2)}) collective-permute-start(bf16[256,2048]{1,0:T(8,128)(2,1)} %get-tuple-element.364), channel_id=1, source_target_pairs={{0,8},{8,0},{1,9},{9,1},{2,10},{10,2},{3,11},{11,3},{4,12},{12,4},... | collective-permute-start | bytes 3145736 | tf_op jit(solution)/shard_map/ppermute | solution.py:33
  218.4 16.6 %collective-permute-start.32 = (bf16[256,2048]{1,0:T(8,128)(2,1)}, bf16[256,2048]{1,0:T(8,128)(2,1)S(1)}, u32[]{:S(2)}, u32[]{:S(2)}) collective-permute-start(bf16[256,2048]{1,0:T(8,128)(2,1)} %get-tuple-element.365), channel_id=1, source_target_pairs={{0,8},{8,0},{1,9},{9,1},{2,10},{10,2},{3,11},{11,3},{4,12},{12,4},... | collective-permute-start | bytes 3145736 | tf_op jit(solution)/shard_map/ppermute | solution.py:33
  218.6 16.5 %collective-permute-start.33 = (bf16[256,2048]{1,0:T(8,128)(2,1)}, bf16[256,2048]{1,0:T(8,128)(2,1)S(1)}, u32[]{:S(2)}, u32[]{:S(2)}) collective-permute-start(bf16[256,2048]{1,0:T(8,128)(2,1)} %get-tuple-element.366), channel_id=1, source_target_pairs={{0,8},{8,0},{1,9},{9,1},{2,10},{10,2},{3,11},{11,3},{4,12},{12,4},... | collective-permute-start | bytes 3145736 | tf_op jit(solution)/shard_map/ppermute | solution.py:33
  239.4 47.8 %collective-permute-start.35 = (bf16[512,2048]{1,0:T(8,128)(2,1)S(1)}, bf16[512,2048]{1,0:T(8,128)(2,1)}, u32[]{:S(2)}, u32[]{:S(2)}) collective-permute-start(bf16[512,2048]{1,0:T(8,128)(2,1)S(1)} %add_convert_fusion.1), channel_id=1, source_target_pairs={{0,1},{1,0},{2,3},{3,2},{4,5},{5,4},{6,7},{7,6},{8,9},{9,8},{10,11... | collective-permute-start | bytes 6291464 | tf_op jit(solution)/shard_map/ppermute | solution.py:33
  254.6 47.7 %collective-permute-start.34 = (bf16[4,2,128,1024]{3,2,1,0:T(8,128)(2,1)}, bf16[4,2,128,1024]{3,2,1,0:T(8,128)(2,1)}, u32[]{:S(2)}, u32[]{:S(2)}) collective-permute-start(bf16[4,2,128,1024]{3,2,1,0:T(8,128)(2,1)} %get-tuple-element.380), channel_id=1, source_target_pairs={{0,16},{16,0},{1,17},{17,1},{2,18},{18,2},{3,19},{19,3},{4,20},{20... | collective-permute-start | bytes 6291464 | tf_op jit(solution)/shard_map/ppermute | solution.py:33
  288.6 13.6 %collective-permute-start.36 = (bf16[128,2048]{1,0:T(8,128)(2,1)S(1)}, bf16[128,2048]{1,0:T(8,128)(2,1)S(1)}, u32[]{:S(2)}, u32[]{:S(2)}) collective-permute-start(bf16[128,2048]{1,0:T(8,128)(2,1)S(1)} %convert_add_fusion.10), channel_id=1, source_target_pairs={{2,0},{4,2},{6,4},{0,6},{3,1},{5,3},{7,5},{1,7},{10,8},{12,10},{14... | collective-permute-start | bytes 1572872 | tf_op jit(solution)/shard_map/ppermute | solution.py:70
  306.4 51.3 %all-to-all-start.2 = ((bf16[4,2,128,1024]{3,2,1,0:T(8,128)(2,1)}), bf16[4,2,128,1024]{3,2,1,0:T(8,128)(2,1)S(1)}, u32[]{:S(2)}, u32[]{:S(2)}) async-start(bf16[4,2,128,1024]{3,2,1,0:T(8,128)(2,1)} %add_convert_fusion), calls=%async_computation.2 | async-start | bytes 4194304 | tf_op jit(solution)/shard_map/all_to_all | solution.py:767
  311.0 21.9 %collective-permute-start.37 = (bf16[4,2,128,384]{3,2,1,0:T(8,128)(2,1)}, bf16[4,2,128,384]{3,2,1,0:T(8,128)(2,1)S(1)}, u32[]{:S(2)}, u32[]{:S(2)}) collective-permute-start(bf16[4,2,128,384]{3,2,1,0:T(8,128)(2,1)} %get-tuple-element.416), channel_id=1, source_target_pairs={{0,16},{16,0},{1,17},{17,1},{2,18},{18,2},{3,19},{19,3},{4,20},{20... | collective-permute-start | bytes 2359304 | tf_op jit(solution)/shard_map/ppermute | solution.py:33
  338.0 12.1 %collective-permute-start.38 = (bf16[256,2048]{1,0:T(8,128)(2,1)}, bf16[256,2048]{1,0:T(8,128)(2,1)}, u32[]{:S(2)}, u32[]{:S(2)}) collective-permute-start(bf16[256,2048]{1,0:T(8,128)(2,1)} %get-tuple-element.419), channel_id=1, source_target_pairs={{0,8},{8,0},{1,9},{9,1},{2,10},{10,2},{3,11},{11,3},{4,12},{12,4},... | collective-permute-start | bytes 3145736 | tf_op jit(solution)/shard_map/ppermute | solution.py:33
  338.0 12.0 %collective-permute-start.39 = (bf16[256,2048]{1,0:T(8,128)(2,1)}, bf16[256,2048]{1,0:T(8,128)(2,1)}, u32[]{:S(2)}, u32[]{:S(2)}) collective-permute-start(bf16[256,2048]{1,0:T(8,128)(2,1)} %get-tuple-element.420), channel_id=1, source_target_pairs={{0,8},{8,0},{1,9},{9,1},{2,10},{10,2},{3,11},{11,3},{4,12},{12,4},... | collective-permute-start | bytes 3145736 | tf_op jit(solution)/shard_map/ppermute | solution.py:33
  338.5 11.5 %collective-permute-start.40 = (bf16[256,2048]{1,0:T(8,128)(2,1)}, bf16[256,2048]{1,0:T(8,128)(2,1)S(1)}, u32[]{:S(2)}, u32[]{:S(2)}) collective-permute-start(bf16[256,2048]{1,0:T(8,128)(2,1)} %get-tuple-element.421), channel_id=1, source_target_pairs={{0,8},{8,0},{1,9},{9,1},{2,10},{10,2},{3,11},{11,3},{4,12},{12,4},... | collective-permute-start | bytes 3145736 | tf_op jit(solution)/shard_map/ppermute | solution.py:33
  338.6 11.4 %collective-permute-start.41 = (bf16[256,2048]{1,0:T(8,128)(2,1)}, bf16[256,2048]{1,0:T(8,128)(2,1)}, u32[]{:S(2)}, u32[]{:S(2)}) collective-permute-start(bf16[256,2048]{1,0:T(8,128)(2,1)} %get-tuple-element.422), channel_id=1, source_target_pairs={{0,8},{8,0},{1,9},{9,1},{2,10},{10,2},{3,11},{11,3},{4,12},{12,4},... | collective-permute-start | bytes 3145736 | tf_op jit(solution)/shard_map/ppermute | solution.py:33
  363.4 29.2 %all-to-all-start.3 = ((bf16[4,2,128,384]{3,2,1,0:T(8,128)(2,1)}), bf16[4,2,128,384]{3,2,1,0:T(8,128)(2,1)S(1)}, u32[]{:S(2)}, u32[]{:S(2)}) async-start(bf16[4,2,128,384]{3,2,1,0:T(8,128)(2,1)} %add_convert_fusion.4), calls=%async_computation.3 | async-start | bytes 1572864 | tf_op jit(solution)/shard_map/all_to_all | solution.py:767
  366.9 25.7 %collective-permute-start.42 = (bf16[256,2048]{1,0:T(8,128)(2,1)}, bf16[256,2048]{1,0:T(8,128)(2,1)}, u32[]{:S(2)}, u32[]{:S(2)}) collective-permute-start(bf16[256,2048]{1,0:T(8,128)(2,1)} %add_convert_fusion.2), channel_id=1, source_target_pairs={{0,1},{1,0},{2,3},{3,2},{4,5},{5,4},{6,7},{7,6},{8,9},{9,8},{10,11... | collective-permute-start | bytes 3145736 | tf_op jit(solution)/shard_map/ppermute | solution.py:33
  368.4 24.1 %collective-permute-start.43 = (bf16[128,2048]{1,0:T(8,128)(2,1)}, bf16[128,2048]{1,0:T(8,128)(2,1)S(1)}, u32[]{:S(2)}, u32[]{:S(2)}) collective-permute-start(bf16[128,2048]{1,0:T(8,128)(2,1)} %convert_add_fusion.9), channel_id=1, source_target_pairs={{2,0},{4,2},{6,4},{0,6},{3,1},{5,3},{7,5},{1,7},{10,8},{12,10},{14... | collective-permute-start | bytes 1572872 | tf_op jit(solution)/shard_map/ppermute | solution.py:70
  397.5 31.6 %collective-permute-start.44 = (bf16[256,2048]{1,0:T(8,128)(2,1)}, bf16[256,2048]{1,0:T(8,128)(2,1)}, u32[]{:S(2)}, u32[]{:S(2)}) collective-permute-start(bf16[256,2048]{1,0:T(8,128)(2,1)} %add_convert_fusion.3), channel_id=1, source_target_pairs={{0,1},{1,0},{2,3},{3,2},{4,5},{5,4},{6,7},{7,6},{8,9},{9,8},{10,11... | collective-permute-start | bytes 3145736 | tf_op jit(solution)/shard_map/ppermute | solution.py:33
  400.8 32.1 %collective-permute-start.61 = (bf16[64,2048]{1,0:T(8,128)(2,1)S(1)}, bf16[64,2048]{1,0:T(8,128)(2,1)S(1)}, u32[]{:S(2)}, u32[]{:S(2)}) collective-permute-start(bf16[64,2048]{1,0:T(8,128)(2,1)S(1)} %fusion.30), channel_id=1, source_target_pairs={{0,16},{16,0},{1,17},{17,1},{2,18},{18,2},{3,19},{19,3},{4,20},{20... | collective-permute-start | bytes 786440 | tf_op jit(solution)/shard_map/ppermute | solution.py:33
  401.4 18.7 %collective-permute-start.45 = (bf16[128,2048]{1,0:T(8,128)(2,1)}, bf16[128,2048]{1,0:T(8,128)(2,1)S(1)}, u32[]{:S(2)}, u32[]{:S(2)}) collective-permute-start(bf16[128,2048]{1,0:T(8,128)(2,1)} %convert_add_fusion.8), channel_id=1, source_target_pairs={{2,0},{4,2},{6,4},{0,6},{3,1},{5,3},{7,5},{1,7},{10,8},{12,10},{14... | collective-permute-start | bytes 1572872 | tf_op jit(solution)/shard_map/ppermute | solution.py:70
  407.3 21.8 %collective-permute-start.46 = (bf16[128,2048]{1,0:T(8,128)(2,1)S(1)}, bf16[128,2048]{1,0:T(8,128)(2,1)S(1)}, u32[]{:S(2)}, u32[]{:S(2)}) collective-permute-start(bf16[128,2048]{1,0:T(8,128)(2,1)S(1)} %convert_add_fusion.7), channel_id=1, source_target_pairs={{2,0},{4,2},{6,4},{0,6},{3,1},{5,3},{7,5},{1,7},{10,8},{12,10},{14... | collective-permute-start | bytes 1572872 | tf_op jit(solution)/shard_map/ppermute | solution.py:70
  432.3 23.1 %collective-permute-start.51 = (bf16[4,2,64,1024]{3,2,0,1:T(8,128)(2,1)S(1)}, bf16[4,2,64,1024]{3,2,0,1:T(8,128)(2,1)S(1)}, u32[]{:S(2)}, u32[]{:S(2)}) collective-permute-start(bf16[4,2,64,1024]{3,2,0,1:T(8,128)(2,1)S(1)} %get-tuple-element.471), channel_id=1, source_target_pairs={{0,1},{1,0},{2,3},{3,2},{4,5},{5,4},{6,7},{7,6},{8,9},{9,8},{10,11... | collective-permute-start | bytes 3145736 | tf_op jit(solution)/shard_map/ppermute | solution.py:33
  433.8 6.6 %collective-permute-start.50 = (f32[1,4,2,640]{3,2,1,0:T(2,128)S(1)}, f32[1,4,2,640]{3,2,1,0:T(2,128)S(1)}, u32[]{:S(2)}, u32[]{:S(2)}) collective-permute-start(f32[1,4,2,640]{3,2,1,0:T(2,128)S(1)} %get-tuple-element.467), channel_id=1, source_target_pairs={{0,16},{16,0},{1,17},{17,1},{2,18},{18,2},{3,19},{19,3},{4,20},{20... | collective-permute-start | bytes 61448 | tf_op jit(solution)/shard_map/ppermute | solution.py:33
  435.2 6.4 %collective-permute-start.49 = (bf16[64,2048]{1,0:T(8,128)(2,1)S(1)}, bf16[64,2048]{1,0:T(8,128)(2,1)S(1)}, u32[]{:S(2)}, u32[]{:S(2)}) collective-permute-start(bf16[64,2048]{1,0:T(8,128)(2,1)S(1)} %slice.261), channel_id=1, source_target_pairs={{0,16},{16,0},{1,17},{17,1},{2,18},{18,2},{3,19},{19,3},{4,20},{20... | collective-permute-start | bytes 786440 | tf_op jit(solution)/shard_map/ppermute | solution.py:33
  435.8 10.8 %collective-permute-start.48 = (bf16[128,2048]{1,0:T(8,128)(2,1)S(1)}, bf16[128,2048]{1,0:T(8,128)(2,1)S(1)}, u32[]{:S(2)}, u32[]{:S(2)}) collective-permute-start(bf16[128,2048]{1,0:T(8,128)(2,1)S(1)} %convert_add_fusion.6), channel_id=1, source_target_pairs={{2,0},{4,2},{6,4},{0,6},{3,1},{5,3},{7,5},{1,7},{10,8},{12,10},{14... | collective-permute-start | bytes 1572872 | tf_op jit(solution)/shard_map/ppermute | solution.py:70
  455.6 8.4 %collective-permute-start.53 = (f32[1,4,640]{2,0,1:T(1,128)S(1)}, f32[1,4,640]{2,0,1:T(1,128)S(1)}, u32[]{:S(2)}, u32[]{:S(2)}) collective-permute-start(f32[1,4,640]{2,0,1:T(1,128)S(1)} %get-tuple-element.481), channel_id=1, source_target_pairs={{0,1},{1,0},{2,3},{3,2},{4,5},{5,4},{6,7},{7,6},{8,9},{9,8},{10,11... | collective-permute-start | bytes 30728 | tf_op jit(solution)/shard_map/ppermute | solution.py:33
  456.2 15.8 %collective-permute-start.57 = (bf16[4,2,64,384]{3,2,0,1:T(8,128)(2,1)}, bf16[4,2,64,384]{3,2,0,1:T(8,128)(2,1)S(1)}, u32[]{:S(2)}, u32[]{:S(2)}) collective-permute-start(bf16[4,2,64,384]{3,2,0,1:T(8,128)(2,1)} %get-tuple-element.484), channel_id=1, source_target_pairs={{0,1},{1,0},{2,3},{3,2},{4,5},{5,4},{6,7},{7,6},{8,9},{9,8},{10,11... | collective-permute-start | bytes 1179656 | tf_op jit(solution)/shard_map/ppermute | solution.py:33
  457.7 14.2 %collective-permute-start.52 = (bf16[128,2048]{1,0:T(8,128)(2,1)S(1)}, bf16[128,2048]{1,0:T(8,128)(2,1)S(1)}, u32[]{:S(2)}, u32[]{:S(2)}) collective-permute-start(bf16[128,2048]{1,0:T(8,128)(2,1)S(1)} %convert_add_fusion.2), channel_id=1, source_target_pairs={{2,0},{4,2},{6,4},{0,6},{3,1},{5,3},{7,5},{1,7},{10,8},{12,10},{14... | collective-permute-start | bytes 1572872 | tf_op jit(solution)/shard_map/ppermute | solution.py:70
  460.6 4.4 collective-permute-start.58
  464.0 7.9 %collective-permute-start.56 = (f32[1,640]{1,0:T(1,128)S(1)}, f32[1,640]{1,0:T(1,128)S(1)}, u32[]{:S(2)}, u32[]{:S(2)}) collective-permute-start(f32[1,640]{1,0:T(1,128)S(1)} %get-tuple-element.588), channel_id=1, source_target_pairs={{0,6},{2,0},{4,2},{6,4},{1,7},{3,1},{5,3},{7,5},{8,14},{10,8},{12,... | collective-permute-start | bytes 7688 | tf_op jit(solution)/shard_map/ppermute | solution.py:993
  464.1 7.8 %collective-permute-start.55 = (f32[1,640]{1,0:T(1,128)S(1)}, f32[1,640]{1,0:T(1,128)S(1)}, u32[]{:S(2)}, u32[]{:S(2)}) collective-permute-start(f32[1,640]{1,0:T(1,128)S(1)} %get-tuple-element.589), channel_id=1, source_target_pairs={{0,4},{2,6},{4,0},{6,2},{1,5},{3,7},{5,1},{7,3},{8,12},{10,14},{12... | collective-permute-start | bytes 7688 | tf_op jit(solution)/shard_map/ppermute | solution.py:993
  465.0 7.0 %collective-permute-start.54 = (f32[1,640]{1,0:T(1,128)S(1)}, f32[1,640]{1,0:T(1,128)S(1)}, u32[]{:S(2)}, u32[]{:S(2)}) collective-permute-start(f32[1,640]{1,0:T(1,128)S(1)} %get-tuple-element.590), channel_id=1, source_target_pairs={{0,2},{2,4},{4,6},{6,0},{1,3},{3,5},{5,7},{7,1},{8,10},{10,12},{12... | collective-permute-start | bytes 7688 | tf_op jit(solution)/shard_map/ppermute | solution.py:993
  472.8 7.1 %collective-permute-start.59 = (bf16[64,2048]{1,0:T(8,128)(2,1)S(1)}, bf16[64,2048]{1,0:T(8,128)(2,1)S(1)}, u32[]{:S(2)}, u32[]{:S(2)}) collective-permute-start(bf16[64,2048]{1,0:T(8,128)(2,1)S(1)} %slice.260), channel_id=1, source_target_pairs={{0,16},{16,0},{1,17},{17,1},{2,18},{18,2},{3,19},{19,3},{4,20},{20... | collective-permute-start | bytes 786440 | tf_op jit(solution)/shard_map/ppermute | solution.py:33
  475.7 6.1 %collective-permute-start.60 = (bf16[2,4,64,384]{3,2,1,0:T(8,128)(2,1)S(1)}, bf16[2,4,64,384]{3,2,1,0:T(8,128)(2,1)S(1)}, u32[]{:S(2)}, u32[]{:S(2)}) collective-permute-start(bf16[2,4,64,384]{3,2,1,0:T(8,128)(2,1)S(1)} %get-tuple-element.562), channel_id=1, source_target_pairs={{0,8},{8,0},{1,9},{9,1},{2,10},{10,2},{3,11},{11,3},{4,12},{12,4},... | collective-permute-start | bytes 1179656 | tf_op jit(solution)/shard_map/ppermute | solution.py:33
  (54 other events, 501.0 us)

commit v6 on v5

--- a/solution.py
+++ b/solution.py
@@ -800,17 +800,19 @@
     small = joined(by, small, swap(small, "by"))
     small = joined(core, small, swap(small, "core"))
     more = swap(small, "hx")
-    cosine, sine = turn_tables(row_pos)
-
-    x_0, in_own, g_b, small, more, cosine, sine = fence((x_0, in_own, g_b, small, more, cosine, sine), table)
+
+    x_0, in_own, g_b, small, more, row_pos = fence((x_0, in_own, g_b, small, more, row_pos), table)
     in_other = swap(in_own, "hx")
+    small = joined(hx, small, more)
+
+    x_0, small, row_pos = fence((x_0, small, row_pos))
     y_0 = swap(x_0, "by")
     x_1 = ring(x_0)
     g_0 = both(g_a, g_b)
-    small = joined(hx, small, more)
     more = across(small, 1)
-
-    y_0, x_1, g_0, small, more = fence((y_0, x_1, g_0, small, more))
+    cosine, sine = turn_tables(row_pos)
+
+    y_0, x_1, g_0, small, more, cosine, sine = fence((y_0, x_1, g_0, small, more, cosine, sine))
     y_1 = swap(x_1, "by")
     x_2 = ring(x_1)
     small = joined(bz % 2, small, more)

time: 496 us -> 500 us (level)
    unnamed x111 -> x117, local copies, waits for them, and re-layouts: 9.32 us -> 14.1 us
  transfers between devices with their start and end apart: 66 -> 66, of which waited for: 22 -> 23; matrix products, arithmetic and copies ran while one was open for 12% -> 12% of each run, Pallas kernels for 32% -> 32%
where the time goes in v6:
time: 500 us; the launch traced here: 491 us
  Pallas kernels  162 us (32%)
  waiting for transfers between devices  156 us (31%)
  starting transfers between devices  78.1 us (16%)
  other arithmetic  45.7 us (9%)
  local copies, waits for them, and re-layouts  40 us (8%)
  matrix products  5.7 us (1%)
    ppermute x6, waiting for transfers between devices, ring_back(): return lax.ppermute(total.astype(BF), 'bz', DOWN)  44.5 us
    ppermute x45, waiting for transfers between devices, swap(): return lax.ppermute(value, axis, SWAP)  39 us
    all_to_all x2, waiting for transfers between devices, to_cols(): got = lax.all_to_all(sent, RANK, split_axis=0, concat_axis=0, tiled=True)  33.8 us
    ppermute x45, starting transfers between devices, swap(): return lax.ppermute(value, axis, SWAP)  29.2 us
    pallas_call x2, Pallas kernels, front(): pl.pallas_call(functools.partial(front_kernel, pieces), grid_spec=pltpu.P...  28.4 us
    pallas_call x1, Pallas kernels, attend_back(): pl.pallas_call(functools.partial(attend_back_kernel, blocks, block), grid...  24.9 us
    pallas_call x1, Pallas kernels, back_partial(): pl.pallas_call(functools.partial(back_kernel, pieces), grid_spec=pltpu.Pr...  21.3 us
    pallas_call x1, Pallas kernels, attend(): pl.pallas_call(functools.partial(attend_kernel, block), grid_spec=pltpu.P...  19.7 us
  transfers between devices with their start and end apart: 66, of which 23 were waited for; matrix products, arithmetic and copies ran while one was open for 12% of the time, Pallas kernels for 32%

profile of v6, /device:TPU:0, one launch (start us, length us, event | category | flops | bytes accessed | tf_op | source)
XLA Modules:
  0.0 490.5 jit_solution(8941512018656991368)
XLA Ops:
  1.7 3.7 shard_map.229
  5.5 7.5 %all-to-all-start = ((bf16[16,64,896]{2,1,0:T(8,128)(2,1)}), bf16[16,64,896]{2,1,0:T(8,128)(2,1)S(1)}, u32[]{:S(2)}, u32[]{:S(2)}) async-start(bf16[16,64,896]{2,1,0:T(8,128)(2,1)} %get-tuple-element.262), calls=%async_computation | async-start | bytes 3670016 | tf_op jit(solution)/shard_map/all_to_all | solution.py:760
  13.2 2.0 collective-permute-start.2
  15.2 1.5 collective-permute-start
  22.7 1.6 collective-permute-start.4
  26.0 3.0 collective-permute-done.4
  29.0 26.3 %all-to-all-done = bf16[16,64,896]{2,1,0:T(8,128)(2,1)S(1)} async-done(((bf16[16,64,896]{2,1,0:T(8,128)(2,1)}), bf16[16,64,896]{2,1,0:T(8,128)(2,1)S(1)}, u32[]{:S(2)}, u32[]{:S(2)}) %all-to-all-start) | async-done | bytes 1835040 | tf_op jit(solution)/shard_map/all_to_all | solution.py:760
  55.4 2.6 collective-permute-start.6
  59.9 1.5 collective-permute-start.15
  63.9 6.5 %collective-permute-done.7 = bf16[8,704]{1,0:T(8,128)(2,1)S(1)} collective-permute-done((bf16[8,704]{1,0:T(8,128)(2,1)S(1)}, bf16[8,704]{1,0:T(8,128)(2,1)S(1)}, u32[]{:S(2)}, u32[]{:S(2)}) %collective-permute-start.7) | collective-permute-done | bytes 11296 | tf_op jit(solution)/shard_map/ppermute | solution.py:78
  73.1 1.6 collective-permute-start.8
  76.8 10.7 %collective-permute-done.10 = bf16[16,704]{1,0:T(8,128)(2,1)S(1)} collective-permute-done((bf16[16,704]{1,0:T(8,128)(2,1)S(1)}, bf16[16,704]{1,0:T(8,128)(2,1)S(1)}, u32[]{:S(2)}, u32[]{:S(2)}) %collective-permute-start.10) | collective-permute-done | bytes 22560 | tf_op jit(solution)/shard_map/ppermute | solution.py:78
  91.5 1.9 constant_dynamic-update-slice_fusion.5
  93.4 10.2 %collective-permute-done.12 = bf16[128,2048]{1,0:T(8,128)(2,1)} collective-permute-done((bf16[128,2048]{1,0:T(8,128)(2,1)}, bf16[128,2048]{1,0:T(8,128)(2,1)}, u32[]{:S(2)}, u32[]{:S(2)}) %collective-permute-start.12) | collective-permute-done | bytes 524320 | tf_op jit(solution)/shard_map/ppermute | solution.py:53
  103.6 1.9 constant_dynamic-update-slice_fusion.4.refs_0_.refs_4_
  106.8 2.6 copy.90.refs_10_.sin_ref
  112.0 14.2 %shard_map.230 = (bf16[2048,2048]{1,0:T(8,128)(2,1)}, bf16[2048,128]{1,0:T(8,128)(2,1)}, bf16[2048,256]{1,0:T(8,128)(2,1)}, f32[2048,512]{1,0:T(8,128)}, bf16[20...) custom-call(s32[1]{0:T(128)} %bitcast.plane_ref, ...), custom_call_target="tpu_custom_call" | custom-call | flops 3783262208 | bytes 12582912 | tf_op jit(solution)/shard_map/pallas_call | solution.py:171
  127.3 6.2 %all-to-all-start.1 = ((bf16[16,64,512]{2,1,0:T(8,128)(2,1)}), bf16[16,64,512]{2,1,0:T(8,128)(2,1)}, u32[]{:S(2)}, u32[]{:S(2)}) async-start(bf16[16,64,512]{2,1,0:T(8,128)(2,1)} %get-tuple-element.324), calls=%async_computation.1 | async-start | bytes 2097152 | tf_op jit(solution)/shard_map/all_to_all | solution.py:760
  138.4 14.2 %shard_map.231 = (bf16[2048,2048]{1,0:T(8,128)(2,1)}, bf16[2048,128]{1,0:T(8,128)(2,1)}, bf16[2048,256]{1,0:T(8,128)(2,1)}, f32[2048,512]{1,0:T(8,128)}, bf16[20...) custom-call(s32[1]{0:T(128)} %bitcast.plane_ref, ...), custom_call_target="tpu_custom_call", output_to_operand_aliasing={{0}: (12, {}), {1}: (13, {}), {2}: (14, {}), {3}: (15, {}),... | custom-call | flops 3783262208 | bytes 12582912 | tf_op jit(solution)/shard_map/pallas_call | solution.py:171
  152.6 7.5 %all-to-all-done.1 = bf16[16,64,512]{2,1,0:T(8,128)(2,1)} async-done(((bf16[16,64,512]{2,1,0:T(8,128)(2,1)}), bf16[16,64,512]{2,1,0:T(8,128)(2,1)}, u32[]{:S(2)}, u32[]{:S(2)}) %all-to-all-start.1) | async-done | bytes 1048608 | tf_op jit(solution)/shard_map/all_to_all | solution.py:760
  163.8 1.9 maximum_select_fusion.3.dense_ref.refs_8_
  167.9 19.7 %shard_map.232 = (f32[2,2,2,2,128,128]{5,4,3,2,1,0:T(8,128)}, bf16[2,2,2,2,128,128]{5,4,3,2,1,0:T(8,128)(2,1)}, f32[8,8,512]{2,1,0:T(8,128)}) custom-call(s32[2]{0:T(128)} %compare_select_fusion.9.meta_ref, s32[8]{0:T(128)} %copy-done.54, s32[8]{0:T(128)} %select_reduce_fusion.order_ref, bf16[2,2,2,2,128,128]{5,4,3,2,1,0:T(8,128)(2,1)} %bitcast.173, ...), custom_call_target="tpu_custom_call" | custom-call | flops 8589934592 | bytes 4194304 | tf_op jit(solution)/shard_map/pallas_call | solution.py:298
  187.6 3.7 collective-permute-done.21
  193.8 14.4 %shard_map.233 = (bf16[256,2048]{1,0:T(8,128)(2,1)}, bf16[256,2048]{1,0:T(8,128)(2,1)}, bf16[256,2048]{1,0:T(8,128)(2,1)}, bf16[256,2048]{1,0:T(8,128)(2,1)}, bf...) custom-call(s32[1]{0:T(128)} %bitcast.plane_ref, ...), custom_call_target="tpu_custom_call" | custom-call | flops 5368709120 | bytes 8388608 | tf_op jit(solution)/shard_map/pallas_call | solution.py:419
  208.2 9.9 %collective-permute-done.25.refs_5_ = bf16[256,2048]{1,0:T(8,128)(2,1)} collective-permute-done((bf16[256,2048]{1,0:T(8,128)(2,1)S(1)}, bf16[256,2048]{1,0:T(8,128)(2,1)}, u32[]{:S(2)}, u32[]{:S(2)}) %collective-permute-start.25) | collective-permute-done | bytes 1048608 | tf_op jit(solution)/shard_map/ppermute | solution.py:33
  218.1 2.9 collective-permute-done.29.refs_7_
  222.5 16.1 %shard_map.234 = (bf16[2048,128]{1,0:T(8,128)(2,1)}, bf16[2048,512]{1,0:T(8,128)(2,1)}, bf16[2048,2048]{1,0:T(8,128)(2,1)}) custom-call(s32[1]{0:T(128)} %bitcast.plane_ref, bf16[256,2048]{1,0:T(8,128)(2,1)} %constant_dynamic-update-slice_fusion.8.refs_0_, bf16[256,2048]{1,0:T(8,128)(2,1)} %copy-done.48, bf16[256,2048]{1,0:T(8,128)(2,1)} %collective-permute-done.26.refs_2_, ...), custom_call_target="tpu_custom_call" | custom-call | flops 5368709120 | bytes 16777216 | tf_op jit(solution)/shard_map/pallas_call | solution.py:454
  240.0 2.9 add_convert_fusion.1
  243.5 14.7 %shard_map.235 = (bf16[4,2,128,1024]{3,2,1,0:T(8,128)(2,1)}, bf16[4,2,128,1024]{3,2,1,0:T(8,128)(2,1)}) custom-call(s32[1]{0:T(128)} %bitcast.plane_ref, bf16[2048,2048]{1,0:T(8,128)(2,1)} %get-tuple-element.438.refs_0_, bf16[2048,512]{1,0:T(8,128)(2,1)} %get-tuple-element.336.units_ref.refs_1_, bf16[2048,2048]{1,0:T(8,128)(2,1)} %get-tuple-element.383.refs_2_.h_ref, ...), custom_call_target="tpu_custom_call" | custom-call | flops 8589934592 | bytes 8388608 | tf_op jit(solution)/shard_map/pallas_call | solution.py:567
  258.7 24.9 %shard_map.236 = (bf16[2,2,2,2,128,128]{5,4,3,2,1,0:T(8,128)(2,1)}, bf16[2,2,2,2,128,256]{5,4,3,2,1,0:T(8,128)(2,1)}) custom-call(s32[2]{0:T(128)} %compare_select_fusion.9.meta_ref, s32[8]{0:T(128)} %copy-done.54, s32[8]{0:T(128)} %select_reduce_fusion.order_ref, bf16[2,2,2,2,128,128]{5,4,3,2,1,0:T(8,128)(2,1)} %bitcast.174, ...), custom_call_target="tpu_custom_call" | custom-call | flops 21474836480 | bytes 6291456 | tf_op jit(solution)/shard_map/pallas_call | solution.py:370
  283.7 7.1 %collective-permute-done.35 = bf16[512,2048]{1,0:T(8,128)(2,1)} collective-permute-done((bf16[512,2048]{1,0:T(8,128)(2,1)S(1)}, bf16[512,2048]{1,0:T(8,128)(2,1)}, u32[]{:S(2)}, u32[]{:S(2)}) %collective-permute-start.35) | collective-permute-done | bytes 2097184 | tf_op jit(solution)/shard_map/ppermute | solution.py:33
  292.2 1.8 collective-permute-start.36
  294.0 11.2 %shard_map.237 = (bf16[4,2,128,384]{3,2,1,0:T(8,128)(2,1)}, bf16[4,2,128,384]{3,2,1,0:T(8,128)(2,1)}, bf16[2048,384]{1,0:T(8,128)(2,1)}) custom-call(s32[1]{0:T(128)} %bitcast.plane_ref, bf16[2048,2048]{1,0:T(8,128)(2,1)} %get-tuple-element.383.refs_2_.h_ref, bf16[2048,128]{1,0:T(8,128)(2,1)} %bitcast.175, bf16[2048,256]{1,0:T(8,128)(2,1)} %bitcast.170, ...), custom_call_target="tpu_custom_call" | custom-call | flops 3221225472 | bytes 8388608 | tf_op jit(solution)/shard_map/pallas_call | solution.py:607
  305.9 4.1 add_convert_fusion
  310.0 4.4 all-to-all-start.2
  315.2 21.3 %shard_map.238 = (bf16[256,2048]{1,0:T(8,128)(2,1)}, bf16[256,2048]{1,0:T(8,128)(2,1)}, bf16[256,2048]{1,0:T(8,128)(2,1)}, bf16[256,2048]{1,0:T(8,128)(2,1)}, bf...) custom-call(s32[1]{0:T(128)} %bitcast.plane_ref, ...), custom_call_target="tpu_custom_call" | custom-call | flops 7516192768 | bytes 16777216 | tf_op jit(solution)/shard_map/pallas_call | solution.py:510
  343.0 2.6 add_convert_fusion.4
  345.6 2.3 convert_add_fusion.9
  347.9 5.7 %fusion.43 = f32[2048,128]{0,1:T(8,128)} fusion(bf16[2048,2048]{1,0:T(8,128)(2,1)} %get-tuple-element.438.refs_0_, bf16[2048,128]{1,0:T(8,128)(2,1)S(1)} %bitcast.188), kind=kOutput, calls=%fused_computation.185 | convolution fusion | flops 1073741824 | bytes 9961472 | tf_op jit(solution)/shard_map/dot_general | solution.py:41
  353.6 7.7 %all-to-all-done.2 = bf16[4,2,128,1024]{3,2,1,0:T(8,128)(2,1)S(1)} async-done(((bf16[4,2,128,1024]{3,2,1,0:T(8,128)(2,1)}), bf16[4,2,128,1024]{3,2,1,0:T(8,128)(2,1)S(1)}, u32[]{:S(2)}, u32[]{:S(2)}) %all-to-all-start.2) | async-done | bytes 2097184 | tf_op jit(solution)/shard_map/all_to_all | solution.py:767
  361.4 3.0 add_convert_fusion.3
  364.4 2.6 add_convert_fusion.2
  367.0 3.5 all-to-all-start.3
  370.5 1.6 collective-permute-start.42
  372.0 4.0 collective-permute-start.43
  376.7 19.5 %collective-permute-done.43 = bf16[128,2048]{1,0:T(8,128)(2,1)S(1)} collective-permute-done((bf16[128,2048]{1,0:T(8,128)(2,1)}, bf16[128,2048]{1,0:T(8,128)(2,1)S(1)}, u32[]{:S(2)}, u32[]{:S(2)}) %collective-permute-start.43) | collective-permute-done | bytes 524320 | tf_op jit(solution)/shard_map/ppermute | solution.py:70
  396.9 1.9 convert_add_fusion.7
  398.8 2.2 convert_add_fusion.8
  401.1 1.5 collective-permute-start.44
  405.0 5.9 %collective-permute-start.45 = (bf16[128,2048]{1,0:T(8,128)(2,1)}, bf16[128,2048]{1,0:T(8,128)(2,1)S(1)}, u32[]{:S(2)}, u32[]{:S(2)}) collective-permute-start(bf16[128,2048]{1,0:T(8,128)(2,1)} %convert_add_fusion.8), channel_id=1, source_target_pairs={{2,0},{4,2},{6,4},{0,6},{3,1},{5,3},{7,5},{1,7},{10,8},{12,10},{14... | collective-permute-start | bytes 1572872 | tf_op jit(solution)/shard_map/ppermute | solution.py:70
  412.7 11.0 %collective-permute-done.45 = bf16[128,2048]{1,0:T(8,128)(2,1)S(1)} collective-permute-done((bf16[128,2048]{1,0:T(8,128)(2,1)}, bf16[128,2048]{1,0:T(8,128)(2,1)S(1)}, u32[]{:S(2)}, u32[]{:S(2)}) %collective-permute-start.45) | collective-permute-done | bytes 524320 | tf_op jit(solution)/shard_map/ppermute | solution.py:70
  423.8 9.0 %collective-permute-done.46 = bf16[128,2048]{1,0:T(8,128)(2,1)S(1)} collective-permute-done((bf16[128,2048]{1,0:T(8,128)(2,1)S(1)}, bf16[128,2048]{1,0:T(8,128)(2,1)S(1)}, u32[]{:S(2)}, u32[]{:S(2)}) %collective-permute-start.46) | collective-permute-done | bytes 524320 | tf_op jit(solution)/shard_map/ppermute | solution.py:70
  434.1 1.7 convert_add_fusion.6
  437.4 1.5 collective-permute-start.50
  439.4 2.8 collective-permute-start.48
  442.2 1.7 convert_add_fusion.3
  445.2 5.0 %collective-permute-done.48 = bf16[128,2048]{1,0:T(8,128)(2,1)S(1)} collective-permute-done((bf16[128,2048]{1,0:T(8,128)(2,1)S(1)}, bf16[128,2048]{1,0:T(8,128)(2,1)S(1)}, u32[]{:S(2)}, u32[]{:S(2)}) %collective-permute-start.48) | collective-permute-done | bytes 524320 | tf_op jit(solution)/shard_map/ppermute | solution.py:70
  450.2 8.8 %collective-permute-done.51 = bf16[4,2,64,1024]{3,2,0,1:T(8,128)(2,1)S(1)} collective-permute-done((bf16[4,2,64,1024]{3,2,0,1:T(8,128)(2,1)S(1)}, bf16[4,2,64,1024]{3,2,0,1:T(8,128)(2,1)S(1)}, u32[]{:S(2)}, u32[]{:S(2)}) %collective-permute-start.51) | collective-permute-done | bytes 1048608 | tf_op jit(solution)/shard_map/ppermute | solution.py:33
  459.8 1.5 collective-permute-start.57
  461.3 2.7 collective-permute-start.52
  471.1 4.5 shard_map.239
  476.4 1.6 collective-permute-start.59
  480.2 3.4 collective-permute-done.59
  486.2 3.4 shard_map.240
  (326 shorter events, 77.4 us)
Async XLA Ops:
  5.5 49.8 %all-to-all-start = ((bf16[16,64,896]{2,1,0:T(8,128)(2,1)}), bf16[16,64,896]{2,1,0:T(8,128)(2,1)S(1)}, u32[]{:S(2)}, u32[]{:S(2)}) async-start(bf16[16,64,896]{2,1,0:T(8,128)(2,1)} %get-tuple-element.262), calls=%async_computation | async-start | bytes 3670016 | tf_op jit(solution)/shard_map/all_to_all | solution.py:760
  13.2 8.0 %collective-permute-start.2 = (bf16[1,704]{1,0:T(2,128)(2,1)S(1)}, bf16[1,704]{1,0:T(2,128)(2,1)S(1)}, u32[]{:S(2)}, u32[]{:S(2)}) collective-permute-start(bf16[1,704]{1,0:T(2,128)(2,1)S(1)} %broadcast_in_dim.122), channel_id=1, source_target_pairs={{0,1},{1,0},{2,3},{3,2},{4,5},{5,4},{6,7},{7,6},{8,9},{9,8},{10,11... | collective-permute-start | bytes 4232 | tf_op jit(solution)/shard_map/ppermute | solution.py:33
  15.2 9.2 %collective-permute-start = (bf16[64,2048]{1,0:T(8,128)(2,1)S(1)}, bf16[64,2048]{1,0:T(8,128)(2,1)S(1)}, u32[]{:S(2)}, u32[]{:S(2)}) collective-permute-start(bf16[64,2048]{1,0:T(8,128)(2,1)S(1)} %get-tuple-element.261), channel_id=1, source_target_pairs={{0,16},{16,0},{1,17},{17,1},{2,18},{18,2},{3,19},{19,3},{4,20},{20... | collective-permute-start | bytes 786440 | tf_op jit(solution)/shard_map/ppermute | solution.py:33
  18.9 10.1 %collective-permute-start.1 = (bf16[64,2048]{1,0:T(8,128)(2,1)S(1)}, bf16[64,2048]{1,0:T(8,128)(2,1)S(1)}, u32[]{:S(2)}, u32[]{:S(2)}) collective-permute-start(bf16[64,2048]{1,0:T(8,128)(2,1)S(1)} %get-tuple-element.577), channel_id=1, source_target_pairs={{0,16},{16,0},{1,17},{17,1},{2,18},{18,2},{3,19},{19,3},{4,20},{20... | collective-permute-start | bytes 786440 | tf_op jit(solution)/shard_map/ppermute | solution.py:33
  22.7 6.3 %collective-permute-start.4 = (bf16[4,704]{1,0:T(4,128)(2,1)S(1)}, bf16[4,704]{1,0:T(4,128)(2,1)S(1)}, u32[]{:S(2)}, u32[]{:S(2)}) collective-permute-start(bf16[4,704]{1,0:T(4,128)(2,1)S(1)} %maximum_select_fusion.7), channel_id=1, source_target_pairs={{0,16},{16,0},{1,17},{17,1},{2,18},{18,2},{3,19},{19,3},{4,20},{20... | collective-permute-start | bytes 16904 | tf_op jit(solution)/shard_map/ppermute | solution.py:33
  55.4 15.1 %collective-permute-start.6 = (bf16[128,2048]{1,0:T(8,128)(2,1)S(1)}, bf16[128,2048]{1,0:T(8,128)(2,1)S(1)}, u32[]{:S(2)}, u32[]{:S(2)}) collective-permute-start(bf16[128,2048]{1,0:T(8,128)(2,1)S(1)} %pad_maximum_fusion), channel_id=1, source_target_pairs={{0,2},{2,4},{4,6},{6,0},{1,3},{3,5},{5,7},{7,1},{8,10},{10,12},{12... | collective-permute-start | bytes 1572872 | tf_op jit(solution)/shard_map/ppermute | solution.py:53
  58.0 13.2 %collective-permute-start.5 = (bf16[128,2048]{1,0:T(8,128)(2,1)S(1)}, bf16[128,2048]{1,0:T(8,128)(2,1)S(1)}, u32[]{:S(2)}, u32[]{:S(2)}) collective-permute-start(bf16[128,2048]{1,0:T(8,128)(2,1)S(1)} %pad_maximum_fusion), channel_id=1, source_target_pairs={{0,1},{1,0},{2,3},{3,2},{4,5},{5,4},{6,7},{7,6},{8,9},{9,8},{10,11... | collective-permute-start | bytes 1572872 | tf_op jit(solution)/shard_map/ppermute | solution.py:33
  58.5 11.9 %collective-permute-start.7 = (bf16[8,704]{1,0:T(8,128)(2,1)S(1)}, bf16[8,704]{1,0:T(8,128)(2,1)S(1)}, u32[]{:S(2)}, u32[]{:S(2)}) collective-permute-start(bf16[8,704]{1,0:T(8,128)(2,1)S(1)} %maximum_select_fusion.6), channel_id=1, source_target_pairs={{0,2},{2,0},{4,6},{6,4},{1,3},{3,1},{5,7},{7,5},{8,10},{10,8},{12,... | collective-permute-start | bytes 33800 | tf_op jit(solution)/shard_map/ppermute | solution.py:78
  59.9 43.6 %collective-permute-start.15 = (bf16[1024,896]{1,0:T(8,128)(2,1)S(1)}, bf16[1024,896]{1,0:T(8,128)(2,1)}, u32[]{:S(2)}, u32[]{:S(2)}) collective-permute-start(bf16[1024,896]{1,0:T(8,128)(2,1)S(1)} %bitcast.157), channel_id=1, source_target_pairs={{0,16},{16,0},{1,17},{17,1},{2,18},{18,2},{3,19},{19,3},{4,20},{20... | collective-permute-start | bytes 5505032 | tf_op jit(solution)/shard_map/ppermute | solution.py:33
  72.3 15.2 %collective-permute-start.9 = (bf16[128,2048]{1,0:T(8,128)(2,1)S(1)}, bf16[128,2048]{1,0:T(8,128)(2,1)}, u32[]{:S(2)}, u32[]{:S(2)}) collective-permute-start(bf16[128,2048]{1,0:T(8,128)(2,1)S(1)} %collective-permute-done.6), channel_id=1, source_target_pairs={{0,2},{2,4},{4,6},{6,0},{1,3},{3,5},{5,7},{7,1},{8,10},{10,12},{12... | collective-permute-start | bytes 1572872 | tf_op jit(solution)/shard_map/ppermute | solution.py:53
  73.1 14.4 %collective-permute-start.8 = (bf16[128,2048]{1,0:T(8,128)(2,1)S(1)}, bf16[128,2048]{1,0:T(8,128)(2,1)S(1)}, u32[]{:S(2)}, u32[]{:S(2)}) collective-permute-start(bf16[128,2048]{1,0:T(8,128)(2,1)S(1)} %collective-permute-done.6), channel_id=1, source_target_pairs={{0,1},{1,0},{2,3},{3,2},{4,5},{5,4},{6,7},{7,6},{8,9},{9,8},{10,11... | collective-permute-start | bytes 1572872 | tf_op jit(solution)/shard_map/ppermute | solution.py:33
  74.7 12.8 %collective-permute-start.10 = (bf16[16,704]{1,0:T(8,128)(2,1)S(1)}, bf16[16,704]{1,0:T(8,128)(2,1)S(1)}, u32[]{:S(2)}, u32[]{:S(2)}) collective-permute-start(bf16[16,704]{1,0:T(8,128)(2,1)S(1)} %maximum_select_fusion.5), channel_id=1, source_target_pairs={{0,4},{2,6},{4,0},{6,2},{1,5},{3,7},{5,1},{7,3},{8,12},{10,14},{12... | collective-permute-start | bytes 67592 | tf_op jit(solution)/shard_map/ppermute | solution.py:78
  76.8 26.7 %collective-permute-start.13 = (bf16[256,2048]{1,0:T(8,128)(2,1)}, bf16[256,2048]{1,0:T(8,128)(2,1)}, u32[]{:S(2)}, u32[]{:S(2)}) collective-permute-start(bf16[256,2048]{1,0:T(8,128)(2,1)} %constant_dynamic-update-slice_fusion.refs_0_), channel_id=1, source_target_pairs={{0,8},{8,0},{1,9},{9,1},{2,10},{10,2},{3,11},{11,3},{4,12},{12,4},... | collective-permute-start | bytes 3145736 | tf_op jit(solution)/shard_map/ppermute | solution.py:33
  87.6 16.0 %collective-permute-start.12 = (bf16[128,2048]{1,0:T(8,128)(2,1)}, bf16[128,2048]{1,0:T(8,128)(2,1)}, u32[]{:S(2)}, u32[]{:S(2)}) collective-permute-start(bf16[128,2048]{1,0:T(8,128)(2,1)} %collective-permute-done.9), channel_id=1, source_target_pairs={{0,2},{2,4},{4,6},{6,0},{1,3},{3,5},{5,7},{7,1},{8,10},{10,12},{12... | collective-permute-start | bytes 1572872 | tf_op jit(solution)/shard_map/ppermute | solution.py:53
  87.7 15.8 %collective-permute-start.11 = (bf16[128,2048]{1,0:T(8,128)(2,1)}, bf16[128,2048]{1,0:T(8,128)(2,1)}, u32[]{:S(2)}, u32[]{:S(2)}) collective-permute-start(bf16[128,2048]{1,0:T(8,128)(2,1)} %collective-permute-done.9), channel_id=1, source_target_pairs={{0,1},{1,0},{2,3},{3,2},{4,5},{5,4},{6,7},{7,6},{8,9},{9,8},{10,11... | collective-permute-start | bytes 1572872 | tf_op jit(solution)/shard_map/ppermute | solution.py:33
  89.1 14.4 %collective-permute-start.14 = (bf16[256,2048]{1,0:T(8,128)(2,1)}, bf16[256,2048]{1,0:T(8,128)(2,1)}, u32[]{:S(2)}, u32[]{:S(2)}) collective-permute-start(bf16[256,2048]{1,0:T(8,128)(2,1)} %constant_dynamic-update-slice_fusion.2.refs_1_), channel_id=1, source_target_pairs={{0,8},{8,0},{1,9},{9,1},{2,10},{10,2},{3,11},{11,3},{4,12},{12,4},... | collective-permute-start | bytes 3145736 | tf_op jit(solution)/shard_map/ppermute | solution.py:33
  105.4 20.7 %collective-permute-start.18 = (bf16[256,2048]{1,0:T(8,128)(2,1)}, bf16[256,2048]{1,0:T(8,128)(2,1)S(1)}, u32[]{:S(2)}, u32[]{:S(2)}) collective-permute-start(bf16[256,2048]{1,0:T(8,128)(2,1)} %constant_dynamic-update-slice_fusion.4.refs_0_.refs_4_), channel_id=1, source_target_pairs={{0,8},{8,0},{1,9},{9,1},{2,10},{10,2},{3,11},{11,3},{4,12},{12,4},... | collective-permute-start | bytes 3145736 | tf_op jit(solution)/shard_map/ppermute | solution.py:33
  105.5 20.7 %collective-permute-start.17 = (bf16[128,2048]{1,0:T(8,128)(2,1)S(1)}, bf16[128,2048]{1,0:T(8,128)(2,1)S(1)}, u32[]{:S(2)}, u32[]{:S(2)}) collective-permute-start(bf16[128,2048]{1,0:T(8,128)(2,1)S(1)} %pad_maximum_fusion.1), channel_id=1, source_target_pairs={{0,2},{2,4},{4,6},{6,0},{1,3},{3,5},{5,7},{7,1},{8,10},{10,12},{12... | collective-permute-start | bytes 1572872 | tf_op jit(solution)/shard_map/ppermute | solution.py:53
  109.4 16.8 %collective-permute-start.16 = (bf16[128,2048]{1,0:T(8,128)(2,1)}, bf16[128,2048]{1,0:T(8,128)(2,1)S(1)}, u32[]{:S(2)}, u32[]{:S(2)}) collective-permute-start(bf16[128,2048]{1,0:T(8,128)(2,1)} %collective-permute-done.12), channel_id=1, source_target_pairs={{0,1},{1,0},{2,3},{3,2},{4,5},{5,4},{6,7},{7,6},{8,9},{9,8},{10,11... | collective-permute-start | bytes 1572872 | tf_op jit(solution)/shard_map/ppermute | solution.py:33
  127.3 32.7 %all-to-all-start.1 = ((bf16[16,64,512]{2,1,0:T(8,128)(2,1)}), bf16[16,64,512]{2,1,0:T(8,128)(2,1)}, u32[]{:S(2)}, u32[]{:S(2)}) async-start(bf16[16,64,512]{2,1,0:T(8,128)(2,1)} %get-tuple-element.324), calls=%async_computation.1 | async-start | bytes 2097152 | tf_op jit(solution)/shard_map/all_to_all | solution.py:760
  134.7 2.7 collective-permute-start.19
  135.1 28.7 %collective-permute-start.24 = (bf16[64,2048]{1,0:T(8,128)(2,1)S(1)}, bf16[64,2048]{1,0:T(8,128)(2,1)}, u32[]{:S(2)}, u32[]{:S(2)}) collective-permute-start(bf16[64,2048]{1,0:T(8,128)(2,1)S(1)} %copy-done.31), channel_id=1, source_target_pairs={{0,16},{16,0},{1,17},{17,1},{2,18},{18,2},{3,19},{19,3},{4,20},{20... | collective-permute-start | bytes 786440 | tf_op jit(solution)/shard_map/ppermute | solution.py:33
  161.7 29.5 %collective-permute-start.20 = (bf16[256,2048]{1,0:T(8,128)(2,1)}, bf16[256,2048]{1,0:T(8,128)(2,1)S(1)}, u32[]{:S(2)}, u32[]{:S(2)}) collective-permute-start(bf16[256,2048]{1,0:T(8,128)(2,1)} %constant_dynamic-update-slice_fusion.8.refs_0_), channel_id=1, source_target_pairs={{0,1},{1,0},{2,3},{3,2},{4,5},{5,4},{6,7},{7,6},{8,9},{9,8},{10,11... | collective-permute-start | bytes 3145736 | tf_op jit(solution)/shard_map/ppermute | solution.py:33
  162.3 29.0 %collective-permute-start.23 = (bf16[1024,512]{1,0:T(8,128)(2,1)}, bf16[1024,512]{1,0:T(8,128)(2,1)}, u32[]{:S(2)}, u32[]{:S(2)}) collective-permute-start(bf16[1024,512]{1,0:T(8,128)(2,1)} %bitcast.15.own_ref.refs_9_), channel_id=1, source_target_pairs={{0,16},{16,0},{1,17},{17,1},{2,18},{18,2},{3,19},{19,3},{4,20},{20... | collective-permute-start | bytes 3145736 | tf_op jit(solution)/shard_map/ppermute | solution.py:33
  165.7 21.9 %collective-permute-start.22 = (bf16[128,2048]{1,0:T(8,128)(2,1)S(1)}, bf16[128,2048]{1,0:T(8,128)(2,1)S(1)}, u32[]{:S(2)}, u32[]{:S(2)}) collective-permute-start(bf16[128,2048]{1,0:T(8,128)(2,1)S(1)} %copy-done.7), channel_id=1, source_target_pairs={{0,6},{2,0},{4,2},{6,4},{1,7},{3,1},{5,3},{7,5},{8,14},{10,8},{12,... | collective-permute-start | bytes 1572872 | tf_op jit(solution)/shard_map/ppermute | solution.py:864
  166.5 24.7 %collective-permute-start.21 = (bf16[128,2048]{1,0:T(8,128)(2,1)S(1)}, bf16[128,2048]{1,0:T(8,128)(2,1)S(1)}, u32[]{:S(2)}, u32[]{:S(2)}) collective-permute-start(bf16[128,2048]{1,0:T(8,128)(2,1)S(1)} %copy-done.29), channel_id=1, source_target_pairs={{0,2},{2,4},{4,6},{6,0},{1,3},{3,5},{5,7},{7,1},{8,10},{10,12},{12... | collective-permute-start | bytes 1572872 | tf_op jit(solution)/shard_map/ppermute | solution.py:53
  192.3 15.9 %collective-permute-start.28 = (bf16[256,2048]{1,0:T(8,128)(2,1)S(1)}, bf16[256,2048]{1,0:T(8,128)(2,1)S(1)}, u32[]{:S(2)}, u32[]{:S(2)}) collective-permute-start(bf16[256,2048]{1,0:T(8,128)(2,1)S(1)} %constant_dynamic-update-slice_fusion.10.refs_4_), channel_id=1, source_target_pairs={{0,8},{8,0},{1,9},{9,1},{2,10},{10,2},{3,11},{11,3},{4,12},{12,4},... | collective-permute-start | bytes 3145736 | tf_op jit(solution)/shard_map/ppermute | solution.py:33
  192.4 25.7 %collective-permute-start.25 = (bf16[256,2048]{1,0:T(8,128)(2,1)S(1)}, bf16[256,2048]{1,0:T(8,128)(2,1)}, u32[]{:S(2)}, u32[]{:S(2)}) collective-permute-start(bf16[256,2048]{1,0:T(8,128)(2,1)S(1)} %constant_dynamic-update-slice_fusion.10.refs_4_), channel_id=1, source_target_pairs={{0,1},{1,0},{2,3},{3,2},{4,5},{5,4},{6,7},{7,6},{8,9},{9,8},{10,11... | collective-permute-start | bytes 3145736 | tf_op jit(solution)/shard_map/ppermute | solution.py:33
  193.0 25.1 %collective-permute-start.26 = (bf16[256,2048]{1,0:T(8,128)(2,1)}, bf16[256,2048]{1,0:T(8,128)(2,1)}, u32[]{:S(2)}, u32[]{:S(2)}) collective-permute-start(bf16[256,2048]{1,0:T(8,128)(2,1)} %constant_dynamic-update-slice_fusion.8.refs_0_), channel_id=1, source_target_pairs={{0,8},{8,0},{1,9},{9,1},{2,10},{10,2},{3,11},{11,3},{4,12},{12,4},... | collective-permute-start | bytes 3145736 | tf_op jit(solution)/shard_map/ppermute | solution.py:33
  193.8 24.3 %collective-permute-start.27 = (bf16[256,2048]{1,0:T(8,128)(2,1)S(1)}, bf16[256,2048]{1,0:T(8,128)(2,1)}, u32[]{:S(2)}, u32[]{:S(2)}) collective-permute-start(bf16[256,2048]{1,0:T(8,128)(2,1)S(1)} %copy-done.49), channel_id=1, source_target_pairs={{0,8},{8,0},{1,9},{9,1},{2,10},{10,2},{3,11},{11,3},{4,12},{12,4},... | collective-permute-start | bytes 3145736 | tf_op jit(solution)/shard_map/ppermute | solution.py:33
  218.1 2.9 collective-permute-start.29
  221.0 17.6 %collective-permute-start.30 = (bf16[256,2048]{1,0:T(8,128)(2,1)}, bf16[256,2048]{1,0:T(8,128)(2,1)}, u32[]{:S(2)}, u32[]{:S(2)}) collective-permute-start(bf16[256,2048]{1,0:T(8,128)(2,1)} %get-tuple-element.371), channel_id=1, source_target_pairs={{0,8},{8,0},{1,9},{9,1},{2,10},{10,2},{3,11},{11,3},{4,12},{12,4},... | collective-permute-start | bytes 3145736 | tf_op jit(solution)/shard_map/ppermute | solution.py:33
  221.1 17.5 %collective-permute-start.31 = (bf16[256,2048]{1,0:T(8,128)(2,1)}, bf16[256,2048]{1,0:T(8,128)(2,1)}, u32[]{:S(2)}, u32[]{:S(2)}) collective-permute-start(bf16[256,2048]{1,0:T(8,128)(2,1)} %get-tuple-element.372), channel_id=1, source_target_pairs={{0,8},{8,0},{1,9},{9,1},{2,10},{10,2},{3,11},{11,3},{4,12},{12,4},... | collective-permute-start | bytes 3145736 | tf_op jit(solution)/shard_map/ppermute | solution.py:33
  222.0 16.6 %collective-permute-start.32 = (bf16[256,2048]{1,0:T(8,128)(2,1)}, bf16[256,2048]{1,0:T(8,128)(2,1)S(1)}, u32[]{:S(2)}, u32[]{:S(2)}) collective-permute-start(bf16[256,2048]{1,0:T(8,128)(2,1)} %get-tuple-element.373), channel_id=1, source_target_pairs={{0,8},{8,0},{1,9},{9,1},{2,10},{10,2},{3,11},{11,3},{4,12},{12,4},... | collective-permute-start | bytes 3145736 | tf_op jit(solution)/shard_map/ppermute | solution.py:33
  222.1 16.5 %collective-permute-start.33 = (bf16[256,2048]{1,0:T(8,128)(2,1)}, bf16[256,2048]{1,0:T(8,128)(2,1)S(1)}, u32[]{:S(2)}, u32[]{:S(2)}) collective-permute-start(bf16[256,2048]{1,0:T(8,128)(2,1)} %get-tuple-element.374), channel_id=1, source_target_pairs={{0,8},{8,0},{1,9},{9,1},{2,10},{10,2},{3,11},{11,3},{4,12},{12,4},... | collective-permute-start | bytes 3145736 | tf_op jit(solution)/shard_map/ppermute | solution.py:33
  242.9 47.8 %collective-permute-start.35 = (bf16[512,2048]{1,0:T(8,128)(2,1)S(1)}, bf16[512,2048]{1,0:T(8,128)(2,1)}, u32[]{:S(2)}, u32[]{:S(2)}) collective-permute-start(bf16[512,2048]{1,0:T(8,128)(2,1)S(1)} %add_convert_fusion.1), channel_id=1, source_target_pairs={{0,1},{1,0},{2,3},{3,2},{4,5},{5,4},{6,7},{7,6},{8,9},{9,8},{10,11... | collective-permute-start | bytes 6291464 | tf_op jit(solution)/shard_map/ppermute | solution.py:33
  258.2 47.7 %collective-permute-start.34 = (bf16[4,2,128,1024]{3,2,1,0:T(8,128)(2,1)}, bf16[4,2,128,1024]{3,2,1,0:T(8,128)(2,1)}, u32[]{:S(2)}, u32[]{:S(2)}) collective-permute-start(bf16[4,2,128,1024]{3,2,1,0:T(8,128)(2,1)} %get-tuple-element.388), channel_id=1, source_target_pairs={{0,16},{16,0},{1,17},{17,1},{2,18},{18,2},{3,19},{19,3},{4,20},{20... | collective-permute-start | bytes 6291464 | tf_op jit(solution)/shard_map/ppermute | solution.py:33
  292.2 13.7 %collective-permute-start.36 = (bf16[128,2048]{1,0:T(8,128)(2,1)S(1)}, bf16[128,2048]{1,0:T(8,128)(2,1)S(1)}, u32[]{:S(2)}, u32[]{:S(2)}) collective-permute-start(bf16[128,2048]{1,0:T(8,128)(2,1)S(1)} %convert_add_fusion.10), channel_id=1, source_target_pairs={{2,0},{4,2},{6,4},{0,6},{3,1},{5,3},{7,5},{1,7},{10,8},{12,10},{14... | collective-permute-start | bytes 1572872 | tf_op jit(solution)/shard_map/ppermute | solution.py:70
  310.0 51.3 %all-to-all-start.2 = ((bf16[4,2,128,1024]{3,2,1,0:T(8,128)(2,1)}), bf16[4,2,128,1024]{3,2,1,0:T(8,128)(2,1)S(1)}, u32[]{:S(2)}, u32[]{:S(2)}) async-start(bf16[4,2,128,1024]{3,2,1,0:T(8,128)(2,1)} %add_convert_fusion), calls=%async_computation.2 | async-start | bytes 4194304 | tf_op jit(solution)/shard_map/all_to_all | solution.py:767
  314.6 21.9 %collective-permute-start.37 = (bf16[4,2,128,384]{3,2,1,0:T(8,128)(2,1)}, bf16[4,2,128,384]{3,2,1,0:T(8,128)(2,1)S(1)}, u32[]{:S(2)}, u32[]{:S(2)}) collective-permute-start(bf16[4,2,128,384]{3,2,1,0:T(8,128)(2,1)} %get-tuple-element.424), channel_id=1, source_target_pairs={{0,16},{16,0},{1,17},{17,1},{2,18},{18,2},{3,19},{19,3},{4,20},{20... | collective-permute-start | bytes 2359304 | tf_op jit(solution)/shard_map/ppermute | solution.py:33
  341.6 12.1 %collective-permute-start.38 = (bf16[256,2048]{1,0:T(8,128)(2,1)}, bf16[256,2048]{1,0:T(8,128)(2,1)}, u32[]{:S(2)}, u32[]{:S(2)}) collective-permute-start(bf16[256,2048]{1,0:T(8,128)(2,1)} %get-tuple-element.427), channel_id=1, source_target_pairs={{0,8},{8,0},{1,9},{9,1},{2,10},{10,2},{3,11},{11,3},{4,12},{12,4},... | collective-permute-start | bytes 3145736 | tf_op jit(solution)/shard_map/ppermute | solution.py:33
  341.6 12.0 %collective-permute-start.39 = (bf16[256,2048]{1,0:T(8,128)(2,1)}, bf16[256,2048]{1,0:T(8,128)(2,1)}, u32[]{:S(2)}, u32[]{:S(2)}) collective-permute-start(bf16[256,2048]{1,0:T(8,128)(2,1)} %get-tuple-element.428), channel_id=1, source_target_pairs={{0,8},{8,0},{1,9},{9,1},{2,10},{10,2},{3,11},{11,3},{4,12},{12,4},... | collective-permute-start | bytes 3145736 | tf_op jit(solution)/shard_map/ppermute | solution.py:33
  342.1 11.5 %collective-permute-start.40 = (bf16[256,2048]{1,0:T(8,128)(2,1)}, bf16[256,2048]{1,0:T(8,128)(2,1)S(1)}, u32[]{:S(2)}, u32[]{:S(2)}) collective-permute-start(bf16[256,2048]{1,0:T(8,128)(2,1)} %get-tuple-element.429), channel_id=1, source_target_pairs={{0,8},{8,0},{1,9},{9,1},{2,10},{10,2},{3,11},{11,3},{4,12},{12,4},... | collective-permute-start | bytes 3145736 | tf_op jit(solution)/shard_map/ppermute | solution.py:33
  342.2 11.4 %collective-permute-start.41 = (bf16[256,2048]{1,0:T(8,128)(2,1)}, bf16[256,2048]{1,0:T(8,128)(2,1)}, u32[]{:S(2)}, u32[]{:S(2)}) collective-permute-start(bf16[256,2048]{1,0:T(8,128)(2,1)} %get-tuple-element.430), channel_id=1, source_target_pairs={{0,8},{8,0},{1,9},{9,1},{2,10},{10,2},{3,11},{11,3},{4,12},{12,4},... | collective-permute-start | bytes 3145736 | tf_op jit(solution)/shard_map/ppermute | solution.py:33
  367.0 29.2 %all-to-all-start.3 = ((bf16[4,2,128,384]{3,2,1,0:T(8,128)(2,1)}), bf16[4,2,128,384]{3,2,1,0:T(8,128)(2,1)S(1)}, u32[]{:S(2)}, u32[]{:S(2)}) async-start(bf16[4,2,128,384]{3,2,1,0:T(8,128)(2,1)} %add_convert_fusion.4), calls=%async_computation.3 | async-start | bytes 1572864 | tf_op jit(solution)/shard_map/all_to_all | solution.py:767
  370.5 25.7 %collective-permute-start.42 = (bf16[256,2048]{1,0:T(8,128)(2,1)}, bf16[256,2048]{1,0:T(8,128)(2,1)}, u32[]{:S(2)}, u32[]{:S(2)}) collective-permute-start(bf16[256,2048]{1,0:T(8,128)(2,1)} %add_convert_fusion.2), channel_id=1, source_target_pairs={{0,1},{1,0},{2,3},{3,2},{4,5},{5,4},{6,7},{7,6},{8,9},{9,8},{10,11... | collective-permute-start | bytes 3145736 | tf_op jit(solution)/shard_map/ppermute | solution.py:33
  372.0 24.1 %collective-permute-start.43 = (bf16[128,2048]{1,0:T(8,128)(2,1)}, bf16[128,2048]{1,0:T(8,128)(2,1)S(1)}, u32[]{:S(2)}, u32[]{:S(2)}) collective-permute-start(bf16[128,2048]{1,0:T(8,128)(2,1)} %convert_add_fusion.9), channel_id=1, source_target_pairs={{2,0},{4,2},{6,4},{0,6},{3,1},{5,3},{7,5},{1,7},{10,8},{12,10},{14... | collective-permute-start | bytes 1572872 | tf_op jit(solution)/shard_map/ppermute | solution.py:70
  401.1 31.7 %collective-permute-start.44 = (bf16[256,2048]{1,0:T(8,128)(2,1)}, bf16[256,2048]{1,0:T(8,128)(2,1)}, u32[]{:S(2)}, u32[]{:S(2)}) collective-permute-start(bf16[256,2048]{1,0:T(8,128)(2,1)} %add_convert_fusion.3), channel_id=1, source_target_pairs={{0,1},{1,0},{2,3},{3,2},{4,5},{5,4},{6,7},{7,6},{8,9},{9,8},{10,11... | collective-permute-start | bytes 3145736 | tf_op jit(solution)/shard_map/ppermute | solution.py:33
  404.4 32.1 %collective-permute-start.61 = (bf16[64,2048]{1,0:T(8,128)(2,1)S(1)}, bf16[64,2048]{1,0:T(8,128)(2,1)S(1)}, u32[]{:S(2)}, u32[]{:S(2)}) collective-permute-start(bf16[64,2048]{1,0:T(8,128)(2,1)S(1)} %fusion.30), channel_id=1, source_target_pairs={{0,16},{16,0},{1,17},{17,1},{2,18},{18,2},{3,19},{19,3},{4,20},{20... | collective-permute-start | bytes 786440 | tf_op jit(solution)/shard_map/ppermute | solution.py:33
  405.0 18.7 %collective-permute-start.45 = (bf16[128,2048]{1,0:T(8,128)(2,1)}, bf16[128,2048]{1,0:T(8,128)(2,1)S(1)}, u32[]{:S(2)}, u32[]{:S(2)}) collective-permute-start(bf16[128,2048]{1,0:T(8,128)(2,1)} %convert_add_fusion.8), channel_id=1, source_target_pairs={{2,0},{4,2},{6,4},{0,6},{3,1},{5,3},{7,5},{1,7},{10,8},{12,10},{14... | collective-permute-start | bytes 1572872 | tf_op jit(solution)/shard_map/ppermute | solution.py:70
  410.9 21.8 %collective-permute-start.46 = (bf16[128,2048]{1,0:T(8,128)(2,1)S(1)}, bf16[128,2048]{1,0:T(8,128)(2,1)S(1)}, u32[]{:S(2)}, u32[]{:S(2)}) collective-permute-start(bf16[128,2048]{1,0:T(8,128)(2,1)S(1)} %convert_add_fusion.7), channel_id=1, source_target_pairs={{2,0},{4,2},{6,4},{0,6},{3,1},{5,3},{7,5},{1,7},{10,8},{12,10},{14... | collective-permute-start | bytes 1572872 | tf_op jit(solution)/shard_map/ppermute | solution.py:70
  435.9 23.1 %collective-permute-start.51 = (bf16[4,2,64,1024]{3,2,0,1:T(8,128)(2,1)S(1)}, bf16[4,2,64,1024]{3,2,0,1:T(8,128)(2,1)S(1)}, u32[]{:S(2)}, u32[]{:S(2)}) collective-permute-start(bf16[4,2,64,1024]{3,2,0,1:T(8,128)(2,1)S(1)} %get-tuple-element.479), channel_id=1, source_target_pairs={{0,1},{1,0},{2,3},{3,2},{4,5},{5,4},{6,7},{7,6},{8,9},{9,8},{10,11... | collective-permute-start | bytes 3145736 | tf_op jit(solution)/shard_map/ppermute | solution.py:33
  437.4 6.6 %collective-permute-start.50 = (f32[1,4,2,640]{3,2,1,0:T(2,128)S(1)}, f32[1,4,2,640]{3,2,1,0:T(2,128)S(1)}, u32[]{:S(2)}, u32[]{:S(2)}) collective-permute-start(f32[1,4,2,640]{3,2,1,0:T(2,128)S(1)} %get-tuple-element.475), channel_id=1, source_target_pairs={{0,16},{16,0},{1,17},{17,1},{2,18},{18,2},{3,19},{19,3},{4,20},{20... | collective-permute-start | bytes 61448 | tf_op jit(solution)/shard_map/ppermute | solution.py:33
  438.9 6.4 %collective-permute-start.49 = (bf16[64,2048]{1,0:T(8,128)(2,1)S(1)}, bf16[64,2048]{1,0:T(8,128)(2,1)S(1)}, u32[]{:S(2)}, u32[]{:S(2)}) collective-permute-start(bf16[64,2048]{1,0:T(8,128)(2,1)S(1)} %slice.261), channel_id=1, source_target_pairs={{0,16},{16,0},{1,17},{17,1},{2,18},{18,2},{3,19},{19,3},{4,20},{20... | collective-permute-start | bytes 786440 | tf_op jit(solution)/shard_map/ppermute | solution.py:33
  439.4 10.8 %collective-permute-start.48 = (bf16[128,2048]{1,0:T(8,128)(2,1)S(1)}, bf16[128,2048]{1,0:T(8,128)(2,1)S(1)}, u32[]{:S(2)}, u32[]{:S(2)}) collective-permute-start(bf16[128,2048]{1,0:T(8,128)(2,1)S(1)} %convert_add_fusion.6), channel_id=1, source_target_pairs={{2,0},{4,2},{6,4},{0,6},{3,1},{5,3},{7,5},{1,7},{10,8},{12,10},{14... | collective-permute-start | bytes 1572872 | tf_op jit(solution)/shard_map/ppermute | solution.py:70
  459.2 8.4 %collective-permute-start.53 = (f32[1,4,640]{2,0,1:T(1,128)S(1)}, f32[1,4,640]{2,0,1:T(1,128)S(1)}, u32[]{:S(2)}, u32[]{:S(2)}) collective-permute-start(f32[1,4,640]{2,0,1:T(1,128)S(1)} %get-tuple-element.489), channel_id=1, source_target_pairs={{0,1},{1,0},{2,3},{3,2},{4,5},{5,4},{6,7},{7,6},{8,9},{9,8},{10,11... | collective-permute-start | bytes 30728 | tf_op jit(solution)/shard_map/ppermute | solution.py:33
  459.8 15.8 %collective-permute-start.57 = (bf16[4,2,64,384]{3,2,0,1:T(8,128)(2,1)}, bf16[4,2,64,384]{3,2,0,1:T(8,128)(2,1)S(1)}, u32[]{:S(2)}, u32[]{:S(2)}) collective-permute-start(bf16[4,2,64,384]{3,2,0,1:T(8,128)(2,1)} %get-tuple-element.492), channel_id=1, source_target_pairs={{0,1},{1,0},{2,3},{3,2},{4,5},{5,4},{6,7},{7,6},{8,9},{9,8},{10,11... | collective-permute-start | bytes 1179656 | tf_op jit(solution)/shard_map/ppermute | solution.py:33
  461.3 14.2 %collective-permute-start.52 = (bf16[128,2048]{1,0:T(8,128)(2,1)S(1)}, bf16[128,2048]{1,0:T(8,128)(2,1)S(1)}, u32[]{:S(2)}, u32[]{:S(2)}) collective-permute-start(bf16[128,2048]{1,0:T(8,128)(2,1)S(1)} %convert_add_fusion.2), channel_id=1, source_target_pairs={{2,0},{4,2},{6,4},{0,6},{3,1},{5,3},{7,5},{1,7},{10,8},{12,10},{14... | collective-permute-start | bytes 1572872 | tf_op jit(solution)/shard_map/ppermute | solution.py:70
  464.2 4.4 collective-permute-start.58
  467.7 7.9 %collective-permute-start.56 = (f32[1,640]{1,0:T(1,128)S(1)}, f32[1,640]{1,0:T(1,128)S(1)}, u32[]{:S(2)}, u32[]{:S(2)}) collective-permute-start(f32[1,640]{1,0:T(1,128)S(1)} %get-tuple-element.596), channel_id=1, source_target_pairs={{0,6},{2,0},{4,2},{6,4},{1,7},{3,1},{5,3},{7,5},{8,14},{10,8},{12,... | collective-permute-start | bytes 7688 | tf_op jit(solution)/shard_map/ppermute | solution.py:995
  467.7 7.8 %collective-permute-start.55 = (f32[1,640]{1,0:T(1,128)S(1)}, f32[1,640]{1,0:T(1,128)S(1)}, u32[]{:S(2)}, u32[]{:S(2)}) collective-permute-start(f32[1,640]{1,0:T(1,128)S(1)} %get-tuple-element.597), channel_id=1, source_target_pairs={{0,4},{2,6},{4,0},{6,2},{1,5},{3,7},{5,1},{7,3},{8,12},{10,14},{12... | collective-permute-start | bytes 7688 | tf_op jit(solution)/shard_map/ppermute | solution.py:995
  468.6 7.0 %collective-permute-start.54 = (f32[1,640]{1,0:T(1,128)S(1)}, f32[1,640]{1,0:T(1,128)S(1)}, u32[]{:S(2)}, u32[]{:S(2)}) collective-permute-start(f32[1,640]{1,0:T(1,128)S(1)} %get-tuple-element.598), channel_id=1, source_target_pairs={{0,2},{2,4},{4,6},{6,0},{1,3},{3,5},{5,7},{7,1},{8,10},{10,12},{12... | collective-permute-start | bytes 7688 | tf_op jit(solution)/shard_map/ppermute | solution.py:995
  476.4 7.1 %collective-permute-start.59 = (bf16[64,2048]{1,0:T(8,128)(2,1)S(1)}, bf16[64,2048]{1,0:T(8,128)(2,1)S(1)}, u32[]{:S(2)}, u32[]{:S(2)}) collective-permute-start(bf16[64,2048]{1,0:T(8,128)(2,1)S(1)} %slice.260), channel_id=1, source_target_pairs={{0,16},{16,0},{1,17},{17,1},{2,18},{18,2},{3,19},{19,3},{4,20},{20... | collective-permute-start | bytes 786440 | tf_op jit(solution)/shard_map/ppermute | solution.py:33
  479.3 6.1 %collective-permute-start.60 = (bf16[2,4,64,384]{3,2,1,0:T(8,128)(2,1)S(1)}, bf16[2,4,64,384]{3,2,1,0:T(8,128)(2,1)S(1)}, u32[]{:S(2)}, u32[]{:S(2)}) collective-permute-start(bf16[2,4,64,384]{3,2,1,0:T(8,128)(2,1)S(1)} %get-tuple-element.570), channel_id=1, source_target_pairs={{0,8},{8,0},{1,9},{9,1},{2,10},{10,2},{3,11},{11,3},{4,12},{12,4},... | collective-permute-start | bytes 1179656 | tf_op jit(solution)/shard_map/ppermute | solution.py:33
  (57 other events, 525.2 us)
